TPU v7x, 32 devices: a whole 2x2x4 slice. The times are simulated.
32 devices in a mesh: exp: 2 (over core), row: 4 (over y, x), col: 4 (over z).
Axes of the slice: x: 2, y: 2, z: 4, core: 2. Of those that a mesh axis runs over, the one named last changes fastest.
Arguments:
- inputs: bfloat16 [4096, 2560], P(('exp', 'row'), 'col'), may hold values from -30 to 30
- routes: int32 [4096, 6], P(('exp', 'row')), may hold values from 0 to 15, all different within a row; in each aligned block of 512 rows (0 to 511, 512 to 1023, ...) at most 256 rows name the same one
- w_query: bfloat16 [2560, 2560], P('col', 'row'), may hold values from -0.15625 to 0.15625
- w_key: bfloat16 [2560, 512], P('col', 'row'), may hold values from -0.15625 to 0.15625
- w_value: bfloat16 [2560, 512], P('col', 'row'), may hold values from -0.125 to 0.125
- w_output: bfloat16 [2560, 2560], P('row', 'col'), may hold values from -0.625 to 0.625
- gain_attn: float32 [2560], P('col'), may hold values from 0.5 to 1.5
- gain_moe: float32 [2560], P('col'), may hold values from 0.5 to 1.5
- w_router: float32 [2560, 16], P('col'), may hold values from -0.0625 to 0.0625
- shared_gate: bfloat16 [2560, 3072], P('col', 'row'), may hold values from -0.125 to 0.125
- shared_up: bfloat16 [2560, 3072], P('col', 'row'), may hold values from -0.125 to 0.125
- shared_down: bfloat16 [3072, 2560], P('row', 'col'), may hold values from -0.21875 to 0.21875
- expert_gate: bfloat16 [16, 2560, 1536], P(('exp', 'row'), None, 'col'), may hold values from -0.125 to 0.125
- expert_up: bfloat16 [16, 2560, 1536], P(('exp', 'row'), None, 'col'), may hold values from -0.125 to 0.125
- expert_down: bfloat16 [16, 1536, 2560], P(('exp', 'row'), 'col'), may hold values from -0.3125 to 0.3125
- out_grad: bfloat16 [4096, 2560], P(('exp', 'row'), 'col'), may hold values from -6 to 6
Outputs:
- output: bfloat16 [4096, 2560], P(('exp', 'row'), 'col')
- grad_inputs: bfloat16 [4096, 2560], P(('exp', 'row'), 'col')
- grad_query: float32 [2560, 2560], P('col', 'row')
- grad_key: float32 [2560, 512], P('col', 'row')
- grad_value: float32 [2560, 512], P('col', 'row')
- grad_output: float32 [2560, 2560], P('row', 'col')
- grad_gain_attn: float32 [2560], P('col')
- grad_gain_moe: float32 [2560], P('col')
- grad_router: float32 [2560, 16], P('col')
- grad_shared_gate: float32 [2560, 3072], P('col', 'row')
- grad_shared_up: float32 [2560, 3072], P('col', 'row')
- grad_shared_down: float32 [3072, 2560], P('row', 'col')
- grad_expert_gate: float32 [16, 2560, 1536], P(('exp', 'row'), None, 'col')
- grad_expert_up: float32 [16, 2560, 1536], P(('exp', 'row'), None, 'col')
- grad_expert_down: float32 [16, 1536, 2560], P(('exp', 'row'), 'col')
Inputs may be any that keep to these rules, and one draw needn't show every extreme that they name: `routes`: in each aligned block of 512 rows no expert is named by more than 256 rows, a bound that some block reaches.
All inputs are finite; a program needn't handle non-finite values.
Results may differ from a plain program's by a relative error of at most 0.02.
Values may be sent and summed in bfloat16 or wider, within the bound.
No kernel may reach another device: no remote copies, remote signals or barrier semaphores. Data moves between devices by JAX's collectives and lax.ppermute only.
A program may use at most 448 MiB of HBM per device.

v0:
```python
import jax
import jax.numpy as jnp
from jax import lax
from jax.sharding import PartitionSpec as P

D = 2560
HEAD_DIM = 128


eps = 1e-05
theta = 500000.0
highest = lax.Precision.HIGHEST
masked_value = -1e30


def for_sending(x):

    def short(part):
        return part.astype(jnp.bfloat16) if part.dtype == jnp.float32 else part

    return jax.tree.map(short, x)


def row_gather(source):
    return lax.all_gather(source, "row", axis=0, tiled=True)


def col_gather(source):
    return jax.tree.map(
        lambda part, own: part.astype(own.dtype),
        lax.all_gather(for_sending(source), "col", axis=0, tiled=True),
        source,
    )


def col_reduce(term_fn, row_count):
    return lax.psum_scatter(
        term_fn(jnp.int32(0), row_count * lax.axis_size("col")),
        "col",
        scatter_dimension=0,
        tiled=True,
    )


def row_reduce(term_fn, row_count):
    return lax.psum_scatter(
        term_fn(jnp.int32(0), row_count * lax.axis_size("row")),
        "row",
        scatter_dimension=0,
        tiled=True,
    )


def col_total(source):
    return lax.psum(source, "col")


def feature_gather(source):
    return lax.all_gather(source, "col", axis=1, tiled=True)


def feature_sum(source):
    return lax.psum_scatter(
        source.astype(jnp.bfloat16), "col", scatter_dimension=1, tiled=True
    ).astype(jnp.float32)


def send_experts(source):
    return lax.all_to_all(source, ("exp", "row"), split_axis=1, concat_axis=1, tiled=True)


def return_rows(source):
    return lax.all_to_all(source, ("exp", "row"), split_axis=1, concat_axis=1, tiled=True)


def times_weight(gathered, weight, contract):

    def times_partial_term(offset, length):
        return lax.dot_general(
            gathered, weight, (((1,), (contract,)), ((), ())), preferred_element_type=jnp.float32
        )

    return times_partial_term


def slice_term(source):

    def slice_partial_term(offset, length):
        return source

    return slice_partial_term


def rms_forward(values, gain):
    squares = col_total(jnp.sum(values * values, axis=1))
    inv_rms = lax.rsqrt(squares / D + eps)
    return (values * inv_rms[:, None] * gain[None, :], inv_rms)


def rms_backward(values, inv_rms, gain, grad_norm):
    scaled_grad = grad_norm * gain[None, :]
    inner_sum = col_total(jnp.sum(scaled_grad * values, axis=1))
    grad_values = inv_rms[:, None] * (
        scaled_grad - values * (inv_rms * inv_rms * inner_sum / D)[:, None]
    )
    grad_gain = jnp.sum(grad_norm * values * inv_rms[:, None], axis=0)
    return (grad_values, grad_gain)


def rope_tables(positions, head_width):
    half_width = head_width // 2
    frequency = theta ** (-2.0 * jnp.arange(half_width, dtype=jnp.float32) / head_width)
    angles = positions.astype(jnp.float32)[:, None] * frequency[None, :]
    return (jnp.cos(angles), jnp.sin(angles))


def rotate(source, cosines, sine_part):
    half_width = source.shape[-1] // 2
    first_half = source[..., :half_width]
    second_half = source[..., half_width:]
    cos_view = cosines[:, None, :]
    sin_view = sine_part[:, None, :]
    return jnp.concatenate(
        [
            first_half * cos_view - second_half * sin_view,
            first_half * sin_view + second_half * cos_view,
        ],
        axis=-1,
    )


def unrotate(source, cosines, sine_part):
    half_width = source.shape[-1] // 2
    first_half = source[..., :half_width]
    second_half = source[..., half_width:]
    cos_view = cosines[:, None, :]
    sin_view = sine_part[:, None, :]
    return jnp.concatenate(
        [
            first_half * cos_view + second_half * sin_view,
            second_half * cos_view - first_half * sin_view,
        ],
        axis=-1,
    )


def silu_back(gate_pre, up_pre, grad_hidden):
    sigmoid_vals = jax.nn.sigmoid(gate_pre)
    grad_gate = grad_hidden * up_pre * sigmoid_vals * (1.0 + gate_pre * (1.0 - sigmoid_vals))
    grad_up = grad_hidden * gate_pre * sigmoid_vals
    return (grad_gate.astype(jnp.bfloat16), grad_up.astype(jnp.bfloat16))


def masked_scores(query_part, key_rows, first_row):
    scores = jnp.einsum("qkgd,skd->kgqs", query_part, key_rows, preferred_element_type=jnp.float32)
    query_pos = first_row + jnp.arange(query_part.shape[0])
    key_pos = jnp.arange(key_rows.shape[0])
    allowed = key_pos[None, :] <= query_pos[:, None]
    return jnp.where(allowed[None, None], scores, masked_value)


def route_slots(routes, n_experts, local_count):
    flat_routes = routes.reshape(-1)
    one_hot = (flat_routes[:, None] == jnp.arange(n_experts)[None, :]).astype(jnp.int32)
    slot_rank = jnp.sum((jnp.cumsum(one_hot, axis=0) - one_hot) * one_hot, axis=1)
    return (flat_routes % local_count, flat_routes // local_count, slot_rank)


def dispatch(route_rows, slots, lead_shape):
    local_of, group_of, slot_rank = slots
    buffer_rows = jnp.zeros(lead_shape + (route_rows.shape[1],), route_rows.dtype)
    return buffer_rows.at[local_of, group_of, slot_rank].set(route_rows)


def collect(buffer_rows, slots, top_count):
    local_of, group_of, slot_rank = slots
    picked = buffer_rows[local_of, group_of, slot_rank]
    return picked.reshape(-1, top_count, picked.shape[-1])


def expert_forward(expert_rows, expert_gate, expert_up, expert_down):
    gate_pre = jnp.einsum(
        "erd,edf->erf", expert_rows, expert_gate, preferred_element_type=jnp.float32
    )
    up_pre = jnp.einsum("erd,edf->erf", expert_rows, expert_up, preferred_element_type=jnp.float32)
    hidden = (jax.nn.silu(gate_pre) * up_pre).astype(jnp.bfloat16)
    partial_out = jnp.einsum(
        "erf,efd->erd", hidden, expert_down, preferred_element_type=jnp.float32
    ).astype(jnp.bfloat16)
    return (gate_pre, up_pre, hidden, partial_out)


def expert_gradient_pass(
    expert_rows, grad_rows_in, gate_pre, up_pre, hidden, expert_gate, expert_up, expert_down
):
    grad_hidden = jnp.einsum(
        "erd,efd->erf", grad_rows_in, expert_down, preferred_element_type=jnp.float32
    )
    grad_down = jnp.einsum("erf,erd->efd", hidden, grad_rows_in, preferred_element_type=jnp.float32)
    grad_gate_pre, grad_up_pre = silu_back(gate_pre, up_pre, grad_hidden)
    grad_gate = jnp.einsum(
        "erd,erf->edf", expert_rows, grad_gate_pre, preferred_element_type=jnp.float32
    )
    grad_up = jnp.einsum(
        "erd,erf->edf", expert_rows, grad_up_pre, preferred_element_type=jnp.float32
    )
    gradient_row_values = jnp.einsum(
        "erf,edf->erd", grad_gate_pre, expert_gate, preferred_element_type=jnp.float32
    )
    gradient_row_values = gradient_row_values + jnp.einsum(
        "erf,edf->erd", grad_up_pre, expert_up, preferred_element_type=jnp.float32
    )
    return (gradient_row_values, grad_gate, grad_up, grad_down)


def shards(
    inputs,
    routes,
    w_query,
    w_key,
    w_value,
    w_output,
    gain_attn,
    gain_moe,
    w_router,
    shared_gate,
    shared_up,
    shared_down,
    expert_gate,
    expert_up,
    expert_down,
    out_grad,
):
    col_index = lax.axis_index("col")
    col_count = lax.axis_size("col")
    group_count = lax.axis_size(("exp", "row"))
    local_count = expert_gate.shape[0]
    n_experts = local_count * group_count
    block_rows = routes.shape[0]
    top_count = routes.shape[1]
    capacity = 4 * block_rows * top_count // (3 * n_experts)
    model_width = expert_gate.shape[1]
    head_width = HEAD_DIM
    query_width = w_query.shape[1]
    key_width = w_key.shape[1]
    kv_local = key_width // head_width
    group_heads = query_width // key_width
    attn_scale = head_width ** (-0.5)
    residual = inputs.astype(jnp.float32)
    norm_one, inv_one = rms_forward(residual, gain_attn)
    gathered_one = row_gather(norm_one.astype(jnp.bfloat16))
    seq_len = gathered_one.shape[0]
    own_rows = seq_len // col_count
    weight_in = jnp.concatenate([w_query, w_key, w_value], axis=1)
    raw_proj = col_reduce(times_weight(gathered_one, weight_in, 0), own_rows)
    positions = col_index * own_rows + jnp.arange(own_rows)
    cosines, sine_part = rope_tables(positions, head_width)
    queries = (
        rotate(
            raw_proj[:, :query_width].reshape(own_rows, kv_local * group_heads, head_width),
            cosines,
            sine_part,
        )
        * attn_scale
    )
    queries = queries.astype(jnp.bfloat16).reshape(own_rows, kv_local, group_heads, head_width)
    key_rows = rotate(
        raw_proj[:, query_width : query_width + key_width].reshape(own_rows, kv_local, head_width),
        cosines,
        sine_part,
    ).astype(jnp.bfloat16)
    value_rows = (
        raw_proj[:, query_width + key_width :]
        .reshape(own_rows, kv_local, head_width)
        .astype(jnp.bfloat16)
    )
    all_keys, all_values = col_gather((key_rows, value_rows))
    block_size = min(512, own_rows)
    block_count = own_rows // block_size
    query_blocks = queries.reshape(block_count, block_size, kv_local, group_heads, head_width)
    block_starts = col_index * own_rows + jnp.arange(block_count) * block_size

    def forward_block(packed):
        query_part, first_row = packed
        scores = masked_scores(query_part, all_keys, first_row)
        peak_score = jnp.max(scores, axis=-1, keepdims=True)
        weights = jnp.exp(scores - peak_score)
        totals = jnp.sum(weights, axis=-1, keepdims=True)
        prob_low = (weights / totals).astype(jnp.bfloat16)
        attended_part = jnp.einsum(
            "kgqs,skd->qkgd", prob_low, all_values, preferred_element_type=jnp.float32
        )
        return (attended_part.astype(jnp.bfloat16), (peak_score + jnp.log(totals))[..., 0])

    attended, log_totals = lax.map(forward_block, (query_blocks, block_starts))
    attended = attended.reshape(own_rows, query_width)
    attended_all = col_gather(attended)
    attn_out = row_reduce(times_weight(attended_all, w_output, 0), block_rows)
    hidden_state = residual + attn_out
    norm_two, inv_two = rms_forward(hidden_state, gain_moe)
    norm_two = norm_two.astype(jnp.bfloat16)
    gathered_two = row_gather(norm_two)
    weight_shared = jnp.concatenate([shared_gate, shared_up], axis=1)
    shared_width = shared_gate.shape[1]
    shared_pre = col_reduce(times_weight(gathered_two, weight_shared, 0), own_rows)
    shared_hidden = (
        jax.nn.silu(shared_pre[:, :shared_width]) * shared_pre[:, shared_width:]
    ).astype(jnp.bfloat16)
    shared_all = col_gather(shared_hidden)
    shared_out = row_reduce(times_weight(shared_all, shared_down, 0), block_rows)
    norm_float = norm_two.astype(jnp.float32)
    logits = col_total(jnp.dot(norm_float, w_router, precision=highest))
    router_probs = jax.nn.softmax(logits, axis=-1)
    chosen = jnp.take_along_axis(router_probs, routes, axis=1)
    chosen_sum = jnp.sum(chosen, axis=1, keepdims=True)
    gate_vals = chosen / chosen_sum
    slots = route_slots(routes, n_experts, local_count)
    lead_shape = (local_count, group_count, capacity)
    token_of = jnp.arange(block_rows * top_count) // top_count
    full_rows = feature_gather(norm_two)
    received = send_experts(dispatch(full_rows[token_of], slots, lead_shape))
    expert_rows = received.reshape(local_count, group_count * capacity, model_width)
    gate_pre, up_pre, expert_hidden, partial_out = expert_forward(
        expert_rows, expert_gate, expert_up, expert_down
    )
    backward_row_values = collect(
        return_rows(partial_out.reshape(lead_shape + (model_width,))), slots, top_count
    )
    moe_wide = jnp.sum(gate_vals[:, :, None] * backward_row_values.astype(jnp.float32), axis=1)
    moe_out = feature_sum(moe_wide)
    output = (hidden_state + moe_out + shared_out).astype(jnp.bfloat16)
    grad_float = out_grad.astype(jnp.float32)
    grad_gathered = row_gather(out_grad)
    grad_shared_down = jnp.einsum(
        "sf,sd->fd", shared_all, grad_gathered, preferred_element_type=jnp.float32
    )
    grad_shared_hidden = col_reduce(times_weight(grad_gathered, shared_down, 1), own_rows)
    grad_sgate, grad_sup = silu_back(
        shared_pre[:, :shared_width], shared_pre[:, shared_width:], grad_shared_hidden
    )
    grad_shared_all = col_gather(jnp.concatenate([grad_sgate, grad_sup], axis=1))
    grad_weight_shared = jnp.einsum(
        "sd,sf->df", gathered_two, grad_shared_all, preferred_element_type=jnp.float32
    )
    grad_norm_two = row_reduce(times_weight(grad_shared_all, weight_shared, 1), block_rows)
    complete_gradient = feature_gather(out_grad)
    gate_terms = col_total(
        jnp.einsum(
            "qol,ql->qo", backward_row_values, complete_gradient, preferred_element_type=jnp.float32
        )
    )
    route_grads = (
        (gate_vals[:, :, None] * complete_gradient[:, None, :].astype(jnp.float32))
        .astype(jnp.bfloat16)
        .reshape(-1, model_width)
    )
    grad_received = send_experts(dispatch(route_grads, slots, lead_shape)).reshape(
        local_count, -1, model_width
    )
    gradient_row_values, expert_gate_gradient, expert_up_gradient, expert_down_gradient = (
        expert_gradient_pass(
            expert_rows,
            grad_received,
            gate_pre,
            up_pre,
            expert_hidden,
            expert_gate,
            expert_up,
            expert_down,
        )
    )
    grad_back = collect(
        return_rows(gradient_row_values.astype(jnp.bfloat16).reshape(lead_shape + (model_width,))),
        slots,
        top_count,
    )
    grad_norm_two = grad_norm_two + feature_sum(jnp.sum(grad_back.astype(jnp.float32), axis=1))
    weighted_terms = jnp.sum(gate_vals * gate_terms, axis=1, keepdims=True)
    grad_chosen = (gate_terms - weighted_terms) / chosen_sum
    expert_ids = jnp.arange(n_experts)
    grad_probs = jnp.sum(
        (routes[:, :, None] == expert_ids[None, None, :]).astype(jnp.float32)
        * grad_chosen[:, :, None],
        axis=1,
    )
    grad_logits = router_probs * (
        grad_probs - jnp.sum(router_probs * grad_probs, axis=1, keepdims=True)
    )
    grad_router = jnp.dot(norm_float.T, grad_logits, precision=highest)
    grad_norm_two = grad_norm_two + jnp.dot(grad_logits, w_router.T, precision=highest)
    grad_hidden_part, grad_gain_moe = rms_backward(hidden_state, inv_two, gain_moe, grad_norm_two)
    grad_hidden = grad_float + grad_hidden_part
    grad_attn_all = row_gather(grad_hidden.astype(jnp.bfloat16))
    grad_output = jnp.einsum(
        "sf,sd->fd", attended_all, grad_attn_all, preferred_element_type=jnp.float32
    )
    grad_attended = col_reduce(times_weight(grad_attn_all, w_output, 1), own_rows).astype(
        jnp.bfloat16
    )
    grad_blocks = grad_attended.reshape(block_count, block_size, kv_local, group_heads, head_width)

    def backward_block(carried, packed):
        grad_keys, grad_values = carried
        query_part, grad_part, log_part, first_row = packed
        scores = masked_scores(query_part, all_keys, first_row)
        prob_vals = jnp.exp(scores - log_part[..., None])
        grad_probs_att = jnp.einsum(
            "qkgd,skd->kgqs", grad_part, all_values, preferred_element_type=jnp.float32
        )
        row_inner = jnp.sum(prob_vals * grad_probs_att, axis=-1, keepdims=True)
        grad_scores = (prob_vals * (grad_probs_att - row_inner)).astype(jnp.bfloat16)
        grad_query_part = jnp.einsum(
            "kgqs,skd->qkgd", grad_scores, all_keys, preferred_element_type=jnp.float32
        )
        grad_keys = grad_keys + jnp.einsum(
            "kgqs,qkgd->skd", grad_scores, query_part, preferred_element_type=jnp.float32
        )
        grad_values = grad_values + jnp.einsum(
            "kgqs,qkgd->skd",
            prob_vals.astype(jnp.bfloat16),
            grad_part,
            preferred_element_type=jnp.float32,
        )
        return ((grad_keys, grad_values), grad_query_part)

    zero_keys = jnp.zeros((seq_len, kv_local, head_width), jnp.float32)
    (grad_keys_all, grad_values_all), grad_query = lax.scan(
        backward_block,
        (zero_keys, zero_keys),
        (query_blocks, grad_blocks, log_totals, block_starts),
    )
    key_value_grads = jnp.concatenate(
        [grad_keys_all.reshape(seq_len, -1), grad_values_all.reshape(seq_len, -1)], axis=1
    )
    own_kv = col_reduce(slice_term(key_value_grads), own_rows)
    grad_query_raw = (
        unrotate(
            grad_query.reshape(own_rows, kv_local * group_heads, head_width), cosines, sine_part
        )
        * attn_scale
    )
    grad_key_raw = unrotate(
        own_kv[:, :key_width].reshape(own_rows, kv_local, head_width), cosines, sine_part
    )
    grad_raw = jnp.concatenate(
        [
            grad_query_raw.reshape(own_rows, -1),
            grad_key_raw.reshape(own_rows, -1),
            own_kv[:, key_width:],
        ],
        axis=1,
    ).astype(jnp.bfloat16)
    grad_raw_all = col_gather(grad_raw)
    grad_weight_in = jnp.einsum(
        "sd,sf->df", gathered_one, grad_raw_all, preferred_element_type=jnp.float32
    )
    grad_norm_one = row_reduce(times_weight(grad_raw_all, weight_in, 1), block_rows)
    grad_in_part, grad_gain_attn = rms_backward(residual, inv_one, gain_attn, grad_norm_one)
    grad_inputs = (grad_hidden + grad_in_part).astype(jnp.bfloat16)
    summed = (
        lax.psum(grad_weight_in.astype(jnp.bfloat16), "exp").astype(jnp.float32),
        lax.psum(grad_output.astype(jnp.bfloat16), "exp").astype(jnp.float32),
        lax.psum(grad_weight_shared.astype(jnp.bfloat16), "exp").astype(jnp.float32),
        lax.psum(grad_shared_down.astype(jnp.bfloat16), "exp").astype(jnp.float32),
    )
    small_sums = (
        lax.psum(grad_gain_attn.astype(jnp.bfloat16), ("exp", "row")).astype(jnp.float32),
        lax.psum(grad_gain_moe.astype(jnp.bfloat16), ("exp", "row")).astype(jnp.float32),
        lax.psum(grad_router.astype(jnp.bfloat16), ("exp", "row")).astype(jnp.float32),
    )
    grad_in_all, grad_output_all, grad_shared_all_w, grad_shared_down_all = summed
    return (
        output,
        grad_inputs,
        grad_in_all[:, :query_width],
        grad_in_all[:, query_width : query_width + key_width],
        grad_in_all[:, query_width + key_width :],
        grad_output_all,
        small_sums[0],
        small_sums[1],
        small_sums[2],
        grad_shared_all_w[:, :shared_width],
        grad_shared_all_w[:, shared_width:],
        grad_shared_down_all,
        expert_gate_gradient,
        expert_up_gradient,
        expert_down_gradient,
    )


def solution(mesh):
    placed = (
        P(("exp", "row"), "col"),
        P(("exp", "row"), None),
        P("col", "row"),
        P("col", "row"),
        P("col", "row"),
        P("row", "col"),
        P("col"),
        P("col"),
        P("col", None),
        P("col", "row"),
        P("col", "row"),
        P("row", "col"),
        P(("exp", "row"), None, "col"),
        P(("exp", "row"), None, "col"),
        P(("exp", "row"), "col", None),
        P(("exp", "row"), "col"),
    )
    return jax.shard_map(
        shards,
        mesh=mesh,
        in_specs=placed,
        out_specs=(
            P(("exp", "row"), "col"),
            P(("exp", "row"), "col"),
            P("col", "row"),
            P("col", "row"),
            P("col", "row"),
            P("row", "col"),
            P("col"),
            P("col"),
            P("col", None),
            P("col", "row"),
            P("col", "row"),
            P("row", "col"),
            P(("exp", "row"), None, "col"),
            P(("exp", "row"), None, "col"),
            P(("exp", "row"), "col", None),
        ),
        check_vma=False,
    )
```

profile of v0, /device:TPU:9, one launch (start us, length us, event | category | flops | bytes accessed | tf_op | source)
XLA Modules:
  0.0 2816.5 jit_solution(1644656614725698591)
XLA Ops:
  18.4 42.4 %all-gather.12.cloned.1.call-done = bf16[2048,640]{1,0:T(8,128)(2,1)} async-done(((bf16[512,640]{1,0:T(8,128)(2,1)}), bf16[2048,640]{1,0:T(8,128)(2,1)}) %all-gather.12.cloned.1.call-update) | async-done | bytes 2621456 | tf_op jit(solution)/shard_map/all_gather | solution.py:25
  71.5 125.2 %reduce-scatter.16.cloned.1.call-done = f32[512,896]{0,1:T(8,128)} async-done(((f32[2048,896]{0,1:T(8,128)}), f32[512,896]{0,1:T(8,128)}) %reduce-scatter.16.cloned.1.call-update) | async-done | bytes 1835024 | tf_op jit(solution)/shard_map/reduce_scatter | solution.py:37
  252.0 58.4 %all-gather.14.cloned.1.call-done = bf16[2048,640]{0,1:T(8,128)(2,1)} async-done(((bf16[512,640]{0,1:T(8,128)(2,1)}), bf16[2048,640]{0,1:T(8,128)(2,1)}) %all-gather.14.cloned.1.call-update) | async-done | bytes 2621456 | tf_op jit(solution)/shard_map/all_gather | solution.py:31
  317.1 62.3 %reduce-scatter.18.cloned.1.call-done = f32[512,640]{1,0:T(8,128)} async-done(((f32[2048,640]{1,0:T(8,128)}), f32[512,640]{1,0:T(8,128)}) %reduce-scatter.18.cloned.1.call-update) | async-done | bytes 1310736 | tf_op jit(solution)/shard_map/reduce_scatter | solution.py:46
  396.8 47.7 %all-gather.16.cloned.1.call-done = bf16[512,2560]{1,0:T(8,128)(2,1)} async-done(((bf16[512,640]{1,0:T(8,128)(2,1)}), bf16[512,2560]{1,0:T(8,128)(2,1)}) %all-gather.16.cloned.1.call-update) | async-done | bytes 2621456 | tf_op jit(solution)/shard_map/all_gather | solution.py:59
  444.4 30.6 %gather_fusion = bf16[3072,2560]{1,0:T(8,128)(2,1)} fusion(bf16[512,2560]{1,0:T(8,128)(2,1)} %all-gather.16.cloned.1.call-done, s32[3072]{0:T(1024)S(1)} %broadcast_clamp_fusion), kind=kCustom, calls=%fused_computation | custom fusion | bytes 31469568 | tf_op jit(solution)/shard_map/gather | solution.py:321
  475.1 34.0 %scatter_custom_fusion = bf16[4096,2560]{1,0:T(8,128)(2,1)} fusion(s32[3072]{0:T(1024)S(1)} %broadcast_select_fusion, bf16[3072,2560]{1,0:T(8,128)(2,1)} %gather_fusion, bf16[]{:T(256)} %constant.125.clone.1), kind=kCustom, calls=%fused_computation.28 | custom fusion | bytes 20972032
  519.7 233.0 %all_to_all.20 = bf16[2,8,256,2560]{3,2,0,1:T(8,128)(2,1)S(1)} all-to-all(bf16[2,8,256,2560]{3,2,0,1:T(8,128)(2,1)S(1)} %copy.204), channel_id=1, replica_groups=mesh['exp'=2,'row'=4,'col'=4] {'exp','row'}, dimensions={1} | all-to-all | bytes 41943040 | tf_op jit(solution)/shard_map/all_to_all | solution.py:69
  841.0 52.7 %all-gather.26.cloned.1.call-done = bf16[512,2560]{1,0:T(8,128)(2,1)} async-done(((bf16[512,640]{1,0:T(8,128)(2,1)}), bf16[512,2560]{1,0:T(8,128)(2,1)}) %all-gather.26.cloned.1.call-update) | async-done | bytes 2621456 | tf_op jit(solution)/shard_map/all_gather | solution.py:59
  909.9 36.2 %mul.390 = f32[3072,2560]{1,0:T(8,128)} reshape(f32[512,6,2560]{2,1,0:T(8,128)} %mul.389) | data formatting | bytes 62914560 | tf_op jit(solution)/shard_map/mul | solution.py:353
  946.1 58.2 %all-gather.22.cloned.1.call-done = bf16[2048,640]{1,0:T(8,128)(2,1)} async-done(((bf16[512,640]{1,0:T(8,128)(2,1)}), bf16[2048,640]{1,0:T(8,128)(2,1)}) %all-gather.22.cloned.1.call-update) | async-done | bytes 2621456 | tf_op jit(solution)/shard_map/all_gather | solution.py:25
  1013.1 95.9 %all-to-all-done.1 = bf16[2,8,256,2560]{3,2,0,1:T(8,128)(2,1)} async-done(((bf16[2,8,256,2560]{3,2,0,1:T(8,128)(2,1)}), bf16[2,8,256,2560]{3,2,0,1:T(8,128)(2,1)}, u32[]{:S(2)}, u32[]{:S(2)}) %all-to-all-start.1) | async-done | bytes 20971552 | tf_op jit(solution)/shard_map/all_to_all | solution.py:73
  1126.3 84.6 %gather_fusion.1 = bf16[3072,2560]{1,0:T(8,128)(2,1)} fusion(bf16[2,8,256,2560]{3,2,1,0:T(8,128)(2,1)} %copy.207, s32[3072]{0:T(1024)S(1)} %bitcast.199), kind=kCustom, calls=%fused_computation.1 | custom fusion | bytes 31494144 | tf_op jit(solution)/shard_map/gather | solution.py:177
  1211.0 24.8 reshape.564
  1265.0 24.9 gather_fusion.3
  1308.1 34.1 %scatter_custom_fusion.1 = bf16[4096,2560]{1,0:T(8,128)(2,1)} fusion(s32[3072]{0:T(1024)} %copy-done.77, bf16[3072,2560]{1,0:T(8,128)(2,1)} %multiply_convert_fusion, bf16[]{:T(256)} %constant.125.clone.1), kind=kCustom, calls=%fused_computation.26 | custom fusion | bytes 20972032
  1382.1 215.9 %all-to-all-done.2 = bf16[2,8,256,2560]{3,2,0,1:T(8,128)(2,1)} async-done(((bf16[2,8,256,2560]{3,2,0,1:T(8,128)(2,1)}), bf16[2,8,256,2560]{3,2,0,1:T(8,128)(2,1)}, u32[]{:S(2)}, u32[]{:S(2)}) %all-to-all-start.2) | async-done | bytes 20971552 | tf_op jit(solution)/shard_map/all_to_all | solution.py:69
  1658.5 24.7 add_convert_fusion
  1712.6 222.8 %all-to-all-done.3 = bf16[2,8,256,2560]{3,2,0,1:T(8,128)(2,1)} async-done(((bf16[2,8,256,2560]{3,2,0,1:T(8,128)(2,1)}), bf16[2,8,256,2560]{3,2,0,1:T(8,128)(2,1)}, u32[]{:S(2)}, u32[]{:S(2)}) %all-to-all-start.3) | async-done | bytes 20971552 | tf_op jit(solution)/shard_map/all_to_all | solution.py:73
  1952.8 84.5 %gather_fusion.2 = bf16[3072,2560]{1,0:T(8,128)(2,1)} fusion(bf16[2,8,256,2560]{3,2,1,0:T(8,128)(2,1)} %copy.212, s32[3072]{0:T(1024)S(1)} %bitcast.200), kind=kCustom, calls=%fused_computation.2 | custom fusion | bytes 31494144 | tf_op jit(solution)/shard_map/gather | solution.py:177
  2037.3 24.9 reshape.567
  2095.8 40.3 %reduce-scatter.36.cloned.1.call-done = bf16[640,512]{1,0:T(8,128)(2,1)} async-done(((bf16[2560,512]{1,0:T(8,128)(2,1)}), bf16[640,512]{1,0:T(8,128)(2,1)}) %reduce-scatter.36.cloned.1.call-update) | async-done | bytes 655376
  2138.3 63.5 %reduce-scatter.26.cloned.1.call-done = f32[512,640]{1,0:T(8,128)} async-done(((f32[2048,640]{1,0:T(8,128)}), f32[512,640]{1,0:T(8,128)}) %reduce-scatter.26.cloned.1.call-update) | async-done | bytes 1310736 | tf_op jit(solution)/shard_map/reduce_scatter | solution.py:46
  2216.3 41.4 %all-gather.28.cloned.1.call-done = bf16[2048,640]{1,0:T(8,128)(2,1)} async-done(((bf16[512,640]{1,0:T(8,128)(2,1)}), bf16[2048,640]{1,0:T(8,128)(2,1)}) %all-gather.28.cloned.1.call-update) | async-done | bytes 2621456 | tf_op jit(solution)/shard_map/all_gather | solution.py:25
  2265.3 93.2 %reduce-scatter.28.cloned.1.call-done = f32[512,640]{1,0:T(8,128)} async-done(((f32[2048,640]{1,0:T(8,128)}), f32[512,640]{1,0:T(8,128)}) %reduce-scatter.28.cloned.1.call-update) | async-done | bytes 1310736 | tf_op jit(solution)/shard_map/reduce_scatter | solution.py:37
  2413.2 32.8 %reduce-scatter.30.cloned.1.call-done = f32[512,256]{0,1:T(8,128)} async-done(((f32[2048,256]{0,1:T(8,128)}), f32[512,256]{0,1:T(8,128)}) %reduce-scatter.30.cloned.1.call-update) | async-done | bytes 524304 | tf_op jit(solution)/shard_map/reduce_scatter | solution.py:37
  2449.6 58.1 %multiply_reduce_fusion = bf16[512,2560]{1,0:T(8,128)(2,1)} fusion(bf16[512,6,2560]{2,1,0:T(8,128)(2,1)} %reshape.564, f32[512,6]{1,0:T(8,128)S(1)} %copy-done.26), kind=kLoop, calls=%fused_computation.7 | loop fusion | flops 22282240 | bytes 18362368 | tf_op jit(solution)/shard_map/reduce_sum | solution.py:329
  2530.6 53.1 %all-gather.30.cloned.1.call-done = bf16[2048,896]{0,1:T(8,128)(2,1)} async-done(((bf16[512,896]{0,1:T(8,128)(2,1)}), bf16[2048,896]{0,1:T(8,128)(2,1)}) %all-gather.30.cloned.1.call-update) | async-done | bytes 3670032 | tf_op jit(solution)/shard_map/all_gather | solution.py:31
  2607.9 31.1 %reduce-scatter.34.cloned.1.call-done = bf16[640,512]{1,0:T(8,128)(2,1)} async-done(((bf16[2560,512]{1,0:T(8,128)(2,1)}), bf16[640,512]{1,0:T(8,128)(2,1)}) %reduce-scatter.34.cloned.1.call-update) | async-done | bytes 655376
  2702.2 37.2 %reduce-scatter.32.cloned.1.call-done = f32[512,640]{1,0:T(8,128)} async-done(((f32[2048,640]{1,0:T(8,128)}), f32[512,640]{1,0:T(8,128)}) %reduce-scatter.32.cloned.1.call-update) | async-done | bytes 1310736 | tf_op jit(solution)/shard_map/reduce_scatter | solution.py:46
  2741.3 27.8 all-reduce.1
  2778.2 26.7 reduce-scatter.22.cloned.1.call-done
  (371 shorter events, 677.4 us)
Async XLA Ops:
  7.2 997.1 %copy-start = (bf16[768,640]{1,0:T(8,128)(2,1)S(1)}, bf16[768,640]{1,0:T(8,128)(2,1)}, u32[]{:S(2)}) copy-start(bf16[768,640]{1,0:T(8,128)(2,1)} %param.27) | copy-start | bytes 2949124
  7.2 53.6 %all-gather.12.cloned.1.call-start = ((), (), s32[]{:S(2)}) async-start(), calls=%async_computation.15 | async-start | bytes 3276800 | tf_op jit(solution)/shard_map/all_gather | solution.py:25
  18.2 178.5 %reduce-scatter.16.cloned.1.call-start = ((), (), s32[]{:S(2)}) async-start(), calls=%async_computation.16 | async-start | bytes 9175040 | tf_op jit(solution)/shard_map/reduce_scatter | solution.py:37
  68.7 241.6 %all-gather.14.cloned.1.call-start = ((), (), s32[]{:S(2)}) async-start(), calls=%async_computation.17 | async-start | bytes 3276800 | tf_op jit(solution)/shard_map/all_gather | solution.py:31
  68.8 130.8 %copy-start.80 = (f32[64]{0:T(128)}, f32[64]{0:T(128)S(1)}, u32[]{:S(2)}) copy-start(f32[64]{0:T(128)S(1)} %multiply_power_fusion) | copy-start | bytes 772
  68.8 130.7 %copy-start.61 = (f32[512]{0:T(512)}, f32[512]{0:T(512)S(1)}, u32[]{:S(2)}) copy-start(f32[512]{0:T(512)S(1)} %fusion.66) | copy-start | bytes 6148
  71.5 170.6 %copy-start.7 = (pred[512,2048]{0,1:T(8,128)(4,1)}, pred[512,2048]{0,1:T(8,128)(4,1)S(1)}, u32[]{:S(2)}) copy-start(pred[512,2048]{0,1:T(8,128)(4,1)S(1)} %iota_compare_fusion) | copy-start | bytes 3145732
  251.9 127.5 %reduce-scatter.18.cloned.1.call-start = ((), (), s32[]{:S(2)}) async-start(), calls=%async_computation.18 | async-start | bytes 6553600 | tf_op jit(solution)/shard_map/reduce_scatter | solution.py:46
  317.0 127.4 %all-gather.16.cloned.1.call-start = ((), (), s32[]{:S(2)}) async-start(), calls=%async_computation.19 | async-start | bytes 3276800 | tf_op jit(solution)/shard_map/all_gather | solution.py:59
  831.8 277.1 %all-to-all-start.1 = ((bf16[2,8,256,2560]{3,2,0,1:T(8,128)(2,1)}), bf16[2,8,256,2560]{3,2,0,1:T(8,128)(2,1)}, u32[]{:S(2)}, u32[]{:S(2)}) async-start(bf16[2,8,256,2560]{3,2,0,1:T(8,128)(2,1)} %copy.206), calls=%async_computation.3 | async-start | bytes 41943040 | tf_op jit(solution)/shard_map/all_to_all | solution.py:73
  838.6 55.1 %all-gather.26.cloned.1.call-start = ((), (), s32[]{:S(2)}) async-start(), calls=%async_computation.28 | async-start | bytes 3276800 | tf_op jit(solution)/shard_map/all_gather | solution.py:59
  839.1 165.2 %all-gather.22.cloned.1.call-start = ((), (), s32[]{:S(2)}) async-start(), calls=%async_computation.24 | async-start | bytes 3276800 | tf_op jit(solution)/shard_map/all_gather | solution.py:25
  839.9 532.4 %all-gather.18.cloned.1.call-start = ((), (), s32[]{:S(2)}) async-start(), calls=%async_computation.20 | async-start | bytes 3276800 | tf_op jit(solution)/shard_map/all_gather | solution.py:25
  840.6 866.5 %reduce-scatter.24.cloned.1.call-start = ((), (), s32[]{:S(2)}) async-start(), calls=%async_computation.25 | async-start | bytes 7864320 | tf_op jit(solution)/shard_map/reduce_scatter | solution.py:37
  1013.1 113.2 %copy-start.3 = (s32[3072,1]{0,1:T(1,128)S(1)}, s32[3072,1]{0,1:T(1,128)}, u32[]{:S(2)}) copy-start(s32[3072,1]{0,1:T(1,128)} %get-tuple-element.81) | copy-start | bytes 36868
  1359.8 238.2 %all-to-all-start.2 = ((bf16[2,8,256,2560]{3,2,0,1:T(8,128)(2,1)}), bf16[2,8,256,2560]{3,2,0,1:T(8,128)(2,1)}, u32[]{:S(2)}, u32[]{:S(2)}) async-start(bf16[2,8,256,2560]{3,2,0,1:T(8,128)(2,1)} %copy.209), calls=%async_computation.8 | async-start | bytes 41943040 | tf_op jit(solution)/shard_map/all_to_all | solution.py:69
  1369.8 337.4 %reduce-scatter.20.cloned.1.call-start = ((), (), s32[]{:S(2)}) async-start(), calls=%async_computation.21 | async-start | bytes 15728640 | tf_op jit(solution)/shard_map/reduce_scatter | solution.py:37
  1700.7 234.6 %all-to-all-start.3 = ((bf16[2,8,256,2560]{3,2,0,1:T(8,128)(2,1)}), bf16[2,8,256,2560]{3,2,0,1:T(8,128)(2,1)}, u32[]{:S(2)}, u32[]{:S(2)}) async-start(bf16[2,8,256,2560]{3,2,0,1:T(8,128)(2,1)} %copy.211), calls=%async_computation.9 | async-start | bytes 41943040 | tf_op jit(solution)/shard_map/all_to_all | solution.py:73
  1707.1 378.6 %all-gather.24.cloned.1.call-start = ((), (), s32[]{:S(2)}) async-start(), calls=%async_computation.26 | async-start | bytes 7864320 | tf_op jit(solution)/shard_map/all_gather | solution.py:31
  1712.5 240.3 %copy-start.4 = (s32[3072,1]{0,1:T(1,128)S(1)}, s32[3072,1]{0,1:T(1,128)}, u32[]{:S(2)}) copy-start(s32[3072,1]{0,1:T(1,128)} %get-tuple-element.81) | copy-start | bytes 36868
  1712.5 423.6 %reduce-scatter.36.cloned.1.call-start = ((), (), s32[]{:S(2)}) async-start(), calls=%async_computation.35 | async-start | bytes 3276800
  2085.6 116.2 %reduce-scatter.26.cloned.1.call-start = ((), (), s32[]{:S(2)}) async-start(), calls=%async_computation.27 | async-start | bytes 6553600 | tf_op jit(solution)/shard_map/reduce_scatter | solution.py:46
  2095.0 106.8 %copy-start.2 = (f32[512,16]{0,1:T(8,128)S(1)}, f32[512,16]{0,1:T(8,128)}, u32[]{:S(2)}) copy-start(f32[512,16]{0,1:T(8,128)} %copy-done.1) | copy-start | bytes 98308
  2095.1 162.6 %all-gather.28.cloned.1.call-start = ((), (), s32[]{:S(2)}) async-start(), calls=%async_computation.29 | async-start | bytes 3276800 | tf_op jit(solution)/shard_map/all_gather | solution.py:25
  2216.1 142.4 %reduce-scatter.28.cloned.1.call-start = ((), (), s32[]{:S(2)}) async-start(), calls=%async_computation.30 | async-start | bytes 6553600 | tf_op jit(solution)/shard_map/reduce_scatter | solution.py:37
  2264.6 181.4 %reduce-scatter.30.cloned.1.call-start = ((), (), s32[]{:S(2)}) async-start(), calls=%async_computation.31 | async-start | bytes 2621440 | tf_op jit(solution)/shard_map/reduce_scatter | solution.py:37
  2403.9 108.5 %all-gather.20.cloned.1.call-start = ((), (), s32[]{:S(2)}) async-start(), calls=%async_computation.22 | async-start | bytes 3932160 | tf_op jit(solution)/shard_map/all_gather | solution.py:31
  2404.5 179.2 %all-gather.30.cloned.1.call-start = ((), (), s32[]{:S(2)}) async-start(), calls=%async_computation.32 | async-start | bytes 4587520 | tf_op jit(solution)/shard_map/all_gather | solution.py:31
  2449.5 189.4 %reduce-scatter.34.cloned.1.call-start = ((), (), s32[]{:S(2)}) async-start(), calls=%async_computation.34 | async-start | bytes 3276800
  2512.1 181.5 %all-reduce.5.cloned.1.call-start = ((), (), s32[]{:S(2)}) async-start(), calls=%async_computation.36 | async-start | bytes 9830400 | tf_op jit(solution)/shard_map/psum | solution.py:461
  2590.5 148.9 %reduce-scatter.32.cloned.1.call-start = ((), (), s32[]{:S(2)}) async-start(), calls=%async_computation.33 | async-start | bytes 6553600 | tf_op jit(solution)/shard_map/reduce_scatter | solution.py:46
  2599.4 205.5 %reduce-scatter.22.cloned.1.call-start = ((), (), s32[]{:S(2)}) async-start(), calls=%async_computation.23 | async-start | bytes 6553600 | tf_op jit(solution)/shard_map/reduce_scatter | solution.py:46
  (83 other events, 2270.4 us)
Sparse Core Ops, SparseCore 0:
  18.3 42.5 all-gather.11
  68.8 127.7 reduce-scatter.15
  252.0 58.2 all-gather.13
  317.1 62.2 reduce-scatter.17
  389.7 54.7 all-gather.15
  840.7 52.9 all-gather.25
  895.6 108.6 all-gather.21
  1006.7 60.9 all-gather.17
  1070.6 109.6 reduce-scatter.23
  1382.3 212.6 reduce-scatter.19
  1712.6 113.2 all-gather.23
  2085.7 50.3 reduce-scatter.35
  2139.7 62.0 reduce-scatter.25
  2216.2 41.4 all-gather.27
  2264.7 93.7 reduce-scatter.27
  2404.0 41.9 reduce-scatter.29
  2448.1 62.7 all-gather.19
  2512.9 70.7 all-gather.29
  2586.7 52.2 reduce-scatter.33
  2643.0 31.1 all-reduce.4
  2677.5 61.8 reduce-scatter.31
  2742.7 62.1 reduce-scatter.21
where the time goes:
time: 2830 us; the launch traced here: 2820 us
  waiting for transfers between devices  1400 us (49%)
  local copies, waits for them, and re-layouts  560 us (20%)
  blocking collectives  330 us (12%)
  matrix products  327 us (12%)
  other arithmetic  155 us (5%)
    all_to_all x2, waiting for transfers between devices, return_rows(): lax.all_to_all(source, ('exp', 'row'), split_axis=1, concat_axis=1, tiled...  319 us
    reduce_scatter x5, waiting for transfers between devices, col_reduce(): lax.psum_scatter(term_fn(jnp.int32(0), row_count * lax.axis_size('col')),...  251 us
    all_to_all x1, blocking collectives, send_experts(): lax.all_to_all(source, ('exp', 'row'), split_axis=1, concat_axis=1, tiled...  233 us
    all_to_all x1, waiting for transfers between devices, send_experts(): lax.all_to_all(source, ('exp', 'row'), split_axis=1, concat_axis=1, tiled...  216 us
    reduce_scatter x4, waiting for transfers between devices, row_reduce(): lax.psum_scatter(term_fn(jnp.int32(0), row_count * lax.axis_size('row')),...  190 us
    gather x2, local copies, waits for them, and re-layouts, collect(): picked = buffer_rows[local_of, group_of, slot_rank]  169 us
    all_gather x4, waiting for transfers between devices, row_gather(): return lax.all_gather(source, 'row', axis=0, tiled=True)  142 us
    all_gather x4, waiting for transfers between devices, col_gather(): lax.all_gather(for_sending(source), 'col', axis=0, tiled=True)  112 us
  transfers between devices with their start and end apart: 25, of which 19 were waited for; matrix products, arithmetic and copies ran while one was open for 27% of the time, Pallas kernels for 0%

commit v1 on v0

v1 whole, which is shorter than its diff:
```python
import functools

import jax
import jax.numpy as jnp
from jax import lax
from jax.experimental import pallas as pl
from jax.experimental.pallas import tpu as pltpu
from jax.sharding import PartitionSpec as P

HEAD_DIM = 128

eps = 1e-05
theta = 500000.0
highest = lax.Precision.HIGHEST
masked_value = -1e30
f32 = jnp.float32
bf16 = jnp.bfloat16
vmem_limit = 56 * 2**20
cheap = 2**14


def swap(x, axis, step):
    return lax.ppermute(x, axis, [(i, i ^ step) for i in range(lax.axis_size(axis))])


def exchange(x, axis):
    return [x] + [swap(x, axis, step) for step in range(1, lax.axis_size(axis))]


def reduce_parts(parts, axis):
    total = parts[0].astype(f32)
    for step in range(1, len(parts)):
        total = total + swap(parts[step], axis, step).astype(f32)
    return total


def all_sum(x, axis):
    step = 1
    while step < lax.axis_size(axis):
        x = x + swap(x, axis, step)
        step *= 2
    return x


def zero_of(*arrays):
    found = jnp.int32(0)
    for x in arrays:
        first = x[(slice(0, 1),) * x.ndim].reshape(())
        found = found + (first != first).astype(jnp.int32)
    return found


def after(x, earlier):
    place = pl.BlockSpec(memory_space=pl.ANY)
    return pl.pallas_call(
        lambda *refs: None,
        out_shape=jax.ShapeDtypeStruct(x.shape, x.dtype),
        in_specs=[place, place],
        out_specs=place,
        input_output_aliases={0: 0},
    )(x, earlier)


def ring_order(n):
    return [0] + list(range(1, n, 2)) + [i for i in range(n - 1, 0, -1) if i % 2 == 0]


def ring_pairs(n, back=False):
    order = ring_order(n)
    pairs = [(order[i], order[(i + 1) % n]) for i in range(n)]
    return [(b, a) for a, b in pairs] if back else pairs


def ring_sources(axis):
    n = lax.axis_size(axis)
    order = ring_order(n)
    place = jnp.array([order.index(i) for i in range(n)])[lax.axis_index(axis)]
    return jnp.array(order)[(place - jnp.arange(n)) % n]


def ring_gather(x, axis):
    parts, n = [x], lax.axis_size(axis)
    for _ in range(n - 1):
        parts.append(lax.ppermute(parts[-1], axis, ring_pairs(n)))
    return parts


def ring_reduce(parts, axis):
    n = len(parts)
    order = ring_order(n)
    total = parts[0].astype(f32)
    for k in range(1, n):
        pairs = [(order[i], order[(i - k) % n]) for i in range(n)]
        total = total + lax.ppermute(parts[k], axis, pairs).astype(f32)
    return total


def row_gather(x):
    if lax.axis_size("row") != 4:
        return exchange(x, "row")
    x_near, y_near = swap(x, "row", 1), swap(x, "row", 2)
    middle = x.shape[0] // 2
    return [x, x_near, y_near, swap(y_near[:middle], "row", 1), swap(x_near[middle:], "row", 2)]


def add(left, right):
    return left.astype(f32) + right.astype(f32)


def row_reduce(blocks):
    if len(blocks) != 4:
        return reduce_parts(blocks, "row")
    own, x_near, y_near, far = blocks
    middle = own.shape[0] // 2
    far_x, far_y = swap(far[:middle], "row", 1), swap(far[middle:], "row", 2)
    y_first = add(y_near[:middle], far_x).astype(bf16)
    x_second = add(x_near[middle:], far_y).astype(bf16)
    y_sum = swap(jnp.concatenate([y_first, y_near[middle:]], axis=0), "row", 2)
    x_sum = swap(jnp.concatenate([x_near[:middle], x_second], axis=0), "row", 1)
    return add(own, x_sum) + y_sum.astype(f32)


def tokens_home(x, wait):
    c, n = lax.axis_index("col"), lax.axis_size("col")
    rows, width = x.shape[0] // n, x.shape[1]
    whole = jnp.zeros((rows, n * width), x.dtype)
    for s in range(n):
        piece = lax.dynamic_slice_in_dim(x, (c ^ s) * rows + wait, rows, 0)
        piece = swap(piece, "col", s) if s else piece
        whole = lax.dynamic_update_slice(whole, piece, (0, (c ^ s) * width))
    return whole


def tokens_back(x):
    c, n = lax.axis_index("col"), lax.axis_size("col")
    rows, width = x.shape[0], x.shape[1] // n
    whole = jnp.zeros((n * rows, width), x.dtype)
    for s in range(n):
        piece = lax.dynamic_slice_in_dim(x, (c ^ s) * width, width, 1)
        piece = swap(piece, "col", s) if s else piece
        whole = lax.dynamic_update_slice(whole, piece, ((c ^ s) * rows, 0))
    return whole


def own_share(weight, wait=0):
    share = weight.shape[0] // lax.axis_size("exp")
    return lax.dynamic_slice_in_dim(weight, lax.axis_index("exp") * share + wait, share, 0)


def all_shares(total):
    e = lax.axis_index("exp")
    shares = lax.axis_size("exp")
    whole = jnp.zeros((shares,) + total.shape, total.dtype)
    for t, piece in enumerate(exchange(total, "exp")):
        whole = lax.dynamic_update_index_in_dim(whole, piece, e ^ t, 0)
    return whole.reshape((shares * total.shape[0],) + total.shape[1:])


def reduce_weight(grad):
    total = lax.psum_scatter(grad, ("col", "exp"), scatter_dimension=0, tiled=True)
    return all_shares(total).astype(f32)


def rope_tables(positions, head_width):
    half_width = head_width // 2
    frequency = theta ** (-2.0 * jnp.arange(half_width, dtype=f32) / head_width)
    angles = positions.astype(f32)[:, None] * frequency[None, :]
    return (jnp.cos(angles), jnp.sin(angles))


def rotate(source, cosines, sines):
    half_width = source.shape[-1] // 2
    first, second = source[..., :half_width], source[..., half_width:]
    cos_view, sin_view = cosines[:, None, :], sines[:, None, :]
    return jnp.concatenate(
        [first * cos_view - second * sin_view, first * sin_view + second * cos_view], axis=-1
    )


def dot(left, right, contract=(1, 0)):
    return lax.dot_general(
        left, right, (((contract[0],), (contract[1],)), ((), ())), preferred_element_type=f32
    )


def batch_dot(spec, left, right):
    return jnp.einsum(spec, left, right, preferred_element_type=f32)


def rms_inverse(values):
    return lax.rsqrt(jnp.mean(values * values, axis=1, keepdims=True) + eps)


def rms_backward(values, inv_rms, gain, grad_norm):
    scaled_grad = grad_norm * gain[None, :]
    inner = jnp.mean(scaled_grad * values, axis=1, keepdims=True)
    grad_values = inv_rms * (scaled_grad - values * (inv_rms * inv_rms * inner))
    return grad_values, jnp.sum(grad_norm * values * inv_rms, axis=0)


def place_keys(place, kv_refs, key_buf, value_buf, chunk):
    row, blocks, width = place[0], kv_refs[0].shape[0] // chunk, key_buf.shape[1]
    for k, ref in enumerate(kv_refs):
        for s in range(blocks):
            at = pl.multiple_of(((row ^ s) * len(kv_refs) + place[2 + k]) * chunk, chunk)
            key_buf[pl.ds(at, chunk), :] = ref[s * chunk : (s + 1) * chunk, :width]
            value_buf[pl.ds(at, chunk), :] = ref[s * chunk : (s + 1) * chunk, width:]


def head_rows(ref, rows, width):
    block = ref[rows, :]
    return jnp.concatenate(
        [block[:, h * width : (h + 1) * width] for h in range(block.shape[1] // width)], axis=0
    )


def scores_tile(place, key_tile, queries, block, tile, chunk):
    scores = dot(key_tile, queries, (1, 1))
    key_at = tile * key_tile.shape[0] + lax.broadcasted_iota(jnp.int32, scores.shape, 0)
    lane = lax.broadcasted_iota(jnp.int32, scores.shape, 1)
    query_at = block * key_tile.shape[0] + place[1] * chunk + lane % chunk
    return jnp.where(key_at <= query_at, scores, masked_value)


def attention_kernel(chunk, place, q_ref, *refs):
    kv_refs, (out_ref, total_ref, lse_ref, key_buf, value_buf) = refs[:-5], refs[-5:]
    width = key_buf.shape[1]
    blocks = q_ref.shape[0] // chunk
    tile_rows = key_buf.shape[0] // blocks
    place_keys(place, kv_refs, key_buf, value_buf, chunk)

    @pl.loop(0, blocks)
    def _(block):
        rows = pl.ds(pl.multiple_of((place[0] ^ block) * chunk, chunk), chunk)
        queries = head_rows(q_ref, rows, width)
        count = queries.shape[0]

        def step(tile, carry):
            peak, total, out = carry
            at = pl.ds(pl.multiple_of(tile * tile_rows, tile_rows), tile_rows)
            scores = scores_tile(place, key_buf[at, :], queries, block, tile, chunk)
            new_peak = jnp.maximum(peak, jnp.max(scores, axis=0, keepdims=True))
            weights = jnp.exp(scores - new_peak)
            shrink = jnp.exp(peak - new_peak)
            total = total * shrink + jnp.sum(weights, axis=0, keepdims=True)
            part = dot(value_buf[at, :], weights.astype(bf16), (0, 0))
            return new_peak, total, out * shrink + part

        start = (
            jnp.full((1, count), masked_value, f32),
            jnp.zeros((1, count), f32),
            jnp.zeros((width, count), f32),
        )
        peak, total, out = lax.fori_loop(0, block + 1, step, start)
        out = out / total
        total_ref[pl.ds(block, 1)] = out[None]
        lse_ref[pl.ds(block, 1)] = (peak + jnp.log(total))[None]
        for h in range(count // chunk):
            head = out[:, h * chunk : (h + 1) * chunk]
            out_ref[rows, h * width : (h + 1) * width] = head.T.astype(bf16)


def attention_back_kernel(chunk, place, q_ref, grad_ref, total_ref, lse_ref, *refs):
    kv_refs = refs[:-6]
    dq_ref, dkv_ref, key_buf, value_buf, dk_buf, dv_buf = refs[-6:]
    width = key_buf.shape[1]
    blocks = q_ref.shape[0] // chunk
    tile_rows = key_buf.shape[0] // blocks
    place_keys(place, kv_refs, key_buf, value_buf, chunk)
    dk_buf[...] = jnp.zeros_like(dk_buf)
    dv_buf[...] = jnp.zeros_like(dv_buf)

    @pl.loop(0, blocks)
    def _(block):
        rows = pl.ds(pl.multiple_of((place[0] ^ block) * chunk, chunk), chunk)
        queries = head_rows(q_ref, rows, width)
        grads = head_rows(grad_ref, rows, width)
        count = queries.shape[0]
        out = total_ref[pl.ds(block, 1)][0]
        lse = lse_ref[pl.ds(block, 1)][0]
        grads_t = jnp.concatenate(
            [grads[h * chunk : (h + 1) * chunk].astype(f32).T for h in range(count // chunk)], axis=1
        )
        inner = jnp.sum(out * grads_t, axis=0, keepdims=True)

        def step(tile, d_queries):
            at = pl.ds(pl.multiple_of(tile * tile_rows, tile_rows), tile_rows)
            keys = key_buf[at, :]
            scores = scores_tile(place, keys, queries, block, tile, chunk)
            probs = jnp.exp(scores - lse)
            d_probs = dot(value_buf[at, :], grads, (1, 1))
            d_scores = (probs * (d_probs - inner)).astype(bf16)
            dk_buf[at, :] += dot(d_scores, queries)
            dv_buf[at, :] += dot(probs.astype(bf16), grads)
            return d_queries + dot(keys, d_scores, (0, 0))

        d_queries = lax.fori_loop(0, block + 1, step, jnp.zeros((width, count), f32))
        for h in range(count // chunk):
            head = d_queries[:, h * chunk : (h + 1) * chunk]
            dq_ref[rows, h * width : (h + 1) * width] = head.T

    for k in range(len(kv_refs)):
        for s in range(blocks):
            at = pl.ds(pl.multiple_of(((place[0] ^ s) * len(kv_refs) + place[2 + k]) * chunk, chunk), chunk)
            dkv_ref[k, s * chunk : (s + 1) * chunk, :width] = dk_buf[at, :].astype(bf16)
            dkv_ref[k, s * chunk : (s + 1) * chunk, width:] = dv_buf[at, :].astype(bf16)


def whole_spec(shape):
    return pl.BlockSpec(shape, lambda *_: (0,) * len(shape))


def side_by_side(left, right, wait):
    count, rows, width = left.shape
    tile = 512

    def kernel(wait_ref, left_ref, right_ref, both_ref):
        both_ref[:, :width] = left_ref[...]
        both_ref[:, width:] = right_ref[...]

    spec = pl.BlockSpec((None, tile, width), lambda i, j, _: (i, j, 0))
    return pl.pallas_call(
        kernel,
        out_shape=jax.ShapeDtypeStruct((count, rows, 2 * width), left.dtype),
        grid_spec=pltpu.PrefetchScalarGridSpec(
            num_scalar_prefetch=1,
            grid=(count, rows // tile),
            in_specs=[spec, spec],
            out_specs=pl.BlockSpec((None, tile, 2 * width), lambda i, j, _: (i, j, 0)),
        ),
        cost_estimate=pl.CostEstimate(flops=0, bytes_accessed=4 * left.nbytes, transcendentals=0),
    )(wait.reshape(1), left, right)


def attention_call(kernel, place, operands, outs, scratch, work):
    return pl.pallas_call(
        kernel,
        out_shape=outs,
        grid_spec=pltpu.PrefetchScalarGridSpec(
            num_scalar_prefetch=1,
            grid=(1,),
            in_specs=[whole_spec(x.shape) for x in operands],
            out_specs=[whole_spec(x.shape) for x in outs],
            scratch_shapes=scratch,
        ),
        compiler_params=pltpu.CompilerParams(vmem_limit_bytes=vmem_limit),
        cost_estimate=pl.CostEstimate(
            flops=work // cheap, bytes_accessed=2**10, transcendentals=0
        ),
    )(place, *operands)


def attention_forward(place, queries, kv_parts, chunk):
    rows, total_width = queries.shape
    width = kv_parts[0].shape[1] // 2
    heads, blocks, keys = total_width // width, rows // chunk, rows * len(kv_parts)
    return attention_call(
        functools.partial(attention_kernel, chunk),
        place,
        (queries, *kv_parts),
        (
            jax.ShapeDtypeStruct((rows, total_width), bf16),
            jax.ShapeDtypeStruct((blocks, width, heads * chunk), f32),
            jax.ShapeDtypeStruct((blocks, 1, heads * chunk), f32),
        ),
        [pltpu.VMEM((keys, width), bf16)] * 2,
        4 * rows * heads * keys * width,
    )


def attention_backward(place, queries, grads, out, lse, kv_parts, chunk):
    rows, total_width = queries.shape
    width = kv_parts[0].shape[1] // 2
    keys = rows * len(kv_parts)
    return attention_call(
        functools.partial(attention_back_kernel, chunk),
        place,
        (queries, grads, out, lse, *kv_parts),
        (
            jax.ShapeDtypeStruct((rows, total_width), f32),
            jax.ShapeDtypeStruct((len(kv_parts), rows, 2 * width), bf16),
        ),
        [pltpu.VMEM((keys, width), bf16)] * 2 + [pltpu.VMEM((keys, width), f32)] * 2,
        10 * rows * total_width * keys,
    )


def silu_back(gate_pre, up_pre, grad_hidden):
    sigmoid_vals = jax.nn.sigmoid(gate_pre)
    silu = gate_pre * sigmoid_vals
    grad_gate = grad_hidden * up_pre * sigmoid_vals * (1.0 + gate_pre * (1.0 - sigmoid_vals))
    return silu * up_pre, grad_gate.astype(bf16), (grad_hidden * silu).astype(bf16)


def experts_kernel(counts, held, local, tiles, chunks, info, *refs):
    groups = len(counts)
    x_refs, refs = refs[: sum(counts)], refs[sum(counts) :]
    mix_refs, refs = refs[: sum(counts)], refs[sum(counts) :]
    g_refs, refs = refs[:groups], refs[groups:]
    refs = refs[:6] + refs[6 + held :]
    (
        slot_ref, slot_t_ref, w_in, w_down, s_in, s_down,
        xs_ref, gs_ref, hidden_ref, pre_ref, own_x_ref, own_g_ref, s_hidden_ref, s_pre_ref,
    ), refs = refs[:14], refs[14:]
    out_refs, refs = refs[:groups], refs[groups:]
    norm_refs, refs = refs[:groups], refs[groups:]
    pick, put, acc_in, acc_down, s_acc_in, s_acc_down, term_buf = refs
    step = pl.program_id(0)
    capacity, tokens = pick.shape[1], pick.shape[2]
    width, s_width = w_down.shape[1], s_down.shape[0]

    @pl.when(step == 0)
    def _():
        for at in range(groups * local):
            slots = lax.broadcasted_iota(jnp.int32, (capacity, tokens), 0)
            pick[at] = jnp.where(slots == slot_ref[at : at + 1, :], 1.0, 0.0).astype(bf16)
            slots = lax.broadcasted_iota(jnp.int32, (tokens, capacity), 1)
            put[at // local, :, (at % local) * capacity : (at % local + 1) * capacity] = jnp.where(
                slots == slot_t_ref[:, at : at + 1], 1.0, 0.0
            ).astype(bf16)
        acc_in[...] = jnp.zeros_like(acc_in)
        acc_down[...] = jnp.zeros_like(acc_down)
        s_acc_in[...] = jnp.zeros_like(s_acc_in)
        s_acc_down[...] = jnp.zeros_like(s_acc_down)

    @pl.when(step < tiles)
    def _():
        for t in range(groups):
            parts = slice(sum(counts[:t]), sum(counts[: t + 1]))
            x = jnp.concatenate([ref[...] for ref in x_refs[parts]], axis=0)
            chunk = tokens // chunks
            g = jnp.concatenate(
                [
                    g_refs[t][pl.ds(pl.multiple_of(info[groups + k] * chunk, chunk), chunk), :]
                    for k in range(chunks)
                ],
                axis=0,
            )
            for l in range(local):
                rows = slice(t * capacity, (t + 1) * capacity)
                xs_ref[l, rows, :] = dot(pick[t * local + l], x).astype(bf16)
                gs_ref[l, rows, :] = dot(pick[t * local + l], g).astype(bf16)
            if t == 0:
                own_x_ref[...] = x
                own_g_ref[...] = g
                s_acc_in[...] += dot(x, s_in[...])
                s_acc_down[...] += dot(g, s_down[...], (1, 1))
        for l in range(local):
            acc_in[l] += dot(xs_ref[l], w_in[l])
            acc_down[l] += dot(gs_ref[l], w_down[l], (1, 1))

    @pl.when(step == tiles - 1)
    def _():
        mixes = [
            jnp.concatenate([ref[...] for ref in mix_refs[sum(counts[:t]) : sum(counts[: t + 1])]], axis=0)
            for t in range(groups)
        ]
        lanes = mixes[0].shape[1]
        lane = lax.broadcasted_iota(jnp.int32, (1, lanes), 1)
        spread = []
        for l in range(local):
            expert = info[groups + chunks] + l
            weights = jnp.concatenate([dot(pick[t * local + l], mixes[t]) for t in range(groups)], axis=0)
            weights = jnp.sum(
                jnp.where(lane % (lanes // 2) == expert, weights, 0.0), axis=1, keepdims=True
            )
            grad = acc_down[l]
            hidden, d_gate, d_up = silu_back(acc_in[l, :, :width], acc_in[l, :, width:], grad * weights)
            terms = jnp.sum(hidden * grad, axis=1, keepdims=True)
            hidden_ref[l] = (hidden * weights).astype(bf16)
            pre_ref[l, :, :width] = d_gate
            pre_ref[l, :, width:] = d_up
            spread.append(jnp.where(lane == expert, terms, 0.0).astype(bf16))
        for t in range(groups):
            rows = slice(t * capacity, (t + 1) * capacity)
            term_buf[t] = dot(
                put[t], jnp.concatenate([terms[rows] for terms in spread], axis=0)
            ).astype(bf16)
        hidden, d_gate, d_up = silu_back(s_acc_in[:, :s_width], s_acc_in[:, s_width:], s_acc_down[...])
        s_hidden_ref[...] = hidden.astype(bf16)
        s_pre_ref[:, :s_width] = d_gate
        s_pre_ref[:, s_width:] = d_up

    @pl.when((step >= tiles) & (step < 2 * tiles))
    def _():
        pieces = [dot(hidden_ref[l], w_down[l]).astype(bf16) for l in range(local)]
        d_pieces = [dot(pre_ref[l], w_in[l], (1, 1)).astype(bf16) for l in range(local)]
        for t in range(groups):
            rows = slice(t * capacity, (t + 1) * capacity)
            out = dot(put[t], jnp.concatenate([piece[rows] for piece in pieces], axis=0))
            norm = dot(put[t], jnp.concatenate([piece[rows] for piece in d_pieces], axis=0))
            if t == 0:
                out = out + dot(s_hidden_ref[...], s_down[...])
                norm = norm + dot(s_pre_ref[...], s_in[...], (1, 1))
            out_refs[t][...] = out.astype(bf16)
            norm_refs[t][...] = norm.astype(bf16)

    @pl.when(step == 2 * tiles)
    def _():
        for t in range(groups):
            norm_refs[t][:, : term_buf.shape[2]] = term_buf[t]


def experts_call(at, blocks, held, x_parts, g_all, info, slots, w_in, w_down, s_in, s_down, capacity):
    counts = [len(parts) for parts in x_parts]
    x_parts = [x for parts in x_parts for x in parts]
    groups, local = len(counts), w_in.shape[0]
    chunks = info.shape[0] - groups - 2
    model, whole_width = g_all.shape[1], x_parts[0].shape[1]
    lanes = whole_width - model
    tokens = sum(x.shape[0] for x in x_parts[: counts[0]])
    tile = 512 if groups <= 2 else 256
    tiles = model // tile
    width, s_width = w_down.shape[1], s_down.shape[0]
    rows = groups * capacity

    def tokens_in(i, info):
        return (0, jnp.minimum(i, tiles - 1))

    def grads_in(t):
        return pl.BlockSpec((tokens, tile), lambda i, info: (info[t], jnp.minimum(i, tiles - 1)))

    def picked(i, info):
        return (0, at, jnp.minimum(i, tiles - 1))

    def own(i, info):
        return (at, jnp.minimum(i, tiles - 1))

    def summed(i, info):
        return (info[groups + chunks + 1], jnp.clip(i - tiles, 0, tiles - 1))

    def summed_norm(i, info):
        return (0, jnp.maximum(i - tiles, 0))

    in_specs = [
        *(pl.BlockSpec((x.shape[0], tile), tokens_in) for x in x_parts),
        *(pl.BlockSpec((x.shape[0], lanes), lambda i, info: (0, model // lanes)) for x in x_parts),
        *(grads_in(t) for t in range(groups)),
        whole_spec(slots.shape),
        whole_spec(slots.shape[::-1]),
        pl.BlockSpec((local, tile, 2 * width), lambda i, info: (0, i % tiles, 0)),
        pl.BlockSpec((local, width, tile), lambda i, info: (0, 0, i % tiles)),
        pl.BlockSpec((tile, 2 * s_width), lambda i, info: (i % tiles, 0)),
        pl.BlockSpec((s_width, tile), lambda i, info: (0, i % tiles)),
        *[pl.BlockSpec(memory_space=pl.ANY)] * len(held),
    ]
    kept = (
        jax.ShapeDtypeStruct((local, blocks * rows, model), bf16),
        jax.ShapeDtypeStruct((local, blocks * rows, model), bf16),
        jax.ShapeDtypeStruct((local, blocks * rows, width), bf16),
        jax.ShapeDtypeStruct((local, blocks * rows, 2 * width), bf16),
        jax.ShapeDtypeStruct((blocks * tokens, model), bf16),
        jax.ShapeDtypeStruct((blocks * tokens, model), bf16),
        jax.ShapeDtypeStruct((blocks * tokens, s_width), bf16),
        jax.ShapeDtypeStruct((blocks * tokens, 2 * s_width), bf16),
        *[jax.ShapeDtypeStruct((blocks * tokens, model), bf16)] * groups,
    )
    norms = (jax.ShapeDtypeStruct((tokens, whole_width), bf16),) * groups
    out_specs = [
        pl.BlockSpec((local, rows, tile), picked),
        pl.BlockSpec((local, rows, tile), picked),
        pl.BlockSpec((local, rows, width), lambda i, info: (0, at, 0)),
        pl.BlockSpec((local, rows, 2 * width), lambda i, info: (0, at, 0)),
        pl.BlockSpec((tokens, tile), own),
        pl.BlockSpec((tokens, tile), own),
        pl.BlockSpec((tokens, s_width), lambda i, info: (at, 0)),
        pl.BlockSpec((tokens, 2 * s_width), lambda i, info: (at, 0)),
        *[pl.BlockSpec((tokens, tile), summed)] * groups,
        *[pl.BlockSpec((tokens, tile), summed_norm)] * groups,
    ]
    work = 2 * model * (
        4 * groups * local * capacity * tokens + 6 * local * rows * width + 6 * tokens * s_width
    )
    first = 1 + len(in_specs) - len(held)
    results = pl.pallas_call(
        functools.partial(experts_kernel, counts, len(held), local, tiles, chunks),
        out_shape=(*kept, *norms),
        grid_spec=pltpu.PrefetchScalarGridSpec(
            num_scalar_prefetch=1,
            grid=(2 * tiles + 1,),
            in_specs=in_specs,
            out_specs=out_specs,
            scratch_shapes=[
                pltpu.VMEM((groups * local, capacity, tokens), bf16),
                pltpu.VMEM((groups, tokens, local * capacity), bf16),
                pltpu.VMEM((local, rows, 2 * width), f32),
                pltpu.VMEM((local, rows, width), f32),
                pltpu.VMEM((tokens, 2 * s_width), f32),
                pltpu.VMEM((tokens, s_width), f32),
                pltpu.VMEM((groups, tokens, lanes), bf16),
            ],
        ),
        input_output_aliases={first + i: i for i in range(len(held))},
        compiler_params=pltpu.CompilerParams(vmem_limit_bytes=vmem_limit),
        cost_estimate=pl.CostEstimate(flops=work // cheap, bytes_accessed=2**10, transcendentals=0),
    )(info, *x_parts, *x_parts, *[g_all] * groups, slots, slots.T, w_in, w_down, s_in, s_down, *held)
    return list(results[: len(kept)]), list(results[len(kept) :])


def shards(
    inputs,
    routes,
    w_query,
    w_key,
    w_value,
    w_output,
    gain_attn,
    gain_moe,
    w_router,
    shared_gate,
    shared_up,
    shared_down,
    expert_gate,
    expert_up,
    expert_down,
    out_grad,
):
    e, r, c = lax.axis_index("exp"), lax.axis_index("row"), lax.axis_index("col")
    E, R, C = lax.axis_size("exp"), lax.axis_size("row"), lax.axis_size("col")
    local_count, model_width, _ = expert_gate.shape
    n_experts = local_count * E * R
    block_rows, top_count = routes.shape
    capacity = 4 * block_rows * top_count // (3 * n_experts)
    home_rows = block_rows // C
    head_width = HEAD_DIM
    query_width, key_width = w_query.shape[1], w_key.shape[1]
    group_heads = query_width // key_width
    attn_scale = head_width ** (-0.5)
    sources = ring_sources("col")

    x = tokens_home(inputs, 0).astype(f32)
    small = jnp.concatenate([w_router.T, gain_attn[None], gain_moe[None]], axis=0)
    small_all = jnp.zeros((small.shape[0], model_width), f32)
    for s, part in enumerate(exchange(small, "col")):
        small_all = lax.dynamic_update_slice(small_all, part, (0, (c ^ s) * small.shape[1]))
    router_t, gain_one, gain_two = (
        small_all[:n_experts],
        small_all[n_experts],
        small_all[n_experts + 1],
    )
    inv_one = rms_inverse(x)
    norm_one = (x * inv_one * gain_one[None, :]).astype(bf16)
    norm_one_all = jnp.concatenate(row_gather(norm_one), axis=0)

    own_weights = own_share(jnp.concatenate([w_key, w_value, w_query, w_output], axis=1))
    weights = lax.all_gather(own_weights, ("col", "exp"), tiled=True)
    in_width = query_width + 2 * key_width
    weight_in = weights[:, :in_width]
    weight_out = weights[:, in_width:].reshape(C, query_width, -1)
    weight_out = weight_out.transpose(1, 0, 2).reshape(query_width, model_width)
    raw = dot(norm_one_all, weight_in)
    wait = zero_of(raw)
    g = tokens_home(out_grad, zero_of(x, small_all))
    g_all = lax.all_gather(g, ("exp", "row", "col"), tiled=True)

    s_width = shared_gate.shape[1] // C
    s_padded = -(-s_width // 128) * 128
    pad = ((0, 0), (0, s_padded - s_width))
    own_gate, own_up = own_share(shared_gate, wait), own_share(shared_up, wait)
    in_rows = own_gate.shape[0]
    down_share, feature_width = s_width // E, shared_down.shape[1]

    def col_swap(x):
        return lax.all_to_all(x, "col", split_axis=0, concat_axis=0, tiled=True)

    to_in = jnp.concatenate([own_gate, own_up], axis=1).reshape(in_rows, 2, C, s_width)
    to_in = to_in.transpose(2, 0, 1, 3).reshape(C, in_rows, 2 * s_width)
    to_down = shared_down.reshape(C, E, down_share, feature_width)
    to_down = lax.dynamic_index_in_dim(to_down, e + wait, 1, keepdims=False)
    sh_in = all_shares(col_swap(to_in)[None]).transpose(1, 0, 2, 3).reshape(model_width, 2, s_width)
    sh_in = jnp.pad(sh_in, ((0, 0), *pad)).reshape(model_width, 2 * s_padded)
    sh_down = all_shares(col_swap(to_down)[None]).transpose(0, 2, 1, 3).reshape(s_width, model_width)
    sh_down = jnp.pad(sh_down, ((0, s_padded - s_width), (0, 0)))
    expert_in = side_by_side(expert_gate, expert_up, wait)

    own_routes = lax.dynamic_slice_in_dim(routes, c * home_rows, home_rows, 0)
    routes_here = routes.reshape(C, home_rows, top_count)[sources].reshape(block_rows, top_count)
    expert_ids = jnp.arange(n_experts)
    first_expert = (e * R + r) * local_count
    own_ids = first_expert + jnp.arange(local_count)
    earlier = (jnp.arange(block_rows)[:, None] < jnp.arange(block_rows)[None, :]).astype(bf16)
    routes_t = routes_here.T
    routes_t = routes_t + wait
    named = jnp.stack(
        [
            (block[None] == own_ids[:, None, None]).any(axis=1)
            for of_row in exchange(routes_t, "row")
            for block in exchange(of_row, "exp")
        ]
    ).reshape(R, E * local_count, block_rows)
    rank = dot(named.reshape(-1, block_rows).astype(bf16), earlier).astype(jnp.int32)
    slots = jnp.where(named, rank.reshape(named.shape), -1)

    positions = (
        ((r ^ jnp.arange(R)) * block_rows + c * home_rows)[:, None]
        + jnp.arange(home_rows)[None, :]
    ).reshape(-1)
    cosines, sines = rope_tables(positions, head_width)
    own_rows = R * home_rows
    keys = rotate(raw[:, :key_width].reshape(own_rows, 1, head_width), cosines, sines)
    kv = jnp.concatenate([keys.reshape(own_rows, key_width), raw[:, key_width : 2 * key_width]], axis=1)
    kv_parts = exchange(kv.astype(bf16), "col")
    queries = rotate(
        raw[:, 2 * key_width :].reshape(own_rows, group_heads, head_width), cosines, sines
    )
    queries = (queries * attn_scale).astype(bf16).reshape(own_rows, query_width)
    place = jnp.concatenate([jnp.stack([r, c]), c ^ jnp.arange(C)]).astype(jnp.int32)
    attended, att_total, lse = attention_forward(place, queries, kv_parts, home_rows)
    attn_part = dot(attended, weight_out).astype(bf16)
    hidden_state = x + row_reduce(jnp.split(attn_part, R, axis=0))
    inv_two = rms_inverse(hidden_state) + zero_of(sh_in, sh_down).astype(f32)
    norm_two = (hidden_state * inv_two * gain_two[None, :]).astype(bf16)

    norm_float = norm_two.astype(f32)
    logits = lax.dot_general(
        norm_float, router_t, (((1,), (1,)), ((), ())), precision=highest
    )
    router_probs = jax.nn.softmax(logits, axis=-1)
    routed = (own_routes[:, :, None] == expert_ids[None, None, :]).any(axis=1)
    chosen = jnp.where(routed, router_probs, 0.0)
    chosen_sum = jnp.sum(chosen, axis=1, keepdims=True)
    mix = chosen / chosen_sum

    mix_lanes = -(-n_experts // 64) * 64
    mix_first = lax.reduce_precision(mix, 8, 7)
    mix_pad = ((0, 0), (0, mix_lanes - n_experts))
    payload = jnp.concatenate(
        [
            norm_two,
            jnp.pad(mix_first.astype(bf16), mix_pad),
            jnp.pad((mix - mix_first).astype(bf16), mix_pad),
        ],
        axis=1,
    )
    payload_rows = exchange(jnp.concatenate(ring_gather(payload, "col"), axis=0), "row")
    kept, norms, moved = [], [], []
    for s in range(R):
        x_block = payload_rows[s]
        if E > 2 and kept:
            x_block = after(x_block, kept[-1])
        waits = [payload_rows[2]] if s == 1 else [payload_rows[3]] if s == 2 else []
        if s:
            waits.append(norms[s - 1])
        if s >= 3:
            waits.append(moved[s - 3])
        info = jnp.concatenate(
            [(e ^ jnp.arange(E)) * R + (r ^ s), sources, jnp.stack([first_expert, r ^ s])]
        ).astype(jnp.int32)
        kept, norm = experts_call(
            s, R, kept, [[block] for block in exchange(x_block, "exp")], g_all, info,
            slots[s] + zero_of(*waits), expert_in, expert_down, sh_in, sh_down, capacity,
        )
        if s == R - 1:
            norm = [norm[0], *(after(x, moved[-1]) for x in norm[1:])]
        norms.append(reduce_parts(norm, "exp").astype(bf16))
        if s:
            moved.append(swap(norms[s], "row", s))
    kept, outs = kept[:8], kept[8:]
    norm_block = norms[0].astype(f32)
    for x_sum in moved:
        norm_block = norm_block + x_sum.astype(f32)
    chunks = jnp.split(norm_block.astype(bf16), C, axis=0)
    home = ring_reduce(chunks, "col")
    d_norm, gate_terms = home[:, :model_width], home[:, model_width : model_width + n_experts]
    outs = [outs[0], *(after(x, norms[-1]) for x in outs[1:])]
    out_sum = after(reduce_parts(outs, "exp").astype(bf16), moved[-1])
    out_rows = lax.psum_scatter(out_sum, "row", scatter_dimension=0, tiled=True)

    rows_x, rows_g, hidden, pre, own_x, own_g, s_hidden, s_pre = kept
    expert_width = expert_gate.shape[2]
    pre = after(pre, moved[-1])
    grad_expert_gate = batch_dot("lrd,lrf->ldf", rows_x, pre[:, :, :expert_width])
    grad_expert_up = batch_dot("lrd,lrf->ldf", rows_x, pre[:, :, expert_width:])
    inner = jnp.sum(mix * gate_terms, axis=1, keepdims=True)
    d_probs = jnp.where(routed, (gate_terms - inner) / chosen_sum, 0.0)
    d_logits = router_probs * (
        d_probs - jnp.sum(router_probs * d_probs, axis=1, keepdims=True)
    )
    d_norm = d_norm + jnp.dot(d_logits, router_t, precision=highest)
    d_norm = d_norm + zero_of(grad_expert_gate, grad_expert_up).astype(f32)
    router_part = lax.dot_general(
        d_logits, norm_float, (((0,), (0,)), ((), ())), precision=highest
    )
    d_v, gain_two_part = rms_backward(hidden_state, inv_two, gain_two, d_norm)
    d_hidden = g.astype(f32) + d_v
    d_attn = d_hidden.astype(bf16)
    d_attn_all = jnp.concatenate(row_gather(d_attn), axis=0)

    grad_expert_down = batch_dot("lrf,lrd->lfd", after(hidden, d_attn), rows_g)

    d_attended = dot(d_attn_all, weight_out, (1, 1)).astype(bf16)
    d_queries, d_kv_parts = attention_backward(
        place + zero_of(grad_expert_down), queries, d_attended, att_total, lse, kv_parts, home_rows
    )
    d_kv = reduce_parts([d_kv_parts[k] for k in range(C)], "col")
    d_query_raw = rotate(
        d_queries.reshape(own_rows, group_heads, head_width), cosines, -sines
    ) * (attn_scale + zero_of(out_rows).astype(f32))
    d_key_raw = rotate(d_kv[:, :key_width].reshape(own_rows, 1, head_width), cosines, -sines)
    d_raw = jnp.concatenate(
        [
            d_key_raw.reshape(own_rows, key_width),
            d_kv[:, key_width:],
            d_query_raw.reshape(own_rows, query_width),
        ],
        axis=1,
    ).astype(bf16)
    norm_one_part = dot(d_raw, weight_in, (1, 1)).astype(bf16)
    d_norm_one = row_reduce(jnp.split(norm_one_part, R, axis=0))
    out_rows = after(out_rows, norm_one_part)
    moe_out = ring_reduce(jnp.split(out_rows, C, axis=0), "col")
    d_x, gain_one_part = rms_backward(
        x, inv_one, gain_one + zero_of(moe_out).astype(f32), d_norm_one
    )
    grad_inputs = tokens_back((d_hidden + d_x).astype(bf16))

    output = tokens_back((hidden_state + moe_out).astype(bf16))
    grad_output = reduce_weight(
        batch_dot("sf,scd->cfd", attended, d_attn_all.reshape(own_rows, C, -1))
        .astype(bf16)
        .reshape(C * query_width, -1)
    )
    grad_in_all = reduce_weight(dot(norm_one_all, d_raw, (0, 0)).astype(bf16))

    small_part = jnp.concatenate([router_part, gain_one_part[None], gain_two_part[None]], axis=0)
    width = small.shape[1]
    mine = [
        lax.dynamic_slice_in_dim(small_part, (c ^ s) * width, width, 1) for s in range(C)
    ]
    small_sum = all_sum(all_sum(reduce_parts(mine, "col"), "row"), "exp")

    s_pre, s_hidden = after(s_pre, d_attn), after(s_hidden, d_attn)
    d_in = dot(own_x, s_pre, (0, 0)).reshape(C, E, in_rows, 2, s_padded)[..., :s_width]
    d_in = d_in.astype(bf16).reshape(C, E, in_rows, 2 * s_width)
    d_down = dot(s_hidden, own_g, (0, 0)).astype(bf16)[:s_width]
    d_down = d_down.reshape(E, down_share, C, feature_width).transpose(2, 0, 1, 3)

    def shared_back(grad):
        mine = [lax.dynamic_index_in_dim(grad, e ^ t, 1, keepdims=False) for t in range(E)]
        return all_shares(col_swap(reduce_parts(mine, "exp").astype(bf16))[None])

    grad_shared_in = shared_back(d_in).reshape(E, C, in_rows, 2, s_width)
    grad_shared_in = grad_shared_in.transpose(3, 0, 2, 1, 4).reshape(2, E * in_rows, C * s_width)
    grad_shared_gate, grad_shared_up = grad_shared_in.astype(f32)
    grad_shared_down = shared_back(d_down).transpose(1, 0, 2, 3).astype(f32)
    return (
        output,
        grad_inputs,
        grad_in_all[:, 2 * key_width :],
        grad_in_all[:, :key_width],
        grad_in_all[:, key_width : 2 * key_width],
        grad_output,
        small_sum[n_experts],
        small_sum[n_experts + 1],
        small_sum[:n_experts].T,
        grad_shared_gate,
        grad_shared_up,
        grad_shared_down.reshape(C * s_width, model_width // C),
        grad_expert_gate,
        grad_expert_up,
        grad_expert_down,
    )


def solution(mesh):
    tokens, weight, experts = P(("exp", "row"), "col"), P("col", "row"), P(("exp", "row"), None, "col")
    expert_down, feature = P(("exp", "row"), "col", None), P("col")
    placed = (
        tokens,
        P(("exp", "row"), None),
        weight,
        weight,
        weight,
        P("row", "col"),
        feature,
        feature,
        P("col", None),
        weight,
        weight,
        P("row", "col"),
        experts,
        experts,
        expert_down,
        tokens,
    )
    return jax.shard_map(
        shards,
        mesh=mesh,
        in_specs=placed,
        out_specs=(
            tokens,
            tokens,
            weight,
            weight,
            weight,
            P("row", "col"),
            feature,
            feature,
            P("col", None),
            weight,
            weight,
            P("row", "col"),
            experts,
            experts,
            expert_down,
        ),
        check_vma=False,
    )
```

time: 2830 us -> 1300 us (0.46)
  waiting for transfers between devices: 1400 us -> 381 us
  blocking collectives: 330 us -> 0 us
  local copies, waits for them, and re-layouts: 560 us -> 254 us
  matrix products: 327 us -> 109 us
  Pallas kernels: 0 us -> 210 us
  starting transfers between devices: 24.9 us -> 210 us
  other arithmetic: 155 us -> 80 us
    all_to_all x3 -> x4, waiting for transfers between devices: 535 us -> 13 us  [col_swap(): return lax.all_to_all(x, 'col', split_axis=0, concat_axis=0, tiled=True)]
    reduce_scatter x9 -> x3, waiting for transfers between devices: 441 us -> 0.02 us  [the longest x2 0.02 us: reduce_weight(): lax.psum_scatter(grad, ('col', 'exp'), scatter_dimension=0, tiled=True)]
    ppermute x0 -> x82, waiting for transfers between devices: none -> 367 us  [the longest x73 269 us: swap(): lax.ppermute(x, axis, [(i, i ^ step) for i in range(lax.axis_size(axis))])]
    all_gather x10 -> x2, waiting for transfers between devices: 354 us -> 0.79 us  [the longest x1 0.79 us: shards(): weights = lax.all_gather(own_weights, ('col', 'exp'), tiled=True)]
    all_to_all x1 -> x0, blocking collectives: 233 us -> none  [send_experts(): lax.all_to_all(source, ('exp', 'row'), split_axis=1, concat_axis=1, tiled...]
    gather x8 -> x2, local copies, waits for them, and re-layouts: 225 us -> 1.19 us  [the longest x1 0.64 us: ring_sources(): return jnp.array(order)[(place - jnp.arange(n)) % n]]
    dot_general x31 -> x15, matrix products: 327 us -> 109 us  [the longest x4 58.4 us: batch_dot(): return jnp.einsum(spec, left, right, preferred_element_type=f32)]
    pallas_call x0 -> x15, Pallas kernels: none -> 210 us  [the longest x4 171 us: experts_call(): pl.pallas_call(functools.partial(experts_kernel, counts, len(held), local...]
  transfers between devices with their start and end apart: 25 -> 91, of which waited for: 19 -> 39; matrix products, arithmetic and copies ran while one was open for 27% -> 33% of each run, Pallas kernels for 0% -> 13%
where the time goes in v1:
time: 1300 us; the launch traced here: 1280 us
  waiting for transfers between devices  381 us (29%)
  local copies, waits for them, and re-layouts  254 us (20%)
  starting transfers between devices  210 us (16%)
  Pallas kernels  210 us (16%)
  matrix products  109 us (8%)
  other arithmetic  80 us (6%)
  between operations  37 us (3%)
    ppermute x73, waiting for transfers between devices, swap(): lax.ppermute(x, axis, [(i, i ^ step) for i in range(lax.axis_size(axis))])  269 us
    pallas_call x4, Pallas kernels, experts_call(): pl.pallas_call(functools.partial(experts_kernel, counts, len(held), local...  171 us
    ppermute x73, starting transfers between devices, swap(): lax.ppermute(x, axis, [(i, i ^ step) for i in range(lax.axis_size(axis))])  169 us
    dynamic_update_slice x12, local copies, waits for them, and re-layouts, all_shares(): whole = lax.dynamic_update_index_in_dim(whole, piece, e ^ t, 0)  89.1 us
    ppermute x6, waiting for transfers between devices, ring_reduce(): total = total + lax.ppermute(parts[k], axis, pairs).astype(f32)  65.8 us
    dot_general x4, matrix products, batch_dot(): return jnp.einsum(spec, left, right, preferred_element_type=f32)  58.4 us
    unnamed x175, local copies, waits for them, and re-layouts  48.6 us
    dot_general x8, matrix products, dot(): lax.dot_general(left, right, (((contract[0],), (contract[1],)), ((), ()))...  46.5 us
  transfers between devices with their start and end apart: 91, of which 39 were waited for; matrix products, arithmetic and copies ran while one was open for 33% of the time, Pallas kernels for 13%

profile of v1, /device:TPU:9, one launch (start us, length us, event | category | flops | bytes accessed | tf_op | source)
XLA Modules:
  0.0 1281.2 jit_solution(16427582029062012673)
XLA Ops:
  28.1 15.7 %collective-permute-done.2 = bf16[128,640]{1,0:T(8,128)(2,1)S(1)} collective-permute-done((bf16[128,640]{1,0:T(8,128)(2,1)S(1)}, bf16[128,640]{1,0:T(8,128)(2,1)S(1)}, u32[]{:S(2)}, u32[]{:S(2)}) %collective-permute-start.2) | collective-permute-done | bytes 163872 | tf_op jit(solution)/shard_map/ppermute | solution.py:23
  67.1 17.4 %collective-permute-done.26 = bf16[128,640]{1,0:T(8,128)(2,1)S(1)} collective-permute-done((bf16[128,640]{1,0:T(8,128)(2,1)S(1)}, bf16[128,640]{1,0:T(8,128)(2,1)S(1)}, u32[]{:S(2)}, u32[]{:S(2)}) %collective-permute-start.26) | collective-permute-done | bytes 163872 | tf_op jit(solution)/shard_map/ppermute | solution.py:23
  148.2 25.5 %collective-permute-done.12.refs_3_ = bf16[512,256]{1,0:T(8,128)(2,1)} collective-permute-done((bf16[512,256]{1,0:T(8,128)(2,1)S(1)}, bf16[512,256]{1,0:T(8,128)(2,1)}, u32[]{:S(2)}, u32[]{:S(2)}) %collective-permute-start.12) | collective-permute-done | bytes 262176 | tf_op jit(solution)/shard_map/ppermute | solution.py:23
  173.7 12.5 shard_map.289
  204.6 17.7 %collective-permute-start.18 = (bf16[1,4,96,640]{3,2,1,0:T(8,128)(2,1)}, bf16[1,4,96,640]{3,2,1,0:T(8,128)(2,1)}, u32[]{:S(2)}, u32[]{:S(2)}) collective-permute-start(bf16[1,4,96,640]{3,2,1,0:T(8,128)(2,1)} %bitcast.24), channel_id=1, source_target_pairs={{0,16},{16,0},{1,17},{17,1},{2,18},{18,2},{3,19},{19,3},{4,20},{20... | collective-permute-start | bytes 1474568 | tf_op jit(solution)/shard_map/ppermute | solution.py:23
  222.4 13.0 %all-to-all-done = bf16[4,320,384]{2,1,0:T(8,128)(2,1)} async-done(((bf16[4,320,384]{2,1,0:T(8,128)(2,1)}), bf16[4,320,384]{2,1,0:T(8,128)(2,1)}, u32[]{:S(2)}, u32[]{:S(2)}) %all-to-all-start) | async-done | bytes 983072 | tf_op jit(solution)/shard_map/all_to_all | solution.py:664
  235.4 17.3 %collective-permute-start.17 = (bf16[1,4,320,384]{3,2,1,0:T(8,128)(2,1)}, bf16[1,4,320,384]{3,2,1,0:T(8,128)(2,1)}, u32[]{:S(2)}, u32[]{:S(2)}) collective-permute-start(bf16[1,4,320,384]{3,2,1,0:T(8,128)(2,1)} %bitcast.19), channel_id=1, source_target_pairs={{0,16},{16,0},{1,17},{17,1},{2,18},{18,2},{3,19},{19,3},{4,20},{20... | collective-permute-start | bytes 2949128 | tf_op jit(solution)/shard_map/ppermute | solution.py:23
  268.9 38.1 %dynamic_update_slice.114 = bf16[2,4,320,384]{2,0,1,3:T(2,128)(2,1)} dynamic-update-slice(bf16[2,4,320,384]{2,0,1,3:T(2,128)(2,1)} %reshape.531, bf16[1,4,320,384]{2,0,1,3:T(2,128)(2,1)} %copy.304, s32[]{:T(128)S(6)} %select_n.162, s32[]{:T(128)} %constant.118.clone.1, s32[]{:T(128)} %constant.118.clone.1, s32[]{:T(128)} %constant.118.clone.1) | dynamic-update-slice | bytes 1966084 | tf_op jit(solution)/shard_map/jit(dynamic_update_index_in_dim)/dynamic_update_slice | solution.py:155
  313.5 38.0 %dynamic_update_slice.115 = bf16[2,4,320,384]{2,0,1,3:T(2,128)(2,1)} dynamic-update-slice(bf16[2,4,320,384]{2,0,1,3:T(2,128)(2,1)} %dynamic_update_slice.114, bf16[1,4,320,384]{2,0,1,3:T(2,128)(2,1)} %copy.305, s32[]{:T(128)S(6)} %select_n.163, s32[]{:T(128)} %constant.118.clone.1, s32[]{:T(128)} %constant.118.clone.1, s32[]{:T(128)} %constant.118.clone.1) | dynamic-update-slice | bytes 1966084 | tf_op jit(solution)/shard_map/jit(dynamic_update_index_in_dim)/dynamic_update_slice | solution.py:155
  371.8 14.9 %collective-permute-done.19 = bf16[128,2688]{1,0:T(8,128)(2,1)S(1)} collective-permute-done((bf16[128,2688]{1,0:T(8,128)(2,1)S(1)}, bf16[128,2688]{1,0:T(8,128)(2,1)S(1)}, u32[]{:S(2)}, u32[]{:S(2)}) %collective-permute-start.19) | collective-permute-done | bytes 688160 | tf_op jit(solution)/shard_map/ppermute | solution.py:84
  391.7 12.1 collective-permute-done.20
  427.1 9.6 shard_map.290.refs_8_
  441.2 42.7 %shard_map.291 = (bf16[2,2048,2560]{2,1,0:T(8,128)(2,1)}, bf16[2,2048,2560]{2,1,0:T(8,128)(2,1)}, bf16[2,2048,384]{2,1,0:T(8,128)(2,1)}, bf16[2,2048,768]{2,1,0:...) custom-call(s32[8]{0:T(128)} %get-tuple-element.308.info, ...), custom_call_target="tpu_custom_call" | custom-call | flops 1638400 | bytes 1024 | tf_op jit(solution)/shard_map/pallas_call | solution.py:575
  484.6 14.0 %collective-permute-done.36.refs_0_.refs_2_ = bf16[512,2688]{1,0:T(8,128)(2,1)} collective-permute-done((bf16[512,2688]{1,0:T(8,128)(2,1)}, bf16[512,2688]{1,0:T(8,128)(2,1)}, u32[]{:S(2)}, u32[]{:S(2)}) %collective-permute-start.36) | collective-permute-done | bytes 2752544 | tf_op jit(solution)/shard_map/ppermute | solution.py:23
  512.9 42.5 %shard_map.292 = (bf16[2,2048,2560]{2,1,0:T(8,128)(2,1)}, bf16[2,2048,2560]{2,1,0:T(8,128)(2,1)}, bf16[2,2048,384]{2,1,0:T(8,128)(2,1)}, bf16[2,2048,768]{2,1,0:...) custom-call(s32[8]{0:T(128)} %get-tuple-element.310.info, ...), custom_call_target="tpu_custom_call", output_to_operand_aliasing={{0}: (13, {}), {1}: (14, {}), {2}: (15, {}), {3}: (16, {}),... | custom-call | flops 1638400 | bytes 1024 | tf_op jit(solution)/shard_map/pallas_call | solution.py:575
  572.4 43.0 %shard_map.293 = (bf16[2,2048,2560]{2,1,0:T(8,128)(2,1)}, bf16[2,2048,2560]{2,1,0:T(8,128)(2,1)}, bf16[2,2048,384]{2,1,0:T(8,128)(2,1)}, bf16[2,2048,768]{2,1,0:...) custom-call(s32[8]{0:T(128)} %get-tuple-element.309.info, ...), custom_call_target="tpu_custom_call", output_to_operand_aliasing={{0}: (13, {}), {1}: (14, {}), {2}: (15, {}), {3}: (16, {}),... | custom-call | flops 1638400 | bytes 1024 | tf_op jit(solution)/shard_map/pallas_call | solution.py:575
  616.4 59.5 %collective-permute-start.42 = (bf16[512,2688]{1,0:T(8,128)(2,1)S(1)}, bf16[512,2688]{1,0:T(8,128)(2,1)S(1)}, u32[]{:S(2)}, u32[]{:S(2)}) collective-permute-start(bf16[512,2688]{1,0:T(8,128)(2,1)S(1)} %copy-done.28), channel_id=1, source_target_pairs={{0,4},{4,0},{8,12},{12,8},{1,5},{5,1},{9,13},{13,9},{2,6},{6,2},{1... | collective-permute-start | bytes 8257544 | tf_op jit(solution)/shard_map/ppermute | solution.py:23
  682.4 53.4 %collective-permute-done.42 = bf16[512,2688]{1,0:T(8,128)(2,1)S(1)} collective-permute-done((bf16[512,2688]{1,0:T(8,128)(2,1)S(1)}, bf16[512,2688]{1,0:T(8,128)(2,1)S(1)}, u32[]{:S(2)}, u32[]{:S(2)}) %collective-permute-start.42) | collective-permute-done | bytes 2752544 | tf_op jit(solution)/shard_map/ppermute | solution.py:23
  739.1 42.7 %shard_map.294 = (bf16[2,2048,2560]{2,1,0:T(8,128)(2,1)}, bf16[2,2048,2560]{2,1,0:T(8,128)(2,1)}, bf16[2,2048,384]{2,1,0:T(8,128)(2,1)}, bf16[2,2048,768]{2,1,0:...) custom-call(s32[8]{0:T(128)} %get-tuple-element.311.info, ...), custom_call_target="tpu_custom_call", output_to_operand_aliasing={{0}: (13, {}), {1}: (14, {}), {2}: (15, {}), {3}: (16, {}),... | custom-call | flops 1638400 | bytes 1024 | tf_op jit(solution)/shard_map/pallas_call | solution.py:575
  792.5 15.5 %collective-permute-done.45 = bf16[2048,2560]{1,0:T(8,128)(2,1)S(1)} collective-permute-done((bf16[2048,2560]{1,0:T(8,128)(2,1)}, bf16[2048,2560]{1,0:T(8,128)(2,1)S(1)}, u32[]{:S(2)}, u32[]{:S(2)}) %collective-permute-start.45) | collective-permute-done | bytes 10485792 | tf_op jit(solution)/shard_map/ppermute | solution.py:23
  807.9 11.1 add_convert_fusion.refs_0_
  819.1 35.2 %collective-permute-done.46.refs_1_ = bf16[512,2688]{1,0:T(8,128)(2,1)} collective-permute-done((bf16[512,2688]{1,0:T(8,128)(2,1)}, bf16[512,2688]{1,0:T(8,128)(2,1)}, u32[]{:S(2)}, u32[]{:S(2)}) %collective-permute-start.46) | collective-permute-done | bytes 2752544 | tf_op jit(solution)/shard_map/ppermute | solution.py:23
  867.2 18.6 %fusion.3 = f32[2,2560,384]{2,1,0:T(8,128)} fusion(bf16[2,2048,2560]{2,1,0:T(8,128)(2,1)} %get-tuple-element.110, bf16[2,2048,768]{2,1,0:T(8,128)(2,1)} %shard_map.298), kind=kOutput, calls=%fused_computation.16 | convolution fusion | flops 8053063680 | bytes 31981568 | tf_op jit(solution)/shard_map/lrd,lrf->ldf/dot_general | solution.py:187
  885.8 18.8 %fusion.5 = f32[2,2560,384]{2,1,0:T(8,128)} fusion(bf16[2,2048,2560]{2,1,0:T(8,128)(2,1)} %get-tuple-element.110, bf16[2,2048,768]{2,1,0:T(8,128)(2,1)} %shard_map.298), kind=kOutput, calls=%fused_computation.18 | convolution fusion | flops 8053063680 | bytes 31981568 | tf_op jit(solution)/shard_map/lrd,lrf->ldf/dot_general | solution.py:187
  911.8 12.8 collective-permute-done.49
  945.6 10.1 convolution_convert_fusion.1
  1002.0 15.7 %fusion.86 = f32[2,384,2560]{2,1,0:T(8,128)} fusion(bf16[2,2048,384]{2,1,0:T(8,128)(2,1)} %shard_map.299, bf16[2,2048,2560]{2,1,0:T(8,128)(2,1)} %get-tuple-element.112), kind=kOutput, calls=%fused_computation.286 | convolution fusion | flops 8053063680 | bytes 31981568 | tf_op jit(solution)/shard_map/lrf,lrd->lfd/dot_general | solution.py:187
  1037.6 16.6 %shard_map.300 = (f32[512,640]{1,0:T(8,128)}, bf16[4,512,256]{2,1,0:T(8,128)(2,1)}) custom-call(s32[6]{0:T(128)} %broadcast_add_fusion.place, bf16[512,640]{1,0:T(8,128)(2,1)} %copy.298.q_ref, bf16[512,640]{1,0:T(8,128)(2,1)} %convolution_convert_fusion.4.grad_ref, f32[4,128,640]{2,1,0:T(8,128)} %get-tuple-element.113.total_ref, ...), custom_call_target="tpu_custom_call" | custom-call | flops 409600 | bytes 1024 | tf_op jit(solution)/shard_map/pallas_call | solution.py:336
  1069.2 11.5 collective-permute-done.55
  1171.1 11.6 collective-permute-done.57
  1182.7 27.8 %collective-permute-done.58 = bf16[128,2560]{1,0:T(8,128)(2,1)S(1)} collective-permute-done((bf16[128,2560]{1,0:T(8,128)(2,1)S(1)}, bf16[128,2560]{1,0:T(8,128)(2,1)S(1)}, u32[]{:S(2)}, u32[]{:S(2)}) %collective-permute-start.58) | collective-permute-done | bytes 655392 | tf_op jit(solution)/shard_map/ppermute | solution.py:94
  1210.5 11.7 collective-permute-done.59
  (572 shorter events, 497.7 us)
Async XLA Ops:
  7.2 102.3 %all-gather.3.cloned.1.call-start = ((), (), s32[]{:S(2)}) async-start(), calls=%async_computation.7 | async-start | bytes 8847360 | tf_op jit(solution)/shard_map/all_gather | solution.py:646
  9.7 431.6 %all-gather.5.cloned.1.call-start = ((), (), s32[]{:S(2)}) async-start(), calls=%async_computation.8 | async-start | bytes 21626880 | tf_op jit(solution)/shard_map/all_gather | solution.py:654
  127.0 46.7 %collective-permute-start.12 = (bf16[512,256]{1,0:T(8,128)(2,1)S(1)}, bf16[512,256]{1,0:T(8,128)(2,1)}, u32[]{:S(2)}, u32[]{:S(2)}) collective-permute-start(bf16[512,256]{1,0:T(8,128)(2,1)S(1)} %pad_maximum_fusion.9.refs_0_), channel_id=1, source_target_pairs={{0,3},{1,2},{2,1},{3,0},{4,7},{5,6},{6,5},{7,4},{8,11},{9,10},{10,... | collective-permute-start | bytes 786440 | tf_op jit(solution)/shard_map/ppermute | solution.py:23
  128.0 69.9 %all-to-all-start.1 = ((bf16[4,96,640]{2,1,0:T(8,128)(2,1)}), bf16[4,96,640]{2,1,0:T(8,128)(2,1)}, u32[]{:S(2)}, u32[]{:S(2)}) async-start(bf16[4,96,640]{2,1,0:T(8,128)(2,1)} %dynamic-slice_bitcast_fusion), calls=%async_computation.1 | async-start | bytes 983040 | tf_op jit(solution)/shard_map/all_to_all | solution.py:664
  198.0 37.4 %all-to-all-start = ((bf16[4,320,384]{2,1,0:T(8,128)(2,1)}), bf16[4,320,384]{2,1,0:T(8,128)(2,1)}, u32[]{:S(2)}, u32[]{:S(2)}) async-start(bf16[4,320,384]{2,1,0:T(8,128)(2,1)} %copy.303), calls=%async_computation | async-start | bytes 1966080 | tf_op jit(solution)/shard_map/all_to_all | solution.py:664
  202.7 904.4 %reduce-scatter.4.cloned.1.call-start = ((), (), s32[]{:S(2)}) async-start(), calls=%async_computation.9 | async-start | bytes 13107200 | tf_op jit(solution)/shard_map/reduce_scatter | solution.py:767
  204.3 53.6 %collective-permute-start.14 = (bf16[128,2560]{1,0:T(8,128)(2,1)S(1)}, bf16[128,2560]{1,0:T(8,128)(2,1)}, u32[]{:S(2)}, u32[]{:S(2)}) collective-permute-start(bf16[128,2560]{1,0:T(8,128)(2,1)S(1)} %pad_maximum_fusion.3), channel_id=1, source_target_pairs={{0,4},{4,0},{8,12},{12,8},{1,5},{5,1},{9,13},{13,9},{2,6},{6,2},{1... | collective-permute-start | bytes 1966088 | tf_op jit(solution)/shard_map/ppermute | solution.py:23
  204.6 49.9 %collective-permute-start.18 = (bf16[1,4,96,640]{3,2,1,0:T(8,128)(2,1)}, bf16[1,4,96,640]{3,2,1,0:T(8,128)(2,1)}, u32[]{:S(2)}, u32[]{:S(2)}) collective-permute-start(bf16[1,4,96,640]{3,2,1,0:T(8,128)(2,1)} %bitcast.24), channel_id=1, source_target_pairs={{0,16},{16,0},{1,17},{17,1},{2,18},{18,2},{3,19},{19,3},{4,20},{20... | collective-permute-start | bytes 1474568 | tf_op jit(solution)/shard_map/ppermute | solution.py:23
  222.4 35.5 %collective-permute-start.16 = (bf16[128,2560]{1,0:T(8,128)(2,1)S(1)}, bf16[128,2560]{1,0:T(8,128)(2,1)S(1)}, u32[]{:S(2)}, u32[]{:S(2)}) collective-permute-start(bf16[128,2560]{1,0:T(8,128)(2,1)S(1)} %pad_maximum_fusion.4), channel_id=1, source_target_pairs={{0,8},{4,12},{8,0},{12,4},{1,9},{5,13},{9,1},{13,5},{2,10},{6,14},... | collective-permute-start | bytes 1966088 | tf_op jit(solution)/shard_map/ppermute | solution.py:23
  235.4 71.6 %collective-permute-start.17 = (bf16[1,4,320,384]{3,2,1,0:T(8,128)(2,1)}, bf16[1,4,320,384]{3,2,1,0:T(8,128)(2,1)}, u32[]{:S(2)}, u32[]{:S(2)}) collective-permute-start(bf16[1,4,320,384]{3,2,1,0:T(8,128)(2,1)} %bitcast.19), channel_id=1, source_target_pairs={{0,16},{16,0},{1,17},{17,1},{2,18},{18,2},{3,19},{19,3},{4,20},{20... | collective-permute-start | bytes 2949128 | tf_op jit(solution)/shard_map/ppermute | solution.py:23
  437.0 61.6 %collective-permute-start.36 = (bf16[512,2688]{1,0:T(8,128)(2,1)}, bf16[512,2688]{1,0:T(8,128)(2,1)}, u32[]{:S(2)}, u32[]{:S(2)}) collective-permute-start(bf16[512,2688]{1,0:T(8,128)(2,1)} %pad_maximum_fusion.refs_0_.refs_2_), channel_id=1, source_target_pairs={{0,4},{4,0},{8,12},{12,8},{1,5},{5,1},{9,13},{13,9},{2,6},{6,2},{1... | collective-permute-start | bytes 8257544 | tf_op jit(solution)/shard_map/ppermute | solution.py:23
  440.9 61.5 %collective-permute-start.34 = (bf16[512,2688]{1,0:T(8,128)(2,1)}, bf16[512,2688]{1,0:T(8,128)(2,1)}, u32[]{:S(2)}, u32[]{:S(2)}) collective-permute-start(bf16[512,2688]{1,0:T(8,128)(2,1)} %pad_maximum_fusion.refs_0_.refs_2_), channel_id=1, source_target_pairs={{0,8},{4,12},{8,0},{12,4},{1,9},{5,13},{9,1},{13,5},{2,10},{6,14},... | collective-permute-start | bytes 8257544 | tf_op jit(solution)/shard_map/ppermute | solution.py:23
  500.1 62.5 %collective-permute-start.22 = (bf16[512,2688]{1,0:T(8,128)(2,1)}, bf16[512,2688]{1,0:T(8,128)(2,1)}, u32[]{:S(2)}, u32[]{:S(2)}) collective-permute-start(bf16[512,2688]{1,0:T(8,128)(2,1)} %pad_maximum_fusion.refs_0_.refs_2_), channel_id=1, source_target_pairs={{0,12},{4,8},{8,4},{12,0},{1,13},{5,9},{9,5},{13,1},{2,14},{6,10},... | collective-permute-start | bytes 8257544 | tf_op jit(solution)/shard_map/ppermute | solution.py:23
  615.5 60.4 %collective-permute-start.41 = (bf16[512,2688]{1,0:T(8,128)(2,1)}, bf16[512,2688]{1,0:T(8,128)(2,1)S(1)}, u32[]{:S(2)}, u32[]{:S(2)}) collective-permute-start(bf16[512,2688]{1,0:T(8,128)(2,1)} %get-tuple-element.94), channel_id=1, source_target_pairs={{0,16},{16,0},{1,17},{17,1},{2,18},{18,2},{3,19},{19,3},{4,20},{20... | collective-permute-start | bytes 8257544 | tf_op jit(solution)/shard_map/ppermute | solution.py:23
  616.3 122.8 %collective-permute-start.23 = (bf16[512,2688]{1,0:T(8,128)(2,1)}, bf16[512,2688]{1,0:T(8,128)(2,1)}, u32[]{:S(2)}, u32[]{:S(2)}) collective-permute-start(bf16[512,2688]{1,0:T(8,128)(2,1)} %collective-permute-done.22.refs_0_.refs_2_), channel_id=1, source_target_pairs={{0,16},{16,0},{1,17},{17,1},{2,18},{18,2},{3,19},{19,3},{4,20},{20... | collective-permute-start | bytes 8257544 | tf_op jit(solution)/shard_map/ppermute | solution.py:23
  616.4 119.3 %collective-permute-start.42 = (bf16[512,2688]{1,0:T(8,128)(2,1)S(1)}, bf16[512,2688]{1,0:T(8,128)(2,1)S(1)}, u32[]{:S(2)}, u32[]{:S(2)}) collective-permute-start(bf16[512,2688]{1,0:T(8,128)(2,1)S(1)} %copy-done.28), channel_id=1, source_target_pairs={{0,4},{4,0},{8,12},{12,8},{1,5},{5,1},{9,13},{13,9},{2,6},{6,2},{1... | collective-permute-start | bytes 8257544 | tf_op jit(solution)/shard_map/ppermute | solution.py:23
  679.8 101.9 %collective-permute-start.43 = (bf16[512,2688]{1,0:T(8,128)(2,1)}, bf16[512,2688]{1,0:T(8,128)(2,1)}, u32[]{:S(2)}, u32[]{:S(2)}) collective-permute-start(bf16[512,2688]{1,0:T(8,128)(2,1)} %add_convert_fusion.3), channel_id=1, source_target_pairs={{0,8},{4,12},{8,0},{12,4},{1,9},{5,13},{9,1},{13,5},{2,10},{6,14},... | collective-permute-start | bytes 8257544 | tf_op jit(solution)/shard_map/ppermute | solution.py:23
  791.9 62.3 %collective-permute-start.46 = (bf16[512,2688]{1,0:T(8,128)(2,1)}, bf16[512,2688]{1,0:T(8,128)(2,1)}, u32[]{:S(2)}, u32[]{:S(2)}) collective-permute-start(bf16[512,2688]{1,0:T(8,128)(2,1)} %add_convert_fusion.2.refs_1_), channel_id=1, source_target_pairs={{0,12},{4,8},{8,4},{12,0},{1,13},{5,9},{9,5},{13,1},{2,14},{6,10},... | collective-permute-start | bytes 8257544 | tf_op jit(solution)/shard_map/ppermute | solution.py:23
  854.3 270.7 %reduce-scatter.8.cloned.1.call-start = ((), (), s32[]{:S(2)}) async-start(), calls=%async_computation.11 | async-start | bytes 3686400 | tf_op jit(solution)/shard_map/reduce_scatter | solution.py:160
  862.8 47.0 %collective-permute-start.47 = (bf16[128,2688]{1,0:T(8,128)(2,1)}, bf16[128,2688]{1,0:T(8,128)(2,1)S(1)}, u32[]{:S(2)}, u32[]{:S(2)}) collective-permute-start(bf16[128,2688]{1,0:T(8,128)(2,1)} %get-tuple-element.239), channel_id=1, source_target_pairs={{0,2},{1,0},{3,1},{2,3},{4,6},{5,4},{7,5},{6,7},{8,10},{9,8},{11,9... | collective-permute-start | bytes 2064392 | tf_op jit(solution)/shard_map/ppermute | solution.py:94
  863.5 48.3 %collective-permute-start.48 = (bf16[128,2688]{1,0:T(8,128)(2,1)}, bf16[128,2688]{1,0:T(8,128)(2,1)}, u32[]{:S(2)}, u32[]{:S(2)}) collective-permute-start(bf16[128,2688]{1,0:T(8,128)(2,1)} %get-tuple-element.241), channel_id=1, source_target_pairs={{0,3},{1,2},{3,0},{2,1},{4,7},{5,6},{7,4},{6,5},{8,11},{9,10},{11,... | collective-permute-start | bytes 2064392 | tf_op jit(solution)/shard_map/ppermute | solution.py:94
  866.4 58.2 %collective-permute-start.49 = (bf16[128,2688]{1,0:T(8,128)(2,1)}, bf16[128,2688]{1,0:T(8,128)(2,1)}, u32[]{:S(2)}, u32[]{:S(2)}) collective-permute-start(bf16[128,2688]{1,0:T(8,128)(2,1)} %get-tuple-element.240), channel_id=1, source_target_pairs={{0,1},{1,3},{3,2},{2,0},{4,5},{5,7},{7,6},{6,4},{8,9},{9,11},{11,1... | collective-permute-start | bytes 2064392 | tf_op jit(solution)/shard_map/ppermute | solution.py:94
  929.9 46.6 %collective-permute-start.50 = (bf16[128,2560]{1,0:T(8,128)(2,1)S(1)}, bf16[128,2560]{1,0:T(8,128)(2,1)}, u32[]{:S(2)}, u32[]{:S(2)}) collective-permute-start(bf16[128,2560]{1,0:T(8,128)(2,1)S(1)} %get-tuple-element.230.refs_1_), channel_id=1, source_target_pairs={{0,4},{4,0},{8,12},{12,8},{1,5},{5,1},{9,13},{13,9},{2,6},{6,2},{1... | collective-permute-start | bytes 1966088 | tf_op jit(solution)/shard_map/ppermute | solution.py:23
  931.4 43.3 %collective-permute-start.51 = (bf16[128,2560]{1,0:T(8,128)(2,1)S(1)}, bf16[128,2560]{1,0:T(8,128)(2,1)}, u32[]{:S(2)}, u32[]{:S(2)}) collective-permute-start(bf16[128,2560]{1,0:T(8,128)(2,1)S(1)} %get-tuple-element.230.refs_1_), channel_id=1, source_target_pairs={{0,8},{4,12},{8,0},{12,4},{1,9},{5,13},{9,1},{13,5},{2,10},{6,14},... | collective-permute-start | bytes 1966088 | tf_op jit(solution)/shard_map/ppermute | solution.py:23
  944.8 47.4 %collective-permute-start.80 = (bf16[4,96,640]{2,1,0:T(8,128)(2,1)}, bf16[4,96,640]{2,1,0:T(8,128)(2,1)}, u32[]{:S(2)}, u32[]{:S(2)}) collective-permute-start(bf16[4,96,640]{2,1,0:T(8,128)(2,1)} %bitcast.185), channel_id=1, source_target_pairs={{0,16},{16,0},{1,17},{17,1},{2,18},{18,2},{3,19},{19,3},{4,20},{20... | collective-permute-start | bytes 1474568 | tf_op jit(solution)/shard_map/ppermute | solution.py:23
  974.6 49.8 %collective-permute-start.78 = (bf16[4,320,384]{2,1,0:T(8,128)(2,1)}, bf16[4,320,384]{2,1,0:T(8,128)(2,1)}, u32[]{:S(2)}, u32[]{:S(2)}) collective-permute-start(bf16[4,320,384]{2,1,0:T(8,128)(2,1)} %bitcast.207), channel_id=1, source_target_pairs={{0,16},{16,0},{1,17},{17,1},{2,18},{18,2},{3,19},{19,3},{4,20},{20... | collective-permute-start | bytes 2949128 | tf_op jit(solution)/shard_map/ppermute | solution.py:23
  1027.2 63.5 %all-to-all-start.2 = ((bf16[4,320,384]{2,1,0:T(8,128)(2,1)}), bf16[4,320,384]{2,1,0:T(8,128)(2,1)S(1)}, u32[]{:S(2)}, u32[]{:S(2)}) async-start(bf16[4,320,384]{2,1,0:T(8,128)(2,1)} %fusion.13), calls=%async_computation.5 | async-start | bytes 1966080 | tf_op jit(solution)/shard_map/all_to_all | solution.py:664
  1031.8 235.5 %reduce-scatter.6.cloned.1.call-start = ((), (), s32[]{:S(2)}) async-start(), calls=%async_computation.10 | async-start | bytes 5160960 | tf_op jit(solution)/shard_map/reduce_scatter | solution.py:160
  1161.7 48.8 %collective-permute-start.58 = (bf16[128,2560]{1,0:T(8,128)(2,1)S(1)}, bf16[128,2560]{1,0:T(8,128)(2,1)S(1)}, u32[]{:S(2)}, u32[]{:S(2)}) collective-permute-start(bf16[128,2560]{1,0:T(8,128)(2,1)S(1)} %get-tuple-element.250), channel_id=1, source_target_pairs={{0,3},{1,2},{3,0},{2,1},{4,7},{5,6},{7,4},{6,5},{8,11},{9,10},{11,... | collective-permute-start | bytes 1966088 | tf_op jit(solution)/shard_map/ppermute | solution.py:94
  1162.3 60.0 %collective-permute-start.59 = (bf16[128,2560]{1,0:T(8,128)(2,1)S(1)}, bf16[128,2560]{1,0:T(8,128)(2,1)S(1)}, u32[]{:S(2)}, u32[]{:S(2)}) collective-permute-start(bf16[128,2560]{1,0:T(8,128)(2,1)S(1)} %get-tuple-element.249), channel_id=1, source_target_pairs={{0,1},{1,3},{3,2},{2,0},{4,5},{5,7},{7,6},{6,4},{8,9},{9,11},{11,1... | collective-permute-start | bytes 1966088 | tf_op jit(solution)/shard_map/ppermute | solution.py:94
  1168.8 64.1 %collective-permute-start.64 = (bf16[128,2560]{1,0:T(8,128)(2,1)S(1)}, bf16[128,2560]{1,0:T(8,128)(2,1)S(1)}, u32[]{:S(2)}, u32[]{:S(2)}) collective-permute-start(bf16[128,2560]{1,0:T(8,128)(2,1)S(1)} %pad_maximum_fusion.5), channel_id=1, source_target_pairs={{0,4},{4,0},{8,12},{12,8},{1,5},{5,1},{9,13},{13,9},{2,6},{6,2},{1... | collective-permute-start | bytes 1966088 | tf_op jit(solution)/shard_map/ppermute | solution.py:23
  1170.0 62.9 %collective-permute-start.66 = (bf16[128,2560]{1,0:T(8,128)(2,1)S(1)}, bf16[128,2560]{1,0:T(8,128)(2,1)S(1)}, u32[]{:S(2)}, u32[]{:S(2)}) collective-permute-start(bf16[128,2560]{1,0:T(8,128)(2,1)S(1)} %pad_maximum_fusion.6), channel_id=1, source_target_pairs={{0,8},{4,12},{8,0},{12,4},{1,9},{5,13},{9,1},{13,5},{2,10},{6,14},... | collective-permute-start | bytes 1966088 | tf_op jit(solution)/shard_map/ppermute | solution.py:23
  (136 other events, 2891.8 us)
Sparse Core Ops, SparseCore 0:
  10.3 99.2 all-gather.2
  112.4 176.3 all-gather.4
  854.4 119.1 reduce-scatter.3
  992.3 88.3 reduce-scatter.7
  1118.3 82.8 reduce-scatter.5

commit v2 on v1

--- a/solution.py
+++ b/solution.py
@@ -16,7 +16,6 @@
 f32 = jnp.float32
 bf16 = jnp.bfloat16
 vmem_limit = 56 * 2**20
-cheap = 2**14
 
 
 def swap(x, axis, step):
@@ -50,15 +49,15 @@
     return found
 
 
-def after(x, earlier):
+def after(x, *earlier):
     place = pl.BlockSpec(memory_space=pl.ANY)
     return pl.pallas_call(
         lambda *refs: None,
         out_shape=jax.ShapeDtypeStruct(x.shape, x.dtype),
-        in_specs=[place, place],
+        in_specs=[place] * (1 + len(earlier)),
         out_specs=place,
         input_output_aliases={0: 0},
-    )(x, earlier)
+    )(x, *earlier)
 
 
 def ring_order(n):
@@ -85,13 +84,16 @@
     return parts
 
 
+def ring_send(x, axis, k):
+    order = ring_order(lax.axis_size(axis))
+    n = len(order)
+    return lax.ppermute(x, axis, [(order[i], order[(i - k) % n]) for i in range(n)])
+
+
 def ring_reduce(parts, axis):
-    n = len(parts)
-    order = ring_order(n)
     total = parts[0].astype(f32)
-    for k in range(1, n):
-        pairs = [(order[i], order[(i - k) % n]) for i in range(n)]
-        total = total + lax.ppermute(parts[k], axis, pairs).astype(f32)
+    for k in range(1, len(parts)):
+        total = total + ring_send(parts[k], axis, k).astype(f32)
     return total
 
 
@@ -109,7 +111,7 @@
 
 def row_reduce(blocks):
     if len(blocks) != 4:
-        return reduce_parts(blocks, "row")
+        return reduce_parts(blocks, "row"), blocks[:1]
     own, x_near, y_near, far = blocks
     middle = own.shape[0] // 2
     far_x, far_y = swap(far[:middle], "row", 1), swap(far[middle:], "row", 2)
@@ -117,7 +119,7 @@
     x_second = add(x_near[middle:], far_y).astype(bf16)
     y_sum = swap(jnp.concatenate([y_first, y_near[middle:]], axis=0), "row", 2)
     x_sum = swap(jnp.concatenate([x_near[:middle], x_second], axis=0), "row", 1)
-    return add(own, x_sum) + y_sum.astype(f32)
+    return add(own, x_sum) + y_sum.astype(f32), [far_x, far_y]
 
 
 def tokens_home(x, wait):
@@ -156,9 +158,9 @@
     return whole.reshape((shares * total.shape[0],) + total.shape[1:])
 
 
-def reduce_weight(grad):
+def reduce_weight(grad, late):
     total = lax.psum_scatter(grad, ("col", "exp"), scatter_dimension=0, tiled=True)
-    return all_shares(total).astype(f32)
+    return all_shares(after(total, late)).astype(f32)
 
 
 def rope_tables(positions, head_width):
@@ -306,6 +308,9 @@
             dkv_ref[k, s * chunk : (s + 1) * chunk, width:] = dv_buf[at, :].astype(bf16)
 
 
+in_place = pl.BlockSpec(memory_space=pl.ANY)
+
+
 def whole_spec(shape):
     return pl.BlockSpec(shape, lambda *_: (0,) * len(shape))
 
@@ -314,43 +319,194 @@
     count, rows, width = left.shape
     tile = 512
 
-    def kernel(wait_ref, left_ref, right_ref, both_ref):
+    def kernel(left_ref, right_ref, _, both_ref):
         both_ref[:, :width] = left_ref[...]
         both_ref[:, width:] = right_ref[...]
 
-    spec = pl.BlockSpec((None, tile, width), lambda i, j, _: (i, j, 0))
+    spec = pl.BlockSpec((None, tile, width), lambda i, j: (i, j, 0))
     return pl.pallas_call(
         kernel,
         out_shape=jax.ShapeDtypeStruct((count, rows, 2 * width), left.dtype),
-        grid_spec=pltpu.PrefetchScalarGridSpec(
-            num_scalar_prefetch=1,
-            grid=(count, rows // tile),
-            in_specs=[spec, spec],
-            out_specs=pl.BlockSpec((None, tile, 2 * width), lambda i, j, _: (i, j, 0)),
-        ),
-        cost_estimate=pl.CostEstimate(flops=0, bytes_accessed=4 * left.nbytes, transcendentals=0),
-    )(wait.reshape(1), left, right)
-
-
-def attention_call(kernel, place, operands, outs, scratch, work):
+        grid=(count, rows // tile),
+        in_specs=[spec, spec, in_place],
+        out_specs=pl.BlockSpec((None, tile, 2 * width), lambda i, j: (i, j, 0)),
+        cost_estimate=pl.CostEstimate(flops=0, bytes_accessed=2**10, transcendentals=0),
+    )(left, right, wait)
+
+
+def rows_at(index, count):
+    return pl.ds(pl.multiple_of(index * count, count), count)
+
+
+def cut_call(kernel, info, operands, outs, waits=()):
     return pl.pallas_call(
-        kernel,
+        lambda info, *refs: kernel(info[0], info[1], *refs[: len(operands)], *refs[len(operands) + len(waits) :]),
         out_shape=outs,
         grid_spec=pltpu.PrefetchScalarGridSpec(
             num_scalar_prefetch=1,
             grid=(1,),
-            in_specs=[whole_spec(x.shape) for x in operands],
+            in_specs=[whole_spec(x.shape) for x in operands] + [in_place] * len(waits),
+            out_specs=[whole_spec(x.shape) for x in outs],
+        ),
+        compiler_params=pltpu.CompilerParams(vmem_limit_bytes=vmem_limit),
+        cost_estimate=pl.CostEstimate(flops=0, bytes_accessed=2**10, transcendentals=0),
+    )(info, *operands, *waits)
+
+
+def join_weight(blocks, first, cols, shares):
+    rows, width = blocks.shape[0] // (cols * shares), blocks.shape[1] - first
+
+    def kernel(ref, out_ref):
+        for k in range(cols):
+            for t in range(shares):
+                at = (k * shares + t) * rows
+                out_ref[t * rows : (t + 1) * rows, k * width : (k + 1) * width] = ref[at : at + rows, first:]
+
+    return pl.pallas_call(
+        kernel,
+        out_shape=jax.ShapeDtypeStruct((shares * rows, cols * width), blocks.dtype),
+        compiler_params=pltpu.CompilerParams(vmem_limit_bytes=vmem_limit),
+        cost_estimate=pl.CostEstimate(flops=0, bytes_accessed=2**10, transcendentals=0),
+    )(blocks)
+
+
+def each_index(index, count, work):
+    for j in range(count):
+        pl.when(index == j)(functools.partial(work, j))
+
+
+def lanes_at(index, width, first, count):
+    return pl.ds(pl.multiple_of(index * width + first, 128), count)
+
+
+def cut_shared(info, gate, up, down, cols, shares, wait):
+    rows, width, features = gate.shape[0] // shares, gate.shape[1] // cols, down.shape[1]
+    both, down_rows = 2 * width, gate.shape[1] // cols // shares
+
+    def kernel(e, c, gate_ref, up_ref, down_ref, out):
+        for k in range(cols):
+            at = rows_at(e, rows)
+            out[c ^ k, :rows, :width] = gate_ref[at, k * width : (k + 1) * width]
+            out[c ^ k, :rows, width:] = up_ref[at, k * width : (k + 1) * width]
+
+        def cut_down(j):
+            for k in range(cols):
+                piece = down_ref[k * width + j * down_rows : k * width + (j + 1) * down_rows, :]
+                out[c ^ k, rows : rows + down_rows, :] = piece[:, :both]
+                out[c ^ k, rows + down_rows :, : features - both] = piece[:, both:]
+
+        each_index(e, shares, cut_down)
+
+    outs = (jax.ShapeDtypeStruct((cols, rows + 2 * down_rows, both), bf16),)
+    return cut_call(kernel, info, (gate, up, down), outs, (wait,))[0]
+
+
+def join_shared(info, parts, rows, features, padded):
+    cols, all_rows, both = parts[0].shape
+    width, shares, down_rows = both // 2, len(parts), (all_rows - rows) // 2
+
+    def kernel(e, c, *refs):
+        in_out, down_out = refs[-2:]
+        in_out[...] = jnp.zeros_like(in_out)
+        down_out[...] = jnp.zeros_like(down_out)
+        for s in range(cols):
+            for t, ref in enumerate(refs[:-2]):
+                at = rows_at((c ^ s) * shares + (e ^ t), rows)
+                in_out[at, :width] = ref[s, :rows, :width]
+                in_out[at, padded : padded + width] = ref[s, :rows, width:]
+
+        def join_down(j):
+            for s in range(cols):
+                for t, ref in enumerate(refs[:-2]):
+                    at = slice((j ^ t) * down_rows, ((j ^ t) + 1) * down_rows)
+                    down_out[at, lanes_at(c ^ s, features, 0, both)] = ref[s, rows : rows + down_rows, :]
+                    down_out[at, lanes_at(c ^ s, features, both, features - both)] = ref[
+                        s, rows + down_rows :, : features - both
+                    ]
+
+        each_index(e, shares, join_down)
+
+    outs = (
+        jax.ShapeDtypeStruct((cols * shares * rows, 2 * padded), bf16),
+        jax.ShapeDtypeStruct((padded, cols * features), bf16),
+    )
+    return cut_call(kernel, info, parts, outs)
+
+
+def cut_shared_grads(info, grad_in, grad_down, cols, shares, width):
+    rows, padded = grad_in.shape[0] // (cols * shares), grad_in.shape[1] // 2
+    both, down_rows, features = 2 * width, width // shares, grad_down.shape[1] // cols
+
+    def kernel(e, c, in_ref, down_ref, *outs):
+        for s in range(cols):
+            for t, out in enumerate(outs):
+                at = rows_at((c ^ s) * shares + (e ^ t), rows)
+                out[s, :rows, :width] = in_ref[at, :width]
+                out[s, :rows, width:] = in_ref[at, padded : padded + width]
+
+        def cut_down(j):
+            for s in range(cols):
+                for t, out in enumerate(outs):
+                    at = slice((j ^ t) * down_rows, ((j ^ t) + 1) * down_rows)
+                    out[s, rows : rows + down_rows, :] = down_ref[at, lanes_at(c ^ s, features, 0, both)]
+                    out[s, rows + down_rows :, : features - both] = down_ref[
+                        at, lanes_at(c ^ s, features, both, features - both)
+                    ]
+
+        each_index(e, shares, cut_down)
+
+    outs = (jax.ShapeDtypeStruct((cols, rows + 2 * down_rows, both), bf16),) * shares
+    return cut_call(kernel, info, (grad_in, grad_down), outs)
+
+
+def join_shared_grads(info, parts, rows, features):
+    cols, all_rows, both = parts[0].shape
+    width, shares, down_rows = both // 2, len(parts), (all_rows - rows) // 2
+
+    def kernel(e, c, *refs):
+        gate_out, up_out, down_out = refs[-3:]
+        for k in range(cols):
+            for t, ref in enumerate(refs[:-3]):
+                at, part = rows_at(e ^ t, rows), ref[c ^ k, :rows, :].astype(f32)
+                gate_out[at, k * width : (k + 1) * width] = part[:, :width]
+                up_out[at, k * width : (k + 1) * width] = part[:, width:]
+
+        def join_down(j):
+            for k in range(cols):
+                for t, ref in enumerate(refs[:-3]):
+                    at = k * width + (j ^ t) * down_rows
+                    at = slice(at, at + down_rows)
+                    down_out[at, :both] = ref[c ^ k, rows : rows + down_rows, :].astype(f32)
+                    down_out[at, both:] = ref[c ^ k, rows + down_rows :, : features - both].astype(f32)
+
+        each_index(e, shares, join_down)
+
+    outs = (
+        *[jax.ShapeDtypeStruct((shares * rows, cols * width), f32)] * 2,
+        jax.ShapeDtypeStruct((cols * width, features), f32),
+    )
+    return cut_call(kernel, info, parts, outs)
+
+
+def attention_call(kernel, place, operands, outs, scratch, work, waits):
+    return pl.pallas_call(
+        lambda place, *refs: kernel(place, *refs[: len(operands)], *refs[len(operands) + len(waits) :]),
+        out_shape=outs,
+        grid_spec=pltpu.PrefetchScalarGridSpec(
+            num_scalar_prefetch=1,
+            grid=(1,),
+            in_specs=[whole_spec(x.shape) for x in operands] + [in_place] * len(waits),
             out_specs=[whole_spec(x.shape) for x in outs],
             scratch_shapes=scratch,
         ),
         compiler_params=pltpu.CompilerParams(vmem_limit_bytes=vmem_limit),
         cost_estimate=pl.CostEstimate(
-            flops=work // cheap, bytes_accessed=2**10, transcendentals=0
+            flops=work, bytes_accessed=2**10, transcendentals=0
         ),
-    )(place, *operands)
-
-
-def attention_forward(place, queries, kv_parts, chunk):
+    )(place, *operands, *waits)
+
+
+def attention_forward(place, queries, kv_parts, chunk, waits):
     rows, total_width = queries.shape
     width = kv_parts[0].shape[1] // 2
     heads, blocks, keys = total_width // width, rows // chunk, rows * len(kv_parts)
@@ -365,10 +521,11 @@
         ),
         [pltpu.VMEM((keys, width), bf16)] * 2,
         4 * rows * heads * keys * width,
-    )
-
-
-def attention_backward(place, queries, grads, out, lse, kv_parts, chunk):
+        waits,
+    )
+
+
+def attention_backward(place, queries, grads, out, lse, kv_parts, chunk, waits):
     rows, total_width = queries.shape
     width = kv_parts[0].shape[1] // 2
     keys = rows * len(kv_parts)
@@ -382,6 +539,7 @@
         ),
         [pltpu.VMEM((keys, width), bf16)] * 2 + [pltpu.VMEM((keys, width), f32)] * 2,
         10 * rows * total_width * keys,
+        waits,
     )
 
 
@@ -392,12 +550,12 @@
     return silu * up_pre, grad_gate.astype(bf16), (grad_hidden * silu).astype(bf16)
 
 
-def experts_kernel(counts, held, local, tiles, chunks, info, *refs):
+def experts_kernel(counts, unused, local, tiles, chunks, info, *refs):
     groups = len(counts)
     x_refs, refs = refs[: sum(counts)], refs[sum(counts) :]
     mix_refs, refs = refs[: sum(counts)], refs[sum(counts) :]
     g_refs, refs = refs[:groups], refs[groups:]
-    refs = refs[:6] + refs[6 + held :]
+    refs = refs[:6] + refs[6 + unused :]
     (
         slot_ref, slot_t_ref, w_in, w_down, s_in, s_down,
         xs_ref, gs_ref, hidden_ref, pre_ref, own_x_ref, own_g_ref, s_hidden_ref, s_pre_ref,
@@ -501,7 +659,7 @@
             norm_refs[t][:, : term_buf.shape[2]] = term_buf[t]
 
 
-def experts_call(at, blocks, held, x_parts, g_all, info, slots, w_in, w_down, s_in, s_down, capacity):
+def experts_call(at, blocks, held, x_parts, g_all, info, slots, w_in, w_down, s_in, s_down, capacity, waits):
     counts = [len(parts) for parts in x_parts]
     x_parts = [x for parts in x_parts for x in parts]
     groups, local = len(counts), w_in.shape[0]
@@ -542,7 +700,7 @@
         pl.BlockSpec((local, width, tile), lambda i, info: (0, 0, i % tiles)),
         pl.BlockSpec((tile, 2 * s_width), lambda i, info: (i % tiles, 0)),
         pl.BlockSpec((s_width, tile), lambda i, info: (0, i % tiles)),
-        *[pl.BlockSpec(memory_space=pl.ANY)] * len(held),
+        *[in_place] * (len(held) + len(waits)),
     ]
     kept = (
         jax.ShapeDtypeStruct((local, blocks * rows, model), bf16),
@@ -571,9 +729,9 @@
     work = 2 * model * (
         4 * groups * local * capacity * tokens + 6 * local * rows * width + 6 * tokens * s_width
     )
-    first = 1 + len(in_specs) - len(held)
+    first = 1 + len(in_specs) - len(held) - len(waits)
     results = pl.pallas_call(
-        functools.partial(experts_kernel, counts, len(held), local, tiles, chunks),
+        functools.partial(experts_kernel, counts, len(held) + len(waits), local, tiles, chunks),
         out_shape=(*kept, *norms),
         grid_spec=pltpu.PrefetchScalarGridSpec(
             num_scalar_prefetch=1,
@@ -592,8 +750,8 @@
         ),
         input_output_aliases={first + i: i for i in range(len(held))},
         compiler_params=pltpu.CompilerParams(vmem_limit_bytes=vmem_limit),
-        cost_estimate=pl.CostEstimate(flops=work // cheap, bytes_accessed=2**10, transcendentals=0),
-    )(info, *x_parts, *x_parts, *[g_all] * groups, slots, slots.T, w_in, w_down, s_in, s_down, *held)
+        cost_estimate=pl.CostEstimate(flops=work, bytes_accessed=2**10, transcendentals=0),
+    )(info, *x_parts, *x_parts, *[g_all] * groups, slots, slots.T, w_in, w_down, s_in, s_down, *held, *waits)
     return list(results[: len(kept)]), list(results[len(kept) :])
 
 
@@ -640,38 +798,31 @@
     )
     inv_one = rms_inverse(x)
     norm_one = (x * inv_one * gain_one[None, :]).astype(bf16)
-    norm_one_all = jnp.concatenate(row_gather(norm_one), axis=0)
+    norm_one_parts = row_gather(norm_one)
+    norm_one_all = jnp.concatenate(norm_one_parts, axis=0)
 
     own_weights = own_share(jnp.concatenate([w_key, w_value, w_query, w_output], axis=1))
     weights = lax.all_gather(own_weights, ("col", "exp"), tiled=True)
-    in_width = query_width + 2 * key_width
-    weight_in = weights[:, :in_width]
-    weight_out = weights[:, in_width:].reshape(C, query_width, -1)
-    weight_out = weight_out.transpose(1, 0, 2).reshape(query_width, model_width)
+    weight_in = weights[:, : query_width + 2 * key_width]
+    g = tokens_home(out_grad, zero_of(*norm_one_parts[1:3]))
+    g_all = lax.all_gather(g, ("exp", "row", "col"), tiled=True)
     raw = dot(norm_one_all, weight_in)
     wait = zero_of(raw)
-    g = tokens_home(out_grad, zero_of(x, small_all))
-    g_all = lax.all_gather(g, ("exp", "row", "col"), tiled=True)
+    here = jnp.stack([e, c]).astype(jnp.int32)
+    weight_out = join_weight(weights, query_width + 2 * key_width, C, E)
 
     s_width = shared_gate.shape[1] // C
     s_padded = -(-s_width // 128) * 128
-    pad = ((0, 0), (0, s_padded - s_width))
-    own_gate, own_up = own_share(shared_gate, wait), own_share(shared_up, wait)
-    in_rows = own_gate.shape[0]
-    down_share, feature_width = s_width // E, shared_down.shape[1]
-
-    def col_swap(x):
-        return lax.all_to_all(x, "col", split_axis=0, concat_axis=0, tiled=True)
-
-    to_in = jnp.concatenate([own_gate, own_up], axis=1).reshape(in_rows, 2, C, s_width)
-    to_in = to_in.transpose(2, 0, 1, 3).reshape(C, in_rows, 2 * s_width)
-    to_down = shared_down.reshape(C, E, down_share, feature_width)
-    to_down = lax.dynamic_index_in_dim(to_down, e + wait, 1, keepdims=False)
-    sh_in = all_shares(col_swap(to_in)[None]).transpose(1, 0, 2, 3).reshape(model_width, 2, s_width)
-    sh_in = jnp.pad(sh_in, ((0, 0), *pad)).reshape(model_width, 2 * s_padded)
-    sh_down = all_shares(col_swap(to_down)[None]).transpose(0, 2, 1, 3).reshape(s_width, model_width)
-    sh_down = jnp.pad(sh_down, ((0, s_padded - s_width), (0, 0)))
-    expert_in = side_by_side(expert_gate, expert_up, wait)
+
+    def col_swap(parts):
+        return jnp.stack([swap(parts[s], "col", s) if s else parts[0] for s in range(C)])
+
+    shared_cut = cut_shared(here, shared_gate, shared_up, shared_down, C, E, raw)
+    in_rows, feature_width = shared_gate.shape[0] // E, shared_down.shape[1]
+    sh_in, sh_down = join_shared(
+        here, exchange(col_swap(shared_cut), "exp"), in_rows, feature_width, s_padded
+    )
+    expert_in = side_by_side(expert_gate, expert_up, raw)
 
     own_routes = lax.dynamic_slice_in_dim(routes, c * home_rows, home_rows, 0)
     routes_here = routes.reshape(C, home_rows, top_count)[sources].reshape(block_rows, top_count)
@@ -705,9 +856,9 @@
     )
     queries = (queries * attn_scale).astype(bf16).reshape(own_rows, query_width)
     place = jnp.concatenate([jnp.stack([r, c]), c ^ jnp.arange(C)]).astype(jnp.int32)
-    attended, att_total, lse = attention_forward(place, queries, kv_parts, home_rows)
+    attended, att_total, lse = attention_forward(place, queries, kv_parts, home_rows, (expert_in, shared_cut))
     attn_part = dot(attended, weight_out).astype(bf16)
-    hidden_state = x + row_reduce(jnp.split(attn_part, R, axis=0))
+    hidden_state = x + row_reduce(jnp.split(attn_part, R, axis=0))[0]
     inv_two = rms_inverse(hidden_state) + zero_of(sh_in, sh_down).astype(f32)
     norm_two = (hidden_state * inv_two * gain_two[None, :]).astype(bf16)
 
@@ -732,30 +883,39 @@
         ],
         axis=1,
     )
-    payload_rows = exchange(jnp.concatenate(ring_gather(payload, "col"), axis=0), "row")
+    payload = jnp.concatenate(ring_gather(payload, "col"), axis=0)
+    payload_rows = row_gather(payload)
+    if R == 4:
+        payload_rows = [[x] for x in payload_rows[:3]] + [payload_rows[3:]]
+    else:
+        payload_rows = [[x] for x in payload_rows]
     kept, norms, moved = [], [], []
     for s in range(R):
         x_block = payload_rows[s]
         if E > 2 and kept:
-            x_block = after(x_block, kept[-1])
-        waits = [payload_rows[2]] if s == 1 else [payload_rows[3]] if s == 2 else []
-        if s:
-            waits.append(norms[s - 1])
-        if s >= 3:
-            waits.append(moved[s - 3])
+            x_block = [after(x, kept[-1]) for x in x_block]
         info = jnp.concatenate(
             [(e ^ jnp.arange(E)) * R + (r ^ s), sources, jnp.stack([first_expert, r ^ s])]
         ).astype(jnp.int32)
         kept, norm = experts_call(
-            s, R, kept, [[block] for block in exchange(x_block, "exp")], g_all, info,
-            slots[s] + zero_of(*waits), expert_in, expert_down, sh_in, sh_down, capacity,
+            s, R, kept, list(zip(*(exchange(x, "exp") for x in x_block))), g_all, info,
+            slots[s], expert_in, expert_down, sh_in, sh_down, capacity, norms[-1:],
         )
-        if s == R - 1:
-            norm = [norm[0], *(after(x, moved[-1]) for x in norm[1:])]
+        seen = moved if s == R - 1 else [x for later in ((1, 2), (3,))[s] for x in payload_rows[later]] if s < 2 else []
+        if seen:
+            norm = [norm[0], *(after(x, *seen) for x in norm[1:])]
         norms.append(reduce_parts(norm, "exp").astype(bf16))
         if s:
             moved.append(swap(norms[s], "row", s))
     kept, outs = kept[:8], kept[8:]
+    rows_x, rows_g, hidden, pre, own_x, own_g, s_hidden, s_pre = kept
+
+    s_pre, s_hidden = after(s_pre, norms[-1]), after(s_hidden, norms[-1])
+    d_in = dot(own_x, s_pre, (0, 0)).astype(bf16)
+    d_down = dot(s_hidden, own_g, (0, 0)).astype(bf16)
+    shared_grads = cut_shared_grads(here, d_in, d_down, C, E, s_width)
+    shared_sums = reduce_parts(shared_grads, "exp").astype(bf16)
+
     norm_block = norms[0].astype(f32)
     for x_sum in moved:
         norm_block = norm_block + x_sum.astype(f32)
@@ -763,21 +923,22 @@
     home = ring_reduce(chunks, "col")
     d_norm, gate_terms = home[:, :model_width], home[:, model_width : model_width + n_experts]
     outs = [outs[0], *(after(x, norms[-1]) for x in outs[1:])]
-    out_sum = after(reduce_parts(outs, "exp").astype(bf16), moved[-1])
+
+    out_sum = after(reduce_parts(outs, "exp").astype(bf16), moved[-1], shared_grads[0])
     out_rows = lax.psum_scatter(out_sum, "row", scatter_dimension=0, tiled=True)
 
-    rows_x, rows_g, hidden, pre, own_x, own_g, s_hidden, s_pre = kept
     expert_width = expert_gate.shape[2]
     pre = after(pre, moved[-1])
     grad_expert_gate = batch_dot("lrd,lrf->ldf", rows_x, pre[:, :, :expert_width])
     grad_expert_up = batch_dot("lrd,lrf->ldf", rows_x, pre[:, :, expert_width:])
+    grad_expert_down = batch_dot("lrf,lrd->lfd", after(hidden, moved[-1]), rows_g)
     inner = jnp.sum(mix * gate_terms, axis=1, keepdims=True)
     d_probs = jnp.where(routed, (gate_terms - inner) / chosen_sum, 0.0)
     d_logits = router_probs * (
         d_probs - jnp.sum(router_probs * d_probs, axis=1, keepdims=True)
     )
     d_norm = d_norm + jnp.dot(d_logits, router_t, precision=highest)
-    d_norm = d_norm + zero_of(grad_expert_gate, grad_expert_up).astype(f32)
+    d_norm = d_norm + zero_of(grad_expert_gate, grad_expert_up, grad_expert_down).astype(f32)
     router_part = lax.dot_general(
         d_logits, norm_float, (((0,), (0,)), ((), ())), precision=highest
     )
@@ -786,16 +947,26 @@
     d_attn = d_hidden.astype(bf16)
     d_attn_all = jnp.concatenate(row_gather(d_attn), axis=0)
 
-    grad_expert_down = batch_dot("lrf,lrd->lfd", after(hidden, d_attn), rows_g)
+    out_grads = batch_dot("sf,scd->cfd", attended, d_attn_all.reshape(own_rows, C, -1))
+    out_grads = out_grads.astype(bf16).reshape(C * query_width, -1)
 
     d_attended = dot(d_attn_all, weight_out, (1, 1)).astype(bf16)
+    out_chunks = jnp.split(after(out_rows, d_attended), C, axis=0)
+    moe_out = out_chunks[0].astype(f32)
+    soon = [ring_send(out_chunks[k], "col", k) for k in range(1, C) if 2 * k != C]
     d_queries, d_kv_parts = attention_backward(
-        place + zero_of(grad_expert_down), queries, d_attended, att_total, lse, kv_parts, home_rows
-    )
+        place, queries, d_attended, att_total, lse, kv_parts, home_rows,
+        (out_grads,),
+    )
+    shared_back = col_swap(after(shared_sums, d_attn))
+    d_kv_parts = after(d_kv_parts, *soon, shared_back)
     d_kv = reduce_parts([d_kv_parts[k] for k in range(C)], "col")
+    soon.append(ring_send(after(out_chunks[C // 2], d_kv), "col", C // 2))
+    for part in soon:
+        moe_out = moe_out + part.astype(f32)
     d_query_raw = rotate(
         d_queries.reshape(own_rows, group_heads, head_width), cosines, -sines
-    ) * (attn_scale + zero_of(out_rows).astype(f32))
+    ) * attn_scale
     d_key_raw = rotate(d_kv[:, :key_width].reshape(own_rows, 1, head_width), cosines, -sines)
     d_raw = jnp.concatenate(
         [
@@ -806,21 +977,15 @@
         axis=1,
     ).astype(bf16)
     norm_one_part = dot(d_raw, weight_in, (1, 1)).astype(bf16)
-    d_norm_one = row_reduce(jnp.split(norm_one_part, R, axis=0))
-    out_rows = after(out_rows, norm_one_part)
-    moe_out = ring_reduce(jnp.split(out_rows, C, axis=0), "col")
-    d_x, gain_one_part = rms_backward(
-        x, inv_one, gain_one + zero_of(moe_out).astype(f32), d_norm_one
-    )
+    d_norm_one, halfway = row_reduce(jnp.split(norm_one_part, R, axis=0))
+    d_x, gain_one_part = rms_backward(x, inv_one, gain_one, d_norm_one)
     grad_inputs = tokens_back((d_hidden + d_x).astype(bf16))
 
     output = tokens_back((hidden_state + moe_out).astype(bf16))
-    grad_output = reduce_weight(
-        batch_dot("sf,scd->cfd", attended, d_attn_all.reshape(own_rows, C, -1))
-        .astype(bf16)
-        .reshape(C * query_width, -1)
-    )
-    grad_in_all = reduce_weight(dot(norm_one_all, d_raw, (0, 0)).astype(bf16))
+    grad_output = reduce_weight(after(out_grads, d_kv), d_norm_one)
+    grad_in_all = reduce_weight(
+        dot(after(norm_one_all, *halfway), d_raw, (0, 0)).astype(bf16), d_norm_one
+    )
 
     small_part = jnp.concatenate([router_part, gain_one_part[None], gain_two_part[None]], axis=0)
     width = small.shape[1]
@@ -829,20 +994,9 @@
     ]
     small_sum = all_sum(all_sum(reduce_parts(mine, "col"), "row"), "exp")
 
-    s_pre, s_hidden = after(s_pre, d_attn), after(s_hidden, d_attn)
-    d_in = dot(own_x, s_pre, (0, 0)).reshape(C, E, in_rows, 2, s_padded)[..., :s_width]
-    d_in = d_in.astype(bf16).reshape(C, E, in_rows, 2 * s_width)
-    d_down = dot(s_hidden, own_g, (0, 0)).astype(bf16)[:s_width]
-    d_down = d_down.reshape(E, down_share, C, feature_width).transpose(2, 0, 1, 3)
-
-    def shared_back(grad):
-        mine = [lax.dynamic_index_in_dim(grad, e ^ t, 1, keepdims=False) for t in range(E)]
-        return all_shares(col_swap(reduce_parts(mine, "exp").astype(bf16))[None])
-
-    grad_shared_in = shared_back(d_in).reshape(E, C, in_rows, 2, s_width)
-    grad_shared_in = grad_shared_in.transpose(3, 0, 2, 1, 4).reshape(2, E * in_rows, C * s_width)
-    grad_shared_gate, grad_shared_up = grad_shared_in.astype(f32)
-    grad_shared_down = shared_back(d_down).transpose(1, 0, 2, 3).astype(f32)
+    grad_shared_gate, grad_shared_up, grad_shared_down = join_shared_grads(
+        here, exchange(after(shared_back, d_norm_one), "exp"), in_rows, feature_width
+    )
     return (
         output,
         grad_inputs,
@@ -855,7 +1009,7 @@
         small_sum[:n_experts].T,
         grad_shared_gate,
         grad_shared_up,
-        grad_shared_down.reshape(C * s_width, model_width // C),
+        grad_shared_down,
         grad_expert_gate,
         grad_expert_up,
         grad_expert_down,

time: 1300 us -> 1030 us (0.79); the launches traced: 1280 us -> 1030 us
  local copies, waits for them, and re-layouts: 254 us -> 60.8 us
  starting transfers between devices: 210 us -> 105 us
  waiting for transfers between devices: 381 us -> 425 us
  Pallas kernels: 210 us -> 235 us
    dynamic_update_slice x12 -> x4, local copies, waits for them, and re-layouts: 89.1 us -> 0.26 us  [all_shares(): whole = lax.dynamic_update_index_in_dim(whole, piece, e ^ t, 0)]
    ppermute x73 -> x78, starting transfers between devices: 169 us -> 91.4 us  [swap(): lax.ppermute(x, axis, [(i, i ^ step) for i in range(lax.axis_size(axis))])]
    ppermute x73 -> x78, waiting for transfers between devices: 269 us -> 345 us  [swap(): lax.ppermute(x, axis, [(i, i ^ step) for i in range(lax.axis_size(axis))])]
    ppermute x6, waiting for transfers between devices: 65.8 us -> 26.5 us  [ring_send(): lax.ppermute(x, axis, [(order[i], order[(i - k) % n]) for i in range(n)])]
    reshape x10 -> x0, local copies, waits for them, and re-layouts: 29.3 us -> none  [the longest x4 9.77 us: all_shares(): return whole.reshape((shares * total.shape[0],) + total.shape[1:])]
    unnamed x175 -> x221, local copies, waits for them, and re-layouts: 48.6 us -> 20.7 us
    pallas_call x6 -> x11, Pallas kernels: 200 us -> 226 us  [the longest x4 171 us: experts_call(): pl.pallas_call(functools.partial(experts_kernel, counts, len(held) + len(...]
    all_to_all x4 -> x0, starting transfers between devices: 23.6 us -> none  [col_swap(): return lax.all_to_all(x, 'col', split_axis=0, concat_axis=0, tiled=True)]
  transfers between devices with their start and end apart: 91 -> 92, of which waited for: 39 -> 51; matrix products, arithmetic and copies ran while one was open for 33% -> 20% of each run, Pallas kernels for 13% -> 19%
where the time goes in v2:
time: 1030 us
  waiting for transfers between devices  425 us (41%)
  Pallas kernels  235 us (23%)
  starting transfers between devices  105 us (10%)
  matrix products  96.2 us (9%)
  other arithmetic  75.7 us (7%)
  local copies, waits for them, and re-layouts  60.8 us (6%)
  between operations  27.6 us (3%)
    ppermute x78, waiting for transfers between devices, swap(): lax.ppermute(x, axis, [(i, i ^ step) for i in range(lax.axis_size(axis))])  345 us
    pallas_call x4, Pallas kernels, experts_call(): pl.pallas_call(functools.partial(experts_kernel, counts, len(held) + len(...  171 us
    ppermute x78, starting transfers between devices, swap(): lax.ppermute(x, axis, [(i, i ^ step) for i in range(lax.axis_size(axis))])  91.4 us
    dot_general x4, matrix products, batch_dot(): return jnp.einsum(spec, left, right, preferred_element_type=f32)  53.1 us
    ppermute x3, waiting for transfers between devices, ring_gather(): parts.append(lax.ppermute(parts[-1], axis, ring_pairs(n)))  50 us
    dot_general x8, matrix products, dot(): lax.dot_general(left, right, (((contract[0],), (contract[1],)), ((), ()))...  39.5 us
    pallas_call x2, Pallas kernels, attention_call(): pl.pallas_call(lambda place, *refs: kernel(place, *refs[:len(operands)],...  28.9 us
    ppermute x6, waiting for transfers between devices, ring_send(): lax.ppermute(x, axis, [(order[i], order[(i - k) % n]) for i in range(n)])  26.5 us
  transfers between devices with their start and end apart: 92, of which 51 were waited for; matrix products, arithmetic and copies ran while one was open for 20% of the time, Pallas kernels for 19%

profile of v2, /device:TPU:9, one launch (start us, length us, event | category | flops | bytes accessed | tf_op | source)
XLA Modules:
  0.0 1025.9 jit_solution(2066484497230021948)
XLA Ops:
  19.6 8.4 collective-permute-done.1
  28.0 15.7 %collective-permute-done.2 = bf16[128,640]{1,0:T(8,128)(2,1)S(1)} collective-permute-done((bf16[128,640]{1,0:T(8,128)(2,1)S(1)}, bf16[128,640]{1,0:T(8,128)(2,1)S(1)}, u32[]{:S(2)}, u32[]{:S(2)}) %collective-permute-start.2) | collective-permute-done | bytes 163872 | tf_op jit(solution)/shard_map/ppermute | solution.py:22
  47.6 8.5 collective-permute-done.6
  73.5 8.2 collective-permute-done.31
  81.8 14.6 %collective-permute-done.32 = bf16[128,640]{1,0:T(8,128)(2,1)S(1)} collective-permute-done((bf16[128,640]{1,0:T(8,128)(2,1)S(1)}, bf16[128,640]{1,0:T(8,128)(2,1)S(1)}, u32[]{:S(2)}, u32[]{:S(2)}) %collective-permute-start.32) | collective-permute-done | bytes 163872 | tf_op jit(solution)/shard_map/ppermute | solution.py:22
  134.7 9.6 shard_map.289.refs_5_.refs_8_.refs_12_
  157.8 12.5 %shard_map.291 = (bf16[512,640]{1,0:T(8,128)(2,1)}, f32[4,128,640]{2,1,0:T(8,128)}, f32[4,1,640]{2,1,0:T(1,128)}) custom-call(s32[6]{0:T(128)} %pad_add_fusion.place, bf16[512,640]{1,0:T(8,128)(2,1)} %copy.160.refs_0_, bf16[512,256]{1,0:T(8,128)(2,1)} %pad_maximum_fusion.10.refs_1_.refs_4_, bf16[512,256]{1,0:T(8,128)(2,1)} %collective-permute-done.10.refs_2_.refs_5_, ...), custom_call_target="tpu_custom_call" | custom-call | flops 2684354560 | bytes 1024 | tf_op jit(solution)/shard_map/pallas_call | solution.py:492
  176.2 20.4 %collective-permute-done.18 = bf16[512,384]{1,0:T(8,128)(2,1)} collective-permute-done((bf16[512,384]{1,0:T(8,128)(2,1)}, bf16[512,384]{1,0:T(8,128)(2,1)}, u32[]{:S(2)}, u32[]{:S(2)}) %collective-permute-start.18) | collective-permute-done | bytes 393248 | tf_op jit(solution)/shard_map/ppermute | solution.py:22
  196.6 21.9 %collective-permute-done.19 = bf16[512,384]{1,0:T(8,128)(2,1)S(1)} collective-permute-done((bf16[512,384]{1,0:T(8,128)(2,1)S(1)}, bf16[512,384]{1,0:T(8,128)(2,1)S(1)}, u32[]{:S(2)}, u32[]{:S(2)}) %collective-permute-start.19) | collective-permute-done | bytes 393248 | tf_op jit(solution)/shard_map/ppermute | solution.py:22
  227.4 24.8 %collective-permute-done.14 = bf16[128,2560]{1,0:T(8,128)(2,1)S(1)} collective-permute-done((bf16[128,2560]{1,0:T(8,128)(2,1)S(1)}, bf16[128,2560]{1,0:T(8,128)(2,1)S(1)}, u32[]{:S(2)}, u32[]{:S(2)}) %collective-permute-start.14) | collective-permute-done | bytes 655392 | tf_op jit(solution)/shard_map/ppermute | solution.py:22
  269.5 35.9 %collective-permute-done.21 = bf16[128,2688]{1,0:T(8,128)(2,1)} collective-permute-done((bf16[128,2688]{1,0:T(8,128)(2,1)S(1)}, bf16[128,2688]{1,0:T(8,128)(2,1)}, u32[]{:S(2)}, u32[]{:S(2)}) %collective-permute-start.21) | collective-permute-done | bytes 688160 | tf_op jit(solution)/shard_map/ppermute | solution.py:83
  310.6 12.6 %collective-permute-done.22 = bf16[128,2688]{1,0:T(8,128)(2,1)} collective-permute-done((bf16[128,2688]{1,0:T(8,128)(2,1)}, bf16[128,2688]{1,0:T(8,128)(2,1)}, u32[]{:S(2)}, u32[]{:S(2)}) %collective-permute-start.22) | collective-permute-done | bytes 688160 | tf_op jit(solution)/shard_map/ppermute | solution.py:83
  351.7 42.5 %shard_map.294 = (bf16[2,2048,2560]{2,1,0:T(8,128)(2,1)}, bf16[2,2048,2560]{2,1,0:T(8,128)(2,1)}, bf16[2,2048,384]{2,1,0:T(8,128)(2,1)}, bf16[2,2048,768]{2,1,0:...) custom-call(s32[8]{0:T(128)} %get-tuple-element.235.info, ...), custom_call_target="tpu_custom_call" | custom-call | flops 26843545600 | bytes 1024 | tf_op jit(solution)/shard_map/pallas_call | solution.py:733
  394.2 15.0 %collective-permute-done.24.refs_2_.refs_0_ = bf16[512,2688]{1,0:T(8,128)(2,1)S(1)} collective-permute-done((bf16[512,2688]{1,0:T(8,128)(2,1)}, bf16[512,2688]{1,0:T(8,128)(2,1)S(1)}, u32[]{:S(2)}, u32[]{:S(2)}) %collective-permute-start.24) | collective-permute-done | bytes 2752544 | tf_op jit(solution)/shard_map/ppermute | solution.py:22
  425.2 42.9 %shard_map.296 = (bf16[2,2048,2560]{2,1,0:T(8,128)(2,1)}, bf16[2,2048,2560]{2,1,0:T(8,128)(2,1)}, bf16[2,2048,384]{2,1,0:T(8,128)(2,1)}, bf16[2,2048,768]{2,1,0:...) custom-call(s32[8]{0:T(128)} %get-tuple-element.237.info, ...), custom_call_target="tpu_custom_call", output_to_operand_aliasing={{0}: (13, {}), {1}: (14, {}), {2}: (15, {}), {3}: (16, {}),... | custom-call | flops 26843545600 | bytes 1024 | tf_op jit(solution)/shard_map/pallas_call | solution.py:733
  480.6 42.9 %shard_map.298 = (bf16[2,2048,2560]{2,1,0:T(8,128)(2,1)}, bf16[2,2048,2560]{2,1,0:T(8,128)(2,1)}, bf16[2,2048,384]{2,1,0:T(8,128)(2,1)}, bf16[2,2048,768]{2,1,0:...) custom-call(s32[8]{0:T(128)} %get-tuple-element.236.info, ...), custom_call_target="tpu_custom_call", output_to_operand_aliasing={{0}: (13, {}), {1}: (14, {}), {2}: (15, {}), {3}: (16, {}),... | custom-call | flops 26843545600 | bytes 1024 | tf_op jit(solution)/shard_map/pallas_call | solution.py:733
  537.4 43.0 %shard_map.299 = (bf16[2,2048,2560]{2,1,0:T(8,128)(2,1)}, bf16[2,2048,2560]{2,1,0:T(8,128)(2,1)}, bf16[2,2048,384]{2,1,0:T(8,128)(2,1)}, bf16[2,2048,768]{2,1,0:...) custom-call(s32[8]{0:T(128)} %get-tuple-element.238.info, ...), custom_call_target="tpu_custom_call", output_to_operand_aliasing={{0}: (17, {}), {1}: (18, {}), {2}: (19, {}), {3}: (20, {}),... | custom-call | flops 26843545600 | bytes 1024 | tf_op jit(solution)/shard_map/pallas_call | solution.py:733
  585.8 10.7 %collective-permute-done.47.refs_2_ = bf16[512,2688]{1,0:T(8,128)(2,1)} collective-permute-done((bf16[512,2688]{1,0:T(8,128)(2,1)}, bf16[512,2688]{1,0:T(8,128)(2,1)}, u32[]{:S(2)}, u32[]{:S(2)}) %collective-permute-start.47) | collective-permute-done | bytes 2752544 | tf_op jit(solution)/shard_map/ppermute | solution.py:22
  606.0 10.4 %convolution_convert_fusion.2.refs_0_ = bf16[2560,512]{1,0:T(8,128)(2,1)} fusion(bf16[2048,2560]{1,0:T(8,128)(2,1)} %get-tuple-element.118, bf16[2048,512]{1,0:T(8,128)(2,1)} %shard_map.302), kind=kOutput, calls=%fused_computation.10 | convolution fusion | flops 5370019840 | bytes 15204352 | tf_op jit(solution)/shard_map/dot_general | solution.py:183
  625.3 13.2 %add_convert_fusion.refs_0_ = bf16[2048,2560]{1,0:T(8,128)(2,1)} fusion(bf16[2048,2560]{1,0:T(8,128)(2,1)} %collective-permute-done.49, bf16[2048,2560]{1,0:T(8,128)(2,1)} %get-tuple-element.114), kind=kLoop, calls=%fused_computation.2 | loop fusion | flops 20971520 | bytes 31457280 | tf_op jit(solution)/shard_map/convert_element_type | solution.py:927
  638.5 29.1 %collective-permute-done.50.refs_1_ = bf16[512,2688]{1,0:T(8,128)(2,1)} collective-permute-done((bf16[512,2688]{1,0:T(8,128)(2,1)}, bf16[512,2688]{1,0:T(8,128)(2,1)}, u32[]{:S(2)}, u32[]{:S(2)}) %collective-permute-start.50) | collective-permute-done | bytes 2752544 | tf_op jit(solution)/shard_map/ppermute | solution.py:22
  687.7 18.4 %fusion.3 = f32[2,2560,384]{2,1,0:T(8,128)} fusion(bf16[2,2048,2560]{2,1,0:T(8,128)(2,1)} %get-tuple-element.123, bf16[2,2048,768]{2,1,0:T(8,128)(2,1)} %shard_map.306), kind=kOutput, calls=%fused_computation.16 | convolution fusion | flops 8053063680 | bytes 31981568 | tf_op jit(solution)/shard_map/lrd,lrf->ldf/dot_general | solution.py:189
  706.1 18.7 %fusion.5 = f32[2,2560,384]{2,1,0:T(8,128)} fusion(bf16[2,2048,2560]{2,1,0:T(8,128)(2,1)} %get-tuple-element.123, bf16[2,2048,768]{2,1,0:T(8,128)(2,1)} %shard_map.306), kind=kOutput, calls=%fused_computation.18 | convolution fusion | flops 8053063680 | bytes 31981568 | tf_op jit(solution)/shard_map/lrd,lrf->ldf/dot_general | solution.py:189
  724.8 12.3 %fusion.79 = f32[2,384,2560]{2,1,0:T(8,128)S(1)} fusion(bf16[2,2048,384]{2,1,0:T(8,128)(2,1)S(1)} %copy-done.3, bf16[2,2048,2560]{2,1,0:T(8,128)(2,1)} %get-tuple-element.126), kind=kOutput, calls=%fused_computation.271 | convolution fusion | flops 8053063680 | bytes 31981568 | tf_op jit(solution)/shard_map/lrf,lrd->lfd/dot_general | solution.py:189
  758.1 13.6 %collective-permute-done.61 = bf16[512,384]{1,0:T(8,128)(2,1)S(1)} collective-permute-done((bf16[512,384]{1,0:T(8,128)(2,1)S(1)}, bf16[512,384]{1,0:T(8,128)(2,1)S(1)}, u32[]{:S(2)}, u32[]{:S(2)}) %collective-permute-start.61) | collective-permute-done | bytes 393248 | tf_op jit(solution)/shard_map/ppermute | solution.py:22
  774.0 17.6 %collective-permute-done.63 = bf16[512,384]{1,0:T(8,128)(2,1)S(1)} collective-permute-done((bf16[512,384]{1,0:T(8,128)(2,1)S(1)}, bf16[512,384]{1,0:T(8,128)(2,1)S(1)}, u32[]{:S(2)}, u32[]{:S(2)}) %collective-permute-start.63) | collective-permute-done | bytes 393248 | tf_op jit(solution)/shard_map/ppermute | solution.py:22
  815.6 16.4 %shard_map.309 = (f32[512,640]{1,0:T(8,128)}, bf16[4,512,256]{2,1,0:T(8,128)(2,1)}) custom-call(s32[6]{0:T(128)} %pad_add_fusion.place, bf16[512,640]{1,0:T(8,128)(2,1)} %copy.160.refs_0_, bf16[512,640]{1,0:T(8,128)(2,1)} %convolution_convert_fusion.5.refs_1_, f32[4,128,640]{2,1,0:T(8,128)} %get-tuple-element.127.refs_2_, ...), custom_call_target="tpu_custom_call" | custom-call | flops 6710886400 | bytes 1024 | tf_op jit(solution)/shard_map/pallas_call | solution.py:492
  845.7 8.6 collective-permute-done.64
  856.4 12.1 %collective-permute-done.66 = bf16[512,256]{1,0:T(8,128)(2,1)S(1)} collective-permute-done((bf16[512,256]{1,0:T(8,128)(2,1)S(1)}, bf16[512,256]{1,0:T(8,128)(2,1)S(1)}, u32[]{:S(2)}, u32[]{:S(2)}) %collective-permute-start.66) | collective-permute-done | bytes 262176 | tf_op jit(solution)/shard_map/ppermute | solution.py:22
  905.7 10.4 %collective-permute-done.72 = bf16[128,2560]{1,0:T(8,128)(2,1)} collective-permute-done((bf16[128,2560]{1,0:T(8,128)(2,1)S(1)}, bf16[128,2560]{1,0:T(8,128)(2,1)}, u32[]{:S(2)}, u32[]{:S(2)}) %collective-permute-start.72) | collective-permute-done | bytes 655392 | tf_op jit(solution)/shard_map/ppermute | solution.py:22
  927.2 18.9 %collective-permute-done.67 = bf16[128,2560]{1,0:T(8,128)(2,1)} collective-permute-done((bf16[128,2560]{1,0:T(8,128)(2,1)}, bf16[128,2560]{1,0:T(8,128)(2,1)}, u32[]{:S(2)}, u32[]{:S(2)}) %collective-permute-start.67) | collective-permute-done | bytes 655392 | tf_op jit(solution)/shard_map/ppermute | solution.py:90
  972.8 14.3 %collective-permute-done.77 = bf16[128,640]{1,0:T(8,128)(2,1)S(1)} collective-permute-done((bf16[128,640]{1,0:T(8,128)(2,1)S(1)}, bf16[128,640]{1,0:T(8,128)(2,1)S(1)}, u32[]{:S(2)}, u32[]{:S(2)}) %collective-permute-start.77) | collective-permute-done | bytes 163872 | tf_op jit(solution)/shard_map/ppermute | solution.py:22
  (590 shorter events, 394.3 us)
Async XLA Ops:
  7.2 102.3 %all-gather.3.cloned.1.call-start = ((), (), s32[]{:S(2)}) async-start(), calls=%async_computation.3 | async-start | bytes 8847360 | tf_op jit(solution)/shard_map/all_gather | solution.py:805
  9.6 342.1 %all-gather.5.cloned.1.call-start = ((), (), s32[]{:S(2)}) async-start(), calls=%async_computation.4 | async-start | bytes 21626880 | tf_op jit(solution)/shard_map/all_gather | solution.py:808
  66.2 30.2 %collective-permute-start.32 = (bf16[128,640]{1,0:T(8,128)(2,1)S(1)}, bf16[128,640]{1,0:T(8,128)(2,1)S(1)}, u32[]{:S(2)}, u32[]{:S(2)}) collective-permute-start(bf16[128,640]{1,0:T(8,128)(2,1)S(1)} %get-tuple-element.213), channel_id=1, source_target_pairs={{0,3},{1,2},{2,1},{3,0},{4,7},{5,6},{6,5},{7,4},{8,11},{9,10},{10,... | collective-permute-start | bytes 491528 | tf_op jit(solution)/shard_map/ppermute | solution.py:22
  97.2 709.7 %reduce-scatter.4.cloned.1.call-start = ((), (), s32[]{:S(2)}) async-start(), calls=%async_computation.5 | async-start | bytes 13107200 | tf_op jit(solution)/shard_map/reduce_scatter | solution.py:928
  117.7 31.9 %collective-permute-start.10 = (bf16[512,256]{1,0:T(8,128)(2,1)}, bf16[512,256]{1,0:T(8,128)(2,1)}, u32[]{:S(2)}, u32[]{:S(2)}) collective-permute-start(bf16[512,256]{1,0:T(8,128)(2,1)} %pad_maximum_fusion.10.refs_1_.refs_4_), channel_id=1, source_target_pairs={{0,1},{1,0},{2,3},{3,2},{4,5},{5,4},{6,7},{7,6},{8,9},{9,8},{10,11... | collective-permute-start | bytes 786440 | tf_op jit(solution)/shard_map/ppermute | solution.py:22
  122.4 35.3 %collective-permute-start.12 = (bf16[512,256]{1,0:T(8,128)(2,1)}, bf16[512,256]{1,0:T(8,128)(2,1)}, u32[]{:S(2)}, u32[]{:S(2)}) collective-permute-start(bf16[512,256]{1,0:T(8,128)(2,1)} %pad_maximum_fusion.10.refs_1_.refs_4_), channel_id=1, source_target_pairs={{0,3},{1,2},{2,1},{3,0},{4,7},{5,6},{6,5},{7,4},{8,11},{9,10},{10,... | collective-permute-start | bytes 786440 | tf_op jit(solution)/shard_map/ppermute | solution.py:22
  129.7 46.5 %collective-permute-start.17 = (bf16[512,384]{1,0:T(8,128)(2,1)}, bf16[512,384]{1,0:T(8,128)(2,1)}, u32[]{:S(2)}, u32[]{:S(2)}) collective-permute-start(bf16[512,384]{1,0:T(8,128)(2,1)} %get-tuple-element.189), channel_id=1, source_target_pairs={{0,1},{1,0},{2,3},{3,2},{4,5},{5,4},{6,7},{7,6},{8,9},{9,8},{10,11... | collective-permute-start | bytes 1179656 | tf_op jit(solution)/shard_map/ppermute | solution.py:22
  131.9 64.6 %collective-permute-start.18 = (bf16[512,384]{1,0:T(8,128)(2,1)}, bf16[512,384]{1,0:T(8,128)(2,1)}, u32[]{:S(2)}, u32[]{:S(2)}) collective-permute-start(bf16[512,384]{1,0:T(8,128)(2,1)} %get-tuple-element.188), channel_id=1, source_target_pairs={{0,2},{1,3},{2,0},{3,1},{4,6},{5,7},{6,4},{7,5},{8,10},{9,11},{10,... | collective-permute-start | bytes 1179656 | tf_op jit(solution)/shard_map/ppermute | solution.py:22
  149.6 68.9 %collective-permute-start.19 = (bf16[512,384]{1,0:T(8,128)(2,1)S(1)}, bf16[512,384]{1,0:T(8,128)(2,1)S(1)}, u32[]{:S(2)}, u32[]{:S(2)}) collective-permute-start(bf16[512,384]{1,0:T(8,128)(2,1)S(1)} %copy-done.60), channel_id=1, source_target_pairs={{0,3},{1,2},{2,1},{3,0},{4,7},{5,6},{6,5},{7,4},{8,11},{9,10},{10,... | collective-permute-start | bytes 1179656 | tf_op jit(solution)/shard_map/ppermute | solution.py:22
  173.7 50.7 %collective-permute-start.13 = (bf16[64,2560]{1,0:T(8,128)(2,1)S(1)}, bf16[64,2560]{1,0:T(8,128)(2,1)S(1)}, u32[]{:S(2)}, u32[]{:S(2)}) collective-permute-start(bf16[64,2560]{1,0:T(8,128)(2,1)S(1)} %get-tuple-element.175), channel_id=1, source_target_pairs={{0,8},{4,12},{8,0},{12,4},{1,9},{5,13},{9,1},{13,5},{2,10},{6,14},... | collective-permute-start | bytes 983048 | tf_op jit(solution)/shard_map/ppermute | solution.py:22
  174.8 49.6 %collective-permute-start.15 = (bf16[64,2560]{1,0:T(8,128)(2,1)S(1)}, bf16[64,2560]{1,0:T(8,128)(2,1)S(1)}, u32[]{:S(2)}, u32[]{:S(2)}) collective-permute-start(bf16[64,2560]{1,0:T(8,128)(2,1)S(1)} %get-tuple-element.174), channel_id=1, source_target_pairs={{0,4},{4,0},{8,12},{12,8},{1,5},{5,1},{9,13},{13,9},{2,6},{6,2},{1... | collective-permute-start | bytes 983048 | tf_op jit(solution)/shard_map/ppermute | solution.py:22
  219.8 36.0 %collective-permute-start.20 = (bf16[4,512,384]{2,1,0:T(8,128)(2,1)S(1)}, bf16[4,512,384]{2,1,0:T(8,128)(2,1)S(1)}, u32[]{:S(2)}, u32[]{:S(2)}) collective-permute-start(bf16[4,512,384]{2,1,0:T(8,128)(2,1)S(1)} %pad_maximum_fusion.1.refs_0_), channel_id=1, source_target_pairs={{0,16},{16,0},{1,17},{17,1},{2,18},{18,2},{3,19},{19,3},{4,20},{20... | collective-permute-start | bytes 4718600 | tf_op jit(solution)/shard_map/ppermute | solution.py:22
  269.4 36.0 %collective-permute-start.21 = (bf16[128,2688]{1,0:T(8,128)(2,1)S(1)}, bf16[128,2688]{1,0:T(8,128)(2,1)}, u32[]{:S(2)}, u32[]{:S(2)}) collective-permute-start(bf16[128,2688]{1,0:T(8,128)(2,1)S(1)} %concatenate.80), channel_id=1, source_target_pairs={{0,1},{1,3},{3,2},{2,0},{4,5},{5,7},{7,6},{6,4},{8,9},{9,11},{11,1... | collective-permute-start | bytes 2064392 | tf_op jit(solution)/shard_map/ppermute | solution.py:83
  347.2 62.0 %collective-permute-start.24 = (bf16[512,2688]{1,0:T(8,128)(2,1)}, bf16[512,2688]{1,0:T(8,128)(2,1)S(1)}, u32[]{:S(2)}, u32[]{:S(2)}) collective-permute-start(bf16[512,2688]{1,0:T(8,128)(2,1)} %pad_maximum_fusion.refs_0_.refs_2_), channel_id=1, source_target_pairs={{0,8},{4,12},{8,0},{12,4},{1,9},{5,13},{9,1},{13,5},{2,10},{6,14},... | collective-permute-start | bytes 8257544 | tf_op jit(solution)/shard_map/ppermute | solution.py:22
  348.9 61.3 %collective-permute-start.26 = (bf16[512,2688]{1,0:T(8,128)(2,1)}, bf16[512,2688]{1,0:T(8,128)(2,1)}, u32[]{:S(2)}, u32[]{:S(2)}) collective-permute-start(bf16[512,2688]{1,0:T(8,128)(2,1)} %pad_maximum_fusion.refs_0_.refs_2_), channel_id=1, source_target_pairs={{0,4},{4,0},{8,12},{12,8},{1,5},{5,1},{9,13},{13,9},{2,6},{6,2},{1... | collective-permute-start | bytes 8257544 | tf_op jit(solution)/shard_map/ppermute | solution.py:22
  414.4 53.7 %collective-permute-start.25 = (bf16[256,2688]{1,0:T(8,128)(2,1)S(1)}, bf16[256,2688]{1,0:T(8,128)(2,1)S(1)}, u32[]{:S(2)}, u32[]{:S(2)}) collective-permute-start(bf16[256,2688]{1,0:T(8,128)(2,1)S(1)} %slice.317), channel_id=1, source_target_pairs={{0,4},{4,0},{8,12},{12,8},{1,5},{5,1},{9,13},{13,9},{2,6},{6,2},{1... | collective-permute-start | bytes 4128776 | tf_op jit(solution)/shard_map/ppermute | solution.py:22
  417.0 51.1 %collective-permute-start.27 = (bf16[256,2688]{1,0:T(8,128)(2,1)}, bf16[256,2688]{1,0:T(8,128)(2,1)S(1)}, u32[]{:S(2)}, u32[]{:S(2)}) collective-permute-start(bf16[256,2688]{1,0:T(8,128)(2,1)} %slice.318), channel_id=1, source_target_pairs={{0,8},{4,12},{8,0},{12,4},{1,9},{5,13},{9,1},{13,5},{2,10},{6,14},... | collective-permute-start | bytes 4128776 | tf_op jit(solution)/shard_map/ppermute | solution.py:22
  524.4 61.5 %collective-permute-start.46 = (bf16[512,2688]{1,0:T(8,128)(2,1)}, bf16[512,2688]{1,0:T(8,128)(2,1)}, u32[]{:S(2)}, u32[]{:S(2)}) collective-permute-start(bf16[512,2688]{1,0:T(8,128)(2,1)} %add_convert_fusion.4.refs_22_), channel_id=1, source_target_pairs={{0,4},{4,0},{8,12},{12,8},{1,5},{5,1},{9,13},{13,9},{2,6},{6,2},{1... | collective-permute-start | bytes 8257544 | tf_op jit(solution)/shard_map/ppermute | solution.py:22
  535.4 61.2 %collective-permute-start.47 = (bf16[512,2688]{1,0:T(8,128)(2,1)}, bf16[512,2688]{1,0:T(8,128)(2,1)}, u32[]{:S(2)}, u32[]{:S(2)}) collective-permute-start(bf16[512,2688]{1,0:T(8,128)(2,1)} %add_convert_fusion.3.refs_26_), channel_id=1, source_target_pairs={{0,8},{4,12},{8,0},{12,4},{1,9},{5,13},{9,1},{13,5},{2,10},{6,14},... | collective-permute-start | bytes 8257544 | tf_op jit(solution)/shard_map/ppermute | solution.py:22
  605.3 62.3 %collective-permute-start.50 = (bf16[512,2688]{1,0:T(8,128)(2,1)}, bf16[512,2688]{1,0:T(8,128)(2,1)}, u32[]{:S(2)}, u32[]{:S(2)}) collective-permute-start(bf16[512,2688]{1,0:T(8,128)(2,1)} %add_convert_fusion.2.refs_1_), channel_id=1, source_target_pairs={{0,12},{4,8},{8,4},{12,0},{1,13},{5,9},{9,5},{13,1},{2,14},{6,10},... | collective-permute-start | bytes 8257544 | tf_op jit(solution)/shard_map/ppermute | solution.py:22
  667.7 335.8 %reduce-scatter.8.cloned.1.call-start = ((), (), s32[]{:S(2)}) async-start(), calls=%async_computation.7 | async-start | bytes 3686400 | tf_op jit(solution)/shard_map/reduce_scatter | solution.py:162
  683.5 61.9 %collective-permute-start.51 = (bf16[128,2688]{1,0:T(8,128)(2,1)}, bf16[128,2688]{1,0:T(8,128)(2,1)}, u32[]{:S(2)}, u32[]{:S(2)}) collective-permute-start(bf16[128,2688]{1,0:T(8,128)(2,1)} %get-tuple-element.160), channel_id=1, source_target_pairs={{0,2},{1,0},{3,1},{2,3},{4,6},{5,4},{7,5},{6,7},{8,10},{9,8},{11,9... | collective-permute-start | bytes 2064392 | tf_op jit(solution)/shard_map/ppermute | solution.py:90
  684.7 60.7 %collective-permute-start.52 = (bf16[128,2688]{1,0:T(8,128)(2,1)}, bf16[128,2688]{1,0:T(8,128)(2,1)}, u32[]{:S(2)}, u32[]{:S(2)}) collective-permute-start(bf16[128,2688]{1,0:T(8,128)(2,1)} %get-tuple-element.162), channel_id=1, source_target_pairs={{0,3},{1,2},{3,0},{2,1},{4,7},{5,6},{7,4},{6,5},{8,11},{9,10},{11,... | collective-permute-start | bytes 2064392 | tf_op jit(solution)/shard_map/ppermute | solution.py:90
  686.6 58.8 %collective-permute-start.53 = (bf16[128,2688]{1,0:T(8,128)(2,1)}, bf16[128,2688]{1,0:T(8,128)(2,1)}, u32[]{:S(2)}, u32[]{:S(2)}) collective-permute-start(bf16[128,2688]{1,0:T(8,128)(2,1)} %get-tuple-element.161), channel_id=1, source_target_pairs={{0,1},{1,3},{3,2},{2,0},{4,5},{5,7},{7,6},{6,4},{8,9},{9,11},{11,1... | collective-permute-start | bytes 2064392 | tf_op jit(solution)/shard_map/ppermute | solution.py:90
  751.0 44.3 %collective-permute-start.54 = (bf16[128,2560]{1,0:T(8,128)(2,1)S(1)}, bf16[128,2560]{1,0:T(8,128)(2,1)S(1)}, u32[]{:S(2)}, u32[]{:S(2)}) collective-permute-start(bf16[128,2560]{1,0:T(8,128)(2,1)S(1)} %get-tuple-element.153.refs_1_), channel_id=1, source_target_pairs={{0,4},{4,0},{8,12},{12,8},{1,5},{5,1},{9,13},{13,9},{2,6},{6,2},{1... | collective-permute-start | bytes 1966088 | tf_op jit(solution)/shard_map/ppermute | solution.py:22
  752.0 41.0 %collective-permute-start.55 = (bf16[128,2560]{1,0:T(8,128)(2,1)S(1)}, bf16[128,2560]{1,0:T(8,128)(2,1)}, u32[]{:S(2)}, u32[]{:S(2)}) collective-permute-start(bf16[128,2560]{1,0:T(8,128)(2,1)S(1)} %get-tuple-element.153.refs_1_), channel_id=1, source_target_pairs={{0,8},{4,12},{8,0},{12,4},{1,9},{5,13},{9,1},{13,5},{2,10},{6,14},... | collective-permute-start | bytes 1966088 | tf_op jit(solution)/shard_map/ppermute | solution.py:22
  757.0 34.6 %collective-permute-start.63 = (bf16[512,384]{1,0:T(8,128)(2,1)S(1)}, bf16[512,384]{1,0:T(8,128)(2,1)S(1)}, u32[]{:S(2)}, u32[]{:S(2)}) collective-permute-start(bf16[512,384]{1,0:T(8,128)(2,1)S(1)} %get-tuple-element.183), channel_id=1, source_target_pairs={{0,3},{1,2},{2,1},{3,0},{4,7},{5,6},{6,5},{7,4},{8,11},{9,10},{10,... | collective-permute-start | bytes 1179656 | tf_op jit(solution)/shard_map/ppermute | solution.py:22
  809.6 30.0 %collective-permute-start.59 = (bf16[128,2560]{1,0:T(8,128)(2,1)S(1)}, bf16[128,2560]{1,0:T(8,128)(2,1)S(1)}, u32[]{:S(2)}, u32[]{:S(2)}) collective-permute-start(bf16[128,2560]{1,0:T(8,128)(2,1)S(1)} %get-tuple-element.169), channel_id=1, source_target_pairs={{0,1},{1,3},{3,2},{2,0},{4,5},{5,7},{7,6},{6,4},{8,9},{9,11},{11,1... | collective-permute-start | bytes 1966088 | tf_op jit(solution)/shard_map/ppermute | solution.py:90
  870.4 144.1 %reduce-scatter.6.cloned.1.call-start = ((), (), s32[]{:S(2)}) async-start(), calls=%async_computation.6 | async-start | bytes 5160960 | tf_op jit(solution)/shard_map/reduce_scatter | solution.py:162
  905.7 40.4 %collective-permute-start.67 = (bf16[128,2560]{1,0:T(8,128)(2,1)}, bf16[128,2560]{1,0:T(8,128)(2,1)}, u32[]{:S(2)}, u32[]{:S(2)}) collective-permute-start(bf16[128,2560]{1,0:T(8,128)(2,1)} %shard_map.312), channel_id=1, source_target_pairs={{0,3},{1,2},{3,0},{2,1},{4,7},{5,6},{7,4},{6,5},{8,11},{9,10},{11,... | collective-permute-start | bytes 1966088 | tf_op jit(solution)/shard_map/ppermute | solution.py:90
  920.3 86.3 %collective-permute-start.86 = (bf16[4,512,384]{2,1,0:T(8,128)(2,1)}, bf16[4,512,384]{2,1,0:T(8,128)(2,1)}, u32[]{:S(2)}, u32[]{:S(2)}) collective-permute-start(bf16[4,512,384]{2,1,0:T(8,128)(2,1)} %shard_map.317.refs_0_), channel_id=1, source_target_pairs={{0,16},{16,0},{1,17},{17,1},{2,18},{18,2},{3,19},{19,3},{4,20},{20... | collective-permute-start | bytes 4718600 | tf_op jit(solution)/shard_map/ppermute | solution.py:22
  972.7 30.7 %collective-permute-start.70 = (bf16[128,640]{1,0:T(8,128)(2,1)S(1)}, bf16[128,640]{1,0:T(8,128)(2,1)S(1)}, u32[]{:S(2)}, u32[]{:S(2)}) collective-permute-start(bf16[128,640]{1,0:T(8,128)(2,1)S(1)} %get-tuple-element.209), channel_id=1, source_target_pairs={{0,3},{1,2},{2,1},{3,0},{4,7},{5,6},{6,5},{7,4},{8,11},{9,10},{10,... | collective-permute-start | bytes 491528 | tf_op jit(solution)/shard_map/ppermute | solution.py:22
  (165 other events, 2449.5 us)
Sparse Core Ops, SparseCore 0:
  10.3 99.2 all-gather.2
  112.4 212.5 all-gather.4
  667.8 118.9 reduce-scatter.3
  870.5 54.1 reduce-scatter.7
  927.0 87.4 reduce-scatter.5

commit v3 on v2

--- a/solution.py
+++ b/solution.py
@@ -158,9 +158,8 @@
     return whole.reshape((shares * total.shape[0],) + total.shape[1:])
 
 
-def reduce_weight(grad, late):
-    total = lax.psum_scatter(grad, ("col", "exp"), scatter_dimension=0, tiled=True)
-    return all_shares(after(total, late)).astype(f32)
+def reduce_weight(grad):
+    return lax.psum_scatter(grad, ("col", "exp"), scatter_dimension=0, tiled=True)
 
 
 def rope_tables(positions, head_width):
@@ -804,8 +803,10 @@
     own_weights = own_share(jnp.concatenate([w_key, w_value, w_query, w_output], axis=1))
     weights = lax.all_gather(own_weights, ("col", "exp"), tiled=True)
     weight_in = weights[:, : query_width + 2 * key_width]
-    g = tokens_home(out_grad, zero_of(*norm_one_parts[1:3]))
-    g_all = lax.all_gather(g, ("exp", "row", "col"), tiled=True)
+    g_block = lax.all_gather(
+        after(out_grad, weights, *norm_one_parts[1:]), "col", axis=1, tiled=True
+    )
+    g = lax.dynamic_slice_in_dim(g_block, c * home_rows, home_rows, 0)
     raw = dot(norm_one_all, weight_in)
     wait = zero_of(raw)
     here = jnp.stack([e, c]).astype(jnp.int32)
@@ -819,8 +820,9 @@
 
     shared_cut = cut_shared(here, shared_gate, shared_up, shared_down, C, E, raw)
     in_rows, feature_width = shared_gate.shape[0] // E, shared_down.shape[1]
+    shared_parts = col_swap(shared_cut)
     sh_in, sh_down = join_shared(
-        here, exchange(col_swap(shared_cut), "exp"), in_rows, feature_width, s_padded
+        here, exchange(shared_parts, "exp"), in_rows, feature_width, s_padded
     )
     expert_in = side_by_side(expert_gate, expert_up, raw)
 
@@ -858,8 +860,9 @@
     place = jnp.concatenate([jnp.stack([r, c]), c ^ jnp.arange(C)]).astype(jnp.int32)
     attended, att_total, lse = attention_forward(place, queries, kv_parts, home_rows, (expert_in, shared_cut))
     attn_part = dot(attended, weight_out).astype(bf16)
+    g_all = lax.all_gather(after(g_block, attn_part), ("exp", "row"), tiled=True)
     hidden_state = x + row_reduce(jnp.split(attn_part, R, axis=0))[0]
-    inv_two = rms_inverse(hidden_state) + zero_of(sh_in, sh_down).astype(f32)
+    inv_two = rms_inverse(hidden_state) + zero_of(*(shared_parts[s] for s in range(1, C))).astype(f32)
     norm_two = (hidden_state * inv_two * gain_two[None, :]).astype(bf16)
 
     norm_float = norm_two.astype(f32)
@@ -945,7 +948,8 @@
     d_v, gain_two_part = rms_backward(hidden_state, inv_two, gain_two, d_norm)
     d_hidden = g.astype(f32) + d_v
     d_attn = d_hidden.astype(bf16)
-    d_attn_all = jnp.concatenate(row_gather(d_attn), axis=0)
+    d_attn_parts = row_gather(d_attn)
+    d_attn_all = jnp.concatenate(d_attn_parts, axis=0)
 
     out_grads = batch_dot("sf,scd->cfd", attended, d_attn_all.reshape(own_rows, C, -1))
     out_grads = out_grads.astype(bf16).reshape(C * query_width, -1)
@@ -958,7 +962,7 @@
         place, queries, d_attended, att_total, lse, kv_parts, home_rows,
         (out_grads,),
     )
-    shared_back = col_swap(after(shared_sums, d_attn))
+    shared_back = col_swap(after(shared_sums, *d_attn_parts[1:3]))
     d_kv_parts = after(d_kv_parts, *soon, shared_back)
     d_kv = reduce_parts([d_kv_parts[k] for k in range(C)], "col")
     soon.append(ring_send(after(out_chunks[C // 2], d_kv), "col", C // 2))
@@ -967,26 +971,25 @@
     d_query_raw = rotate(
         d_queries.reshape(own_rows, group_heads, head_width), cosines, -sines
     ) * attn_scale
+    d_query_raw = d_query_raw.reshape(own_rows, query_width).astype(bf16)
+    norm_one_late = after(norm_one_all, d_kv_parts)
+    query_grads = dot(norm_one_late, d_query_raw, (0, 0)).astype(bf16)
     d_key_raw = rotate(d_kv[:, :key_width].reshape(own_rows, 1, head_width), cosines, -sines)
-    d_raw = jnp.concatenate(
-        [
-            d_key_raw.reshape(own_rows, key_width),
-            d_kv[:, key_width:],
-            d_query_raw.reshape(own_rows, query_width),
-        ],
-        axis=1,
+    d_kv_raw = jnp.concatenate(
+        [d_key_raw.reshape(own_rows, key_width), d_kv[:, key_width:]], axis=1
     ).astype(bf16)
-    norm_one_part = dot(d_raw, weight_in, (1, 1)).astype(bf16)
+    norm_one_part = dot(jnp.concatenate([d_kv_raw, d_query_raw], axis=1), weight_in, (1, 1)).astype(bf16)
     d_norm_one, halfway = row_reduce(jnp.split(norm_one_part, R, axis=0))
     d_x, gain_one_part = rms_backward(x, inv_one, gain_one, d_norm_one)
     grad_inputs = tokens_back((d_hidden + d_x).astype(bf16))
 
     output = tokens_back((hidden_state + moe_out).astype(bf16))
-    grad_output = reduce_weight(after(out_grads, d_kv), d_norm_one)
-    grad_in_all = reduce_weight(
-        dot(after(norm_one_all, *halfway), d_raw, (0, 0)).astype(bf16), d_norm_one
-    )
-
+    out_total, query_total = reduce_weight(out_grads), reduce_weight(query_grads)
+    kv_grads = dot(after(norm_one_late, *halfway), d_kv_raw, (0, 0)).astype(bf16)
+    kv_total = reduce_weight(after(kv_grads, query_total, d_norm_one))
+    grad_output = all_shares(after(out_total, d_norm_one)).astype(f32)
+    grad_query = all_shares(after(query_total, d_norm_one)).astype(f32)
+    grad_kv = all_shares(kv_total).astype(f32)
     small_part = jnp.concatenate([router_part, gain_one_part[None], gain_two_part[None]], axis=0)
     width = small.shape[1]
     mine = [
@@ -1000,9 +1003,9 @@
     return (
         output,
         grad_inputs,
-        grad_in_all[:, 2 * key_width :],
-        grad_in_all[:, :key_width],
-        grad_in_all[:, key_width : 2 * key_width],
+        grad_query,
+        grad_kv[:, :key_width],
+        grad_kv[:, key_width:],
         grad_output,
         small_sum[n_experts],
         small_sum[n_experts + 1],

time: 1030 us -> 1020 us (level)
  waiting for transfers between devices: 425 us -> 400 us
    ppermute x78 -> x76, waiting for transfers between devices: 345 us -> 319 us  [swap(): lax.ppermute(x, axis, [(i, i ^ step) for i in range(lax.axis_size(axis))])]
    ppermute x3, waiting for transfers between devices: 50 us -> 24.4 us  [ring_gather(): parts.append(lax.ppermute(parts[-1], axis, ring_pairs(n)))]
    all_gather x1, waiting for transfers between devices: 1.54 us -> 26.7 us  [shards(): weights = lax.all_gather(own_weights, ('col', 'exp'), tiled=True)]
    unnamed x221 -> x219, local copies, waits for them, and re-layouts: 20.7 us -> 27.1 us
    dot_general x8 -> x9, matrix products: 39.5 us -> 45.1 us  [dot(): lax.dot_general(left, right, (((contract[0],), (contract[1],)), ((), ()))...]
    ppermute x78 -> x76, starting transfers between devices: 91.4 us -> 87.8 us  [swap(): lax.ppermute(x, axis, [(i, i ^ step) for i in range(lax.axis_size(axis))])]
  transfers between devices with their start and end apart: 92 -> 92, of which waited for: 51 -> 45; matrix products, arithmetic and copies ran while one was open for 20% -> 23% of each run, Pallas kernels for 19% -> 19%
where the time goes in v3:
time: 1020 us; the launch traced here: 1010 us
  waiting for transfers between devices  400 us (39%)
  Pallas kernels  235 us (23%)
  matrix products  103 us (10%)
  starting transfers between devices  97.3 us (10%)
  other arithmetic  82.1 us (8%)
  local copies, waits for them, and re-layouts  71.1 us (7%)
  between operations  26.7 us (3%)
    ppermute x76, waiting for transfers between devices, swap(): lax.ppermute(x, axis, [(i, i ^ step) for i in range(lax.axis_size(axis))])  319 us
    pallas_call x4, Pallas kernels, experts_call(): pl.pallas_call(functools.partial(experts_kernel, counts, len(held) + len(...  171 us
    ppermute x76, starting transfers between devices, swap(): lax.ppermute(x, axis, [(i, i ^ step) for i in range(lax.axis_size(axis))])  87.8 us
    dot_general x4, matrix products, batch_dot(): return jnp.einsum(spec, left, right, preferred_element_type=f32)  53.5 us
    dot_general x9, matrix products, dot(): lax.dot_general(left, right, (((contract[0],), (contract[1],)), ((), ()))...  45.1 us
    pallas_call x2, Pallas kernels, attention_call(): pl.pallas_call(lambda place, *refs: kernel(place, *refs[:len(operands)],...  28.9 us
    unnamed x219, local copies, waits for them, and re-layouts  27.1 us
    all_gather x1, waiting for transfers between devices, shards(): weights = lax.all_gather(own_weights, ('col', 'exp'), tiled=True)  26.7 us
  transfers between devices with their start and end apart: 92, of which 45 were waited for; matrix products, arithmetic and copies ran while one was open for 23% of the time, Pallas kernels for 19%

profile of v3, /device:TPU:9, one launch (start us, length us, event | category | flops | bytes accessed | tf_op | source)
XLA Modules:
  0.0 1014.9 jit_solution(9506516962448350307)
XLA Ops:
  21.6 8.3 collective-permute-done.1
  30.0 18.0 %collective-permute-done.2 = bf16[128,640]{1,0:T(8,128)(2,1)S(1)} collective-permute-done((bf16[128,640]{1,0:T(8,128)(2,1)S(1)}, bf16[128,640]{1,0:T(8,128)(2,1)S(1)}, u32[]{:S(2)}, u32[]{:S(2)}) %collective-permute-start.2) | collective-permute-done | bytes 163872 | tf_op jit(solution)/shard_map/ppermute | solution.py:22
  52.5 8.4 collective-permute-done.7.refs_3_
  70.9 26.7 %all-gather.4.cloned.1.call-done.ref.refs_1_ = bf16[2560,1536]{1,0:T(8,128)(2,1)} async-done(((bf16[320,1536]{1,0:T(8,128)(2,1)}), bf16[2560,1536]{1,0:T(8,128)(2,1)}) %all-gather.4.cloned.1.call-update) | async-done | bytes 7864336 | tf_op jit(solution)/shard_map/all_gather | solution.py:804
  122.5 9.6 shard_map.289.refs_5_.refs_8_.refs_12_
  141.2 25.7 %collective-permute-done.12.refs_4_.refs_7_ = bf16[512,256]{1,0:T(8,128)(2,1)} collective-permute-done((bf16[512,256]{1,0:T(8,128)(2,1)S(1)}, bf16[512,256]{1,0:T(8,128)(2,1)}, u32[]{:S(2)}, u32[]{:S(2)}) %collective-permute-start.12) | collective-permute-done | bytes 262176 | tf_op jit(solution)/shard_map/ppermute | solution.py:22
  166.9 12.5 %shard_map.291 = (bf16[512,640]{1,0:T(8,128)(2,1)}, f32[4,128,640]{2,1,0:T(8,128)}, f32[4,1,640]{2,1,0:T(1,128)}) custom-call(s32[6]{0:T(128)} %pad_add_fusion.place, bf16[512,640]{1,0:T(8,128)(2,1)} %copy.163.refs_0_, bf16[512,256]{1,0:T(8,128)(2,1)} %copy-done.53, bf16[512,256]{1,0:T(8,128)(2,1)} %collective-permute-done.10.refs_2_.refs_5_, ...), custom_call_target="tpu_custom_call" | custom-call | flops 2684354560 | bytes 1024 | tf_op jit(solution)/shard_map/pallas_call | solution.py:491
  204.6 9.0 collective-permute-done.17
  220.5 15.0 %collective-permute-done.19 = bf16[512,384]{1,0:T(8,128)(2,1)S(1)} collective-permute-done((bf16[512,384]{1,0:T(8,128)(2,1)S(1)}, bf16[512,384]{1,0:T(8,128)(2,1)S(1)}, u32[]{:S(2)}, u32[]{:S(2)}) %collective-permute-start.19) | collective-permute-done | bytes 393248 | tf_op jit(solution)/shard_map/ppermute | solution.py:22
  241.4 13.2 %collective-permute-done.20 = bf16[128,2688]{1,0:T(8,128)(2,1)S(1)} collective-permute-done((bf16[128,2688]{1,0:T(8,128)(2,1)S(1)}, bf16[128,2688]{1,0:T(8,128)(2,1)S(1)}, u32[]{:S(2)}, u32[]{:S(2)}) %collective-permute-start.20) | collective-permute-done | bytes 688160 | tf_op jit(solution)/shard_map/ppermute | solution.py:83
  257.4 11.2 %collective-permute-done.21 = bf16[128,2688]{1,0:T(8,128)(2,1)S(1)} collective-permute-done((bf16[128,2688]{1,0:T(8,128)(2,1)S(1)}, bf16[128,2688]{1,0:T(8,128)(2,1)S(1)}, u32[]{:S(2)}, u32[]{:S(2)}) %collective-permute-start.21) | collective-permute-done | bytes 688160 | tf_op jit(solution)/shard_map/ppermute | solution.py:83
  276.6 9.2 collective-permute-start.29
  308.2 10.2 %all-gather.8.cloned.1.call-done.refs_4_.refs_5_.refs_8_.refs_9_ = bf16[4096,2560]{1,0:T(8,128)(2,1)} async-done(((bf16[512,2560]{1,0:T(8,128)(2,1)}), bf16[4096,2560]{1,0:T(8,128)(2,1)}) %all-gather.8.cloned.1.call-update) | async-done | bytes 20971536 | tf_op jit(solution)/shard_map/all_gather | solution.py:863
  318.4 42.6 %shard_map.296 = (bf16[2,2048,2560]{2,1,0:T(8,128)(2,1)}, bf16[2,2048,2560]{2,1,0:T(8,128)(2,1)}, bf16[2,2048,384]{2,1,0:T(8,128)(2,1)}, bf16[2,2048,768]{2,1,0:...) custom-call(s32[8]{0:T(128)} %get-tuple-element.231.info, ...), custom_call_target="tpu_custom_call" | custom-call | flops 26843545600 | bytes 1024 | tf_op jit(solution)/shard_map/pallas_call | solution.py:732
  382.6 43.1 %shard_map.298 = (bf16[2,2048,2560]{2,1,0:T(8,128)(2,1)}, bf16[2,2048,2560]{2,1,0:T(8,128)(2,1)}, bf16[2,2048,384]{2,1,0:T(8,128)(2,1)}, bf16[2,2048,768]{2,1,0:...) custom-call(s32[8]{0:T(128)} %get-tuple-element.233.info, ...), custom_call_target="tpu_custom_call", output_to_operand_aliasing={{0}: (13, {}), {1}: (14, {}), {2}: (15, {}), {3}: (16, {}),... | custom-call | flops 26843545600 | bytes 1024 | tf_op jit(solution)/shard_map/pallas_call | solution.py:732
  438.0 42.9 %shard_map.300 = (bf16[2,2048,2560]{2,1,0:T(8,128)(2,1)}, bf16[2,2048,2560]{2,1,0:T(8,128)(2,1)}, bf16[2,2048,384]{2,1,0:T(8,128)(2,1)}, bf16[2,2048,768]{2,1,0:...) custom-call(s32[8]{0:T(128)} %get-tuple-element.232.info, ...), custom_call_target="tpu_custom_call", output_to_operand_aliasing={{0}: (13, {}), {1}: (14, {}), {2}: (15, {}), {3}: (16, {}),... | custom-call | flops 26843545600 | bytes 1024 | tf_op jit(solution)/shard_map/pallas_call | solution.py:732
  494.3 42.8 %shard_map.301 = (bf16[2,2048,2560]{2,1,0:T(8,128)(2,1)}, bf16[2,2048,2560]{2,1,0:T(8,128)(2,1)}, bf16[2,2048,384]{2,1,0:T(8,128)(2,1)}, bf16[2,2048,768]{2,1,0:...) custom-call(s32[8]{0:T(128)} %get-tuple-element.234.info, ...), custom_call_target="tpu_custom_call", output_to_operand_aliasing={{0}: (17, {}), {1}: (18, {}), {2}: (19, {}), {3}: (20, {}),... | custom-call | flops 26843545600 | bytes 1024 | tf_op jit(solution)/shard_map/pallas_call | solution.py:732
  543.4 10.7 %collective-permute-done.44.refs_2_ = bf16[512,2688]{1,0:T(8,128)(2,1)} collective-permute-done((bf16[512,2688]{1,0:T(8,128)(2,1)}, bf16[512,2688]{1,0:T(8,128)(2,1)}, u32[]{:S(2)}, u32[]{:S(2)}) %collective-permute-start.44) | collective-permute-done | bytes 2752544 | tf_op jit(solution)/shard_map/ppermute | solution.py:22
  563.9 10.2 %convolution_convert_fusion.2.refs_0_ = bf16[2560,512]{1,0:T(8,128)(2,1)} fusion(bf16[2048,2560]{1,0:T(8,128)(2,1)} %get-tuple-element.118, bf16[2048,512]{1,0:T(8,128)(2,1)} %shard_map.304), kind=kOutput, calls=%fused_computation.10 | convolution fusion | flops 5370019840 | bytes 15204352 | tf_op jit(solution)/shard_map/dot_general | solution.py:182
  583.0 13.2 %add_convert_fusion.refs_0_ = bf16[2048,2560]{1,0:T(8,128)(2,1)} fusion(bf16[2048,2560]{1,0:T(8,128)(2,1)} %collective-permute-done.46, bf16[2048,2560]{1,0:T(8,128)(2,1)} %get-tuple-element.114), kind=kLoop, calls=%fused_computation.2 | loop fusion | flops 20971520 | bytes 31457280 | tf_op jit(solution)/shard_map/convert_element_type | solution.py:930
  596.3 28.9 %collective-permute-done.47.refs_1_ = bf16[512,2688]{1,0:T(8,128)(2,1)} collective-permute-done((bf16[512,2688]{1,0:T(8,128)(2,1)}, bf16[512,2688]{1,0:T(8,128)(2,1)}, u32[]{:S(2)}, u32[]{:S(2)}) %collective-permute-start.47) | collective-permute-done | bytes 2752544 | tf_op jit(solution)/shard_map/ppermute | solution.py:22
  639.2 18.8 %fusion.3 = f32[2,2560,384]{2,1,0:T(8,128)} fusion(bf16[2,2048,2560]{2,1,0:T(8,128)(2,1)} %get-tuple-element.123, bf16[2,2048,768]{2,1,0:T(8,128)(2,1)} %shard_map.308), kind=kOutput, calls=%fused_computation.17 | convolution fusion | flops 8053063680 | bytes 31981568 | tf_op jit(solution)/shard_map/lrd,lrf->ldf/dot_general | solution.py:188
  658.0 18.5 %fusion.5 = f32[2,2560,384]{2,1,0:T(8,128)} fusion(bf16[2,2048,2560]{2,1,0:T(8,128)(2,1)} %get-tuple-element.123, bf16[2,2048,768]{2,1,0:T(8,128)(2,1)} %shard_map.308), kind=kOutput, calls=%fused_computation.19 | convolution fusion | flops 8053063680 | bytes 31981568 | tf_op jit(solution)/shard_map/lrd,lrf->ldf/dot_general | solution.py:188
  676.6 12.5 %fusion.87 = f32[2,384,2560]{2,1,0:T(8,128)S(1)} fusion(bf16[2,2048,384]{2,1,0:T(8,128)(2,1)S(1)} %copy-done.3, bf16[2,2048,2560]{2,1,0:T(8,128)(2,1)} %get-tuple-element.126), kind=kOutput, calls=%fused_computation.275 | convolution fusion | flops 8053063680 | bytes 31981568 | tf_op jit(solution)/shard_map/lrf,lrd->lfd/dot_general | solution.py:188
  706.3 29.1 %collective-permute-done.52.refs_2_ = bf16[128,2560]{1,0:T(8,128)(2,1)S(1)} collective-permute-done((bf16[128,2560]{1,0:T(8,128)(2,1)S(1)}, bf16[128,2560]{1,0:T(8,128)(2,1)S(1)}, u32[]{:S(2)}, u32[]{:S(2)}) %collective-permute-start.52) | collective-permute-done | bytes 655392 | tf_op jit(solution)/shard_map/ppermute | solution.py:22
  737.7 10.4 %collective-permute-done.53 = bf16[64,2560]{1,0:T(8,128)(2,1)S(1)} collective-permute-done((bf16[64,2560]{1,0:T(8,128)(2,1)S(1)}, bf16[64,2560]{1,0:T(8,128)(2,1)S(1)}, u32[]{:S(2)}, u32[]{:S(2)}) %collective-permute-start.53) | collective-permute-done | bytes 327712 | tf_op jit(solution)/shard_map/ppermute | solution.py:22
  774.2 16.4 %shard_map.311 = (f32[512,640]{1,0:T(8,128)}, bf16[4,512,256]{2,1,0:T(8,128)(2,1)}) custom-call(s32[6]{0:T(128)} %pad_add_fusion.place, bf16[512,640]{1,0:T(8,128)(2,1)} %copy.163.refs_0_, bf16[512,640]{1,0:T(8,128)(2,1)} %convolution_convert_fusion.6.refs_1_, f32[4,128,640]{2,1,0:T(8,128)} %get-tuple-element.127.refs_2_, ...), custom_call_target="tpu_custom_call" | custom-call | flops 6710886400 | bytes 1024 | tf_op jit(solution)/shard_map/pallas_call | solution.py:491
  796.4 38.0 %collective-permute-done.60 = bf16[512,384]{1,0:T(8,128)(2,1)} collective-permute-done((bf16[512,384]{1,0:T(8,128)(2,1)}, bf16[512,384]{1,0:T(8,128)(2,1)}, u32[]{:S(2)}, u32[]{:S(2)}) %collective-permute-start.60) | collective-permute-done | bytes 393248 | tf_op jit(solution)/shard_map/ppermute | solution.py:22
  837.0 13.8 %collective-permute-done.56.refs_2_ = bf16[128,2560]{1,0:T(8,128)(2,1)} collective-permute-done((bf16[128,2560]{1,0:T(8,128)(2,1)}, bf16[128,2560]{1,0:T(8,128)(2,1)}, u32[]{:S(2)}, u32[]{:S(2)}) %collective-permute-start.56) | collective-permute-done | bytes 655392 | tf_op jit(solution)/shard_map/ppermute | solution.py:90
  867.7 24.7 %collective-permute-done.63 = bf16[512,256]{1,0:T(8,128)(2,1)} collective-permute-done((bf16[512,256]{1,0:T(8,128)(2,1)}, bf16[512,256]{1,0:T(8,128)(2,1)}, u32[]{:S(2)}, u32[]{:S(2)}) %collective-permute-start.63) | collective-permute-done | bytes 262176 | tf_op jit(solution)/shard_map/ppermute | solution.py:22
  963.5 8.6 collective-permute-done.74
  984.3 8.5 collective-permute-done.67
  (590 shorter events, 377.4 us)
Async XLA Ops:
  7.2 90.4 %all-gather.4.cloned.1.call-start = ((), (), s32[]{:S(2)}) async-start(), calls=%async_computation.4 | async-start | bytes 8847360 | tf_op jit(solution)/shard_map/all_gather | solution.py:804
  11.6 172.6 %all-gather.6.cloned.1.call-start = ((), (), s32[]{:S(2)}) async-start(), calls=%async_computation.5 | async-start | bytes 3276800 | tf_op jit(solution)/shard_map/all_gather | solution.py:806
  97.7 220.8 %all-gather.8.cloned.1.call-start = ((), (), s32[]{:S(2)}) async-start(), calls=%async_computation.6 | async-start | bytes 23592960 | tf_op jit(solution)/shard_map/all_gather | solution.py:863
  110.7 30.5 %collective-permute-start.10 = (bf16[512,256]{1,0:T(8,128)(2,1)S(1)}, bf16[512,256]{1,0:T(8,128)(2,1)}, u32[]{:S(2)}, u32[]{:S(2)}) collective-permute-start(bf16[512,256]{1,0:T(8,128)(2,1)S(1)} %pad_maximum_fusion.7.refs_1_.refs_4_), channel_id=1, source_target_pairs={{0,1},{1,0},{2,3},{3,2},{4,5},{5,4},{6,7},{7,6},{8,9},{9,8},{10,11... | collective-permute-start | bytes 786440 | tf_op jit(solution)/shard_map/ppermute | solution.py:22
  115.6 51.3 %collective-permute-start.12 = (bf16[512,256]{1,0:T(8,128)(2,1)S(1)}, bf16[512,256]{1,0:T(8,128)(2,1)}, u32[]{:S(2)}, u32[]{:S(2)}) collective-permute-start(bf16[512,256]{1,0:T(8,128)(2,1)S(1)} %pad_maximum_fusion.7.refs_1_.refs_4_), channel_id=1, source_target_pairs={{0,3},{1,2},{2,1},{3,0},{4,7},{5,6},{6,5},{7,4},{8,11},{9,10},{10,... | collective-permute-start | bytes 786440 | tf_op jit(solution)/shard_map/ppermute | solution.py:22
  187.6 580.8 %reduce-scatter.5.cloned.1.call-start = ((), (), s32[]{:S(2)}) async-start(), calls=%async_computation.7 | async-start | bytes 13107200 | tf_op jit(solution)/shard_map/reduce_scatter | solution.py:931
  198.8 38.6 %collective-permute-start.14 = (bf16[128,2560]{1,0:T(8,128)(2,1)S(1)}, bf16[128,2560]{1,0:T(8,128)(2,1)S(1)}, u32[]{:S(2)}, u32[]{:S(2)}) collective-permute-start(bf16[128,2560]{1,0:T(8,128)(2,1)S(1)} %pad_maximum_fusion.3), channel_id=1, source_target_pairs={{0,4},{4,0},{8,12},{12,8},{1,5},{5,1},{9,13},{13,9},{2,6},{6,2},{1... | collective-permute-start | bytes 1966088 | tf_op jit(solution)/shard_map/ppermute | solution.py:22
  200.1 37.4 %collective-permute-start.16 = (bf16[128,2560]{1,0:T(8,128)(2,1)S(1)}, bf16[128,2560]{1,0:T(8,128)(2,1)S(1)}, u32[]{:S(2)}, u32[]{:S(2)}) collective-permute-start(bf16[128,2560]{1,0:T(8,128)(2,1)S(1)} %pad_maximum_fusion.4), channel_id=1, source_target_pairs={{0,8},{4,12},{8,0},{12,4},{1,9},{5,13},{9,1},{13,5},{2,10},{6,14},... | collective-permute-start | bytes 1966088 | tf_op jit(solution)/shard_map/ppermute | solution.py:22
  204.4 31.2 %collective-permute-start.19 = (bf16[512,384]{1,0:T(8,128)(2,1)S(1)}, bf16[512,384]{1,0:T(8,128)(2,1)S(1)}, u32[]{:S(2)}, u32[]{:S(2)}) collective-permute-start(bf16[512,384]{1,0:T(8,128)(2,1)S(1)} %get-tuple-element.185), channel_id=1, source_target_pairs={{0,3},{1,2},{2,1},{3,0},{4,7},{5,6},{6,5},{7,4},{8,11},{9,10},{10,... | collective-permute-start | bytes 1179656 | tf_op jit(solution)/shard_map/ppermute | solution.py:22
  297.2 69.5 %collective-permute-start.23 = (bf16[512,2688]{1,0:T(8,128)(2,1)}, bf16[512,2688]{1,0:T(8,128)(2,1)S(1)}, u32[]{:S(2)}, u32[]{:S(2)}) collective-permute-start(bf16[512,2688]{1,0:T(8,128)(2,1)} %pad_maximum_fusion.refs_0_.refs_2_), channel_id=1, source_target_pairs={{0,8},{4,12},{8,0},{12,4},{1,9},{5,13},{9,1},{13,5},{2,10},{6,14},... | collective-permute-start | bytes 8257544 | tf_op jit(solution)/shard_map/ppermute | solution.py:22
  297.5 69.2 %collective-permute-start.25 = (bf16[512,2688]{1,0:T(8,128)(2,1)}, bf16[512,2688]{1,0:T(8,128)(2,1)}, u32[]{:S(2)}, u32[]{:S(2)}) collective-permute-start(bf16[512,2688]{1,0:T(8,128)(2,1)} %pad_maximum_fusion.refs_0_.refs_2_), channel_id=1, source_target_pairs={{0,4},{4,0},{8,12},{12,8},{1,5},{5,1},{9,13},{13,9},{2,6},{6,2},{1... | collective-permute-start | bytes 8257544 | tf_op jit(solution)/shard_map/ppermute | solution.py:22
  371.8 53.9 %collective-permute-start.24 = (bf16[256,2688]{1,0:T(8,128)(2,1)S(1)}, bf16[256,2688]{1,0:T(8,128)(2,1)S(1)}, u32[]{:S(2)}, u32[]{:S(2)}) collective-permute-start(bf16[256,2688]{1,0:T(8,128)(2,1)S(1)} %slice.311), channel_id=1, source_target_pairs={{0,4},{4,0},{8,12},{12,8},{1,5},{5,1},{9,13},{13,9},{2,6},{6,2},{1... | collective-permute-start | bytes 4128776 | tf_op jit(solution)/shard_map/ppermute | solution.py:22
  375.4 50.2 %collective-permute-start.26 = (bf16[256,2688]{1,0:T(8,128)(2,1)}, bf16[256,2688]{1,0:T(8,128)(2,1)S(1)}, u32[]{:S(2)}, u32[]{:S(2)}) collective-permute-start(bf16[256,2688]{1,0:T(8,128)(2,1)} %slice.312), channel_id=1, source_target_pairs={{0,8},{4,12},{8,0},{12,4},{1,9},{5,13},{9,1},{13,5},{2,10},{6,14},... | collective-permute-start | bytes 4128776 | tf_op jit(solution)/shard_map/ppermute | solution.py:22
  481.9 61.5 %collective-permute-start.43 = (bf16[512,2688]{1,0:T(8,128)(2,1)}, bf16[512,2688]{1,0:T(8,128)(2,1)}, u32[]{:S(2)}, u32[]{:S(2)}) collective-permute-start(bf16[512,2688]{1,0:T(8,128)(2,1)} %add_convert_fusion.4.refs_22_), channel_id=1, source_target_pairs={{0,4},{4,0},{8,12},{12,8},{1,5},{5,1},{9,13},{13,9},{2,6},{6,2},{1... | collective-permute-start | bytes 8257544 | tf_op jit(solution)/shard_map/ppermute | solution.py:22
  492.8 61.2 %collective-permute-start.44 = (bf16[512,2688]{1,0:T(8,128)(2,1)}, bf16[512,2688]{1,0:T(8,128)(2,1)}, u32[]{:S(2)}, u32[]{:S(2)}) collective-permute-start(bf16[512,2688]{1,0:T(8,128)(2,1)} %add_convert_fusion.3.refs_26_), channel_id=1, source_target_pairs={{0,8},{4,12},{8,0},{12,4},{1,9},{5,13},{9,1},{13,5},{2,10},{6,14},... | collective-permute-start | bytes 8257544 | tf_op jit(solution)/shard_map/ppermute | solution.py:22
  562.8 62.3 %collective-permute-start.47 = (bf16[512,2688]{1,0:T(8,128)(2,1)}, bf16[512,2688]{1,0:T(8,128)(2,1)}, u32[]{:S(2)}, u32[]{:S(2)}) collective-permute-start(bf16[512,2688]{1,0:T(8,128)(2,1)} %add_convert_fusion.2.refs_1_), channel_id=1, source_target_pairs={{0,12},{4,8},{8,4},{12,0},{1,13},{5,9},{9,5},{13,1},{2,14},{6,10},... | collective-permute-start | bytes 8257544 | tf_op jit(solution)/shard_map/ppermute | solution.py:22
  625.1 312.4 %reduce-scatter.11.cloned.1.call-start = ((), (), s32[]{:S(2)}) async-start(), calls=%async_computation.10 | async-start | bytes 3686400 | tf_op jit(solution)/shard_map/reduce_scatter | solution.py:162
  634.7 62.6 %collective-permute-start.48 = (bf16[128,2688]{1,0:T(8,128)(2,1)}, bf16[128,2688]{1,0:T(8,128)(2,1)}, u32[]{:S(2)}, u32[]{:S(2)}) collective-permute-start(bf16[128,2688]{1,0:T(8,128)(2,1)} %get-tuple-element.160), channel_id=1, source_target_pairs={{0,2},{1,0},{3,1},{2,3},{4,6},{5,4},{7,5},{6,7},{8,10},{9,8},{11,9... | collective-permute-start | bytes 2064392 | tf_op jit(solution)/shard_map/ppermute | solution.py:90
  635.1 62.3 %collective-permute-start.49 = (bf16[128,2688]{1,0:T(8,128)(2,1)}, bf16[128,2688]{1,0:T(8,128)(2,1)}, u32[]{:S(2)}, u32[]{:S(2)}) collective-permute-start(bf16[128,2688]{1,0:T(8,128)(2,1)} %get-tuple-element.162), channel_id=1, source_target_pairs={{0,3},{1,2},{3,0},{2,1},{4,7},{5,6},{7,4},{6,5},{8,11},{9,10},{11,... | collective-permute-start | bytes 2064392 | tf_op jit(solution)/shard_map/ppermute | solution.py:90
  637.1 60.2 %collective-permute-start.50 = (bf16[128,2688]{1,0:T(8,128)(2,1)}, bf16[128,2688]{1,0:T(8,128)(2,1)}, u32[]{:S(2)}, u32[]{:S(2)}) collective-permute-start(bf16[128,2688]{1,0:T(8,128)(2,1)} %get-tuple-element.161), channel_id=1, source_target_pairs={{0,1},{1,3},{3,2},{2,0},{4,5},{5,7},{7,6},{6,4},{8,9},{9,11},{11,1... | collective-permute-start | bytes 2064392 | tf_op jit(solution)/shard_map/ppermute | solution.py:90
  705.0 30.5 %collective-permute-start.52 = (bf16[128,2560]{1,0:T(8,128)(2,1)S(1)}, bf16[128,2560]{1,0:T(8,128)(2,1)S(1)}, u32[]{:S(2)}, u32[]{:S(2)}) collective-permute-start(bf16[128,2560]{1,0:T(8,128)(2,1)S(1)} %get-tuple-element.153), channel_id=1, source_target_pairs={{0,8},{4,12},{8,0},{12,4},{1,9},{5,13},{9,1},{13,5},{2,10},{6,14},... | collective-permute-start | bytes 1966088 | tf_op jit(solution)/shard_map/ppermute | solution.py:22
  705.7 31.1 %collective-permute-start.51 = (bf16[128,2560]{1,0:T(8,128)(2,1)S(1)}, bf16[128,2560]{1,0:T(8,128)(2,1)S(1)}, u32[]{:S(2)}, u32[]{:S(2)}) collective-permute-start(bf16[128,2560]{1,0:T(8,128)(2,1)S(1)} %get-tuple-element.153), channel_id=1, source_target_pairs={{0,4},{4,0},{8,12},{12,8},{1,5},{5,1},{9,13},{13,9},{2,6},{6,2},{1... | collective-permute-start | bytes 1966088 | tf_op jit(solution)/shard_map/ppermute | solution.py:22
  751.8 201.1 %reduce-scatter.7.cloned.1.call-start = ((), (), s32[]{:S(2)}) async-start(), calls=%async_computation.8 | async-start | bytes 3686400 | tf_op jit(solution)/shard_map/reduce_scatter | solution.py:162
  760.7 33.8 %collective-permute-start.58 = (bf16[512,384]{1,0:T(8,128)(2,1)}, bf16[512,384]{1,0:T(8,128)(2,1)}, u32[]{:S(2)}, u32[]{:S(2)}) collective-permute-start(bf16[512,384]{1,0:T(8,128)(2,1)} %get-tuple-element.183), channel_id=1, source_target_pairs={{0,1},{1,0},{2,3},{3,2},{4,5},{5,4},{6,7},{7,6},{8,9},{9,8},{10,11... | collective-permute-start | bytes 1179656 | tf_op jit(solution)/shard_map/ppermute | solution.py:22
  761.0 35.3 %collective-permute-start.59 = (bf16[512,384]{1,0:T(8,128)(2,1)}, bf16[512,384]{1,0:T(8,128)(2,1)}, u32[]{:S(2)}, u32[]{:S(2)}) collective-permute-start(bf16[512,384]{1,0:T(8,128)(2,1)} %get-tuple-element.182), channel_id=1, source_target_pairs={{0,2},{1,3},{2,0},{3,1},{4,6},{5,7},{6,4},{7,5},{8,10},{9,11},{10,... | collective-permute-start | bytes 1179656 | tf_op jit(solution)/shard_map/ppermute | solution.py:22
  763.1 71.2 %collective-permute-start.60 = (bf16[512,384]{1,0:T(8,128)(2,1)}, bf16[512,384]{1,0:T(8,128)(2,1)}, u32[]{:S(2)}, u32[]{:S(2)}) collective-permute-start(bf16[512,384]{1,0:T(8,128)(2,1)} %get-tuple-element.181), channel_id=1, source_target_pairs={{0,3},{1,2},{2,1},{3,0},{4,7},{5,6},{6,5},{7,4},{8,11},{9,10},{10,... | collective-permute-start | bytes 1179656 | tf_op jit(solution)/shard_map/ppermute | solution.py:22
  771.2 65.8 %collective-permute-start.55 = (bf16[128,2560]{1,0:T(8,128)(2,1)}, bf16[128,2560]{1,0:T(8,128)(2,1)S(1)}, u32[]{:S(2)}, u32[]{:S(2)}) collective-permute-start(bf16[128,2560]{1,0:T(8,128)(2,1)} %get-tuple-element.171), channel_id=1, source_target_pairs={{0,2},{1,0},{3,1},{2,3},{4,6},{5,4},{7,5},{6,7},{8,10},{9,8},{11,9... | collective-permute-start | bytes 1966088 | tf_op jit(solution)/shard_map/ppermute | solution.py:90
  772.4 78.4 %collective-permute-start.56 = (bf16[128,2560]{1,0:T(8,128)(2,1)}, bf16[128,2560]{1,0:T(8,128)(2,1)}, u32[]{:S(2)}, u32[]{:S(2)}) collective-permute-start(bf16[128,2560]{1,0:T(8,128)(2,1)} %get-tuple-element.169), channel_id=1, source_target_pairs={{0,1},{1,3},{3,2},{2,0},{4,5},{5,7},{7,6},{6,4},{8,9},{9,11},{11,1... | collective-permute-start | bytes 1966088 | tf_op jit(solution)/shard_map/ppermute | solution.py:90
  856.6 35.8 %collective-permute-start.63 = (bf16[512,256]{1,0:T(8,128)(2,1)}, bf16[512,256]{1,0:T(8,128)(2,1)}, u32[]{:S(2)}, u32[]{:S(2)}) collective-permute-start(bf16[512,256]{1,0:T(8,128)(2,1)} %get-tuple-element.193), channel_id=1, source_target_pairs={{0,3},{1,2},{2,1},{3,0},{4,7},{5,6},{6,5},{7,4},{8,11},{9,10},{10,... | collective-permute-start | bytes 786440 | tf_op jit(solution)/shard_map/ppermute | solution.py:22
  863.5 141.6 %reduce-scatter.9.cloned.1.call-start = ((), (), s32[]{:S(2)}) async-start(), calls=%async_computation.9 | async-start | bytes 1474560 | tf_op jit(solution)/shard_map/reduce_scatter | solution.py:162
  925.5 72.3 %collective-permute-start.84 = (bf16[4,512,384]{2,1,0:T(8,128)(2,1)}, bf16[4,512,384]{2,1,0:T(8,128)(2,1)}, u32[]{:S(2)}, u32[]{:S(2)}) collective-permute-start(bf16[4,512,384]{2,1,0:T(8,128)(2,1)} %shard_map.320.refs_0_), channel_id=1, source_target_pairs={{0,16},{16,0},{1,17},{17,1},{2,18},{18,2},{3,19},{19,3},{4,20},{20... | collective-permute-start | bytes 4718600 | tf_op jit(solution)/shard_map/ppermute | solution.py:22
  943.8 50.4 %collective-permute-start.77 = (bf16[320,640]{1,0:T(8,128)(2,1)}, bf16[320,640]{1,0:T(8,128)(2,1)}, u32[]{:S(2)}, u32[]{:S(2)}) collective-permute-start(bf16[320,640]{1,0:T(8,128)(2,1)} %shard_map.319), channel_id=1, source_target_pairs={{0,16},{16,0},{1,17},{17,1},{2,18},{18,2},{3,19},{19,3},{4,20},{20... | collective-permute-start | bytes 1228808 | tf_op jit(solution)/shard_map/ppermute | solution.py:22
  (162 other events, 2762.6 us)
Sparse Core Ops, SparseCore 0:
  11.7 85.8 all-gather.3
  99.8 76.5 all-gather.5
  187.8 130.6 all-gather.7
  625.3 120.4 reduce-scatter.4
  752.0 97.5 reduce-scatter.10
  863.7 66.8 reduce-scatter.6
  953.0 42.1 reduce-scatter.8

commit v4 on v3

--- a/solution.py
+++ b/solution.py
@@ -352,21 +352,16 @@
     )(info, *operands, *waits)
 
 
-def join_weight(blocks, first, cols, shares):
-    rows, width = blocks.shape[0] // (cols * shares), blocks.shape[1] - first
-
-    def kernel(ref, out_ref):
-        for k in range(cols):
-            for t in range(shares):
-                at = (k * shares + t) * rows
-                out_ref[t * rows : (t + 1) * rows, k * width : (k + 1) * width] = ref[at : at + rows, first:]
-
-    return pl.pallas_call(
-        kernel,
-        out_shape=jax.ShapeDtypeStruct((shares * rows, cols * width), blocks.dtype),
-        compiler_params=pltpu.CompilerParams(vmem_limit_bytes=vmem_limit),
-        cost_estimate=pl.CostEstimate(flops=0, bytes_accessed=2**10, transcendentals=0),
-    )(blocks)
+def join_weight(info, parts):
+    cols, rows, width = parts[0].shape
+
+    def kernel(e, c, *refs):
+        for s in range(cols):
+            for t, ref in enumerate(refs[:-1]):
+                refs[-1][rows_at(e ^ t, rows), rows_at(c ^ s, width)] = ref[s]
+
+    outs = (jax.ShapeDtypeStruct((len(parts) * rows, cols * width), parts[0].dtype),)
+    return cut_call(kernel, info, parts, outs)[0]
 
 
 def each_index(index, count, work):
@@ -800,17 +795,17 @@
     norm_one_parts = row_gather(norm_one)
     norm_one_all = jnp.concatenate(norm_one_parts, axis=0)
 
-    own_weights = own_share(jnp.concatenate([w_key, w_value, w_query, w_output], axis=1))
-    weights = lax.all_gather(own_weights, ("col", "exp"), tiled=True)
-    weight_in = weights[:, : query_width + 2 * key_width]
+    own_in = own_share(jnp.concatenate([w_key, w_value, w_query], axis=1))
+    weight_in = lax.all_gather(own_in, ("col", "exp"), tiled=True)
     g_block = lax.all_gather(
-        after(out_grad, weights, *norm_one_parts[1:]), "col", axis=1, tiled=True
+        after(out_grad, weight_in, *norm_one_parts[1:]), "col", axis=1, tiled=True
     )
     g = lax.dynamic_slice_in_dim(g_block, c * home_rows, home_rows, 0)
     raw = dot(norm_one_all, weight_in)
     wait = zero_of(raw)
     here = jnp.stack([e, c]).astype(jnp.int32)
-    weight_out = join_weight(weights, query_width + 2 * key_width, C, E)
+    out_parts = exchange(own_share(w_output, wait), "col")
+    weight_out = join_weight(here, exchange(jnp.stack(out_parts), "exp"))
 
     s_width = shared_gate.shape[1] // C
     s_padded = -(-s_width // 128) * 128
@@ -860,7 +855,7 @@
     place = jnp.concatenate([jnp.stack([r, c]), c ^ jnp.arange(C)]).astype(jnp.int32)
     attended, att_total, lse = attention_forward(place, queries, kv_parts, home_rows, (expert_in, shared_cut))
     attn_part = dot(attended, weight_out).astype(bf16)
-    g_all = lax.all_gather(after(g_block, attn_part), ("exp", "row"), tiled=True)
+    g_all = lax.all_gather(after(g_block, attended), ("exp", "row"), tiled=True)
     hidden_state = x + row_reduce(jnp.split(attn_part, R, axis=0))[0]
     inv_two = rms_inverse(hidden_state) + zero_of(*(shared_parts[s] for s in range(1, C))).astype(f32)
     norm_two = (hidden_state * inv_two * gain_two[None, :]).astype(bf16)
@@ -892,6 +887,13 @@
         payload_rows = [[x] for x in payload_rows[:3]] + [payload_rows[3:]]
     else:
         payload_rows = [[x] for x in payload_rows]
+
+    def shared_gradients(kept):
+        own_x, own_g, s_hidden, s_pre = kept[4:8]
+        d_in = dot(own_x, s_pre, (0, 0)).astype(bf16)
+        d_down = dot(s_hidden, own_g, (0, 0)).astype(bf16)
+        return cut_shared_grads(here, d_in, d_down, C, E, s_width)
+
     kept, norms, moved = [], [], []
     for s in range(R):
         x_block = payload_rows[s]
@@ -904,21 +906,18 @@
             s, R, kept, list(zip(*(exchange(x, "exp") for x in x_block))), g_all, info,
             slots[s], expert_in, expert_down, sh_in, sh_down, capacity, norms[-1:],
         )
-        seen = moved if s == R - 1 else [x for later in ((1, 2), (3,))[s] for x in payload_rows[later]] if s < 2 else []
+        if s == R - 1:
+            shared_grads = shared_gradients(kept)
+        seen = [*moved, shared_grads[0]] if s == R - 1 else [x for later in ((1, 2), (3,))[s] for x in payload_rows[later]] if s < 2 else []
         if seen:
             norm = [norm[0], *(after(x, *seen) for x in norm[1:])]
         norms.append(reduce_parts(norm, "exp").astype(bf16))
         if s:
             moved.append(swap(norms[s], "row", s))
     kept, outs = kept[:8], kept[8:]
-    rows_x, rows_g, hidden, pre, own_x, own_g, s_hidden, s_pre = kept
-
-    s_pre, s_hidden = after(s_pre, norms[-1]), after(s_hidden, norms[-1])
-    d_in = dot(own_x, s_pre, (0, 0)).astype(bf16)
-    d_down = dot(s_hidden, own_g, (0, 0)).astype(bf16)
-    shared_grads = cut_shared_grads(here, d_in, d_down, C, E, s_width)
-    shared_sums = reduce_parts(shared_grads, "exp").astype(bf16)
-
+    rows_x, rows_g, hidden, pre = kept[:4]
+
+    shared_back = col_swap(reduce_parts(shared_grads, "exp").astype(bf16))
     norm_block = norms[0].astype(f32)
     for x_sum in moved:
         norm_block = norm_block + x_sum.astype(f32)
@@ -927,7 +926,7 @@
     d_norm, gate_terms = home[:, :model_width], home[:, model_width : model_width + n_experts]
     outs = [outs[0], *(after(x, norms[-1]) for x in outs[1:])]
 
-    out_sum = after(reduce_parts(outs, "exp").astype(bf16), moved[-1], shared_grads[0])
+    out_sum = after(reduce_parts(outs, "exp").astype(bf16), moved[-1], shared_back)
     out_rows = lax.psum_scatter(out_sum, "row", scatter_dimension=0, tiled=True)
 
     expert_width = expert_gate.shape[2]
@@ -956,18 +955,17 @@
 
     d_attended = dot(d_attn_all, weight_out, (1, 1)).astype(bf16)
     out_chunks = jnp.split(after(out_rows, d_attended), C, axis=0)
-    moe_out = out_chunks[0].astype(f32)
-    soon = [ring_send(out_chunks[k], "col", k) for k in range(1, C) if 2 * k != C]
+    moe_out = ring_send(out_chunks[C - 1], "col", 1)
     d_queries, d_kv_parts = attention_backward(
         place, queries, d_attended, att_total, lse, kv_parts, home_rows,
         (out_grads,),
     )
-    shared_back = col_swap(after(shared_sums, *d_attn_parts[1:3]))
-    d_kv_parts = after(d_kv_parts, *soon, shared_back)
+    d_kv_parts = after(d_kv_parts, moe_out)
     d_kv = reduce_parts([d_kv_parts[k] for k in range(C)], "col")
-    soon.append(ring_send(after(out_chunks[C // 2], d_kv), "col", C // 2))
-    for part in soon:
-        moe_out = moe_out + part.astype(f32)
+    moe_out = after(moe_out, d_kv)
+    for k in range(C - 2, 0, -1):
+        moe_out = ring_send(add(out_chunks[k], moe_out).astype(bf16), "col", 1)
+    moe_out = add(out_chunks[0], moe_out)
     d_query_raw = rotate(
         d_queries.reshape(own_rows, group_heads, head_width), cosines, -sines
     ) * attn_scale

time: 1020 us -> 1020 us (level)
  starting transfers between devices: 97.3 us -> 112 us
  local copies, waits for them, and re-layouts: 71.1 us -> 57.5 us
    all_gather x3, waiting for transfers between devices: 36.9 us -> 0.5 us  [the longest x1 0.35 us: shards(): lax.all_gather(after(out_grad, weight_in, *norm_one_parts[1:]), 'col', ax...]
    ppermute x76 -> x80, waiting for transfers between devices: 319 us -> 354 us  [swap(): lax.ppermute(x, axis, [(i, i ^ step) for i in range(lax.axis_size(axis))])]
    ppermute x76 -> x80, starting transfers between devices: 87.8 us -> 105 us  [swap(): lax.ppermute(x, axis, [(i, i ^ step) for i in range(lax.axis_size(axis))])]
    unnamed x219 -> x211, local copies, waits for them, and re-layouts: 27.1 us -> 21 us
    pallas_call x4 -> x5, Pallas kernels: 20 us -> 24.5 us  [cut_call(): pl.pallas_call(lambda info, *refs: kernel(info[0], info[1], *refs[:len(op...]
  transfers between devices with their start and end apart: 92 -> 96, of which waited for: 45 -> 53; matrix products, arithmetic and copies ran while one was open for 23% -> 21% of each run, Pallas kernels for 19% -> 19%
where the time goes in v4:
time: 1020 us; the launch traced here: 1010 us
  waiting for transfers between devices  396 us (39%)
  Pallas kernels  235 us (23%)
  starting transfers between devices  112 us (11%)
  matrix products  105 us (10%)
  other arithmetic  76.5 us (8%)
  local copies, waits for them, and re-layouts  57.5 us (6%)
  between operations  26.7 us (3%)
    ppermute x80, waiting for transfers between devices, swap(): lax.ppermute(x, axis, [(i, i ^ step) for i in range(lax.axis_size(axis))])  354 us
    pallas_call x4, Pallas kernels, experts_call(): pl.pallas_call(functools.partial(experts_kernel, counts, len(held) + len(...  172 us
    ppermute x80, starting transfers between devices, swap(): lax.ppermute(x, axis, [(i, i ^ step) for i in range(lax.axis_size(axis))])  105 us
    dot_general x4, matrix products, batch_dot(): return jnp.einsum(spec, left, right, preferred_element_type=f32)  55.4 us
    dot_general x9, matrix products, dot(): lax.dot_general(left, right, (((contract[0],), (contract[1],)), ((), ()))...  45.7 us
    pallas_call x2, Pallas kernels, attention_call(): pl.pallas_call(lambda place, *refs: kernel(place, *refs[:len(operands)],...  29.1 us
    ppermute x3, waiting for transfers between devices, ring_gather(): parts.append(lax.ppermute(parts[-1], axis, ring_pairs(n)))  24.9 us
    pallas_call x5, Pallas kernels, cut_call(): pl.pallas_call(lambda info, *refs: kernel(info[0], info[1], *refs[:len(op...  24.5 us
  transfers between devices with their start and end apart: 96, of which 53 were waited for; matrix products, arithmetic and copies ran while one was open for 21% of the time, Pallas kernels for 19%

profile of v4, /device:TPU:9, one launch (start us, length us, event | category | flops | bytes accessed | tf_op | source)
XLA Modules:
  0.0 1009.0 jit_solution(10022330475212874042)
XLA Ops:
  27.6 19.6 %collective-permute-done.2 = bf16[128,640]{1,0:T(8,128)(2,1)S(1)} collective-permute-done((bf16[128,640]{1,0:T(8,128)(2,1)S(1)}, bf16[128,640]{1,0:T(8,128)(2,1)S(1)}, u32[]{:S(2)}, u32[]{:S(2)}) %collective-permute-start.2) | collective-permute-done | bytes 163872 | tf_op jit(solution)/shard_map/ppermute | solution.py:22
  51.3 9.8 collective-permute-done.7.refs_3_
  96.5 9.6 shard_map.289.refs_5_.refs_8_.refs_12_
  110.8 27.9 %collective-permute-done.12.refs_4_.refs_7_ = bf16[512,256]{1,0:T(8,128)(2,1)} collective-permute-done((bf16[512,256]{1,0:T(8,128)(2,1)}, bf16[512,256]{1,0:T(8,128)(2,1)}, u32[]{:S(2)}, u32[]{:S(2)}) %collective-permute-start.12) | collective-permute-done | bytes 262176 | tf_op jit(solution)/shard_map/ppermute | solution.py:22
  138.7 12.5 %shard_map.291 = (bf16[512,640]{1,0:T(8,128)(2,1)}, f32[4,128,640]{2,1,0:T(8,128)}, f32[4,1,640]{2,1,0:T(1,128)}) custom-call(s32[6]{0:T(128)} %pad_add_fusion.place, bf16[512,640]{1,0:T(8,128)(2,1)} %copy.156.refs_0_, bf16[512,256]{1,0:T(8,128)(2,1)} %pad_maximum_fusion.8.refs_1_.refs_4_, bf16[512,256]{1,0:T(8,128)(2,1)} %collective-permute-done.10.refs_2_.refs_5_, ...), custom_call_target="tpu_custom_call" | custom-call | flops 2684354560 | bytes 1024 | tf_op jit(solution)/shard_map/pallas_call | solution.py:486
  162.9 17.0 %collective-permute-done.13 = bf16[320,640]{1,0:T(8,128)(2,1)S(1)} collective-permute-done((bf16[320,640]{1,0:T(8,128)(2,1)S(1)}, bf16[320,640]{1,0:T(8,128)(2,1)S(1)}, u32[]{:S(2)}, u32[]{:S(2)}) %collective-permute-start.13) | collective-permute-done | bytes 409632 | tf_op jit(solution)/shard_map/ppermute | solution.py:22
  179.9 16.6 %collective-permute-done.15 = bf16[320,640]{1,0:T(8,128)(2,1)S(1)} collective-permute-done((bf16[320,640]{1,0:T(8,128)(2,1)S(1)}, bf16[320,640]{1,0:T(8,128)(2,1)S(1)}, u32[]{:S(2)}, u32[]{:S(2)}) %collective-permute-start.15) | collective-permute-done | bytes 409632 | tf_op jit(solution)/shard_map/ppermute | solution.py:22
  216.4 14.2 %collective-permute-done.17 = bf16[64,2560]{1,0:T(8,128)(2,1)S(1)} collective-permute-done((bf16[64,2560]{1,0:T(8,128)(2,1)S(1)}, bf16[64,2560]{1,0:T(8,128)(2,1)S(1)}, u32[]{:S(2)}, u32[]{:S(2)}) %collective-permute-start.17) | collective-permute-done | bytes 327712 | tf_op jit(solution)/shard_map/ppermute | solution.py:22
  236.6 9.9 collective-permute-done.21
  251.7 17.0 %collective-permute-done.23 = bf16[512,384]{1,0:T(8,128)(2,1)S(1)} collective-permute-done((bf16[512,384]{1,0:T(8,128)(2,1)S(1)}, bf16[512,384]{1,0:T(8,128)(2,1)S(1)}, u32[]{:S(2)}, u32[]{:S(2)}) %collective-permute-start.23) | collective-permute-done | bytes 393248 | tf_op jit(solution)/shard_map/ppermute | solution.py:22
  274.4 14.0 %collective-permute-done.24 = bf16[128,2688]{1,0:T(8,128)(2,1)S(1)} collective-permute-done((bf16[128,2688]{1,0:T(8,128)(2,1)S(1)}, bf16[128,2688]{1,0:T(8,128)(2,1)S(1)}, u32[]{:S(2)}, u32[]{:S(2)}) %collective-permute-start.24) | collective-permute-done | bytes 688160 | tf_op jit(solution)/shard_map/ppermute | solution.py:83
  291.4 10.9 %collective-permute-done.25 = bf16[128,2688]{1,0:T(8,128)(2,1)S(1)} collective-permute-done((bf16[128,2688]{1,0:T(8,128)(2,1)S(1)}, bf16[128,2688]{1,0:T(8,128)(2,1)S(1)}, u32[]{:S(2)}, u32[]{:S(2)}) %collective-permute-start.25) | collective-permute-done | bytes 688160 | tf_op jit(solution)/shard_map/ppermute | solution.py:83
  338.6 42.6 %shard_map.296 = (bf16[2,2048,2560]{2,1,0:T(8,128)(2,1)}, bf16[2,2048,2560]{2,1,0:T(8,128)(2,1)}, bf16[2,2048,384]{2,1,0:T(8,128)(2,1)}, bf16[2,2048,768]{2,1,0:...) custom-call(s32[8]{0:T(128)} %get-tuple-element.228.info, ...), custom_call_target="tpu_custom_call" | custom-call | flops 26843545600 | bytes 1024 | tf_op jit(solution)/shard_map/pallas_call | solution.py:727
  400.9 42.9 %shard_map.298 = (bf16[2,2048,2560]{2,1,0:T(8,128)(2,1)}, bf16[2,2048,2560]{2,1,0:T(8,128)(2,1)}, bf16[2,2048,384]{2,1,0:T(8,128)(2,1)}, bf16[2,2048,768]{2,1,0:...) custom-call(s32[8]{0:T(128)} %get-tuple-element.230.info, ...), custom_call_target="tpu_custom_call", output_to_operand_aliasing={{0}: (13, {}), {1}: (14, {}), {2}: (15, {}), {3}: (16, {}),... | custom-call | flops 26843545600 | bytes 1024 | tf_op jit(solution)/shard_map/pallas_call | solution.py:727
  455.8 42.9 %shard_map.300 = (bf16[2,2048,2560]{2,1,0:T(8,128)(2,1)}, bf16[2,2048,2560]{2,1,0:T(8,128)(2,1)}, bf16[2,2048,384]{2,1,0:T(8,128)(2,1)}, bf16[2,2048,768]{2,1,0:...) custom-call(s32[8]{0:T(128)} %get-tuple-element.229.info, ...), custom_call_target="tpu_custom_call", output_to_operand_aliasing={{0}: (13, {}), {1}: (14, {}), {2}: (15, {}), {3}: (16, {}),... | custom-call | flops 26843545600 | bytes 1024 | tf_op jit(solution)/shard_map/pallas_call | solution.py:727
  511.0 43.1 %shard_map.301 = (bf16[2,2048,2560]{2,1,0:T(8,128)(2,1)}, bf16[2,2048,2560]{2,1,0:T(8,128)(2,1)}, bf16[2,2048,384]{2,1,0:T(8,128)(2,1)}, bf16[2,2048,768]{2,1,0:...) custom-call(s32[8]{0:T(128)} %get-tuple-element.231.info, ...), custom_call_target="tpu_custom_call", output_to_operand_aliasing={{0}: (17, {}), {1}: (18, {}), {2}: (19, {}), {3}: (20, {}),... | custom-call | flops 26843545600 | bytes 1024 | tf_op jit(solution)/shard_map/pallas_call | solution.py:727
  584.5 18.1 %collective-permute-done.52 = bf16[4,512,384]{2,1,0:T(8,128)(2,1)S(1)} collective-permute-done((bf16[4,512,384]{2,1,0:T(8,128)(2,1)}, bf16[4,512,384]{2,1,0:T(8,128)(2,1)S(1)}, u32[]{:S(2)}, u32[]{:S(2)}) %collective-permute-start.52) | collective-permute-done | bytes 1572896 | tf_op jit(solution)/shard_map/ppermute | solution.py:22
  607.8 10.9 %collective-permute-done.53 = bf16[512,384]{1,0:T(8,128)(2,1)S(1)} collective-permute-done((bf16[512,384]{1,0:T(8,128)(2,1)S(1)}, bf16[512,384]{1,0:T(8,128)(2,1)S(1)}, u32[]{:S(2)}, u32[]{:S(2)}) %collective-permute-start.53) | collective-permute-done | bytes 393248 | tf_op jit(solution)/shard_map/ppermute | solution.py:22
  622.2 17.7 %collective-permute-done.55 = bf16[512,384]{1,0:T(8,128)(2,1)S(1)} collective-permute-done((bf16[512,384]{1,0:T(8,128)(2,1)S(1)}, bf16[512,384]{1,0:T(8,128)(2,1)S(1)}, u32[]{:S(2)}, u32[]{:S(2)}) %collective-permute-start.55) | collective-permute-done | bytes 393248 | tf_op jit(solution)/shard_map/ppermute | solution.py:22
  641.3 11.0 %add_convert_fusion.refs_0_ = bf16[2048,2560]{1,0:T(8,128)(2,1)} fusion(bf16[2048,2560]{1,0:T(8,128)(2,1)S(1)} %collective-permute-done.50, bf16[2048,2560]{1,0:T(8,128)(2,1)} %get-tuple-element.114), kind=kLoop, calls=%fused_computation.2 | loop fusion | flops 20971520 | bytes 31457280 | tf_op jit(solution)/shard_map/convert_element_type | solution.py:929
  652.3 14.5 %collective-permute-done.51.refs_1_ = bf16[512,2688]{1,0:T(8,128)(2,1)} collective-permute-done((bf16[512,2688]{1,0:T(8,128)(2,1)S(1)}, bf16[512,2688]{1,0:T(8,128)(2,1)}, u32[]{:S(2)}, u32[]{:S(2)}) %collective-permute-start.51) | collective-permute-done | bytes 2752544 | tf_op jit(solution)/shard_map/ppermute | solution.py:22
  679.0 18.4 %fusion = f32[2,2560,384]{2,1,0:T(8,128)} fusion(bf16[2,2048,2560]{2,1,0:T(8,128)(2,1)} %get-tuple-element.124, bf16[2,2048,768]{2,1,0:T(8,128)(2,1)} %shard_map.306), kind=kOutput, calls=%fused_computation.14 | convolution fusion | flops 8053063680 | bytes 31981568 | tf_op jit(solution)/shard_map/lrd,lrf->ldf/dot_general | solution.py:188
  697.4 18.4 %fusion.2 = f32[2,2560,384]{2,1,0:T(8,128)} fusion(bf16[2,2048,2560]{2,1,0:T(8,128)(2,1)} %get-tuple-element.124, bf16[2,2048,768]{2,1,0:T(8,128)(2,1)} %shard_map.306), kind=kOutput, calls=%fused_computation.16 | convolution fusion | flops 8053063680 | bytes 31981568 | tf_op jit(solution)/shard_map/lrd,lrf->ldf/dot_general | solution.py:188
  715.8 15.0 %fusion.83 = f32[2,384,2560]{2,1,0:T(8,128)S(1)} fusion(bf16[2,2048,384]{2,1,0:T(8,128)(2,1)} %shard_map.307, bf16[2,2048,2560]{2,1,0:T(8,128)(2,1)} %get-tuple-element.127), kind=kOutput, calls=%fused_computation.274 | convolution fusion | flops 8053063680 | bytes 31981568 | tf_op jit(solution)/shard_map/lrf,lrd->lfd/dot_general | solution.py:188
  748.5 27.2 %collective-permute-done.60 = bf16[128,2560]{1,0:T(8,128)(2,1)S(1)} collective-permute-done((bf16[128,2560]{1,0:T(8,128)(2,1)S(1)}, bf16[128,2560]{1,0:T(8,128)(2,1)S(1)}, u32[]{:S(2)}, u32[]{:S(2)}) %collective-permute-start.60) | collective-permute-done | bytes 655392 | tf_op jit(solution)/shard_map/ppermute | solution.py:22
  778.5 12.6 %collective-permute-done.61 = bf16[64,2560]{1,0:T(8,128)(2,1)S(1)} collective-permute-done((bf16[64,2560]{1,0:T(8,128)(2,1)S(1)}, bf16[64,2560]{1,0:T(8,128)(2,1)S(1)}, u32[]{:S(2)}, u32[]{:S(2)}) %collective-permute-start.61) | collective-permute-done | bytes 327712 | tf_op jit(solution)/shard_map/ppermute | solution.py:22
  802.9 16.6 %shard_map.309 = (f32[512,640]{1,0:T(8,128)}, bf16[4,512,256]{2,1,0:T(8,128)(2,1)}) custom-call(s32[6]{0:T(128)} %pad_add_fusion.place, bf16[512,640]{1,0:T(8,128)(2,1)} %copy.156.refs_0_, bf16[512,640]{1,0:T(8,128)(2,1)} %convolution_convert_fusion.6.refs_1_, f32[4,128,640]{2,1,0:T(8,128)} %get-tuple-element.128.refs_2_, ...), custom_call_target="tpu_custom_call" | custom-call | flops 6710886400 | bytes 1024 | tf_op jit(solution)/shard_map/pallas_call | solution.py:486
  823.4 10.2 %collective-permute-done.63.refs_1_.refs_0_ = bf16[128,2560]{1,0:T(8,128)(2,1)S(1)} collective-permute-done((bf16[128,2560]{1,0:T(8,128)(2,1)}, bf16[128,2560]{1,0:T(8,128)(2,1)S(1)}, u32[]{:S(2)}, u32[]{:S(2)}) %collective-permute-start.63) | collective-permute-done | bytes 655392 | tf_op jit(solution)/shard_map/ppermute | solution.py:90
  845.1 10.0 collective-permute-done.64
  860.0 10.7 %collective-permute-done.66 = bf16[512,256]{1,0:T(8,128)(2,1)} collective-permute-done((bf16[512,256]{1,0:T(8,128)(2,1)}, bf16[512,256]{1,0:T(8,128)(2,1)}, u32[]{:S(2)}, u32[]{:S(2)}) %collective-permute-start.66) | collective-permute-done | bytes 262176 | tf_op jit(solution)/shard_map/ppermute | solution.py:22
  896.7 9.5 collective-permute-done.73
  976.1 11.1 %collective-permute-start.79 = (bf16[320,640]{1,0:T(8,128)(2,1)}, bf16[320,640]{1,0:T(8,128)(2,1)S(1)}, u32[]{:S(2)}, u32[]{:S(2)}) collective-permute-start(bf16[320,640]{1,0:T(8,128)(2,1)} %shard_map.313), channel_id=1, source_target_pairs={{0,16},{16,0},{1,17},{17,1},{2,18},{18,2},{3,19},{19,3},{4,20},{20... | collective-permute-start | bytes 1228808 | tf_op jit(solution)/shard_map/ppermute | solution.py:22
  (591 shorter events, 399.8 us)
Async XLA Ops:
  7.2 63.6 %all-gather.4.cloned.1.call-start = ((), (), s32[]{:S(2)}) async-start(), calls=%async_computation.4 | async-start | bytes 5160960 | tf_op jit(solution)/shard_map/all_gather | solution.py:799
  11.3 140.2 %all-gather.6.cloned.1.call-start = ((), (), s32[]{:S(2)}) async-start(), calls=%async_computation.5 | async-start | bytes 3276800 | tf_op jit(solution)/shard_map/all_gather | solution.py:800
  18.3 28.9 %collective-permute-start.2 = (bf16[128,640]{1,0:T(8,128)(2,1)S(1)}, bf16[128,640]{1,0:T(8,128)(2,1)S(1)}, u32[]{:S(2)}, u32[]{:S(2)}) collective-permute-start(bf16[128,640]{1,0:T(8,128)(2,1)S(1)} %get-tuple-element.210), channel_id=1, source_target_pairs={{0,3},{1,2},{2,1},{3,0},{4,7},{5,6},{6,5},{7,4},{8,11},{9,10},{10,... | collective-permute-start | bytes 491528 | tf_op jit(solution)/shard_map/ppermute | solution.py:22
  71.5 267.1 %all-gather.8.cloned.1.call-start = ((), (), s32[]{:S(2)}) async-start(), calls=%async_computation.6 | async-start | bytes 23592960 | tf_op jit(solution)/shard_map/all_gather | solution.py:858
  89.5 49.1 %collective-permute-start.12 = (bf16[512,256]{1,0:T(8,128)(2,1)}, bf16[512,256]{1,0:T(8,128)(2,1)}, u32[]{:S(2)}, u32[]{:S(2)}) collective-permute-start(bf16[512,256]{1,0:T(8,128)(2,1)} %pad_maximum_fusion.8.refs_1_.refs_4_), channel_id=1, source_target_pairs={{0,3},{1,2},{2,1},{3,0},{4,7},{5,6},{6,5},{7,4},{8,11},{9,10},{10,... | collective-permute-start | bytes 786440 | tf_op jit(solution)/shard_map/ppermute | solution.py:22
  154.9 645.8 %reduce-scatter.5.cloned.1.call-start = ((), (), s32[]{:S(2)}) async-start(), calls=%async_computation.7 | async-start | bytes 13107200 | tf_op jit(solution)/shard_map/reduce_scatter | solution.py:930
  161.6 34.9 %collective-permute-start.15 = (bf16[320,640]{1,0:T(8,128)(2,1)S(1)}, bf16[320,640]{1,0:T(8,128)(2,1)S(1)}, u32[]{:S(2)}, u32[]{:S(2)}) collective-permute-start(bf16[320,640]{1,0:T(8,128)(2,1)S(1)} %constant_dynamic-slice_fusion.10), channel_id=1, source_target_pairs={{0,3},{1,2},{2,1},{3,0},{4,7},{5,6},{6,5},{7,4},{8,11},{9,10},{10,... | collective-permute-start | bytes 1228808 | tf_op jit(solution)/shard_map/ppermute | solution.py:22
  231.9 38.7 %collective-permute-start.18 = (bf16[128,2560]{1,0:T(8,128)(2,1)S(1)}, bf16[128,2560]{1,0:T(8,128)(2,1)S(1)}, u32[]{:S(2)}, u32[]{:S(2)}) collective-permute-start(bf16[128,2560]{1,0:T(8,128)(2,1)S(1)} %pad_maximum_fusion.4), channel_id=1, source_target_pairs={{0,4},{4,0},{8,12},{12,8},{1,5},{5,1},{9,13},{13,9},{2,6},{6,2},{1... | collective-permute-start | bytes 1966088 | tf_op jit(solution)/shard_map/ppermute | solution.py:22
  233.1 37.5 %collective-permute-start.20 = (bf16[128,2560]{1,0:T(8,128)(2,1)S(1)}, bf16[128,2560]{1,0:T(8,128)(2,1)S(1)}, u32[]{:S(2)}, u32[]{:S(2)}) collective-permute-start(bf16[128,2560]{1,0:T(8,128)(2,1)S(1)} %pad_maximum_fusion.5), channel_id=1, source_target_pairs={{0,8},{4,12},{8,0},{12,4},{1,9},{5,13},{9,1},{13,5},{2,10},{6,14},... | collective-permute-start | bytes 1966088 | tf_op jit(solution)/shard_map/ppermute | solution.py:22
  234.2 34.5 %collective-permute-start.23 = (bf16[512,384]{1,0:T(8,128)(2,1)S(1)}, bf16[512,384]{1,0:T(8,128)(2,1)S(1)}, u32[]{:S(2)}, u32[]{:S(2)}) collective-permute-start(bf16[512,384]{1,0:T(8,128)(2,1)S(1)} %get-tuple-element.182), channel_id=1, source_target_pairs={{0,3},{1,2},{2,1},{3,0},{4,7},{5,6},{6,5},{7,4},{8,11},{9,10},{10,... | collective-permute-start | bytes 1179656 | tf_op jit(solution)/shard_map/ppermute | solution.py:22
  328.1 61.1 %collective-permute-start.27 = (bf16[512,2688]{1,0:T(8,128)(2,1)}, bf16[512,2688]{1,0:T(8,128)(2,1)}, u32[]{:S(2)}, u32[]{:S(2)}) collective-permute-start(bf16[512,2688]{1,0:T(8,128)(2,1)} %pad_maximum_fusion.refs_0_.refs_2_), channel_id=1, source_target_pairs={{0,8},{4,12},{8,0},{12,4},{1,9},{5,13},{9,1},{13,5},{2,10},{6,14},... | collective-permute-start | bytes 8257544 | tf_op jit(solution)/shard_map/ppermute | solution.py:22
  329.3 60.8 %collective-permute-start.29 = (bf16[512,2688]{1,0:T(8,128)(2,1)}, bf16[512,2688]{1,0:T(8,128)(2,1)}, u32[]{:S(2)}, u32[]{:S(2)}) collective-permute-start(bf16[512,2688]{1,0:T(8,128)(2,1)} %pad_maximum_fusion.refs_0_.refs_2_), channel_id=1, source_target_pairs={{0,4},{4,0},{8,12},{12,8},{1,5},{5,1},{9,13},{13,9},{2,6},{6,2},{1... | collective-permute-start | bytes 8257544 | tf_op jit(solution)/shard_map/ppermute | solution.py:22
  394.6 49.2 %collective-permute-start.28 = (bf16[256,2688]{1,0:T(8,128)(2,1)S(1)}, bf16[256,2688]{1,0:T(8,128)(2,1)S(1)}, u32[]{:S(2)}, u32[]{:S(2)}) collective-permute-start(bf16[256,2688]{1,0:T(8,128)(2,1)S(1)} %slice.307), channel_id=1, source_target_pairs={{0,4},{4,0},{8,12},{12,8},{1,5},{5,1},{9,13},{13,9},{2,6},{6,2},{1... | collective-permute-start | bytes 4128776 | tf_op jit(solution)/shard_map/ppermute | solution.py:22
  396.5 47.4 %collective-permute-start.30 = (bf16[256,2688]{1,0:T(8,128)(2,1)S(1)}, bf16[256,2688]{1,0:T(8,128)(2,1)}, u32[]{:S(2)}, u32[]{:S(2)}) collective-permute-start(bf16[256,2688]{1,0:T(8,128)(2,1)S(1)} %slice.308), channel_id=1, source_target_pairs={{0,8},{4,12},{8,0},{12,4},{1,9},{5,13},{9,1},{13,5},{2,10},{6,14},... | collective-permute-start | bytes 4128776 | tf_op jit(solution)/shard_map/ppermute | solution.py:22
  500.4 74.2 %collective-permute-start.47 = (bf16[512,2688]{1,0:T(8,128)(2,1)}, bf16[512,2688]{1,0:T(8,128)(2,1)}, u32[]{:S(2)}, u32[]{:S(2)}) collective-permute-start(bf16[512,2688]{1,0:T(8,128)(2,1)} %add_convert_fusion.4.refs_22_), channel_id=1, source_target_pairs={{0,4},{4,0},{8,12},{12,8},{1,5},{5,1},{9,13},{13,9},{2,6},{6,2},{1... | collective-permute-start | bytes 8257544 | tf_op jit(solution)/shard_map/ppermute | solution.py:22
  509.5 65.1 %collective-permute-start.48 = (bf16[512,2688]{1,0:T(8,128)(2,1)S(1)}, bf16[512,2688]{1,0:T(8,128)(2,1)}, u32[]{:S(2)}, u32[]{:S(2)}) collective-permute-start(bf16[512,2688]{1,0:T(8,128)(2,1)S(1)} %add_convert_fusion.3.refs_26_), channel_id=1, source_target_pairs={{0,8},{4,12},{8,0},{12,4},{1,9},{5,13},{9,1},{13,5},{2,10},{6,14},... | collective-permute-start | bytes 8257544 | tf_op jit(solution)/shard_map/ppermute | solution.py:22
  584.0 57.3 %collective-permute-start.50 = (bf16[2048,2560]{1,0:T(8,128)(2,1)}, bf16[2048,2560]{1,0:T(8,128)(2,1)S(1)}, u32[]{:S(2)}, u32[]{:S(2)}) collective-permute-start(bf16[2048,2560]{1,0:T(8,128)(2,1)} %shard_map.304), channel_id=1, source_target_pairs={{0,16},{16,0},{1,17},{17,1},{2,18},{18,2},{3,19},{19,3},{4,20},{20... | collective-permute-start | bytes 31457288 | tf_op jit(solution)/shard_map/ppermute | solution.py:22
  604.5 35.4 %collective-permute-start.55 = (bf16[512,384]{1,0:T(8,128)(2,1)S(1)}, bf16[512,384]{1,0:T(8,128)(2,1)S(1)}, u32[]{:S(2)}, u32[]{:S(2)}) collective-permute-start(bf16[512,384]{1,0:T(8,128)(2,1)S(1)} %get-tuple-element.178), channel_id=1, source_target_pairs={{0,3},{1,2},{2,1},{3,0},{4,7},{5,6},{6,5},{7,4},{8,11},{9,10},{10,... | collective-permute-start | bytes 1179656 | tf_op jit(solution)/shard_map/ppermute | solution.py:22
  605.9 61.0 %collective-permute-start.51 = (bf16[512,2688]{1,0:T(8,128)(2,1)S(1)}, bf16[512,2688]{1,0:T(8,128)(2,1)}, u32[]{:S(2)}, u32[]{:S(2)}) collective-permute-start(bf16[512,2688]{1,0:T(8,128)(2,1)S(1)} %copy-done.16), channel_id=1, source_target_pairs={{0,12},{4,8},{8,4},{12,0},{1,13},{5,9},{9,5},{13,1},{2,14},{6,10},... | collective-permute-start | bytes 8257544 | tf_op jit(solution)/shard_map/ppermute | solution.py:22
  666.9 267.3 %reduce-scatter.11.cloned.1.call-start = ((), (), s32[]{:S(2)}) async-start(), calls=%async_computation.10 | async-start | bytes 3686400 | tf_op jit(solution)/shard_map/reduce_scatter | solution.py:162
  675.4 63.8 %collective-permute-start.56 = (bf16[128,2688]{1,0:T(8,128)(2,1)}, bf16[128,2688]{1,0:T(8,128)(2,1)S(1)}, u32[]{:S(2)}, u32[]{:S(2)}) collective-permute-start(bf16[128,2688]{1,0:T(8,128)(2,1)} %get-tuple-element.160), channel_id=1, source_target_pairs={{0,2},{1,0},{3,1},{2,3},{4,6},{5,4},{7,5},{6,7},{8,10},{9,8},{11,9... | collective-permute-start | bytes 2064392 | tf_op jit(solution)/shard_map/ppermute | solution.py:90
  676.6 62.5 %collective-permute-start.57 = (bf16[128,2688]{1,0:T(8,128)(2,1)}, bf16[128,2688]{1,0:T(8,128)(2,1)}, u32[]{:S(2)}, u32[]{:S(2)}) collective-permute-start(bf16[128,2688]{1,0:T(8,128)(2,1)} %get-tuple-element.162), channel_id=1, source_target_pairs={{0,3},{1,2},{3,0},{2,1},{4,7},{5,6},{7,4},{6,5},{8,11},{9,10},{11,... | collective-permute-start | bytes 2064392 | tf_op jit(solution)/shard_map/ppermute | solution.py:90
  677.7 61.4 %collective-permute-start.58 = (bf16[128,2688]{1,0:T(8,128)(2,1)}, bf16[128,2688]{1,0:T(8,128)(2,1)}, u32[]{:S(2)}, u32[]{:S(2)}) collective-permute-start(bf16[128,2688]{1,0:T(8,128)(2,1)} %get-tuple-element.161), channel_id=1, source_target_pairs={{0,1},{1,3},{3,2},{2,0},{4,5},{5,7},{7,6},{6,4},{8,9},{9,11},{11,1... | collective-permute-start | bytes 2064392 | tf_op jit(solution)/shard_map/ppermute | solution.py:90
  745.9 29.8 %collective-permute-start.60 = (bf16[128,2560]{1,0:T(8,128)(2,1)S(1)}, bf16[128,2560]{1,0:T(8,128)(2,1)S(1)}, u32[]{:S(2)}, u32[]{:S(2)}) collective-permute-start(bf16[128,2560]{1,0:T(8,128)(2,1)S(1)} %get-tuple-element.153), channel_id=1, source_target_pairs={{0,8},{4,12},{8,0},{12,4},{1,9},{5,13},{9,1},{13,5},{2,10},{6,14},... | collective-permute-start | bytes 1966088 | tf_op jit(solution)/shard_map/ppermute | solution.py:22
  747.0 29.9 %collective-permute-start.59 = (bf16[128,2560]{1,0:T(8,128)(2,1)S(1)}, bf16[128,2560]{1,0:T(8,128)(2,1)S(1)}, u32[]{:S(2)}, u32[]{:S(2)}) collective-permute-start(bf16[128,2560]{1,0:T(8,128)(2,1)S(1)} %get-tuple-element.153), channel_id=1, source_target_pairs={{0,4},{4,0},{8,12},{12,8},{1,5},{5,1},{9,13},{13,9},{2,6},{6,2},{1... | collective-permute-start | bytes 1966088 | tf_op jit(solution)/shard_map/ppermute | solution.py:22
  794.9 146.4 %reduce-scatter.7.cloned.1.call-start = ((), (), s32[]{:S(2)}) async-start(), calls=%async_computation.8 | async-start | bytes 3686400 | tf_op jit(solution)/shard_map/reduce_scatter | solution.py:162
  802.7 30.9 %collective-permute-start.63 = (bf16[128,2560]{1,0:T(8,128)(2,1)}, bf16[128,2560]{1,0:T(8,128)(2,1)S(1)}, u32[]{:S(2)}, u32[]{:S(2)}) collective-permute-start(bf16[128,2560]{1,0:T(8,128)(2,1)} %split.54), channel_id=1, source_target_pairs={{0,2},{1,0},{3,1},{2,3},{4,6},{5,4},{7,5},{6,7},{8,10},{9,8},{11,9... | collective-permute-start | bytes 1966088 | tf_op jit(solution)/shard_map/ppermute | solution.py:90
  838.4 32.4 %collective-permute-start.66 = (bf16[512,256]{1,0:T(8,128)(2,1)}, bf16[512,256]{1,0:T(8,128)(2,1)}, u32[]{:S(2)}, u32[]{:S(2)}) collective-permute-start(bf16[512,256]{1,0:T(8,128)(2,1)} %get-tuple-element.190), channel_id=1, source_target_pairs={{0,3},{1,2},{2,1},{3,0},{4,7},{5,6},{6,5},{7,4},{8,11},{9,10},{10,... | collective-permute-start | bytes 786440 | tf_op jit(solution)/shard_map/ppermute | solution.py:22
  845.0 152.6 %reduce-scatter.9.cloned.1.call-start = ((), (), s32[]{:S(2)}) async-start(), calls=%async_computation.9 | async-start | bytes 1474560 | tf_op jit(solution)/shard_map/reduce_scatter | solution.py:162
  896.4 33.4 %collective-permute-start.67 = (bf16[128,2560]{1,0:T(8,128)(2,1)S(1)}, bf16[128,2560]{1,0:T(8,128)(2,1)}, u32[]{:S(2)}, u32[]{:S(2)}) collective-permute-start(bf16[128,2560]{1,0:T(8,128)(2,1)S(1)} %add_convert_fusion.9), channel_id=1, source_target_pairs={{0,2},{1,0},{3,1},{2,3},{4,6},{5,4},{7,5},{6,7},{8,10},{9,8},{11,9... | collective-permute-start | bytes 1966088 | tf_op jit(solution)/shard_map/ppermute | solution.py:90
  932.1 58.2 %collective-permute-start.88 = (bf16[4,512,384]{2,1,0:T(8,128)(2,1)}, bf16[4,512,384]{2,1,0:T(8,128)(2,1)}, u32[]{:S(2)}, u32[]{:S(2)}) collective-permute-start(bf16[4,512,384]{2,1,0:T(8,128)(2,1)} %shard_map.317.refs_0_), channel_id=1, source_target_pairs={{0,16},{16,0},{1,17},{17,1},{2,18},{18,2},{3,19},{19,3},{4,20},{20... | collective-permute-start | bytes 4718600 | tf_op jit(solution)/shard_map/ppermute | solution.py:22
  959.3 27.9 %collective-permute-start.70 = (bf16[128,640]{1,0:T(8,128)(2,1)S(1)}, bf16[128,640]{1,0:T(8,128)(2,1)S(1)}, u32[]{:S(2)}, u32[]{:S(2)}) collective-permute-start(bf16[128,640]{1,0:T(8,128)(2,1)S(1)} %get-tuple-element.207), channel_id=1, source_target_pairs={{0,2},{1,3},{2,0},{3,1},{4,6},{5,7},{6,4},{7,5},{8,10},{9,11},{10,... | collective-permute-start | bytes 491528 | tf_op jit(solution)/shard_map/ppermute | solution.py:22
  (162 other events, 2556.9 us)
Sparse Core Ops, SparseCore 0:
  11.5 59.3 all-gather.3
  73.0 78.4 all-gather.5
  155.1 136.5 all-gather.7
  667.0 124.5 reduce-scatter.4
  795.0 73.4 reduce-scatter.10
  870.8 53.7 reduce-scatter.6
  941.4 45.7 reduce-scatter.8

commit v5 on v4

--- a/solution.py
+++ b/solution.py
@@ -136,12 +136,14 @@
 def tokens_back(x):
     c, n = lax.axis_index("col"), lax.axis_size("col")
     rows, width = x.shape[0], x.shape[1] // n
-    whole = jnp.zeros((n * rows, width), x.dtype)
+    whole, moved = jnp.zeros((n * rows, width), x.dtype), []
     for s in range(n):
         piece = lax.dynamic_slice_in_dim(x, (c ^ s) * width, width, 1)
-        piece = swap(piece, "col", s) if s else piece
+        if s:
+            piece = swap(piece, "col", s)
+            moved.append(piece)
         whole = lax.dynamic_update_slice(whole, piece, ((c ^ s) * rows, 0))
-    return whole
+    return whole, moved
 
 
 def own_share(weight, wait=0):
@@ -811,13 +813,14 @@
     s_padded = -(-s_width // 128) * 128
 
     def col_swap(parts):
-        return jnp.stack([swap(parts[s], "col", s) if s else parts[0] for s in range(C)])
+        return [swap(parts[s], "col", s) if s else parts[0] for s in range(C)]
 
     shared_cut = cut_shared(here, shared_gate, shared_up, shared_down, C, E, raw)
     in_rows, feature_width = shared_gate.shape[0] // E, shared_down.shape[1]
     shared_parts = col_swap(shared_cut)
+    shared_moved = shared_parts[1:]
     sh_in, sh_down = join_shared(
-        here, exchange(shared_parts, "exp"), in_rows, feature_width, s_padded
+        here, exchange(jnp.stack(shared_parts), "exp"), in_rows, feature_width, s_padded
     )
     expert_in = side_by_side(expert_gate, expert_up, raw)
 
@@ -853,11 +856,11 @@
     )
     queries = (queries * attn_scale).astype(bf16).reshape(own_rows, query_width)
     place = jnp.concatenate([jnp.stack([r, c]), c ^ jnp.arange(C)]).astype(jnp.int32)
-    attended, att_total, lse = attention_forward(place, queries, kv_parts, home_rows, (expert_in, shared_cut))
-    attn_part = dot(attended, weight_out).astype(bf16)
+    attended, att_total, lse = attention_forward(place, queries, kv_parts, home_rows, (expert_in, shared_cut, *out_parts[1:]))
+    attn_part = dot(after(attended, *shared_moved), weight_out).astype(bf16)
     g_all = lax.all_gather(after(g_block, attended), ("exp", "row"), tiled=True)
     hidden_state = x + row_reduce(jnp.split(attn_part, R, axis=0))[0]
-    inv_two = rms_inverse(hidden_state) + zero_of(*(shared_parts[s] for s in range(1, C))).astype(f32)
+    inv_two = rms_inverse(hidden_state)
     norm_two = (hidden_state * inv_two * gain_two[None, :]).astype(bf16)
 
     norm_float = norm_two.astype(f32)
@@ -917,16 +920,19 @@
     kept, outs = kept[:8], kept[8:]
     rows_x, rows_g, hidden, pre = kept[:4]
 
-    shared_back = col_swap(reduce_parts(shared_grads, "exp").astype(bf16))
+    shared_sum = reduce_parts(shared_grads, "exp").astype(bf16)
+    outs_moved = [swap(after(outs[t], norms[-1], shared_sum), "exp", t) for t in range(1, E)]
+    shared_back = jnp.stack(col_swap(shared_sum))
     norm_block = norms[0].astype(f32)
     for x_sum in moved:
         norm_block = norm_block + x_sum.astype(f32)
     chunks = jnp.split(norm_block.astype(bf16), C, axis=0)
     home = ring_reduce(chunks, "col")
     d_norm, gate_terms = home[:, :model_width], home[:, model_width : model_width + n_experts]
-    outs = [outs[0], *(after(x, norms[-1]) for x in outs[1:])]
-
-    out_sum = after(reduce_parts(outs, "exp").astype(bf16), moved[-1], shared_back)
+    out_sum = outs[0].astype(f32)
+    for part in outs_moved:
+        out_sum = add(out_sum, part)
+    out_sum = after(out_sum.astype(bf16), moved[-1], shared_back)
     out_rows = lax.psum_scatter(out_sum, "row", scatter_dimension=0, tiled=True)
 
     expert_width = expert_gate.shape[2]
@@ -962,7 +968,6 @@
     )
     d_kv_parts = after(d_kv_parts, moe_out)
     d_kv = reduce_parts([d_kv_parts[k] for k in range(C)], "col")
-    moe_out = after(moe_out, d_kv)
     for k in range(C - 2, 0, -1):
         moe_out = ring_send(add(out_chunks[k], moe_out).astype(bf16), "col", 1)
     moe_out = add(out_chunks[0], moe_out)
@@ -978,10 +983,12 @@
     ).astype(bf16)
     norm_one_part = dot(jnp.concatenate([d_kv_raw, d_query_raw], axis=1), weight_in, (1, 1)).astype(bf16)
     d_norm_one, halfway = row_reduce(jnp.split(norm_one_part, R, axis=0))
-    d_x, gain_one_part = rms_backward(x, inv_one, gain_one, d_norm_one)
-    grad_inputs = tokens_back((d_hidden + d_x).astype(bf16))
-
-    output = tokens_back((hidden_state + moe_out).astype(bf16))
+    d_x, gain_one_part = rms_backward(
+        x, inv_one, gain_one + zero_of(moe_out).astype(f32), d_norm_one
+    )
+    grad_inputs, back = tokens_back((d_hidden + d_x).astype(bf16))
+
+    output = tokens_back((hidden_state + moe_out).astype(bf16))[0]
     out_total, query_total = reduce_weight(out_grads), reduce_weight(query_grads)
     kv_grads = dot(after(norm_one_late, *halfway), d_kv_raw, (0, 0)).astype(bf16)
     kv_total = reduce_weight(after(kv_grads, query_total, d_norm_one))
@@ -989,6 +996,7 @@
     grad_query = all_shares(after(query_total, d_norm_one)).astype(f32)
     grad_kv = all_shares(kv_total).astype(f32)
     small_part = jnp.concatenate([router_part, gain_one_part[None], gain_two_part[None]], axis=0)
+    small_part = small_part + zero_of(*back).astype(f32)
     width = small.shape[1]
     mine = [
         lax.dynamic_slice_in_dim(small_part, (c ^ s) * width, width, 1) for s in range(C)

time: 1020 us -> 1040 us (1.020)
  waiting for transfers between devices: 396 us -> 415 us
    ppermute x6, waiting for transfers between devices: 17.2 us -> 41.3 us  [ring_send(): lax.ppermute(x, axis, [(order[i], order[(i - k) % n]) for i in range(n)])]
    unnamed x211 -> x200, local copies, waits for them, and re-layouts: 21 us -> 24.6 us
  transfers between devices with their start and end apart: 96 -> 96, of which waited for: 53 -> 43; matrix products, arithmetic and copies ran while one was open for 21% -> 22% of each run, Pallas kernels for 19% -> 19%
where the time goes in v5:
time: 1040 us; the launch traced here: 1030 us
  waiting for transfers between devices  415 us (40%)
  Pallas kernels  235 us (23%)
  matrix products  108 us (10%)
  starting transfers between devices  106 us (10%)
  other arithmetic  76.7 us (7%)
  local copies, waits for them, and re-layouts  66.1 us (6%)
  between operations  27.9 us (3%)
    ppermute x80, waiting for transfers between devices, swap(): lax.ppermute(x, axis, [(i, i ^ step) for i in range(lax.axis_size(axis))])  349 us
    pallas_call x4, Pallas kernels, experts_call(): pl.pallas_call(functools.partial(experts_kernel, counts, len(held) + len(...  171 us
    ppermute x80, starting transfers between devices, swap(): lax.ppermute(x, axis, [(i, i ^ step) for i in range(lax.axis_size(axis))])  98.7 us
    dot_general x4, matrix products, batch_dot(): return jnp.einsum(spec, left, right, preferred_element_type=f32)  55.7 us
    dot_general x9, matrix products, dot(): lax.dot_general(left, right, (((contract[0],), (contract[1],)), ((), ()))...  47.6 us
    ppermute x6, waiting for transfers between devices, ring_send(): lax.ppermute(x, axis, [(order[i], order[(i - k) % n]) for i in range(n)])  41.3 us
    pallas_call x2, Pallas kernels, attention_call(): pl.pallas_call(lambda place, *refs: kernel(place, *refs[:len(operands)],...  29.1 us
    pallas_call x5, Pallas kernels, cut_call(): pl.pallas_call(lambda info, *refs: kernel(info[0], info[1], *refs[:len(op...  24.8 us
  transfers between devices with their start and end apart: 96, of which 43 were waited for; matrix products, arithmetic and copies ran while one was open for 22% of the time, Pallas kernels for 19%

profile of v5, /device:TPU:9, one launch (start us, length us, event | category | flops | bytes accessed | tf_op | source)
XLA Modules:
  0.0 1034.2 jit_solution(15971349797220971723)
XLA Ops:
  27.6 19.6 %collective-permute-done.2 = bf16[128,640]{1,0:T(8,128)(2,1)S(1)} collective-permute-done((bf16[128,640]{1,0:T(8,128)(2,1)S(1)}, bf16[128,640]{1,0:T(8,128)(2,1)S(1)}, u32[]{:S(2)}, u32[]{:S(2)}) %collective-permute-start.2) | collective-permute-done | bytes 163872 | tf_op jit(solution)/shard_map/ppermute | solution.py:22
  51.3 9.7 collective-permute-done.7.refs_3_
  100.7 18.9 %collective-permute-done.10.refs_2_.refs_5_ = bf16[512,256]{1,0:T(8,128)(2,1)} collective-permute-done((bf16[512,256]{1,0:T(8,128)(2,1)}, bf16[512,256]{1,0:T(8,128)(2,1)}, u32[]{:S(2)}, u32[]{:S(2)}) %collective-permute-start.10) | collective-permute-done | bytes 262176 | tf_op jit(solution)/shard_map/ppermute | solution.py:22
  125.2 9.6 shard_map.289.refs_5_.refs_8_.refs_12_
  138.7 40.5 %collective-permute-done.11.refs_3_.refs_6_ = bf16[512,256]{1,0:T(8,128)(2,1)} collective-permute-done((bf16[512,256]{1,0:T(8,128)(2,1)}, bf16[512,256]{1,0:T(8,128)(2,1)}, u32[]{:S(2)}, u32[]{:S(2)}) %collective-permute-start.11) | collective-permute-done | bytes 262176 | tf_op jit(solution)/shard_map/ppermute | solution.py:22
  179.3 8.3 collective-permute-done.12.refs_4_.refs_7_
  188.3 12.5 %shard_map.291 = (bf16[512,640]{1,0:T(8,128)(2,1)}, f32[4,128,640]{2,1,0:T(8,128)}, f32[4,1,640]{2,1,0:T(1,128)}) custom-call(s32[6]{0:T(128)} %pad_add_fusion.place, bf16[512,640]{1,0:T(8,128)(2,1)} %copy.156.refs_0_, bf16[512,256]{1,0:T(8,128)(2,1)} %pad_maximum_fusion.8.refs_1_.refs_4_, bf16[512,256]{1,0:T(8,128)(2,1)} %collective-permute-done.10.refs_2_.refs_5_, ...), custom_call_target="tpu_custom_call" | custom-call | flops 2684354560 | bytes 1024 | tf_op jit(solution)/shard_map/pallas_call | solution.py:488
  212.9 11.9 %collective-permute-done.16.refs_1_ = bf16[512,384]{1,0:T(8,128)(2,1)S(1)} collective-permute-done((bf16[512,384]{1,0:T(8,128)(2,1)S(1)}, bf16[512,384]{1,0:T(8,128)(2,1)S(1)}, u32[]{:S(2)}, u32[]{:S(2)}) %collective-permute-start.16) | collective-permute-done | bytes 393248 | tf_op jit(solution)/shard_map/ppermute | solution.py:22
  228.0 18.4 %collective-permute-done.18.refs_3_ = bf16[512,384]{1,0:T(8,128)(2,1)S(1)} collective-permute-done((bf16[512,384]{1,0:T(8,128)(2,1)S(1)}, bf16[512,384]{1,0:T(8,128)(2,1)S(1)}, u32[]{:S(2)}, u32[]{:S(2)}) %collective-permute-start.18) | collective-permute-done | bytes 393248 | tf_op jit(solution)/shard_map/ppermute | solution.py:22
  259.5 13.8 %collective-permute-done.20 = bf16[64,2560]{1,0:T(8,128)(2,1)S(1)} collective-permute-done((bf16[64,2560]{1,0:T(8,128)(2,1)S(1)}, bf16[64,2560]{1,0:T(8,128)(2,1)S(1)}, u32[]{:S(2)}, u32[]{:S(2)}) %collective-permute-start.20) | collective-permute-done | bytes 327712 | tf_op jit(solution)/shard_map/ppermute | solution.py:22
  276.4 28.1 %collective-permute-done.21 = bf16[128,2560]{1,0:T(8,128)(2,1)S(1)} collective-permute-done((bf16[128,2560]{1,0:T(8,128)(2,1)S(1)}, bf16[128,2560]{1,0:T(8,128)(2,1)S(1)}, u32[]{:S(2)}, u32[]{:S(2)}) %collective-permute-start.21) | collective-permute-done | bytes 655392 | tf_op jit(solution)/shard_map/ppermute | solution.py:22
  309.6 13.4 %collective-permute-done.24 = bf16[128,2688]{1,0:T(8,128)(2,1)S(1)} collective-permute-done((bf16[128,2688]{1,0:T(8,128)(2,1)S(1)}, bf16[128,2688]{1,0:T(8,128)(2,1)S(1)}, u32[]{:S(2)}, u32[]{:S(2)}) %collective-permute-start.24) | collective-permute-done | bytes 688160 | tf_op jit(solution)/shard_map/ppermute | solution.py:83
  326.0 11.0 %collective-permute-done.25 = bf16[128,2688]{1,0:T(8,128)(2,1)} collective-permute-done((bf16[128,2688]{1,0:T(8,128)(2,1)S(1)}, bf16[128,2688]{1,0:T(8,128)(2,1)}, u32[]{:S(2)}, u32[]{:S(2)}) %collective-permute-start.25) | collective-permute-done | bytes 688160 | tf_op jit(solution)/shard_map/ppermute | solution.py:83
  373.8 42.5 %shard_map.297 = (bf16[2,2048,2560]{2,1,0:T(8,128)(2,1)}, bf16[2,2048,2560]{2,1,0:T(8,128)(2,1)}, bf16[2,2048,384]{2,1,0:T(8,128)(2,1)}, bf16[2,2048,768]{2,1,0:...) custom-call(s32[8]{0:T(128)} %get-tuple-element.228.info, ...), custom_call_target="tpu_custom_call" | custom-call | flops 26843545600 | bytes 1024 | tf_op jit(solution)/shard_map/pallas_call | solution.py:729
  435.9 42.7 %shard_map.299 = (bf16[2,2048,2560]{2,1,0:T(8,128)(2,1)}, bf16[2,2048,2560]{2,1,0:T(8,128)(2,1)}, bf16[2,2048,384]{2,1,0:T(8,128)(2,1)}, bf16[2,2048,768]{2,1,0:...) custom-call(s32[8]{0:T(128)} %get-tuple-element.230.info, ...), custom_call_target="tpu_custom_call", output_to_operand_aliasing={{0}: (13, {}), {1}: (14, {}), {2}: (15, {}), {3}: (16, {}),... | custom-call | flops 26843545600 | bytes 1024 | tf_op jit(solution)/shard_map/pallas_call | solution.py:729
  490.6 43.0 %shard_map.301 = (bf16[2,2048,2560]{2,1,0:T(8,128)(2,1)}, bf16[2,2048,2560]{2,1,0:T(8,128)(2,1)}, bf16[2,2048,384]{2,1,0:T(8,128)(2,1)}, bf16[2,2048,768]{2,1,0:...) custom-call(s32[8]{0:T(128)} %get-tuple-element.229.info, ...), custom_call_target="tpu_custom_call", output_to_operand_aliasing={{0}: (13, {}), {1}: (14, {}), {2}: (15, {}), {3}: (16, {}),... | custom-call | flops 26843545600 | bytes 1024 | tf_op jit(solution)/shard_map/pallas_call | solution.py:729
  545.8 43.1 %shard_map.302 = (bf16[2,2048,2560]{2,1,0:T(8,128)(2,1)}, bf16[2,2048,2560]{2,1,0:T(8,128)(2,1)}, bf16[2,2048,384]{2,1,0:T(8,128)(2,1)}, bf16[2,2048,768]{2,1,0:...) custom-call(s32[8]{0:T(128)} %get-tuple-element.231.info, ...), custom_call_target="tpu_custom_call", output_to_operand_aliasing={{0}: (17, {}), {1}: (18, {}), {2}: (19, {}), {3}: (20, {}),... | custom-call | flops 26843545600 | bytes 1024 | tf_op jit(solution)/shard_map/pallas_call | solution.py:729
  588.9 8.4 convolution_convert_fusion.5.refs_1_
  626.4 11.3 %collective-permute-done.53 = bf16[512,384]{1,0:T(8,128)(2,1)S(1)} collective-permute-done((bf16[512,384]{1,0:T(8,128)(2,1)S(1)}, bf16[512,384]{1,0:T(8,128)(2,1)S(1)}, u32[]{:S(2)}, u32[]{:S(2)}) %collective-permute-start.53) | collective-permute-done | bytes 393248 | tf_op jit(solution)/shard_map/ppermute | solution.py:22
  640.9 18.2 %collective-permute-done.55 = bf16[512,384]{1,0:T(8,128)(2,1)S(1)} collective-permute-done((bf16[512,384]{1,0:T(8,128)(2,1)S(1)}, bf16[512,384]{1,0:T(8,128)(2,1)S(1)}, u32[]{:S(2)}, u32[]{:S(2)}) %collective-permute-start.55) | collective-permute-done | bytes 393248 | tf_op jit(solution)/shard_map/ppermute | solution.py:22
  660.5 11.0 %add_convert_fusion.refs_0_ = bf16[2048,2560]{1,0:T(8,128)(2,1)} fusion(bf16[2048,2560]{1,0:T(8,128)(2,1)S(1)} %collective-permute-done.51, bf16[2048,2560]{1,0:T(8,128)(2,1)} %get-tuple-element.114), kind=kLoop, calls=%fused_computation.2 | loop fusion | flops 20971520 | bytes 31457280 | tf_op jit(solution)/shard_map/convert_element_type | solution.py:935
  671.5 14.5 %collective-permute-done.52.refs_1_ = bf16[512,2688]{1,0:T(8,128)(2,1)} collective-permute-done((bf16[512,2688]{1,0:T(8,128)(2,1)S(1)}, bf16[512,2688]{1,0:T(8,128)(2,1)}, u32[]{:S(2)}, u32[]{:S(2)}) %collective-permute-start.52) | collective-permute-done | bytes 2752544 | tf_op jit(solution)/shard_map/ppermute | solution.py:22
  698.1 18.4 %fusion = f32[2,2560,384]{2,1,0:T(8,128)} fusion(bf16[2,2048,2560]{2,1,0:T(8,128)(2,1)} %get-tuple-element.124, bf16[2,2048,768]{2,1,0:T(8,128)(2,1)} %shard_map.307), kind=kOutput, calls=%fused_computation.14 | convolution fusion | flops 8053063680 | bytes 31981568 | tf_op jit(solution)/shard_map/lrd,lrf->ldf/dot_general | solution.py:190
  716.5 18.4 %fusion.2 = f32[2,2560,384]{2,1,0:T(8,128)} fusion(bf16[2,2048,2560]{2,1,0:T(8,128)(2,1)} %get-tuple-element.124, bf16[2,2048,768]{2,1,0:T(8,128)(2,1)} %shard_map.307), kind=kOutput, calls=%fused_computation.16 | convolution fusion | flops 8053063680 | bytes 31981568 | tf_op jit(solution)/shard_map/lrd,lrf->ldf/dot_general | solution.py:190
  734.9 15.4 %fusion.83 = f32[2,384,2560]{2,1,0:T(8,128)S(1)} fusion(bf16[2,2048,384]{2,1,0:T(8,128)(2,1)} %shard_map.308, bf16[2,2048,2560]{2,1,0:T(8,128)(2,1)} %get-tuple-element.127), kind=kOutput, calls=%fused_computation.276 | convolution fusion | flops 8053063680 | bytes 31981568 | tf_op jit(solution)/shard_map/lrf,lrd->lfd/dot_general | solution.py:190
  767.1 28.5 %collective-permute-done.60 = bf16[128,2560]{1,0:T(8,128)(2,1)S(1)} collective-permute-done((bf16[128,2560]{1,0:T(8,128)(2,1)S(1)}, bf16[128,2560]{1,0:T(8,128)(2,1)S(1)}, u32[]{:S(2)}, u32[]{:S(2)}) %collective-permute-start.60) | collective-permute-done | bytes 655392 | tf_op jit(solution)/shard_map/ppermute | solution.py:22
  797.2 12.3 %collective-permute-done.61 = bf16[64,2560]{1,0:T(8,128)(2,1)S(1)} collective-permute-done((bf16[64,2560]{1,0:T(8,128)(2,1)S(1)}, bf16[64,2560]{1,0:T(8,128)(2,1)S(1)}, u32[]{:S(2)}, u32[]{:S(2)}) %collective-permute-start.61) | collective-permute-done | bytes 327712 | tf_op jit(solution)/shard_map/ppermute | solution.py:22
  824.3 16.6 %shard_map.310 = (f32[512,640]{1,0:T(8,128)}, bf16[4,512,256]{2,1,0:T(8,128)(2,1)}) custom-call(s32[6]{0:T(128)} %pad_add_fusion.place, bf16[512,640]{1,0:T(8,128)(2,1)} %copy.156.refs_0_, bf16[512,640]{1,0:T(8,128)(2,1)} %convolution_convert_fusion.6.refs_1_, f32[4,128,640]{2,1,0:T(8,128)} %get-tuple-element.128.refs_2_, ...), custom_call_target="tpu_custom_call" | custom-call | flops 6710886400 | bytes 1024 | tf_op jit(solution)/shard_map/pallas_call | solution.py:488
  844.8 10.4 %collective-permute-done.63.refs_1_ = bf16[128,2560]{1,0:T(8,128)(2,1)S(1)} collective-permute-done((bf16[128,2560]{1,0:T(8,128)(2,1)}, bf16[128,2560]{1,0:T(8,128)(2,1)S(1)}, u32[]{:S(2)}, u32[]{:S(2)}) %collective-permute-start.63) | collective-permute-done | bytes 655392 | tf_op jit(solution)/shard_map/ppermute | solution.py:90
  866.6 9.5 collective-permute-done.69
  878.5 10.6 %collective-permute-done.71 = bf16[512,256]{1,0:T(8,128)(2,1)} collective-permute-done((bf16[512,256]{1,0:T(8,128)(2,1)}, bf16[512,256]{1,0:T(8,128)(2,1)}, u32[]{:S(2)}, u32[]{:S(2)}) %collective-permute-start.71) | collective-permute-done | bytes 262176 | tf_op jit(solution)/shard_map/ppermute | solution.py:22
  907.5 23.2 %collective-permute-done.64 = bf16[128,2560]{1,0:T(8,128)(2,1)S(1)} collective-permute-done((bf16[128,2560]{1,0:T(8,128)(2,1)S(1)}, bf16[128,2560]{1,0:T(8,128)(2,1)S(1)}, u32[]{:S(2)}, u32[]{:S(2)}) %collective-permute-start.64) | collective-permute-done | bytes 655392 | tf_op jit(solution)/shard_map/ppermute | solution.py:90
  (583 shorter events, 392.6 us)
Async XLA Ops:
  7.2 63.6 %all-gather.4.cloned.1.call-start = ((), (), s32[]{:S(2)}) async-start(), calls=%async_computation.4 | async-start | bytes 5160960 | tf_op jit(solution)/shard_map/all_gather | solution.py:801
  11.3 189.5 %all-gather.6.cloned.1.call-start = ((), (), s32[]{:S(2)}) async-start(), calls=%async_computation.5 | async-start | bytes 3276800 | tf_op jit(solution)/shard_map/all_gather | solution.py:802
  71.5 302.4 %all-gather.8.cloned.1.call-start = ((), (), s32[]{:S(2)}) async-start(), calls=%async_computation.6 | async-start | bytes 23592960 | tf_op jit(solution)/shard_map/all_gather | solution.py:861
  85.2 34.4 %collective-permute-start.10 = (bf16[512,256]{1,0:T(8,128)(2,1)}, bf16[512,256]{1,0:T(8,128)(2,1)}, u32[]{:S(2)}, u32[]{:S(2)}) collective-permute-start(bf16[512,256]{1,0:T(8,128)(2,1)} %pad_maximum_fusion.8.refs_1_.refs_4_), channel_id=1, source_target_pairs={{0,1},{1,0},{2,3},{3,2},{4,5},{5,4},{6,7},{7,6},{8,9},{9,8},{10,11... | collective-permute-start | bytes 786440 | tf_op jit(solution)/shard_map/ppermute | solution.py:22
  92.2 95.4 %collective-permute-start.13 = (bf16[320,640]{1,0:T(8,128)(2,1)}, bf16[320,640]{1,0:T(8,128)(2,1)}, u32[]{:S(2)}, u32[]{:S(2)}) collective-permute-start(bf16[320,640]{1,0:T(8,128)(2,1)} %constant_dynamic-slice_fusion.10), channel_id=1, source_target_pairs={{0,1},{1,0},{2,3},{3,2},{4,5},{5,4},{6,7},{7,6},{8,9},{9,8},{10,11... | collective-permute-start | bytes 1228808 | tf_op jit(solution)/shard_map/ppermute | solution.py:22
  92.2 95.4 %collective-permute-start.14 = (bf16[320,640]{1,0:T(8,128)(2,1)}, bf16[320,640]{1,0:T(8,128)(2,1)}, u32[]{:S(2)}, u32[]{:S(2)}) collective-permute-start(bf16[320,640]{1,0:T(8,128)(2,1)} %constant_dynamic-slice_fusion.10), channel_id=1, source_target_pairs={{0,2},{1,3},{2,0},{3,1},{4,6},{5,7},{6,4},{7,5},{8,10},{9,11},{10,... | collective-permute-start | bytes 1228808 | tf_op jit(solution)/shard_map/ppermute | solution.py:22
  94.6 93.0 %collective-permute-start.15 = (bf16[320,640]{1,0:T(8,128)(2,1)}, bf16[320,640]{1,0:T(8,128)(2,1)}, u32[]{:S(2)}, u32[]{:S(2)}) collective-permute-start(bf16[320,640]{1,0:T(8,128)(2,1)} %constant_dynamic-slice_fusion.10), channel_id=1, source_target_pairs={{0,3},{1,2},{2,1},{3,0},{4,7},{5,6},{6,5},{7,4},{8,11},{9,10},{10,... | collective-permute-start | bytes 1228808 | tf_op jit(solution)/shard_map/ppermute | solution.py:22
  94.9 84.4 %collective-permute-start.11 = (bf16[512,256]{1,0:T(8,128)(2,1)}, bf16[512,256]{1,0:T(8,128)(2,1)}, u32[]{:S(2)}, u32[]{:S(2)}) collective-permute-start(bf16[512,256]{1,0:T(8,128)(2,1)} %pad_maximum_fusion.8.refs_1_.refs_4_), channel_id=1, source_target_pairs={{0,2},{1,3},{2,0},{3,1},{4,6},{5,7},{6,4},{7,5},{8,10},{9,11},{10,... | collective-permute-start | bytes 786440 | tf_op jit(solution)/shard_map/ppermute | solution.py:22
  119.6 68.1 %collective-permute-start.12 = (bf16[512,256]{1,0:T(8,128)(2,1)}, bf16[512,256]{1,0:T(8,128)(2,1)S(1)}, u32[]{:S(2)}, u32[]{:S(2)}) collective-permute-start(bf16[512,256]{1,0:T(8,128)(2,1)} %pad_maximum_fusion.8.refs_1_.refs_4_), channel_id=1, source_target_pairs={{0,3},{1,2},{2,1},{3,0},{4,7},{5,6},{6,5},{7,4},{8,11},{9,10},{10,... | collective-permute-start | bytes 786440 | tf_op jit(solution)/shard_map/ppermute | solution.py:22
  204.3 617.8 %reduce-scatter.5.cloned.1.call-start = ((), (), s32[]{:S(2)}) async-start(), calls=%async_computation.7 | async-start | bytes 13107200 | tf_op jit(solution)/shard_map/reduce_scatter | solution.py:936
  207.4 39.8 %collective-permute-start.19 = (bf16[4,320,640]{2,1,0:T(8,128)(2,1)}, bf16[4,320,640]{2,1,0:T(8,128)(2,1)}, u32[]{:S(2)}, u32[]{:S(2)}) collective-permute-start(bf16[4,320,640]{2,1,0:T(8,128)(2,1)} %pad_maximum_fusion.1.refs_0_), channel_id=1, source_target_pairs={{0,16},{16,0},{1,17},{17,1},{2,18},{18,2},{3,19},{19,3},{4,20},{20... | collective-permute-start | bytes 4915208 | tf_op jit(solution)/shard_map/ppermute | solution.py:22
  210.3 36.1 %collective-permute-start.18 = (bf16[512,384]{1,0:T(8,128)(2,1)S(1)}, bf16[512,384]{1,0:T(8,128)(2,1)S(1)}, u32[]{:S(2)}, u32[]{:S(2)}) collective-permute-start(bf16[512,384]{1,0:T(8,128)(2,1)S(1)} %get-tuple-element.184), channel_id=1, source_target_pairs={{0,3},{1,2},{2,1},{3,0},{4,7},{5,6},{6,5},{7,4},{8,11},{9,10},{10,... | collective-permute-start | bytes 1179656 | tf_op jit(solution)/shard_map/ppermute | solution.py:22
  363.1 61.1 %collective-permute-start.27 = (bf16[512,2688]{1,0:T(8,128)(2,1)}, bf16[512,2688]{1,0:T(8,128)(2,1)}, u32[]{:S(2)}, u32[]{:S(2)}) collective-permute-start(bf16[512,2688]{1,0:T(8,128)(2,1)} %pad_maximum_fusion.refs_0_.refs_2_), channel_id=1, source_target_pairs={{0,8},{4,12},{8,0},{12,4},{1,9},{5,13},{9,1},{13,5},{2,10},{6,14},... | collective-permute-start | bytes 8257544 | tf_op jit(solution)/shard_map/ppermute | solution.py:22
  363.4 60.8 %collective-permute-start.29 = (bf16[512,2688]{1,0:T(8,128)(2,1)}, bf16[512,2688]{1,0:T(8,128)(2,1)}, u32[]{:S(2)}, u32[]{:S(2)}) collective-permute-start(bf16[512,2688]{1,0:T(8,128)(2,1)} %pad_maximum_fusion.refs_0_.refs_2_), channel_id=1, source_target_pairs={{0,4},{4,0},{8,12},{12,8},{1,5},{5,1},{9,13},{13,9},{2,6},{6,2},{1... | collective-permute-start | bytes 8257544 | tf_op jit(solution)/shard_map/ppermute | solution.py:22
  428.7 49.8 %collective-permute-start.28 = (bf16[256,2688]{1,0:T(8,128)(2,1)S(1)}, bf16[256,2688]{1,0:T(8,128)(2,1)S(1)}, u32[]{:S(2)}, u32[]{:S(2)}) collective-permute-start(bf16[256,2688]{1,0:T(8,128)(2,1)S(1)} %slice.308), channel_id=1, source_target_pairs={{0,4},{4,0},{8,12},{12,8},{1,5},{5,1},{9,13},{13,9},{2,6},{6,2},{1... | collective-permute-start | bytes 4128776 | tf_op jit(solution)/shard_map/ppermute | solution.py:22
  430.5 48.0 %collective-permute-start.30 = (bf16[256,2688]{1,0:T(8,128)(2,1)S(1)}, bf16[256,2688]{1,0:T(8,128)(2,1)}, u32[]{:S(2)}, u32[]{:S(2)}) collective-permute-start(bf16[256,2688]{1,0:T(8,128)(2,1)S(1)} %slice.309), channel_id=1, source_target_pairs={{0,8},{4,12},{8,0},{12,4},{1,9},{5,13},{9,1},{13,5},{2,10},{6,14},... | collective-permute-start | bytes 4128776 | tf_op jit(solution)/shard_map/ppermute | solution.py:22
  535.2 74.2 %collective-permute-start.47 = (bf16[512,2688]{1,0:T(8,128)(2,1)}, bf16[512,2688]{1,0:T(8,128)(2,1)}, u32[]{:S(2)}, u32[]{:S(2)}) collective-permute-start(bf16[512,2688]{1,0:T(8,128)(2,1)} %add_convert_fusion.4.refs_22_), channel_id=1, source_target_pairs={{0,4},{4,0},{8,12},{12,8},{1,5},{5,1},{9,13},{13,9},{2,6},{6,2},{1... | collective-permute-start | bytes 8257544 | tf_op jit(solution)/shard_map/ppermute | solution.py:22
  544.3 65.1 %collective-permute-start.48 = (bf16[512,2688]{1,0:T(8,128)(2,1)S(1)}, bf16[512,2688]{1,0:T(8,128)(2,1)}, u32[]{:S(2)}, u32[]{:S(2)}) collective-permute-start(bf16[512,2688]{1,0:T(8,128)(2,1)S(1)} %add_convert_fusion.3.refs_26_), channel_id=1, source_target_pairs={{0,8},{4,12},{8,0},{12,4},{1,9},{5,13},{9,1},{13,5},{2,10},{6,14},... | collective-permute-start | bytes 8257544 | tf_op jit(solution)/shard_map/ppermute | solution.py:22
  620.8 39.7 %collective-permute-start.51 = (bf16[2048,2560]{1,0:T(8,128)(2,1)}, bf16[2048,2560]{1,0:T(8,128)(2,1)S(1)}, u32[]{:S(2)}, u32[]{:S(2)}) collective-permute-start(bf16[2048,2560]{1,0:T(8,128)(2,1)} %shard_map.305), channel_id=1, source_target_pairs={{0,16},{16,0},{1,17},{17,1},{2,18},{18,2},{3,19},{19,3},{4,20},{20... | collective-permute-start | bytes 31457288 | tf_op jit(solution)/shard_map/ppermute | solution.py:22
  623.4 35.7 %collective-permute-start.55 = (bf16[512,384]{1,0:T(8,128)(2,1)S(1)}, bf16[512,384]{1,0:T(8,128)(2,1)S(1)}, u32[]{:S(2)}, u32[]{:S(2)}) collective-permute-start(bf16[512,384]{1,0:T(8,128)(2,1)S(1)} %get-tuple-element.180), channel_id=1, source_target_pairs={{0,3},{1,2},{2,1},{3,0},{4,7},{5,6},{6,5},{7,4},{8,11},{9,10},{10,... | collective-permute-start | bytes 1179656 | tf_op jit(solution)/shard_map/ppermute | solution.py:22
  625.1 61.0 %collective-permute-start.52 = (bf16[512,2688]{1,0:T(8,128)(2,1)S(1)}, bf16[512,2688]{1,0:T(8,128)(2,1)}, u32[]{:S(2)}, u32[]{:S(2)}) collective-permute-start(bf16[512,2688]{1,0:T(8,128)(2,1)S(1)} %copy-done.15), channel_id=1, source_target_pairs={{0,12},{4,8},{8,4},{12,0},{1,13},{5,9},{9,5},{13,1},{2,14},{6,10},... | collective-permute-start | bytes 8257544 | tf_op jit(solution)/shard_map/ppermute | solution.py:22
  686.1 277.9 %reduce-scatter.11.cloned.1.call-start = ((), (), s32[]{:S(2)}) async-start(), calls=%async_computation.10 | async-start | bytes 3686400 | tf_op jit(solution)/shard_map/reduce_scatter | solution.py:164
  694.6 64.0 %collective-permute-start.56 = (bf16[128,2688]{1,0:T(8,128)(2,1)}, bf16[128,2688]{1,0:T(8,128)(2,1)S(1)}, u32[]{:S(2)}, u32[]{:S(2)}) collective-permute-start(bf16[128,2688]{1,0:T(8,128)(2,1)} %get-tuple-element.162), channel_id=1, source_target_pairs={{0,2},{1,0},{3,1},{2,3},{4,6},{5,4},{7,5},{6,7},{8,10},{9,8},{11,9... | collective-permute-start | bytes 2064392 | tf_op jit(solution)/shard_map/ppermute | solution.py:90
  695.9 62.8 %collective-permute-start.57 = (bf16[128,2688]{1,0:T(8,128)(2,1)}, bf16[128,2688]{1,0:T(8,128)(2,1)}, u32[]{:S(2)}, u32[]{:S(2)}) collective-permute-start(bf16[128,2688]{1,0:T(8,128)(2,1)} %get-tuple-element.164), channel_id=1, source_target_pairs={{0,3},{1,2},{3,0},{2,1},{4,7},{5,6},{7,4},{6,5},{8,11},{9,10},{11,... | collective-permute-start | bytes 2064392 | tf_op jit(solution)/shard_map/ppermute | solution.py:90
  696.7 62.0 %collective-permute-start.58 = (bf16[128,2688]{1,0:T(8,128)(2,1)}, bf16[128,2688]{1,0:T(8,128)(2,1)}, u32[]{:S(2)}, u32[]{:S(2)}) collective-permute-start(bf16[128,2688]{1,0:T(8,128)(2,1)} %get-tuple-element.163), channel_id=1, source_target_pairs={{0,1},{1,3},{3,2},{2,0},{4,5},{5,7},{7,6},{6,4},{8,9},{9,11},{11,1... | collective-permute-start | bytes 2064392 | tf_op jit(solution)/shard_map/ppermute | solution.py:90
  765.7 31.3 %collective-permute-start.59 = (bf16[128,2560]{1,0:T(8,128)(2,1)S(1)}, bf16[128,2560]{1,0:T(8,128)(2,1)S(1)}, u32[]{:S(2)}, u32[]{:S(2)}) collective-permute-start(bf16[128,2560]{1,0:T(8,128)(2,1)S(1)} %get-tuple-element.153), channel_id=1, source_target_pairs={{0,4},{4,0},{8,12},{12,8},{1,5},{5,1},{9,13},{13,9},{2,6},{6,2},{1... | collective-permute-start | bytes 1966088 | tf_op jit(solution)/shard_map/ppermute | solution.py:22
  813.2 167.7 %reduce-scatter.7.cloned.1.call-start = ((), (), s32[]{:S(2)}) async-start(), calls=%async_computation.8 | async-start | bytes 3686400 | tf_op jit(solution)/shard_map/reduce_scatter | solution.py:164
  824.1 31.1 %collective-permute-start.63 = (bf16[128,2560]{1,0:T(8,128)(2,1)}, bf16[128,2560]{1,0:T(8,128)(2,1)S(1)}, u32[]{:S(2)}, u32[]{:S(2)}) collective-permute-start(bf16[128,2560]{1,0:T(8,128)(2,1)} %split.54), channel_id=1, source_target_pairs={{0,2},{1,0},{3,1},{2,3},{4,6},{5,4},{7,5},{6,7},{8,10},{9,8},{11,9... | collective-permute-start | bytes 1966088 | tf_op jit(solution)/shard_map/ppermute | solution.py:90
  866.6 158.0 %reduce-scatter.9.cloned.1.call-start = ((), (), s32[]{:S(2)}) async-start(), calls=%async_computation.9 | async-start | bytes 1474560 | tf_op jit(solution)/shard_map/reduce_scatter | solution.py:164
  906.3 43.8 %collective-permute-start.73 = (bf16[128,2560]{1,0:T(8,128)(2,1)}, bf16[128,2560]{1,0:T(8,128)(2,1)}, u32[]{:S(2)}, u32[]{:S(2)}) collective-permute-start(bf16[128,2560]{1,0:T(8,128)(2,1)} %pad_maximum_fusion.6), channel_id=1, source_target_pairs={{0,4},{4,0},{8,12},{12,8},{1,5},{5,1},{9,13},{13,9},{2,6},{6,2},{1... | collective-permute-start | bytes 1966088 | tf_op jit(solution)/shard_map/ppermute | solution.py:22
  953.1 64.2 %collective-permute-start.88 = (bf16[4,512,384]{2,1,0:T(8,128)(2,1)}, bf16[4,512,384]{2,1,0:T(8,128)(2,1)}, u32[]{:S(2)}, u32[]{:S(2)}) collective-permute-start(bf16[4,512,384]{2,1,0:T(8,128)(2,1)} %shard_map.317.refs_0_), channel_id=1, source_target_pairs={{0,16},{16,0},{1,17},{17,1},{2,18},{18,2},{3,19},{19,3},{4,20},{20... | collective-permute-start | bytes 4718600 | tf_op jit(solution)/shard_map/ppermute | solution.py:22
  964.0 49.0 %collective-permute-start.81 = (bf16[320,640]{1,0:T(8,128)(2,1)}, bf16[320,640]{1,0:T(8,128)(2,1)S(1)}, u32[]{:S(2)}, u32[]{:S(2)}) collective-permute-start(bf16[320,640]{1,0:T(8,128)(2,1)} %shard_map.316), channel_id=1, source_target_pairs={{0,16},{16,0},{1,17},{17,1},{2,18},{18,2},{3,19},{19,3},{4,20},{20... | collective-permute-start | bytes 1228808 | tf_op jit(solution)/shard_map/ppermute | solution.py:22
  (156 other events, 2524.3 us)
Sparse Core Ops, SparseCore 0:
  11.5 59.3 all-gather.3
  73.0 100.6 all-gather.5
  204.4 129.2 all-gather.7
  686.2 122.4 reduce-scatter.4
  813.3 58.4 reduce-scatter.10
  874.1 74.1 reduce-scatter.6
  981.1 39.1 reduce-scatter.8

commit v6 on v5

--- a/solution.py
+++ b/solution.py
@@ -354,16 +354,21 @@
     )(info, *operands, *waits)
 
 
-def join_weight(info, parts):
-    cols, rows, width = parts[0].shape
-
-    def kernel(e, c, *refs):
-        for s in range(cols):
-            for t, ref in enumerate(refs[:-1]):
-                refs[-1][rows_at(e ^ t, rows), rows_at(c ^ s, width)] = ref[s]
-
-    outs = (jax.ShapeDtypeStruct((len(parts) * rows, cols * width), parts[0].dtype),)
-    return cut_call(kernel, info, parts, outs)[0]
+def join_weight(blocks, first, cols, shares):
+    rows, width = blocks.shape[0] // (cols * shares), blocks.shape[1] - first
+
+    def kernel(ref, out_ref):
+        for k in range(cols):
+            for t in range(shares):
+                at = (k * shares + t) * rows
+                out_ref[t * rows : (t + 1) * rows, k * width : (k + 1) * width] = ref[at : at + rows, first:]
+
+    return pl.pallas_call(
+        kernel,
+        out_shape=jax.ShapeDtypeStruct((shares * rows, cols * width), blocks.dtype),
+        compiler_params=pltpu.CompilerParams(vmem_limit_bytes=vmem_limit),
+        cost_estimate=pl.CostEstimate(flops=0, bytes_accessed=2**10, transcendentals=0),
+    )(blocks)
 
 
 def each_index(index, count, work):
@@ -585,7 +590,7 @@
             chunk = tokens // chunks
             g = jnp.concatenate(
                 [
-                    g_refs[t][pl.ds(pl.multiple_of(info[groups + k] * chunk, chunk), chunk), :]
+                    g_refs[t][pl.ds(pl.multiple_of(info[k] * chunk, chunk), chunk), :]
                     for k in range(chunks)
                 ],
                 axis=0,
@@ -613,7 +618,7 @@
         lane = lax.broadcasted_iota(jnp.int32, (1, lanes), 1)
         spread = []
         for l in range(local):
-            expert = info[groups + chunks] + l
+            expert = info[chunks] + l
             weights = jnp.concatenate([dot(pick[t * local + l], mixes[t]) for t in range(groups)], axis=0)
             weights = jnp.sum(
                 jnp.where(lane % (lanes // 2) == expert, weights, 0.0), axis=1, keepdims=True
@@ -655,12 +660,12 @@
             norm_refs[t][:, : term_buf.shape[2]] = term_buf[t]
 
 
-def experts_call(at, blocks, held, x_parts, g_all, info, slots, w_in, w_down, s_in, s_down, capacity, waits):
+def experts_call(at, blocks, held, x_parts, g_parts, info, slots, w_in, w_down, s_in, s_down, capacity, waits):
     counts = [len(parts) for parts in x_parts]
     x_parts = [x for parts in x_parts for x in parts]
     groups, local = len(counts), w_in.shape[0]
-    chunks = info.shape[0] - groups - 2
-    model, whole_width = g_all.shape[1], x_parts[0].shape[1]
+    chunks = info.shape[0] - 2
+    model, whole_width = g_parts[0].shape[1], x_parts[0].shape[1]
     lanes = whole_width - model
     tokens = sum(x.shape[0] for x in x_parts[: counts[0]])
     tile = 512 if groups <= 2 else 256
@@ -671,9 +676,6 @@
     def tokens_in(i, info):
         return (0, jnp.minimum(i, tiles - 1))
 
-    def grads_in(t):
-        return pl.BlockSpec((tokens, tile), lambda i, info: (info[t], jnp.minimum(i, tiles - 1)))
-
     def picked(i, info):
         return (0, at, jnp.minimum(i, tiles - 1))
 
@@ -681,7 +683,7 @@
         return (at, jnp.minimum(i, tiles - 1))
 
     def summed(i, info):
-        return (info[groups + chunks + 1], jnp.clip(i - tiles, 0, tiles - 1))
+        return (info[chunks + 1], jnp.clip(i - tiles, 0, tiles - 1))
 
     def summed_norm(i, info):
         return (0, jnp.maximum(i - tiles, 0))
@@ -689,7 +691,7 @@
     in_specs = [
         *(pl.BlockSpec((x.shape[0], tile), tokens_in) for x in x_parts),
         *(pl.BlockSpec((x.shape[0], lanes), lambda i, info: (0, model // lanes)) for x in x_parts),
-        *(grads_in(t) for t in range(groups)),
+        *[pl.BlockSpec((tokens, tile), tokens_in)] * groups,
         whole_spec(slots.shape),
         whole_spec(slots.shape[::-1]),
         pl.BlockSpec((local, tile, 2 * width), lambda i, info: (0, i % tiles, 0)),
@@ -747,7 +749,7 @@
         input_output_aliases={first + i: i for i in range(len(held))},
         compiler_params=pltpu.CompilerParams(vmem_limit_bytes=vmem_limit),
         cost_estimate=pl.CostEstimate(flops=work, bytes_accessed=2**10, transcendentals=0),
-    )(info, *x_parts, *x_parts, *[g_all] * groups, slots, slots.T, w_in, w_down, s_in, s_down, *held, *waits)
+    )(info, *x_parts, *x_parts, *g_parts, slots, slots.T, w_in, w_down, s_in, s_down, *held, *waits)
     return list(results[: len(kept)]), list(results[len(kept) :])
 
 
@@ -797,17 +799,13 @@
     norm_one_parts = row_gather(norm_one)
     norm_one_all = jnp.concatenate(norm_one_parts, axis=0)
 
-    own_in = own_share(jnp.concatenate([w_key, w_value, w_query], axis=1))
-    weight_in = lax.all_gather(own_in, ("col", "exp"), tiled=True)
-    g_block = lax.all_gather(
-        after(out_grad, weight_in, *norm_one_parts[1:]), "col", axis=1, tiled=True
-    )
-    g = lax.dynamic_slice_in_dim(g_block, c * home_rows, home_rows, 0)
+    own_weights = own_share(jnp.concatenate([w_key, w_value, w_query, w_output], axis=1))
+    weights = lax.all_gather(own_weights, ("col", "exp"), tiled=True)
+    weight_in = weights[:, : query_width + 2 * key_width]
     raw = dot(norm_one_all, weight_in)
     wait = zero_of(raw)
     here = jnp.stack([e, c]).astype(jnp.int32)
-    out_parts = exchange(own_share(w_output, wait), "col")
-    weight_out = join_weight(here, exchange(jnp.stack(out_parts), "exp"))
+    weight_out = join_weight(weights, query_width + 2 * key_width, C, E)
 
     s_width = shared_gate.shape[1] // C
     s_padded = -(-s_width // 128) * 128
@@ -817,11 +815,6 @@
 
     shared_cut = cut_shared(here, shared_gate, shared_up, shared_down, C, E, raw)
     in_rows, feature_width = shared_gate.shape[0] // E, shared_down.shape[1]
-    shared_parts = col_swap(shared_cut)
-    shared_moved = shared_parts[1:]
-    sh_in, sh_down = join_shared(
-        here, exchange(jnp.stack(shared_parts), "exp"), in_rows, feature_width, s_padded
-    )
     expert_in = side_by_side(expert_gate, expert_up, raw)
 
     own_routes = lax.dynamic_slice_in_dim(routes, c * home_rows, home_rows, 0)
@@ -851,16 +844,21 @@
     keys = rotate(raw[:, :key_width].reshape(own_rows, 1, head_width), cosines, sines)
     kv = jnp.concatenate([keys.reshape(own_rows, key_width), raw[:, key_width : 2 * key_width]], axis=1)
     kv_parts = exchange(kv.astype(bf16), "col")
+    g_block = lax.all_gather(after(out_grad, *kv_parts[1:]), "col", axis=1, tiled=True)
+    g = lax.dynamic_slice_in_dim(g_block, c * home_rows, home_rows, 0)
     queries = rotate(
         raw[:, 2 * key_width :].reshape(own_rows, group_heads, head_width), cosines, sines
     )
     queries = (queries * attn_scale).astype(bf16).reshape(own_rows, query_width)
     place = jnp.concatenate([jnp.stack([r, c]), c ^ jnp.arange(C)]).astype(jnp.int32)
-    attended, att_total, lse = attention_forward(place, queries, kv_parts, home_rows, (expert_in, shared_cut, *out_parts[1:]))
-    attn_part = dot(after(attended, *shared_moved), weight_out).astype(bf16)
-    g_all = lax.all_gather(after(g_block, attended), ("exp", "row"), tiled=True)
+    attended, att_total, lse = attention_forward(place, queries, kv_parts, home_rows, (expert_in, shared_cut))
+    attn_part = dot(attended, weight_out).astype(bf16)
+    shared_parts = col_swap(after(shared_cut, attended))
+    sh_in, sh_down = join_shared(
+        here, exchange(jnp.stack(shared_parts), "exp"), in_rows, feature_width, s_padded
+    )
     hidden_state = x + row_reduce(jnp.split(attn_part, R, axis=0))[0]
-    inv_two = rms_inverse(hidden_state)
+    inv_two = rms_inverse(hidden_state) + zero_of(g_block, *shared_parts[1:]).astype(f32)
     norm_two = (hidden_state * inv_two * gain_two[None, :]).astype(bf16)
 
     norm_float = norm_two.astype(f32)
@@ -885,8 +883,11 @@
         axis=1,
     )
     payload = jnp.concatenate(ring_gather(payload, "col"), axis=0)
+    grad_rows = row_gather(g_block)
+    payload = after(payload, *grad_rows[1:3])
     payload_rows = row_gather(payload)
     if R == 4:
+        grad_rows = grad_rows[:3] + [jnp.concatenate(grad_rows[3:], axis=0)]
         payload_rows = [[x] for x in payload_rows[:3]] + [payload_rows[3:]]
     else:
         payload_rows = [[x] for x in payload_rows]
@@ -902,11 +903,13 @@
         x_block = payload_rows[s]
         if E > 2 and kept:
             x_block = [after(x, kept[-1]) for x in x_block]
+            grad_rows[s] = after(grad_rows[s], kept[-1])
         info = jnp.concatenate(
-            [(e ^ jnp.arange(E)) * R + (r ^ s), sources, jnp.stack([first_expert, r ^ s])]
+            [sources, jnp.stack([first_expert, r ^ s])]
         ).astype(jnp.int32)
         kept, norm = experts_call(
-            s, R, kept, list(zip(*(exchange(x, "exp") for x in x_block))), g_all, info,
+            s, R, kept, list(zip(*(exchange(x, "exp") for x in x_block))),
+            exchange(grad_rows[s], "exp"), info,
             slots[s], expert_in, expert_down, sh_in, sh_down, capacity, norms[-1:],
         )
         if s == R - 1:

time: 1040 us -> 991 us (0.953)
  waiting for transfers between devices: 415 us -> 369 us
    ppermute x80 -> x84, waiting for transfers between devices: 349 us -> 275 us  [swap(): lax.ppermute(x, axis, [(i, i ^ step) for i in range(lax.axis_size(axis))])]
    all_gather x3 -> x2, waiting for transfers between devices: 0.21 us -> 26 us  [the longest x1 26 us: shards(): weights = lax.all_gather(own_weights, ('col', 'exp'), tiled=True)]
    ppermute x80 -> x84, starting transfers between devices: 98.7 us -> 86.9 us  [swap(): lax.ppermute(x, axis, [(i, i ^ step) for i in range(lax.axis_size(axis))])]
    pallas_call x5 -> x4, Pallas kernels: 24.8 us -> 20.3 us  [cut_call(): pl.pallas_call(lambda info, *refs: kernel(info[0], info[1], *refs[:len(op...]
    unnamed x200 -> x203, local copies, waits for them, and re-layouts: 24.6 us -> 23.4 us
  transfers between devices with their start and end apart: 96 -> 99, of which waited for: 43 -> 43; matrix products, arithmetic and copies ran while one was open for 22% -> 22% of each run, Pallas kernels for 19% -> 24%
where the time goes in v6:
time: 991 us; the launch traced here: 984 us
  waiting for transfers between devices  369 us (37%)
  Pallas kernels  236 us (24%)
  matrix products  104 us (10%)
  starting transfers between devices  95.7 us (10%)
  other arithmetic  73.9 us (7%)
  local copies, waits for them, and re-layouts  72.3 us (7%)
  between operations  33.2 us (3%)
    ppermute x84, waiting for transfers between devices, swap(): lax.ppermute(x, axis, [(i, i ^ step) for i in range(lax.axis_size(axis))])  275 us
    pallas_call x4, Pallas kernels, experts_call(): pl.pallas_call(functools.partial(experts_kernel, counts, len(held) + len(...  171 us
    ppermute x84, starting transfers between devices, swap(): lax.ppermute(x, axis, [(i, i ^ step) for i in range(lax.axis_size(axis))])  86.9 us
    dot_general x4, matrix products, batch_dot(): return jnp.einsum(spec, left, right, preferred_element_type=f32)  53.4 us
    dot_general x9, matrix products, dot(): lax.dot_general(left, right, (((contract[0],), (contract[1],)), ((), ()))...  45.9 us
    ppermute x6, waiting for transfers between devices, ring_send(): lax.ppermute(x, axis, [(order[i], order[(i - k) % n]) for i in range(n)])  41.6 us
    pallas_call x2, Pallas kernels, attention_call(): pl.pallas_call(lambda place, *refs: kernel(place, *refs[:len(operands)],...  29.6 us
    ppermute x3, waiting for transfers between devices, ring_gather(): parts.append(lax.ppermute(parts[-1], axis, ring_pairs(n)))  26.2 us
  transfers between devices with their start and end apart: 99, of which 43 were waited for; matrix products, arithmetic and copies ran while one was open for 22% of the time, Pallas kernels for 24%

profile of v6, /device:TPU:9, one launch (start us, length us, event | category | flops | bytes accessed | tf_op | source)
XLA Modules:
  0.0 983.6 jit_solution(4356368409109249162)
XLA Ops:
  21.6 8.3 collective-permute-done.1
  30.0 18.0 %collective-permute-done.2 = bf16[128,640]{1,0:T(8,128)(2,1)S(1)} collective-permute-done((bf16[128,640]{1,0:T(8,128)(2,1)S(1)}, bf16[128,640]{1,0:T(8,128)(2,1)S(1)}, u32[]{:S(2)}, u32[]{:S(2)}) %collective-permute-start.2) | collective-permute-done | bytes 163872 | tf_op jit(solution)/shard_map/ppermute | solution.py:22
  71.6 26.0 %all-gather.3.cloned.1.call-done.ref = bf16[2560,1536]{1,0:T(8,128)(2,1)} async-done(((bf16[320,1536]{1,0:T(8,128)(2,1)}), bf16[2560,1536]{1,0:T(8,128)(2,1)}) %all-gather.3.cloned.1.call-update) | async-done | bytes 7864336 | tf_op jit(solution)/shard_map/all_gather | solution.py:803
  113.7 9.6 shard_map.289.refs_5_.refs_8_.refs_12_
  134.6 12.8 %shard_map.291 = (bf16[512,640]{1,0:T(8,128)(2,1)}, f32[4,128,640]{2,1,0:T(8,128)}, f32[4,1,640]{2,1,0:T(1,128)}) custom-call(s32[6]{0:T(128)} %pad_add_fusion.place, bf16[512,640]{1,0:T(8,128)(2,1)} %copy.156.refs_0_, bf16[512,256]{1,0:T(8,128)(2,1)} %pad_maximum_fusion.7.refs_1_.refs_4_, bf16[512,256]{1,0:T(8,128)(2,1)} %collective-permute-done.10.refs_2_.refs_1_.refs_5_, ...), custom_call_target="tpu_custom_call" | custom-call | flops 2684354560 | bytes 1024 | tf_op jit(solution)/shard_map/pallas_call | solution.py:493
  167.1 31.7 %collective-permute-done.17 = bf16[512,384]{1,0:T(8,128)(2,1)S(1)} collective-permute-done((bf16[512,384]{1,0:T(8,128)(2,1)S(1)}, bf16[512,384]{1,0:T(8,128)(2,1)S(1)}, u32[]{:S(2)}, u32[]{:S(2)}) %collective-permute-start.17) | collective-permute-done | bytes 393248 | tf_op jit(solution)/shard_map/ppermute | solution.py:22
  202.5 19.0 %collective-permute-done.19 = bf16[512,384]{1,0:T(8,128)(2,1)S(1)} collective-permute-done((bf16[512,384]{1,0:T(8,128)(2,1)S(1)}, bf16[512,384]{1,0:T(8,128)(2,1)S(1)}, u32[]{:S(2)}, u32[]{:S(2)}) %collective-permute-start.19) | collective-permute-done | bytes 393248 | tf_op jit(solution)/shard_map/ppermute | solution.py:22
  233.1 15.0 %collective-permute-done.20 = bf16[128,2688]{1,0:T(8,128)(2,1)} collective-permute-done((bf16[128,2688]{1,0:T(8,128)(2,1)S(1)}, bf16[128,2688]{1,0:T(8,128)(2,1)}, u32[]{:S(2)}, u32[]{:S(2)}) %collective-permute-start.20) | collective-permute-done | bytes 688160 | tf_op jit(solution)/shard_map/ppermute | solution.py:83
  251.2 11.2 %collective-permute-done.21 = bf16[128,2688]{1,0:T(8,128)(2,1)} collective-permute-done((bf16[128,2688]{1,0:T(8,128)(2,1)}, bf16[128,2688]{1,0:T(8,128)(2,1)}, u32[]{:S(2)}, u32[]{:S(2)}) %collective-permute-start.21) | collective-permute-done | bytes 688160 | tf_op jit(solution)/shard_map/ppermute | solution.py:83
  269.8 17.6 %collective-permute-done.35 = s32[6,512]{1,0:T(8,128)S(1)} collective-permute-done((s32[6,512]{1,0:T(8,128)S(1)}, s32[6,512]{1,0:T(8,128)S(1)}, u32[]{:S(2)}, u32[]{:S(2)}) %collective-permute-start.35) | collective-permute-done | bytes 12320 | tf_op jit(solution)/shard_map/ppermute | solution.py:22
  314.9 42.5 %shard_map.297 = (bf16[2,2048,2560]{2,1,0:T(8,128)(2,1)}, bf16[2,2048,2560]{2,1,0:T(8,128)(2,1)}, bf16[2,2048,384]{2,1,0:T(8,128)(2,1)}, bf16[2,2048,768]{2,1,0:...) custom-call(s32[6]{0:T(128)} %get-tuple-element.154.info, ...), custom_call_target="tpu_custom_call" | custom-call | flops 26843545600 | bytes 1024 | tf_op jit(solution)/shard_map/pallas_call | solution.py:731
  380.0 42.8 %shard_map.299 = (bf16[2,2048,2560]{2,1,0:T(8,128)(2,1)}, bf16[2,2048,2560]{2,1,0:T(8,128)(2,1)}, bf16[2,2048,384]{2,1,0:T(8,128)(2,1)}, bf16[2,2048,768]{2,1,0:...) custom-call(s32[6]{0:T(128)} %get-tuple-element.230.info, ...), custom_call_target="tpu_custom_call", output_to_operand_aliasing={{0}: (13, {}), {1}: (14, {}), {2}: (15, {}), {3}: (16, {}),... | custom-call | flops 26843545600 | bytes 1024 | tf_op jit(solution)/shard_map/pallas_call | solution.py:731
  438.2 42.7 %shard_map.301 = (bf16[2,2048,2560]{2,1,0:T(8,128)(2,1)}, bf16[2,2048,2560]{2,1,0:T(8,128)(2,1)}, bf16[2,2048,384]{2,1,0:T(8,128)(2,1)}, bf16[2,2048,768]{2,1,0:...) custom-call(s32[6]{0:T(128)} %get-tuple-element.231.info, ...), custom_call_target="tpu_custom_call", output_to_operand_aliasing={{0}: (13, {}), {1}: (14, {}), {2}: (15, {}), {3}: (16, {}),... | custom-call | flops 26843545600 | bytes 1024 | tf_op jit(solution)/shard_map/pallas_call | solution.py:731
  494.5 43.2 %shard_map.302 = (bf16[2,2048,2560]{2,1,0:T(8,128)(2,1)}, bf16[2,2048,2560]{2,1,0:T(8,128)(2,1)}, bf16[2,2048,384]{2,1,0:T(8,128)(2,1)}, bf16[2,2048,768]{2,1,0:...) custom-call(s32[6]{0:T(128)} %get-tuple-element.232.info, ...), custom_call_target="tpu_custom_call", output_to_operand_aliasing={{0}: (17, {}), {1}: (18, {}), {2}: (19, {}), {3}: (20, {}),... | custom-call | flops 26843545600 | bytes 1024 | tf_op jit(solution)/shard_map/pallas_call | solution.py:731
  537.7 8.4 convolution_convert_fusion.5.refs_1_
  546.1 7.2 convolution_convert_fusion.2.refs_0_
  574.5 12.2 %collective-permute-done.57 = bf16[512,384]{1,0:T(8,128)(2,1)S(1)} collective-permute-done((bf16[512,384]{1,0:T(8,128)(2,1)S(1)}, bf16[512,384]{1,0:T(8,128)(2,1)S(1)}, u32[]{:S(2)}, u32[]{:S(2)}) %collective-permute-start.57) | collective-permute-done | bytes 393248 | tf_op jit(solution)/shard_map/ppermute | solution.py:22
  589.8 17.8 %collective-permute-done.59 = bf16[512,384]{1,0:T(8,128)(2,1)S(1)} collective-permute-done((bf16[512,384]{1,0:T(8,128)(2,1)S(1)}, bf16[512,384]{1,0:T(8,128)(2,1)S(1)}, u32[]{:S(2)}, u32[]{:S(2)}) %collective-permute-start.59) | collective-permute-done | bytes 393248 | tf_op jit(solution)/shard_map/ppermute | solution.py:22
  608.9 11.1 %add_convert_fusion.refs_0_ = bf16[2048,2560]{1,0:T(8,128)(2,1)} fusion(bf16[2048,2560]{1,0:T(8,128)(2,1)S(1)} %collective-permute-done.55, bf16[2048,2560]{1,0:T(8,128)(2,1)} %get-tuple-element.114), kind=kLoop, calls=%fused_computation.2 | loop fusion | flops 20971520 | bytes 31457280 | tf_op jit(solution)/shard_map/convert_element_type | solution.py:938
  620.0 14.5 %collective-permute-done.56.refs_1_ = bf16[512,2688]{1,0:T(8,128)(2,1)S(1)} collective-permute-done((bf16[512,2688]{1,0:T(8,128)(2,1)S(1)}, bf16[512,2688]{1,0:T(8,128)(2,1)S(1)}, u32[]{:S(2)}, u32[]{:S(2)}) %collective-permute-start.56) | collective-permute-done | bytes 2752544 | tf_op jit(solution)/shard_map/ppermute | solution.py:22
  649.0 18.7 %fusion.3 = f32[2,2560,384]{2,1,0:T(8,128)} fusion(bf16[2,2048,2560]{2,1,0:T(8,128)(2,1)} %get-tuple-element.124, bf16[2,2048,768]{2,1,0:T(8,128)(2,1)} %shard_map.307), kind=kOutput, calls=%fused_computation.17 | convolution fusion | flops 8053063680 | bytes 31981568 | tf_op jit(solution)/shard_map/lrd,lrf->ldf/dot_general | solution.py:190
  667.7 18.5 %fusion.5 = f32[2,2560,384]{2,1,0:T(8,128)} fusion(bf16[2,2048,2560]{2,1,0:T(8,128)(2,1)} %get-tuple-element.124, bf16[2,2048,768]{2,1,0:T(8,128)(2,1)} %shard_map.307), kind=kOutput, calls=%fused_computation.19 | convolution fusion | flops 8053063680 | bytes 31981568 | tf_op jit(solution)/shard_map/lrd,lrf->ldf/dot_general | solution.py:190
  686.2 12.4 %fusion.86 = f32[2,384,2560]{2,1,0:T(8,128)S(1)} fusion(bf16[2,2048,384]{2,1,0:T(8,128)(2,1)S(1)} %copy-done.4, bf16[2,2048,2560]{2,1,0:T(8,128)(2,1)} %get-tuple-element.127), kind=kOutput, calls=%fused_computation.276 | convolution fusion | flops 8053063680 | bytes 31981568 | tf_op jit(solution)/shard_map/lrf,lrd->lfd/dot_general | solution.py:190
  714.8 29.1 %collective-permute-done.64 = bf16[128,2560]{1,0:T(8,128)(2,1)S(1)} collective-permute-done((bf16[128,2560]{1,0:T(8,128)(2,1)S(1)}, bf16[128,2560]{1,0:T(8,128)(2,1)S(1)}, u32[]{:S(2)}, u32[]{:S(2)}) %collective-permute-start.64) | collective-permute-done | bytes 655392 | tf_op jit(solution)/shard_map/ppermute | solution.py:22
  745.5 12.7 %collective-permute-done.65 = bf16[64,2560]{1,0:T(8,128)(2,1)S(1)} collective-permute-done((bf16[64,2560]{1,0:T(8,128)(2,1)S(1)}, bf16[64,2560]{1,0:T(8,128)(2,1)S(1)}, u32[]{:S(2)}, u32[]{:S(2)}) %collective-permute-start.65) | collective-permute-done | bytes 327712 | tf_op jit(solution)/shard_map/ppermute | solution.py:22
  773.8 16.8 %shard_map.310 = (f32[512,640]{1,0:T(8,128)}, bf16[4,512,256]{2,1,0:T(8,128)(2,1)}) custom-call(s32[6]{0:T(128)} %pad_add_fusion.place, bf16[512,640]{1,0:T(8,128)(2,1)} %copy.156.refs_0_, bf16[512,640]{1,0:T(8,128)(2,1)} %convolution_convert_fusion.6.refs_1_, f32[4,128,640]{2,1,0:T(8,128)} %get-tuple-element.128.refs_2_, ...), custom_call_target="tpu_custom_call" | custom-call | flops 6710886400 | bytes 1024 | tf_op jit(solution)/shard_map/pallas_call | solution.py:493
  793.7 10.6 %collective-permute-done.67.refs_1_ = bf16[128,2560]{1,0:T(8,128)(2,1)S(1)} collective-permute-done((bf16[128,2560]{1,0:T(8,128)(2,1)}, bf16[128,2560]{1,0:T(8,128)(2,1)S(1)}, u32[]{:S(2)}, u32[]{:S(2)}) %collective-permute-start.67) | collective-permute-done | bytes 655392 | tf_op jit(solution)/shard_map/ppermute | solution.py:90
  815.6 9.6 collective-permute-done.73
  827.4 10.6 %collective-permute-done.75 = bf16[512,256]{1,0:T(8,128)(2,1)} collective-permute-done((bf16[512,256]{1,0:T(8,128)(2,1)S(1)}, bf16[512,256]{1,0:T(8,128)(2,1)}, u32[]{:S(2)}, u32[]{:S(2)}) %collective-permute-start.75) | collective-permute-done | bytes 262176 | tf_op jit(solution)/shard_map/ppermute | solution.py:22
  856.6 23.3 %collective-permute-done.68 = bf16[128,2560]{1,0:T(8,128)(2,1)S(1)} collective-permute-done((bf16[128,2560]{1,0:T(8,128)(2,1)S(1)}, bf16[128,2560]{1,0:T(8,128)(2,1)S(1)}, u32[]{:S(2)}, u32[]{:S(2)}) %collective-permute-start.68) | collective-permute-done | bytes 655392 | tf_op jit(solution)/shard_map/ppermute | solution.py:90
  886.6 7.8 collective-permute-done.69
  938.6 7.7 collective-permute-done.70
  (593 shorter events, 361.1 us)
Async XLA Ops:
  7.2 90.4 %all-gather.3.cloned.1.call-start = ((), (), s32[]{:S(2)}) async-start(), calls=%async_computation.4 | async-start | bytes 8847360 | tf_op jit(solution)/shard_map/all_gather | solution.py:803
  11.6 213.9 %all-gather.5.cloned.1.call-start = ((), (), s32[]{:S(2)}) async-start(), calls=%async_computation.5 | async-start | bytes 3276800 | tf_op jit(solution)/shard_map/all_gather | solution.py:847
  134.3 636.7 %reduce-scatter.5.cloned.1.call-start = ((), (), s32[]{:S(2)}) async-start(), calls=%async_computation.6 | async-start | bytes 13107200 | tf_op jit(solution)/shard_map/reduce_scatter | solution.py:939
  161.1 62.3 %collective-permute-start.14 = (bf16[128,2560]{1,0:T(8,128)(2,1)}, bf16[128,2560]{1,0:T(8,128)(2,1)}, u32[]{:S(2)}, u32[]{:S(2)}) collective-permute-start(bf16[128,2560]{1,0:T(8,128)(2,1)} %pad_maximum_fusion.3), channel_id=1, source_target_pairs={{0,4},{4,0},{8,12},{12,8},{1,5},{5,1},{9,13},{13,9},{2,6},{6,2},{1... | collective-permute-start | bytes 1966088 | tf_op jit(solution)/shard_map/ppermute | solution.py:22
  162.3 61.0 %collective-permute-start.16 = (bf16[128,2560]{1,0:T(8,128)(2,1)S(1)}, bf16[128,2560]{1,0:T(8,128)(2,1)}, u32[]{:S(2)}, u32[]{:S(2)}) collective-permute-start(bf16[128,2560]{1,0:T(8,128)(2,1)S(1)} %pad_maximum_fusion.4), channel_id=1, source_target_pairs={{0,8},{4,12},{8,0},{12,4},{1,9},{5,13},{9,1},{13,5},{2,10},{6,14},... | collective-permute-start | bytes 1966088 | tf_op jit(solution)/shard_map/ppermute | solution.py:22
  164.2 34.6 %collective-permute-start.17 = (bf16[512,384]{1,0:T(8,128)(2,1)S(1)}, bf16[512,384]{1,0:T(8,128)(2,1)S(1)}, u32[]{:S(2)}, u32[]{:S(2)}) collective-permute-start(bf16[512,384]{1,0:T(8,128)(2,1)S(1)} %get-tuple-element.188), channel_id=1, source_target_pairs={{0,1},{1,0},{2,3},{3,2},{4,5},{5,4},{6,7},{7,6},{8,9},{9,8},{10,11... | collective-permute-start | bytes 1179656 | tf_op jit(solution)/shard_map/ppermute | solution.py:22
  164.7 36.0 %collective-permute-start.18 = (bf16[512,384]{1,0:T(8,128)(2,1)S(1)}, bf16[512,384]{1,0:T(8,128)(2,1)S(1)}, u32[]{:S(2)}, u32[]{:S(2)}) collective-permute-start(bf16[512,384]{1,0:T(8,128)(2,1)S(1)} %get-tuple-element.187), channel_id=1, source_target_pairs={{0,2},{1,3},{2,0},{3,1},{4,6},{5,7},{6,4},{7,5},{8,10},{9,11},{10,... | collective-permute-start | bytes 1179656 | tf_op jit(solution)/shard_map/ppermute | solution.py:22
  166.6 54.9 %collective-permute-start.19 = (bf16[512,384]{1,0:T(8,128)(2,1)S(1)}, bf16[512,384]{1,0:T(8,128)(2,1)S(1)}, u32[]{:S(2)}, u32[]{:S(2)}) collective-permute-start(bf16[512,384]{1,0:T(8,128)(2,1)S(1)} %get-tuple-element.186), channel_id=1, source_target_pairs={{0,3},{1,2},{2,1},{3,0},{4,7},{5,6},{6,5},{7,4},{8,11},{9,10},{10,... | collective-permute-start | bytes 1179656 | tf_op jit(solution)/shard_map/ppermute | solution.py:22
  229.6 64.6 %collective-permute-start.23 = (bf16[512,2560]{1,0:T(8,128)(2,1)}, bf16[512,2560]{1,0:T(8,128)(2,1)}, u32[]{:S(2)}, u32[]{:S(2)}) collective-permute-start(bf16[512,2560]{1,0:T(8,128)(2,1)} %all-gather.5.cloned.1.call-done.refs_4_), channel_id=1, source_target_pairs={{0,4},{4,0},{8,12},{12,8},{1,5},{5,1},{9,13},{13,9},{2,6},{6,2},{1... | collective-permute-start | bytes 7864328 | tf_op jit(solution)/shard_map/ppermute | solution.py:22
  230.8 66.8 %collective-permute-start.24 = (bf16[512,2560]{1,0:T(8,128)(2,1)}, bf16[512,2560]{1,0:T(8,128)(2,1)}, u32[]{:S(2)}, u32[]{:S(2)}) collective-permute-start(bf16[512,2560]{1,0:T(8,128)(2,1)} %all-gather.5.cloned.1.call-done.refs_4_), channel_id=1, source_target_pairs={{0,8},{4,12},{8,0},{12,4},{1,9},{5,13},{9,1},{13,5},{2,10},{6,14},... | collective-permute-start | bytes 7864328 | tf_op jit(solution)/shard_map/ppermute | solution.py:22
  262.4 31.7 %collective-permute-start.22 = (bf16[128,2688]{1,0:T(8,128)(2,1)}, bf16[128,2688]{1,0:T(8,128)(2,1)S(1)}, u32[]{:S(2)}, u32[]{:S(2)}) collective-permute-start(bf16[128,2688]{1,0:T(8,128)(2,1)} %collective-permute-done.21), channel_id=1, source_target_pairs={{0,1},{1,3},{3,2},{2,0},{4,5},{5,7},{7,6},{6,4},{8,9},{9,11},{11,1... | collective-permute-start | bytes 2064392 | tf_op jit(solution)/shard_map/ppermute | solution.py:83
  301.5 61.2 %collective-permute-start.25 = (bf16[512,2688]{1,0:T(8,128)(2,1)}, bf16[512,2688]{1,0:T(8,128)(2,1)S(1)}, u32[]{:S(2)}, u32[]{:S(2)}) collective-permute-start(bf16[512,2688]{1,0:T(8,128)(2,1)} %shard_map.295.refs_0_.refs_2_), channel_id=1, source_target_pairs={{0,8},{4,12},{8,0},{12,4},{1,9},{5,13},{9,1},{13,5},{2,10},{6,14},... | collective-permute-start | bytes 8257544 | tf_op jit(solution)/shard_map/ppermute | solution.py:22
  302.7 60.8 %collective-permute-start.27 = (bf16[512,2688]{1,0:T(8,128)(2,1)}, bf16[512,2688]{1,0:T(8,128)(2,1)}, u32[]{:S(2)}, u32[]{:S(2)}) collective-permute-start(bf16[512,2688]{1,0:T(8,128)(2,1)} %shard_map.295.refs_0_.refs_2_), channel_id=1, source_target_pairs={{0,4},{4,0},{8,12},{12,8},{1,5},{5,1},{9,13},{13,9},{2,6},{6,2},{1... | collective-permute-start | bytes 8257544 | tf_op jit(solution)/shard_map/ppermute | solution.py:22
  368.9 53.9 %collective-permute-start.26 = (bf16[256,2688]{1,0:T(8,128)(2,1)S(1)}, bf16[256,2688]{1,0:T(8,128)(2,1)S(1)}, u32[]{:S(2)}, u32[]{:S(2)}) collective-permute-start(bf16[256,2688]{1,0:T(8,128)(2,1)S(1)} %slice.340), channel_id=1, source_target_pairs={{0,4},{4,0},{8,12},{12,8},{1,5},{5,1},{9,13},{13,9},{2,6},{6,2},{1... | collective-permute-start | bytes 4128776 | tf_op jit(solution)/shard_map/ppermute | solution.py:22
  372.5 50.3 %collective-permute-start.28 = (bf16[256,2688]{1,0:T(8,128)(2,1)}, bf16[256,2688]{1,0:T(8,128)(2,1)S(1)}, u32[]{:S(2)}, u32[]{:S(2)}) collective-permute-start(bf16[256,2688]{1,0:T(8,128)(2,1)} %slice.341), channel_id=1, source_target_pairs={{0,8},{4,12},{8,0},{12,4},{1,9},{5,13},{9,1},{13,5},{2,10},{6,14},... | collective-permute-start | bytes 4128776 | tf_op jit(solution)/shard_map/ppermute | solution.py:22
  430.6 51.3 %collective-permute-start.31 = (bf16[256,2560]{1,0:T(8,128)(2,1)}, bf16[256,2560]{1,0:T(8,128)(2,1)S(1)}, u32[]{:S(2)}, u32[]{:S(2)}) collective-permute-start(bf16[256,2560]{1,0:T(8,128)(2,1)} %slice.342), channel_id=1, source_target_pairs={{0,4},{4,0},{8,12},{12,8},{1,5},{5,1},{9,13},{13,9},{2,6},{6,2},{1... | collective-permute-start | bytes 3932168 | tf_op jit(solution)/shard_map/ppermute | solution.py:22
  432.8 50.2 %collective-permute-start.32 = (bf16[256,2560]{1,0:T(8,128)(2,1)S(1)}, bf16[256,2560]{1,0:T(8,128)(2,1)S(1)}, u32[]{:S(2)}, u32[]{:S(2)}) collective-permute-start(bf16[256,2560]{1,0:T(8,128)(2,1)S(1)} %slice.343), channel_id=1, source_target_pairs={{0,8},{4,12},{8,0},{12,4},{1,9},{5,13},{9,1},{13,5},{2,10},{6,14},... | collective-permute-start | bytes 3932168 | tf_op jit(solution)/shard_map/ppermute | solution.py:22
  485.5 72.7 %collective-permute-start.51 = (bf16[512,2688]{1,0:T(8,128)(2,1)}, bf16[512,2688]{1,0:T(8,128)(2,1)}, u32[]{:S(2)}, u32[]{:S(2)}) collective-permute-start(bf16[512,2688]{1,0:T(8,128)(2,1)} %add_convert_fusion.4.refs_22_), channel_id=1, source_target_pairs={{0,4},{4,0},{8,12},{12,8},{1,5},{5,1},{9,13},{13,9},{2,6},{6,2},{1... | collective-permute-start | bytes 8257544 | tf_op jit(solution)/shard_map/ppermute | solution.py:22
  490.2 67.9 %collective-permute-start.52 = (bf16[512,2688]{1,0:T(8,128)(2,1)S(1)}, bf16[512,2688]{1,0:T(8,128)(2,1)}, u32[]{:S(2)}, u32[]{:S(2)}) collective-permute-start(bf16[512,2688]{1,0:T(8,128)(2,1)S(1)} %add_convert_fusion.3.refs_26_), channel_id=1, source_target_pairs={{0,8},{4,12},{8,0},{12,4},{1,9},{5,13},{9,1},{13,5},{2,10},{6,14},... | collective-permute-start | bytes 8257544 | tf_op jit(solution)/shard_map/ppermute | solution.py:22
  569.3 39.6 %collective-permute-start.55 = (bf16[2048,2560]{1,0:T(8,128)(2,1)}, bf16[2048,2560]{1,0:T(8,128)(2,1)S(1)}, u32[]{:S(2)}, u32[]{:S(2)}) collective-permute-start(bf16[2048,2560]{1,0:T(8,128)(2,1)} %shard_map.305), channel_id=1, source_target_pairs={{0,16},{16,0},{1,17},{17,1},{2,18},{18,2},{3,19},{19,3},{4,20},{20... | collective-permute-start | bytes 31457288 | tf_op jit(solution)/shard_map/ppermute | solution.py:22
  572.4 35.1 %collective-permute-start.59 = (bf16[512,384]{1,0:T(8,128)(2,1)S(1)}, bf16[512,384]{1,0:T(8,128)(2,1)S(1)}, u32[]{:S(2)}, u32[]{:S(2)}) collective-permute-start(bf16[512,384]{1,0:T(8,128)(2,1)S(1)} %get-tuple-element.182), channel_id=1, source_target_pairs={{0,3},{1,2},{2,1},{3,0},{4,7},{5,6},{6,5},{7,4},{8,11},{9,10},{10,... | collective-permute-start | bytes 1179656 | tf_op jit(solution)/shard_map/ppermute | solution.py:22
  573.6 60.9 %collective-permute-start.56 = (bf16[512,2688]{1,0:T(8,128)(2,1)S(1)}, bf16[512,2688]{1,0:T(8,128)(2,1)S(1)}, u32[]{:S(2)}, u32[]{:S(2)}) collective-permute-start(bf16[512,2688]{1,0:T(8,128)(2,1)S(1)} %copy-done.23), channel_id=1, source_target_pairs={{0,12},{4,8},{8,4},{12,0},{1,13},{5,9},{9,5},{13,1},{2,14},{6,10},... | collective-permute-start | bytes 8257544 | tf_op jit(solution)/shard_map/ppermute | solution.py:22
  636.0 277.1 %reduce-scatter.11.cloned.1.call-start = ((), (), s32[]{:S(2)}) async-start(), calls=%async_computation.9 | async-start | bytes 3686400 | tf_op jit(solution)/shard_map/reduce_scatter | solution.py:164
  645.6 61.3 %collective-permute-start.60 = (bf16[128,2688]{1,0:T(8,128)(2,1)}, bf16[128,2688]{1,0:T(8,128)(2,1)}, u32[]{:S(2)}, u32[]{:S(2)}) collective-permute-start(bf16[128,2688]{1,0:T(8,128)(2,1)} %get-tuple-element.164), channel_id=1, source_target_pairs={{0,2},{1,0},{3,1},{2,3},{4,6},{5,4},{7,5},{6,7},{8,10},{9,8},{11,9... | collective-permute-start | bytes 2064392 | tf_op jit(solution)/shard_map/ppermute | solution.py:90
  646.7 60.2 %collective-permute-start.61 = (bf16[128,2688]{1,0:T(8,128)(2,1)}, bf16[128,2688]{1,0:T(8,128)(2,1)}, u32[]{:S(2)}, u32[]{:S(2)}) collective-permute-start(bf16[128,2688]{1,0:T(8,128)(2,1)} %get-tuple-element.166), channel_id=1, source_target_pairs={{0,3},{1,2},{3,0},{2,1},{4,7},{5,6},{7,4},{6,5},{8,11},{9,10},{11,... | collective-permute-start | bytes 2064392 | tf_op jit(solution)/shard_map/ppermute | solution.py:90
  647.0 60.0 %collective-permute-start.62 = (bf16[128,2688]{1,0:T(8,128)(2,1)}, bf16[128,2688]{1,0:T(8,128)(2,1)}, u32[]{:S(2)}, u32[]{:S(2)}) collective-permute-start(bf16[128,2688]{1,0:T(8,128)(2,1)} %get-tuple-element.165), channel_id=1, source_target_pairs={{0,1},{1,3},{3,2},{2,0},{4,5},{5,7},{7,6},{6,4},{8,9},{9,11},{11,1... | collective-permute-start | bytes 2064392 | tf_op jit(solution)/shard_map/ppermute | solution.py:90
  762.1 168.1 %reduce-scatter.7.cloned.1.call-start = ((), (), s32[]{:S(2)}) async-start(), calls=%async_computation.7 | async-start | bytes 3686400 | tf_op jit(solution)/shard_map/reduce_scatter | solution.py:164
  773.0 31.3 %collective-permute-start.67 = (bf16[128,2560]{1,0:T(8,128)(2,1)}, bf16[128,2560]{1,0:T(8,128)(2,1)S(1)}, u32[]{:S(2)}, u32[]{:S(2)}) collective-permute-start(bf16[128,2560]{1,0:T(8,128)(2,1)} %split.54), channel_id=1, source_target_pairs={{0,2},{1,0},{3,1},{2,3},{4,6},{5,4},{7,5},{6,7},{8,10},{9,8},{11,9... | collective-permute-start | bytes 1966088 | tf_op jit(solution)/shard_map/ppermute | solution.py:90
  815.6 158.4 %reduce-scatter.9.cloned.1.call-start = ((), (), s32[]{:S(2)}) async-start(), calls=%async_computation.8 | async-start | bytes 1474560 | tf_op jit(solution)/shard_map/reduce_scatter | solution.py:164
  855.4 44.0 %collective-permute-start.77 = (bf16[128,2560]{1,0:T(8,128)(2,1)}, bf16[128,2560]{1,0:T(8,128)(2,1)}, u32[]{:S(2)}, u32[]{:S(2)}) collective-permute-start(bf16[128,2560]{1,0:T(8,128)(2,1)} %pad_maximum_fusion.5), channel_id=1, source_target_pairs={{0,4},{4,0},{8,12},{12,8},{1,5},{5,1},{9,13},{13,9},{2,6},{6,2},{1... | collective-permute-start | bytes 1966088 | tf_op jit(solution)/shard_map/ppermute | solution.py:22
  902.4 64.2 %collective-permute-start.92 = (bf16[4,512,384]{2,1,0:T(8,128)(2,1)}, bf16[4,512,384]{2,1,0:T(8,128)(2,1)}, u32[]{:S(2)}, u32[]{:S(2)}) collective-permute-start(bf16[4,512,384]{2,1,0:T(8,128)(2,1)} %shard_map.317.refs_0_), channel_id=1, source_target_pairs={{0,16},{16,0},{1,17},{17,1},{2,18},{18,2},{3,19},{19,3},{4,20},{20... | collective-permute-start | bytes 4718600 | tf_op jit(solution)/shard_map/ppermute | solution.py:22
  913.2 47.9 %collective-permute-start.85 = (bf16[320,640]{1,0:T(8,128)(2,1)}, bf16[320,640]{1,0:T(8,128)(2,1)S(1)}, u32[]{:S(2)}, u32[]{:S(2)}) collective-permute-start(bf16[320,640]{1,0:T(8,128)(2,1)} %shard_map.316), channel_id=1, source_target_pairs={{0,16},{16,0},{1,17},{17,1},{2,18},{18,2},{3,19},{19,3},{4,20},{20... | collective-permute-start | bytes 1228808 | tf_op jit(solution)/shard_map/ppermute | solution.py:22
  (161 other events, 2563.0 us)
Sparse Core Ops, SparseCore 0:
  11.7 85.8 all-gather.2
  134.4 72.0 all-gather.4
  636.2 121.5 reduce-scatter.4
  762.2 58.3 reduce-scatter.10
  822.9 61.6 reduce-scatter.6
  930.3 38.7 reduce-scatter.8

commit v7 on v6

--- a/solution.py
+++ b/solution.py
@@ -35,6 +35,9 @@
 
 def all_sum(x, axis):
     step = 1
+    if lax.axis_size(axis) == 4:
+        own, near, other, far = exchange(x, axis)
+        return (own + near) + (other + far)
     while step < lax.axis_size(axis):
         x = x + swap(x, axis, step)
         step *= 2
@@ -884,7 +887,8 @@
     )
     payload = jnp.concatenate(ring_gather(payload, "col"), axis=0)
     grad_rows = row_gather(g_block)
-    payload = after(payload, *grad_rows[1:3])
+    grad_own = exchange(g_block, "exp")
+    payload = after(payload, *grad_rows[1:3], *grad_own[1:], sh_in)
     payload_rows = row_gather(payload)
     if R == 4:
         grad_rows = grad_rows[:3] + [jnp.concatenate(grad_rows[3:], axis=0)]
@@ -909,7 +913,7 @@
         ).astype(jnp.int32)
         kept, norm = experts_call(
             s, R, kept, list(zip(*(exchange(x, "exp") for x in x_block))),
-            exchange(grad_rows[s], "exp"), info,
+            exchange(grad_rows[s], "exp") if s else grad_own, info,
             slots[s], expert_in, expert_down, sh_in, sh_down, capacity, norms[-1:],
         )
         if s == R - 1:
@@ -971,12 +975,14 @@
     )
     d_kv_parts = after(d_kv_parts, moe_out)
     d_kv = reduce_parts([d_kv_parts[k] for k in range(C)], "col")
-    for k in range(C - 2, 0, -1):
+    moe_out = ring_send(add(out_chunks[C - 2], moe_out).astype(bf16), "col", 1)
+    ring_here = zero_of(moe_out)
+    for k in range(C - 3, 0, -1):
         moe_out = ring_send(add(out_chunks[k], moe_out).astype(bf16), "col", 1)
     moe_out = add(out_chunks[0], moe_out)
     d_query_raw = rotate(
         d_queries.reshape(own_rows, group_heads, head_width), cosines, -sines
-    ) * attn_scale
+    ) * (attn_scale + ring_here.astype(f32))
     d_query_raw = d_query_raw.reshape(own_rows, query_width).astype(bf16)
     norm_one_late = after(norm_one_all, d_kv_parts)
     query_grads = dot(norm_one_late, d_query_raw, (0, 0)).astype(bf16)
@@ -986,15 +992,17 @@
     ).astype(bf16)
     norm_one_part = dot(jnp.concatenate([d_kv_raw, d_query_raw], axis=1), weight_in, (1, 1)).astype(bf16)
     d_norm_one, halfway = row_reduce(jnp.split(norm_one_part, R, axis=0))
-    d_x, gain_one_part = rms_backward(
-        x, inv_one, gain_one + zero_of(moe_out).astype(f32), d_norm_one
-    )
+    grad_shared_gate, grad_shared_up, grad_shared_down = join_shared_grads(
+        here, exchange(after(shared_back, d_kv), "exp"), in_rows, feature_width
+    )
+    late = zero_of(moe_out, grad_shared_gate).astype(f32)
+    d_x, gain_one_part = rms_backward(x, inv_one, gain_one + late, d_norm_one)
     grad_inputs, back = tokens_back((d_hidden + d_x).astype(bf16))
 
     output = tokens_back((hidden_state + moe_out).astype(bf16))[0]
     out_total, query_total = reduce_weight(out_grads), reduce_weight(query_grads)
     kv_grads = dot(after(norm_one_late, *halfway), d_kv_raw, (0, 0)).astype(bf16)
-    kv_total = reduce_weight(after(kv_grads, query_total, d_norm_one))
+    kv_total = reduce_weight(after(kv_grads, query_total, moe_out))
     grad_output = all_shares(after(out_total, d_norm_one)).astype(f32)
     grad_query = all_shares(after(query_total, d_norm_one)).astype(f32)
     grad_kv = all_shares(kv_total).astype(f32)
@@ -1006,9 +1014,6 @@
     ]
     small_sum = all_sum(all_sum(reduce_parts(mine, "col"), "row"), "exp")
 
-    grad_shared_gate, grad_shared_up, grad_shared_down = join_shared_grads(
-        here, exchange(after(shared_back, d_norm_one), "exp"), in_rows, feature_width
-    )
     return (
         output,
         grad_inputs,

time: 991 us -> 1020 us (1.029)
  waiting for transfers between devices: 369 us -> 388 us
    ppermute x84 -> x85, waiting for transfers between devices: 275 us -> 293 us  [swap(): lax.ppermute(x, axis, [(i, i ^ step) for i in range(lax.axis_size(axis))])]
    ppermute x84 -> x85, starting transfers between devices: 86.9 us -> 84.4 us  [swap(): lax.ppermute(x, axis, [(i, i ^ step) for i in range(lax.axis_size(axis))])]
    unnamed x203 -> x199, local copies, waits for them, and re-layouts: 23.4 us -> 24.4 us
  transfers between devices with their start and end apart: 99 -> 100, of which waited for: 43 -> 51; matrix products, arithmetic and copies ran while one was open for 22% -> 21% of each run, Pallas kernels for 24% -> 23%
where the time goes in v7:
time: 1020 us; the launch traced here: 1000 us
  waiting for transfers between devices  388 us (38%)
  Pallas kernels  236 us (23%)
  matrix products  103 us (10%)
  starting transfers between devices  94 us (9%)
  other arithmetic  75.7 us (7%)
  local copies, waits for them, and re-layouts  73.5 us (7%)
  between operations  35.8 us (4%)
    ppermute x85, waiting for transfers between devices, swap(): lax.ppermute(x, axis, [(i, i ^ step) for i in range(lax.axis_size(axis))])  293 us
    pallas_call x4, Pallas kernels, experts_call(): pl.pallas_call(functools.partial(experts_kernel, counts, len(held) + len(...  171 us
    ppermute x85, starting transfers between devices, swap(): lax.ppermute(x, axis, [(i, i ^ step) for i in range(lax.axis_size(axis))])  84.4 us
    dot_general x4, matrix products, batch_dot(): return jnp.einsum(spec, left, right, preferred_element_type=f32)  53.5 us
    dot_general x9, matrix products, dot(): lax.dot_general(left, right, (((contract[0],), (contract[1],)), ((), ()))...  45.8 us
    ppermute x6, waiting for transfers between devices, ring_send(): lax.ppermute(x, axis, [(order[i], order[(i - k) % n]) for i in range(n)])  34.6 us
    pallas_call x2, Pallas kernels, attention_call(): pl.pallas_call(lambda place, *refs: kernel(place, *refs[:len(operands)],...  29.2 us
    ppermute x3, waiting for transfers between devices, ring_gather(): parts.append(lax.ppermute(parts[-1], axis, ring_pairs(n)))  28.8 us
  transfers between devices with their start and end apart: 100, of which 51 were waited for; matrix products, arithmetic and copies ran while one was open for 21% of the time, Pallas kernels for 23%

profile of v7, /device:TPU:9, one launch (start us, length us, event | category | flops | bytes accessed | tf_op | source)
XLA Modules:
  0.0 1004.9 jit_solution(15129113599836697268)
XLA Ops:
  21.6 8.3 collective-permute-done.1
  30.0 18.0 %collective-permute-done.2 = bf16[128,640]{1,0:T(8,128)(2,1)S(1)} collective-permute-done((bf16[128,640]{1,0:T(8,128)(2,1)S(1)}, bf16[128,640]{1,0:T(8,128)(2,1)S(1)}, u32[]{:S(2)}, u32[]{:S(2)}) %collective-permute-start.2) | collective-permute-done | bytes 163872 | tf_op jit(solution)/shard_map/ppermute | solution.py:22
  54.2 6.7 collective-permute-done.7
  71.6 26.0 %all-gather.3.cloned.1.call-done.ref = bf16[2560,1536]{1,0:T(8,128)(2,1)} async-done(((bf16[320,1536]{1,0:T(8,128)(2,1)}), bf16[2560,1536]{1,0:T(8,128)(2,1)}) %all-gather.3.cloned.1.call-update) | async-done | bytes 7864336 | tf_op jit(solution)/shard_map/all_gather | solution.py:806
  112.8 9.6 shard_map.289.refs_5_.refs_8_.refs_12_
  134.5 12.8 %shard_map.291 = (bf16[512,640]{1,0:T(8,128)(2,1)}, f32[4,128,640]{2,1,0:T(8,128)}, f32[4,1,640]{2,1,0:T(1,128)}) custom-call(s32[6]{0:T(128)} %pad_add_fusion.place, bf16[512,640]{1,0:T(8,128)(2,1)} %copy.156.refs_0_, bf16[512,256]{1,0:T(8,128)(2,1)} %pad_maximum_fusion.7.refs_1_.refs_4_, bf16[512,256]{1,0:T(8,128)(2,1)} %collective-permute-done.10.refs_2_.refs_1_.refs_5_, ...), custom_call_target="tpu_custom_call" | custom-call | flops 2684354560 | bytes 1024 | tf_op jit(solution)/shard_map/pallas_call | solution.py:496
  166.9 30.8 %collective-permute-done.17 = bf16[512,384]{1,0:T(8,128)(2,1)S(1)} collective-permute-done((bf16[512,384]{1,0:T(8,128)(2,1)S(1)}, bf16[512,384]{1,0:T(8,128)(2,1)S(1)}, u32[]{:S(2)}, u32[]{:S(2)}) %collective-permute-start.17) | collective-permute-done | bytes 393248 | tf_op jit(solution)/shard_map/ppermute | solution.py:22
  202.3 19.0 %collective-permute-done.19 = bf16[512,384]{1,0:T(8,128)(2,1)S(1)} collective-permute-done((bf16[512,384]{1,0:T(8,128)(2,1)S(1)}, bf16[512,384]{1,0:T(8,128)(2,1)S(1)}, u32[]{:S(2)}, u32[]{:S(2)}) %collective-permute-start.19) | collective-permute-done | bytes 393248 | tf_op jit(solution)/shard_map/ppermute | solution.py:22
  237.7 14.6 %collective-permute-done.20 = bf16[128,2688]{1,0:T(8,128)(2,1)} collective-permute-done((bf16[128,2688]{1,0:T(8,128)(2,1)}, bf16[128,2688]{1,0:T(8,128)(2,1)}, u32[]{:S(2)}, u32[]{:S(2)}) %collective-permute-start.20) | collective-permute-done | bytes 688160 | tf_op jit(solution)/shard_map/ppermute | solution.py:86
  254.7 14.1 %collective-permute-done.21 = bf16[128,2688]{1,0:T(8,128)(2,1)} collective-permute-done((bf16[128,2688]{1,0:T(8,128)(2,1)}, bf16[128,2688]{1,0:T(8,128)(2,1)}, u32[]{:S(2)}, u32[]{:S(2)}) %collective-permute-start.21) | collective-permute-done | bytes 688160 | tf_op jit(solution)/shard_map/ppermute | solution.py:86
  281.2 6.2 collective-permute-done.37
  303.7 42.6 %shard_map.297 = (bf16[2,2048,2560]{2,1,0:T(8,128)(2,1)}, bf16[2,2048,2560]{2,1,0:T(8,128)(2,1)}, bf16[2,2048,384]{2,1,0:T(8,128)(2,1)}, bf16[2,2048,768]{2,1,0:...) custom-call(s32[6]{0:T(128)} %get-tuple-element.154.info, ...), custom_call_target="tpu_custom_call" | custom-call | flops 26843545600 | bytes 1024 | tf_op jit(solution)/shard_map/pallas_call | solution.py:734
  346.2 14.3 %collective-permute-done.27.refs_2_.refs_0_ = bf16[512,2688]{1,0:T(8,128)(2,1)S(1)} collective-permute-done((bf16[512,2688]{1,0:T(8,128)(2,1)}, bf16[512,2688]{1,0:T(8,128)(2,1)S(1)}, u32[]{:S(2)}, u32[]{:S(2)}) %collective-permute-start.27) | collective-permute-done | bytes 2752544 | tf_op jit(solution)/shard_map/ppermute | solution.py:22
  377.7 43.0 %shard_map.299 = (bf16[2,2048,2560]{2,1,0:T(8,128)(2,1)}, bf16[2,2048,2560]{2,1,0:T(8,128)(2,1)}, bf16[2,2048,384]{2,1,0:T(8,128)(2,1)}, bf16[2,2048,768]{2,1,0:...) custom-call(s32[6]{0:T(128)} %get-tuple-element.230.info, ...), custom_call_target="tpu_custom_call", output_to_operand_aliasing={{0}: (13, {}), {1}: (14, {}), {2}: (15, {}), {3}: (16, {}),... | custom-call | flops 26843545600 | bytes 1024 | tf_op jit(solution)/shard_map/pallas_call | solution.py:734
  435.8 42.7 %shard_map.301 = (bf16[2,2048,2560]{2,1,0:T(8,128)(2,1)}, bf16[2,2048,2560]{2,1,0:T(8,128)(2,1)}, bf16[2,2048,384]{2,1,0:T(8,128)(2,1)}, bf16[2,2048,768]{2,1,0:...) custom-call(s32[6]{0:T(128)} %get-tuple-element.231.info, ...), custom_call_target="tpu_custom_call", output_to_operand_aliasing={{0}: (13, {}), {1}: (14, {}), {2}: (15, {}), {3}: (16, {}),... | custom-call | flops 26843545600 | bytes 1024 | tf_op jit(solution)/shard_map/pallas_call | solution.py:734
  491.9 43.1 %shard_map.302 = (bf16[2,2048,2560]{2,1,0:T(8,128)(2,1)}, bf16[2,2048,2560]{2,1,0:T(8,128)(2,1)}, bf16[2,2048,384]{2,1,0:T(8,128)(2,1)}, bf16[2,2048,768]{2,1,0:...) custom-call(s32[6]{0:T(128)} %get-tuple-element.232.info, ...), custom_call_target="tpu_custom_call", output_to_operand_aliasing={{0}: (17, {}), {1}: (18, {}), {2}: (19, {}), {3}: (20, {}),... | custom-call | flops 26843545600 | bytes 1024 | tf_op jit(solution)/shard_map/pallas_call | solution.py:734
  535.1 8.4 convolution_convert_fusion.5.refs_1_
  543.5 7.2 convolution_convert_fusion.2.refs_0_
  572.1 11.7 %collective-permute-done.57 = bf16[512,384]{1,0:T(8,128)(2,1)S(1)} collective-permute-done((bf16[512,384]{1,0:T(8,128)(2,1)S(1)}, bf16[512,384]{1,0:T(8,128)(2,1)S(1)}, u32[]{:S(2)}, u32[]{:S(2)}) %collective-permute-start.57) | collective-permute-done | bytes 393248 | tf_op jit(solution)/shard_map/ppermute | solution.py:22
  586.9 18.1 %collective-permute-done.59 = bf16[512,384]{1,0:T(8,128)(2,1)S(1)} collective-permute-done((bf16[512,384]{1,0:T(8,128)(2,1)S(1)}, bf16[512,384]{1,0:T(8,128)(2,1)S(1)}, u32[]{:S(2)}, u32[]{:S(2)}) %collective-permute-start.59) | collective-permute-done | bytes 393248 | tf_op jit(solution)/shard_map/ppermute | solution.py:22
  606.4 11.0 %add_convert_fusion.refs_0_ = bf16[2048,2560]{1,0:T(8,128)(2,1)} fusion(bf16[2048,2560]{1,0:T(8,128)(2,1)S(1)} %collective-permute-done.55, bf16[2048,2560]{1,0:T(8,128)(2,1)} %get-tuple-element.114), kind=kLoop, calls=%fused_computation.2 | loop fusion | flops 20971520 | bytes 31457280 | tf_op jit(solution)/shard_map/convert_element_type | solution.py:942
  617.3 14.6 %collective-permute-done.56.refs_1_ = bf16[512,2688]{1,0:T(8,128)(2,1)S(1)} collective-permute-done((bf16[512,2688]{1,0:T(8,128)(2,1)S(1)}, bf16[512,2688]{1,0:T(8,128)(2,1)S(1)}, u32[]{:S(2)}, u32[]{:S(2)}) %collective-permute-start.56) | collective-permute-done | bytes 2752544 | tf_op jit(solution)/shard_map/ppermute | solution.py:22
  646.2 18.6 %fusion.3 = f32[2,2560,384]{2,1,0:T(8,128)} fusion(bf16[2,2048,2560]{2,1,0:T(8,128)(2,1)} %get-tuple-element.124, bf16[2,2048,768]{2,1,0:T(8,128)(2,1)} %shard_map.307), kind=kOutput, calls=%fused_computation.17 | convolution fusion | flops 8053063680 | bytes 31981568 | tf_op jit(solution)/shard_map/lrd,lrf->ldf/dot_general | solution.py:193
  664.8 18.6 %fusion.5 = f32[2,2560,384]{2,1,0:T(8,128)} fusion(bf16[2,2048,2560]{2,1,0:T(8,128)(2,1)} %get-tuple-element.124, bf16[2,2048,768]{2,1,0:T(8,128)(2,1)} %shard_map.307), kind=kOutput, calls=%fused_computation.19 | convolution fusion | flops 8053063680 | bytes 31981568 | tf_op jit(solution)/shard_map/lrd,lrf->ldf/dot_general | solution.py:193
  683.4 12.5 %fusion.86 = f32[2,384,2560]{2,1,0:T(8,128)S(1)} fusion(bf16[2,2048,384]{2,1,0:T(8,128)(2,1)S(1)} %copy-done.4, bf16[2,2048,2560]{2,1,0:T(8,128)(2,1)} %get-tuple-element.127), kind=kOutput, calls=%fused_computation.277 | convolution fusion | flops 8053063680 | bytes 31981568 | tf_op jit(solution)/shard_map/lrf,lrd->lfd/dot_general | solution.py:193
  712.2 28.2 %collective-permute-done.64 = bf16[128,2560]{1,0:T(8,128)(2,1)S(1)} collective-permute-done((bf16[128,2560]{1,0:T(8,128)(2,1)S(1)}, bf16[128,2560]{1,0:T(8,128)(2,1)S(1)}, u32[]{:S(2)}, u32[]{:S(2)}) %collective-permute-start.64) | collective-permute-done | bytes 655392 | tf_op jit(solution)/shard_map/ppermute | solution.py:22
  742.2 13.5 %collective-permute-done.65 = bf16[64,2560]{1,0:T(8,128)(2,1)S(1)} collective-permute-done((bf16[64,2560]{1,0:T(8,128)(2,1)S(1)}, bf16[64,2560]{1,0:T(8,128)(2,1)S(1)}, u32[]{:S(2)}, u32[]{:S(2)}) %collective-permute-start.65) | collective-permute-done | bytes 327712 | tf_op jit(solution)/shard_map/ppermute | solution.py:22
  770.4 16.4 %shard_map.310 = (f32[512,640]{1,0:T(8,128)}, bf16[4,512,256]{2,1,0:T(8,128)(2,1)}) custom-call(s32[6]{0:T(128)} %pad_add_fusion.place, bf16[512,640]{1,0:T(8,128)(2,1)} %copy.156.refs_0_, bf16[512,640]{1,0:T(8,128)(2,1)} %convolution_convert_fusion.6.refs_1_, f32[4,128,640]{2,1,0:T(8,128)} %get-tuple-element.128.refs_2_, ...), custom_call_target="tpu_custom_call" | custom-call | flops 6710886400 | bytes 1024 | tf_op jit(solution)/shard_map/pallas_call | solution.py:496
  789.7 11.2 %collective-permute-done.67.refs_1_ = bf16[128,2560]{1,0:T(8,128)(2,1)} collective-permute-done((bf16[128,2560]{1,0:T(8,128)(2,1)}, bf16[128,2560]{1,0:T(8,128)(2,1)}, u32[]{:S(2)}, u32[]{:S(2)}) %collective-permute-start.67) | collective-permute-done | bytes 655392 | tf_op jit(solution)/shard_map/ppermute | solution.py:93
  808.9 12.7 %collective-permute-done.73 = bf16[512,256]{1,0:T(8,128)(2,1)S(1)} collective-permute-done((bf16[512,256]{1,0:T(8,128)(2,1)S(1)}, bf16[512,256]{1,0:T(8,128)(2,1)S(1)}, u32[]{:S(2)}, u32[]{:S(2)}) %collective-permute-start.73) | collective-permute-done | bytes 262176 | tf_op jit(solution)/shard_map/ppermute | solution.py:22
  824.9 24.6 %collective-permute-done.75 = bf16[512,256]{1,0:T(8,128)(2,1)S(1)} collective-permute-done((bf16[512,256]{1,0:T(8,128)(2,1)S(1)}, bf16[512,256]{1,0:T(8,128)(2,1)S(1)}, u32[]{:S(2)}, u32[]{:S(2)}) %collective-permute-start.75) | collective-permute-done | bytes 262176 | tf_op jit(solution)/shard_map/ppermute | solution.py:22
  885.4 23.4 %collective-permute-done.69 = bf16[128,2560]{1,0:T(8,128)(2,1)S(1)} collective-permute-done((bf16[128,2560]{1,0:T(8,128)(2,1)}, bf16[128,2560]{1,0:T(8,128)(2,1)S(1)}, u32[]{:S(2)}, u32[]{:S(2)}) %collective-permute-start.69) | collective-permute-done | bytes 655392 | tf_op jit(solution)/shard_map/ppermute | solution.py:93
  (592 shorter events, 366.5 us)
Async XLA Ops:
  7.2 90.4 %all-gather.3.cloned.1.call-start = ((), (), s32[]{:S(2)}) async-start(), calls=%async_computation.4 | async-start | bytes 8847360 | tf_op jit(solution)/shard_map/all_gather | solution.py:806
  11.6 213.4 %all-gather.5.cloned.1.call-start = ((), (), s32[]{:S(2)}) async-start(), calls=%async_computation.5 | async-start | bytes 3276800 | tf_op jit(solution)/shard_map/all_gather | solution.py:850
  134.3 633.3 %reduce-scatter.5.cloned.1.call-start = ((), (), s32[]{:S(2)}) async-start(), calls=%async_computation.6 | async-start | bytes 13107200 | tf_op jit(solution)/shard_map/reduce_scatter | solution.py:943
  160.1 63.0 %collective-permute-start.14 = (bf16[128,2560]{1,0:T(8,128)(2,1)S(1)}, bf16[128,2560]{1,0:T(8,128)(2,1)S(1)}, u32[]{:S(2)}, u32[]{:S(2)}) collective-permute-start(bf16[128,2560]{1,0:T(8,128)(2,1)S(1)} %pad_maximum_fusion.3), channel_id=1, source_target_pairs={{0,4},{4,0},{8,12},{12,8},{1,5},{5,1},{9,13},{13,9},{2,6},{6,2},{1... | collective-permute-start | bytes 1966088 | tf_op jit(solution)/shard_map/ppermute | solution.py:22
  161.4 61.7 %collective-permute-start.16 = (bf16[128,2560]{1,0:T(8,128)(2,1)S(1)}, bf16[128,2560]{1,0:T(8,128)(2,1)}, u32[]{:S(2)}, u32[]{:S(2)}) collective-permute-start(bf16[128,2560]{1,0:T(8,128)(2,1)S(1)} %pad_maximum_fusion.4), channel_id=1, source_target_pairs={{0,8},{4,12},{8,0},{12,4},{1,9},{5,13},{9,1},{13,5},{2,10},{6,14},... | collective-permute-start | bytes 1966088 | tf_op jit(solution)/shard_map/ppermute | solution.py:22
  166.5 54.8 %collective-permute-start.19 = (bf16[512,384]{1,0:T(8,128)(2,1)S(1)}, bf16[512,384]{1,0:T(8,128)(2,1)S(1)}, u32[]{:S(2)}, u32[]{:S(2)}) collective-permute-start(bf16[512,384]{1,0:T(8,128)(2,1)S(1)} %get-tuple-element.186), channel_id=1, source_target_pairs={{0,3},{1,2},{2,1},{3,0},{4,7},{5,6},{6,5},{7,4},{8,11},{9,10},{10,... | collective-permute-start | bytes 1179656 | tf_op jit(solution)/shard_map/ppermute | solution.py:22
  229.6 66.1 %collective-permute-start.23 = (bf16[512,2560]{1,0:T(8,128)(2,1)}, bf16[512,2560]{1,0:T(8,128)(2,1)}, u32[]{:S(2)}, u32[]{:S(2)}) collective-permute-start(bf16[512,2560]{1,0:T(8,128)(2,1)} %all-gather.5.cloned.1.call-done.refs_4_), channel_id=1, source_target_pairs={{0,4},{4,0},{8,12},{12,8},{1,5},{5,1},{9,13},{13,9},{2,6},{6,2},{1... | collective-permute-start | bytes 7864328 | tf_op jit(solution)/shard_map/ppermute | solution.py:22
  230.6 65.4 %collective-permute-start.24 = (bf16[512,2560]{1,0:T(8,128)(2,1)}, bf16[512,2560]{1,0:T(8,128)(2,1)S(1)}, u32[]{:S(2)}, u32[]{:S(2)}) collective-permute-start(bf16[512,2560]{1,0:T(8,128)(2,1)} %all-gather.5.cloned.1.call-done.refs_4_), channel_id=1, source_target_pairs={{0,8},{4,12},{8,0},{12,4},{1,9},{5,13},{9,1},{13,5},{2,10},{6,14},... | collective-permute-start | bytes 7864328 | tf_op jit(solution)/shard_map/ppermute | solution.py:22
  231.8 64.4 %collective-permute-start.25 = (bf16[512,2560]{1,0:T(8,128)(2,1)}, bf16[512,2560]{1,0:T(8,128)(2,1)}, u32[]{:S(2)}, u32[]{:S(2)}) collective-permute-start(bf16[512,2560]{1,0:T(8,128)(2,1)} %all-gather.5.cloned.1.call-done.refs_4_), channel_id=1, source_target_pairs={{0,16},{16,0},{1,17},{17,1},{2,18},{18,2},{3,19},{19,3},{4,20},{20... | collective-permute-start | bytes 7864328 | tf_op jit(solution)/shard_map/ppermute | solution.py:22
  237.7 37.1 %collective-permute-start.26 = (bf16[4,512,384]{2,1,0:T(8,128)(2,1)}, bf16[4,512,384]{2,1,0:T(8,128)(2,1)}, u32[]{:S(2)}, u32[]{:S(2)}) collective-permute-start(bf16[4,512,384]{2,1,0:T(8,128)(2,1)} %pad_maximum_fusion.1.refs_0_), channel_id=1, source_target_pairs={{0,16},{16,0},{1,17},{17,1},{2,18},{18,2},{3,19},{19,3},{4,20},{20... | collective-permute-start | bytes 4718600 | tf_op jit(solution)/shard_map/ppermute | solution.py:22
  299.2 61.3 %collective-permute-start.27 = (bf16[512,2688]{1,0:T(8,128)(2,1)}, bf16[512,2688]{1,0:T(8,128)(2,1)S(1)}, u32[]{:S(2)}, u32[]{:S(2)}) collective-permute-start(bf16[512,2688]{1,0:T(8,128)(2,1)} %shard_map.296.refs_0_.refs_2_), channel_id=1, source_target_pairs={{0,8},{4,12},{8,0},{12,4},{1,9},{5,13},{9,1},{13,5},{2,10},{6,14},... | collective-permute-start | bytes 8257544 | tf_op jit(solution)/shard_map/ppermute | solution.py:22
  300.3 60.8 %collective-permute-start.29 = (bf16[512,2688]{1,0:T(8,128)(2,1)}, bf16[512,2688]{1,0:T(8,128)(2,1)}, u32[]{:S(2)}, u32[]{:S(2)}) collective-permute-start(bf16[512,2688]{1,0:T(8,128)(2,1)} %shard_map.296.refs_0_.refs_2_), channel_id=1, source_target_pairs={{0,4},{4,0},{8,12},{12,8},{1,5},{5,1},{9,13},{13,9},{2,6},{6,2},{1... | collective-permute-start | bytes 8257544 | tf_op jit(solution)/shard_map/ppermute | solution.py:22
  366.6 54.1 %collective-permute-start.28 = (bf16[256,2688]{1,0:T(8,128)(2,1)S(1)}, bf16[256,2688]{1,0:T(8,128)(2,1)S(1)}, u32[]{:S(2)}, u32[]{:S(2)}) collective-permute-start(bf16[256,2688]{1,0:T(8,128)(2,1)S(1)} %slice.349), channel_id=1, source_target_pairs={{0,4},{4,0},{8,12},{12,8},{1,5},{5,1},{9,13},{13,9},{2,6},{6,2},{1... | collective-permute-start | bytes 4128776 | tf_op jit(solution)/shard_map/ppermute | solution.py:22
  370.1 50.7 %collective-permute-start.30 = (bf16[256,2688]{1,0:T(8,128)(2,1)}, bf16[256,2688]{1,0:T(8,128)(2,1)S(1)}, u32[]{:S(2)}, u32[]{:S(2)}) collective-permute-start(bf16[256,2688]{1,0:T(8,128)(2,1)} %slice.350), channel_id=1, source_target_pairs={{0,8},{4,12},{8,0},{12,4},{1,9},{5,13},{9,1},{13,5},{2,10},{6,14},... | collective-permute-start | bytes 4128776 | tf_op jit(solution)/shard_map/ppermute | solution.py:22
  428.5 50.8 %collective-permute-start.33 = (bf16[256,2560]{1,0:T(8,128)(2,1)}, bf16[256,2560]{1,0:T(8,128)(2,1)S(1)}, u32[]{:S(2)}, u32[]{:S(2)}) collective-permute-start(bf16[256,2560]{1,0:T(8,128)(2,1)} %slice.351), channel_id=1, source_target_pairs={{0,4},{4,0},{8,12},{12,8},{1,5},{5,1},{9,13},{13,9},{2,6},{6,2},{1... | collective-permute-start | bytes 3932168 | tf_op jit(solution)/shard_map/ppermute | solution.py:22
  430.7 49.7 %collective-permute-start.34 = (bf16[256,2560]{1,0:T(8,128)(2,1)S(1)}, bf16[256,2560]{1,0:T(8,128)(2,1)S(1)}, u32[]{:S(2)}, u32[]{:S(2)}) collective-permute-start(bf16[256,2560]{1,0:T(8,128)(2,1)S(1)} %slice.352), channel_id=1, source_target_pairs={{0,8},{4,12},{8,0},{12,4},{1,9},{5,13},{9,1},{13,5},{2,10},{6,14},... | collective-permute-start | bytes 3932168 | tf_op jit(solution)/shard_map/ppermute | solution.py:22
  482.9 72.6 %collective-permute-start.51 = (bf16[512,2688]{1,0:T(8,128)(2,1)}, bf16[512,2688]{1,0:T(8,128)(2,1)}, u32[]{:S(2)}, u32[]{:S(2)}) collective-permute-start(bf16[512,2688]{1,0:T(8,128)(2,1)} %add_convert_fusion.4.refs_22_), channel_id=1, source_target_pairs={{0,4},{4,0},{8,12},{12,8},{1,5},{5,1},{9,13},{13,9},{2,6},{6,2},{1... | collective-permute-start | bytes 8257544 | tf_op jit(solution)/shard_map/ppermute | solution.py:22
  487.7 67.9 %collective-permute-start.52 = (bf16[512,2688]{1,0:T(8,128)(2,1)S(1)}, bf16[512,2688]{1,0:T(8,128)(2,1)}, u32[]{:S(2)}, u32[]{:S(2)}) collective-permute-start(bf16[512,2688]{1,0:T(8,128)(2,1)S(1)} %add_convert_fusion.3.refs_26_), channel_id=1, source_target_pairs={{0,8},{4,12},{8,0},{12,4},{1,9},{5,13},{9,1},{13,5},{2,10},{6,14},... | collective-permute-start | bytes 8257544 | tf_op jit(solution)/shard_map/ppermute | solution.py:22
  566.7 39.6 %collective-permute-start.55 = (bf16[2048,2560]{1,0:T(8,128)(2,1)}, bf16[2048,2560]{1,0:T(8,128)(2,1)S(1)}, u32[]{:S(2)}, u32[]{:S(2)}) collective-permute-start(bf16[2048,2560]{1,0:T(8,128)(2,1)} %shard_map.305), channel_id=1, source_target_pairs={{0,16},{16,0},{1,17},{17,1},{2,18},{18,2},{3,19},{19,3},{4,20},{20... | collective-permute-start | bytes 31457288 | tf_op jit(solution)/shard_map/ppermute | solution.py:22
  571.0 60.9 %collective-permute-start.56 = (bf16[512,2688]{1,0:T(8,128)(2,1)S(1)}, bf16[512,2688]{1,0:T(8,128)(2,1)S(1)}, u32[]{:S(2)}, u32[]{:S(2)}) collective-permute-start(bf16[512,2688]{1,0:T(8,128)(2,1)S(1)} %copy-done.24), channel_id=1, source_target_pairs={{0,12},{4,8},{8,4},{12,0},{1,13},{5,9},{9,5},{13,1},{2,14},{6,10},... | collective-permute-start | bytes 8257544 | tf_op jit(solution)/shard_map/ppermute | solution.py:22
  633.5 313.7 %reduce-scatter.11.cloned.1.call-start = ((), (), s32[]{:S(2)}) async-start(), calls=%async_computation.9 | async-start | bytes 3686400 | tf_op jit(solution)/shard_map/reduce_scatter | solution.py:167
  643.1 61.2 %collective-permute-start.60 = (bf16[128,2688]{1,0:T(8,128)(2,1)}, bf16[128,2688]{1,0:T(8,128)(2,1)}, u32[]{:S(2)}, u32[]{:S(2)}) collective-permute-start(bf16[128,2688]{1,0:T(8,128)(2,1)} %get-tuple-element.164), channel_id=1, source_target_pairs={{0,2},{1,0},{3,1},{2,3},{4,6},{5,4},{7,5},{6,7},{8,10},{9,8},{11,9... | collective-permute-start | bytes 2064392 | tf_op jit(solution)/shard_map/ppermute | solution.py:93
  644.1 60.1 %collective-permute-start.61 = (bf16[128,2688]{1,0:T(8,128)(2,1)}, bf16[128,2688]{1,0:T(8,128)(2,1)}, u32[]{:S(2)}, u32[]{:S(2)}) collective-permute-start(bf16[128,2688]{1,0:T(8,128)(2,1)} %get-tuple-element.166), channel_id=1, source_target_pairs={{0,3},{1,2},{3,0},{2,1},{4,7},{5,6},{7,4},{6,5},{8,11},{9,10},{11,... | collective-permute-start | bytes 2064392 | tf_op jit(solution)/shard_map/ppermute | solution.py:93
  644.3 59.9 %collective-permute-start.62 = (bf16[128,2688]{1,0:T(8,128)(2,1)}, bf16[128,2688]{1,0:T(8,128)(2,1)}, u32[]{:S(2)}, u32[]{:S(2)}) collective-permute-start(bf16[128,2688]{1,0:T(8,128)(2,1)} %get-tuple-element.165), channel_id=1, source_target_pairs={{0,1},{1,3},{3,2},{2,0},{4,5},{5,7},{7,6},{6,4},{8,9},{9,11},{11,1... | collective-permute-start | bytes 2064392 | tf_op jit(solution)/shard_map/ppermute | solution.py:93
  759.6 202.3 %reduce-scatter.7.cloned.1.call-start = ((), (), s32[]{:S(2)}) async-start(), calls=%async_computation.7 | async-start | bytes 3686400 | tf_op jit(solution)/shard_map/reduce_scatter | solution.py:167
  804.4 45.0 %collective-permute-start.75 = (bf16[512,256]{1,0:T(8,128)(2,1)S(1)}, bf16[512,256]{1,0:T(8,128)(2,1)S(1)}, u32[]{:S(2)}, u32[]{:S(2)}) collective-permute-start(bf16[512,256]{1,0:T(8,128)(2,1)S(1)} %get-tuple-element.192), channel_id=1, source_target_pairs={{0,3},{1,2},{2,1},{3,0},{4,7},{5,6},{6,5},{7,4},{8,11},{9,10},{10,... | collective-permute-start | bytes 786440 | tf_op jit(solution)/shard_map/ppermute | solution.py:22
  807.1 49.3 %collective-permute-start.68 = (bf16[128,2560]{1,0:T(8,128)(2,1)}, bf16[128,2560]{1,0:T(8,128)(2,1)}, u32[]{:S(2)}, u32[]{:S(2)}) collective-permute-start(bf16[128,2560]{1,0:T(8,128)(2,1)} %add_convert_fusion.9), channel_id=1, source_target_pairs={{0,2},{1,0},{3,1},{2,3},{4,6},{5,4},{7,5},{6,7},{8,10},{9,8},{11,9... | collective-permute-start | bytes 1966088 | tf_op jit(solution)/shard_map/ppermute | solution.py:93
  854.8 72.8 %collective-permute-start.80 = (bf16[4,512,384]{2,1,0:T(8,128)(2,1)}, bf16[4,512,384]{2,1,0:T(8,128)(2,1)}, u32[]{:S(2)}, u32[]{:S(2)}) collective-permute-start(bf16[4,512,384]{2,1,0:T(8,128)(2,1)} %shard_map.312.refs_0_), channel_id=1, source_target_pairs={{0,16},{16,0},{1,17},{17,1},{2,18},{18,2},{3,19},{19,3},{4,20},{20... | collective-permute-start | bytes 4718600 | tf_op jit(solution)/shard_map/ppermute | solution.py:22
  865.6 127.1 %reduce-scatter.9.cloned.1.call-start = ((), (), s32[]{:S(2)}) async-start(), calls=%async_computation.8 | async-start | bytes 1474560 | tf_op jit(solution)/shard_map/reduce_scatter | solution.py:167
  883.0 54.2 %collective-permute-start.77 = (bf16[128,2560]{1,0:T(8,128)(2,1)S(1)}, bf16[128,2560]{1,0:T(8,128)(2,1)}, u32[]{:S(2)}, u32[]{:S(2)}) collective-permute-start(bf16[128,2560]{1,0:T(8,128)(2,1)S(1)} %pad_maximum_fusion.5), channel_id=1, source_target_pairs={{0,4},{4,0},{8,12},{12,8},{1,5},{5,1},{9,13},{13,9},{2,6},{6,2},{1... | collective-permute-start | bytes 1966088 | tf_op jit(solution)/shard_map/ppermute | solution.py:22
  885.1 52.1 %collective-permute-start.79 = (bf16[128,2560]{1,0:T(8,128)(2,1)}, bf16[128,2560]{1,0:T(8,128)(2,1)}, u32[]{:S(2)}, u32[]{:S(2)}) collective-permute-start(bf16[128,2560]{1,0:T(8,128)(2,1)} %pad_maximum_fusion.6), channel_id=1, source_target_pairs={{0,8},{4,12},{8,0},{12,4},{1,9},{5,13},{9,1},{13,5},{2,10},{6,14},... | collective-permute-start | bytes 1966088 | tf_op jit(solution)/shard_map/ppermute | solution.py:22
  947.2 37.2 %collective-permute-start.86 = (bf16[320,640]{1,0:T(8,128)(2,1)}, bf16[320,640]{1,0:T(8,128)(2,1)S(1)}, u32[]{:S(2)}, u32[]{:S(2)}) collective-permute-start(bf16[320,640]{1,0:T(8,128)(2,1)} %shard_map.318), channel_id=1, source_target_pairs={{0,16},{16,0},{1,17},{17,1},{2,18},{18,2},{3,19},{19,3},{4,20},{20... | collective-permute-start | bytes 1228808 | tf_op jit(solution)/shard_map/ppermute | solution.py:22
  (160 other events, 2225.5 us)
Sparse Core Ops, SparseCore 0:
  11.7 85.8 all-gather.2
  134.4 71.5 all-gather.4
  633.6 122.4 reduce-scatter.4
  759.7 86.7 reduce-scatter.10
  865.8 53.5 reduce-scatter.6
  962.1 30.5 reduce-scatter.8

commit v8 on v6

--- a/solution.py
+++ b/solution.py
@@ -35,6 +35,9 @@
 
 def all_sum(x, axis):
     step = 1
+    if lax.axis_size(axis) == 4:
+        own, near, other, far = exchange(x, axis)
+        return (own + near) + (other + far)
     while step < lax.axis_size(axis):
         x = x + swap(x, axis, step)
         step *= 2
@@ -884,7 +887,8 @@
     )
     payload = jnp.concatenate(ring_gather(payload, "col"), axis=0)
     grad_rows = row_gather(g_block)
-    payload = after(payload, *grad_rows[1:3])
+    grad_own = exchange(g_block, "exp")
+    payload = after(payload, *grad_rows[1:3], *grad_own[1:], sh_in)
     payload_rows = row_gather(payload)
     if R == 4:
         grad_rows = grad_rows[:3] + [jnp.concatenate(grad_rows[3:], axis=0)]
@@ -909,7 +913,7 @@
         ).astype(jnp.int32)
         kept, norm = experts_call(
             s, R, kept, list(zip(*(exchange(x, "exp") for x in x_block))),
-            exchange(grad_rows[s], "exp"), info,
+            exchange(grad_rows[s], "exp") if s else grad_own, info,
             slots[s], expert_in, expert_down, sh_in, sh_down, capacity, norms[-1:],
         )
         if s == R - 1:
@@ -973,7 +977,6 @@
     d_kv = reduce_parts([d_kv_parts[k] for k in range(C)], "col")
     for k in range(C - 2, 0, -1):
         moe_out = ring_send(add(out_chunks[k], moe_out).astype(bf16), "col", 1)
-    moe_out = add(out_chunks[0], moe_out)
     d_query_raw = rotate(
         d_queries.reshape(own_rows, group_heads, head_width), cosines, -sines
     ) * attn_scale
@@ -986,11 +989,10 @@
     ).astype(bf16)
     norm_one_part = dot(jnp.concatenate([d_kv_raw, d_query_raw], axis=1), weight_in, (1, 1)).astype(bf16)
     d_norm_one, halfway = row_reduce(jnp.split(norm_one_part, R, axis=0))
-    d_x, gain_one_part = rms_backward(
-        x, inv_one, gain_one + zero_of(moe_out).astype(f32), d_norm_one
-    )
+    d_x, gain_one_part = rms_backward(x, inv_one, gain_one, d_norm_one)
     grad_inputs, back = tokens_back((d_hidden + d_x).astype(bf16))
 
+    moe_out = add(out_chunks[0], after(moe_out, *back))
     output = tokens_back((hidden_state + moe_out).astype(bf16))[0]
     out_total, query_total = reduce_weight(out_grads), reduce_weight(query_grads)
     kv_grads = dot(after(norm_one_late, *halfway), d_kv_raw, (0, 0)).astype(bf16)

time: 991 us -> 982 us (level)
    ppermute x6, waiting for transfers between devices: 41.6 us -> 31.5 us  [ring_send(): lax.ppermute(x, axis, [(order[i], order[(i - k) % n]) for i in range(n)])]
    ppermute x84 -> x85, starting transfers between devices: 86.9 us -> 80.5 us  [swap(): lax.ppermute(x, axis, [(i, i ^ step) for i in range(lax.axis_size(axis))])]
    ppermute x84 -> x85, waiting for transfers between devices: 275 us -> 281 us  [swap(): lax.ppermute(x, axis, [(i, i ^ step) for i in range(lax.axis_size(axis))])]
    unnamed x203 -> x217, local copies, waits for them, and re-layouts: 23.4 us -> 25 us
  transfers between devices with their start and end apart: 99 -> 100, of which waited for: 43 -> 48; matrix products, arithmetic and copies ran while one was open for 22% -> 22% of each run, Pallas kernels for 24% -> 24%
where the time goes in v8:
time: 982 us; the launch traced here: 975 us
  waiting for transfers between devices  367 us (37%)
  Pallas kernels  236 us (24%)
  matrix products  103 us (10%)
  starting transfers between devices  88.6 us (9%)
  other arithmetic  76.3 us (8%)
  local copies, waits for them, and re-layouts  71.3 us (7%)
  between operations  31.9 us (3%)
    ppermute x85, waiting for transfers between devices, swap(): lax.ppermute(x, axis, [(i, i ^ step) for i in range(lax.axis_size(axis))])  281 us
    pallas_call x4, Pallas kernels, experts_call(): pl.pallas_call(functools.partial(experts_kernel, counts, len(held) + len(...  171 us
    ppermute x85, starting transfers between devices, swap(): lax.ppermute(x, axis, [(i, i ^ step) for i in range(lax.axis_size(axis))])  80.5 us
    dot_general x4, matrix products, batch_dot(): return jnp.einsum(spec, left, right, preferred_element_type=f32)  53.2 us
    dot_general x9, matrix products, dot(): lax.dot_general(left, right, (((contract[0],), (contract[1],)), ((), ()))...  45.9 us
    ppermute x6, waiting for transfers between devices, ring_send(): lax.ppermute(x, axis, [(order[i], order[(i - k) % n]) for i in range(n)])  31.5 us
    pallas_call x2, Pallas kernels, attention_call(): pl.pallas_call(lambda place, *refs: kernel(place, *refs[:len(operands)],...  29.6 us
    ppermute x3, waiting for transfers between devices, ring_gather(): parts.append(lax.ppermute(parts[-1], axis, ring_pairs(n)))  28.8 us
  transfers between devices with their start and end apart: 100, of which 48 were waited for; matrix products, arithmetic and copies ran while one was open for 22% of the time, Pallas kernels for 24%

profile of v8, /device:TPU:9, one launch (start us, length us, event | category | flops | bytes accessed | tf_op | source)
XLA Modules:
  0.0 974.7 jit_solution(11617646839068130434)
XLA Ops:
  21.6 8.3 collective-permute-done.1
  30.0 18.0 %collective-permute-done.2 = bf16[128,640]{1,0:T(8,128)(2,1)S(1)} collective-permute-done((bf16[128,640]{1,0:T(8,128)(2,1)S(1)}, bf16[128,640]{1,0:T(8,128)(2,1)S(1)}, u32[]{:S(2)}, u32[]{:S(2)}) %collective-permute-start.2) | collective-permute-done | bytes 163872 | tf_op jit(solution)/shard_map/ppermute | solution.py:22
  54.2 6.7 collective-permute-done.7
  71.6 26.0 %all-gather.3.cloned.1.call-done.ref = bf16[2560,1536]{1,0:T(8,128)(2,1)} async-done(((bf16[320,1536]{1,0:T(8,128)(2,1)}), bf16[2560,1536]{1,0:T(8,128)(2,1)}) %all-gather.3.cloned.1.call-update) | async-done | bytes 7864336 | tf_op jit(solution)/shard_map/all_gather | solution.py:806
  112.8 9.6 shard_map.289.refs_5_.refs_8_.refs_12_
  134.6 12.8 %shard_map.291 = (bf16[512,640]{1,0:T(8,128)(2,1)}, f32[4,128,640]{2,1,0:T(8,128)}, f32[4,1,640]{2,1,0:T(1,128)}) custom-call(s32[6]{0:T(128)} %pad_add_fusion.place, bf16[512,640]{1,0:T(8,128)(2,1)} %copy.157.refs_0_, bf16[512,256]{1,0:T(8,128)(2,1)} %pad_maximum_fusion.7.refs_1_.refs_4_, bf16[512,256]{1,0:T(8,128)(2,1)} %collective-permute-done.10.refs_2_.refs_1_.refs_5_, ...), custom_call_target="tpu_custom_call" | custom-call | flops 2684354560 | bytes 1024 | tf_op jit(solution)/shard_map/pallas_call | solution.py:496
  167.0 31.4 %collective-permute-done.17 = bf16[512,384]{1,0:T(8,128)(2,1)S(1)} collective-permute-done((bf16[512,384]{1,0:T(8,128)(2,1)S(1)}, bf16[512,384]{1,0:T(8,128)(2,1)S(1)}, u32[]{:S(2)}, u32[]{:S(2)}) %collective-permute-start.17) | collective-permute-done | bytes 393248 | tf_op jit(solution)/shard_map/ppermute | solution.py:22
  202.4 18.9 %collective-permute-done.19 = bf16[512,384]{1,0:T(8,128)(2,1)S(1)} collective-permute-done((bf16[512,384]{1,0:T(8,128)(2,1)S(1)}, bf16[512,384]{1,0:T(8,128)(2,1)S(1)}, u32[]{:S(2)}, u32[]{:S(2)}) %collective-permute-start.19) | collective-permute-done | bytes 393248 | tf_op jit(solution)/shard_map/ppermute | solution.py:22
  237.7 14.6 %collective-permute-done.20 = bf16[128,2688]{1,0:T(8,128)(2,1)} collective-permute-done((bf16[128,2688]{1,0:T(8,128)(2,1)}, bf16[128,2688]{1,0:T(8,128)(2,1)}, u32[]{:S(2)}, u32[]{:S(2)}) %collective-permute-start.20) | collective-permute-done | bytes 688160 | tf_op jit(solution)/shard_map/ppermute | solution.py:86
  254.7 14.1 %collective-permute-done.21 = bf16[128,2688]{1,0:T(8,128)(2,1)} collective-permute-done((bf16[128,2688]{1,0:T(8,128)(2,1)}, bf16[128,2688]{1,0:T(8,128)(2,1)}, u32[]{:S(2)}, u32[]{:S(2)}) %collective-permute-start.21) | collective-permute-done | bytes 688160 | tf_op jit(solution)/shard_map/ppermute | solution.py:86
  303.7 42.6 %shard_map.297 = (bf16[2,2048,2560]{2,1,0:T(8,128)(2,1)}, bf16[2,2048,2560]{2,1,0:T(8,128)(2,1)}, bf16[2,2048,384]{2,1,0:T(8,128)(2,1)}, bf16[2,2048,768]{2,1,0:...) custom-call(s32[6]{0:T(128)} %get-tuple-element.154.info, ...), custom_call_target="tpu_custom_call" | custom-call | flops 26843545600 | bytes 1024 | tf_op jit(solution)/shard_map/pallas_call | solution.py:734
  346.3 14.3 %collective-permute-done.27.refs_2_.refs_0_ = bf16[512,2688]{1,0:T(8,128)(2,1)S(1)} collective-permute-done((bf16[512,2688]{1,0:T(8,128)(2,1)}, bf16[512,2688]{1,0:T(8,128)(2,1)S(1)}, u32[]{:S(2)}, u32[]{:S(2)}) %collective-permute-start.27) | collective-permute-done | bytes 2752544 | tf_op jit(solution)/shard_map/ppermute | solution.py:22
  377.8 42.9 %shard_map.299 = (bf16[2,2048,2560]{2,1,0:T(8,128)(2,1)}, bf16[2,2048,2560]{2,1,0:T(8,128)(2,1)}, bf16[2,2048,384]{2,1,0:T(8,128)(2,1)}, bf16[2,2048,768]{2,1,0:...) custom-call(s32[6]{0:T(128)} %get-tuple-element.228.info, ...), custom_call_target="tpu_custom_call", output_to_operand_aliasing={{0}: (13, {}), {1}: (14, {}), {2}: (15, {}), {3}: (16, {}),... | custom-call | flops 26843545600 | bytes 1024 | tf_op jit(solution)/shard_map/pallas_call | solution.py:734
  435.8 42.7 %shard_map.301 = (bf16[2,2048,2560]{2,1,0:T(8,128)(2,1)}, bf16[2,2048,2560]{2,1,0:T(8,128)(2,1)}, bf16[2,2048,384]{2,1,0:T(8,128)(2,1)}, bf16[2,2048,768]{2,1,0:...) custom-call(s32[6]{0:T(128)} %get-tuple-element.229.info, ...), custom_call_target="tpu_custom_call", output_to_operand_aliasing={{0}: (13, {}), {1}: (14, {}), {2}: (15, {}), {3}: (16, {}),... | custom-call | flops 26843545600 | bytes 1024 | tf_op jit(solution)/shard_map/pallas_call | solution.py:734
  491.9 43.2 %shard_map.302 = (bf16[2,2048,2560]{2,1,0:T(8,128)(2,1)}, bf16[2,2048,2560]{2,1,0:T(8,128)(2,1)}, bf16[2,2048,384]{2,1,0:T(8,128)(2,1)}, bf16[2,2048,768]{2,1,0:...) custom-call(s32[6]{0:T(128)} %get-tuple-element.230.info, ...), custom_call_target="tpu_custom_call", output_to_operand_aliasing={{0}: (17, {}), {1}: (18, {}), {2}: (19, {}), {3}: (20, {}),... | custom-call | flops 26843545600 | bytes 1024 | tf_op jit(solution)/shard_map/pallas_call | solution.py:734
  535.1 8.4 convolution_convert_fusion.5.refs_1_
  543.5 7.2 convolution_convert_fusion.2.refs_0_
  572.1 11.7 %collective-permute-done.57 = bf16[512,384]{1,0:T(8,128)(2,1)S(1)} collective-permute-done((bf16[512,384]{1,0:T(8,128)(2,1)S(1)}, bf16[512,384]{1,0:T(8,128)(2,1)S(1)}, u32[]{:S(2)}, u32[]{:S(2)}) %collective-permute-start.57) | collective-permute-done | bytes 393248 | tf_op jit(solution)/shard_map/ppermute | solution.py:22
  586.9 18.2 %collective-permute-done.59 = bf16[512,384]{1,0:T(8,128)(2,1)S(1)} collective-permute-done((bf16[512,384]{1,0:T(8,128)(2,1)S(1)}, bf16[512,384]{1,0:T(8,128)(2,1)S(1)}, u32[]{:S(2)}, u32[]{:S(2)}) %collective-permute-start.59) | collective-permute-done | bytes 393248 | tf_op jit(solution)/shard_map/ppermute | solution.py:22
  606.4 11.1 %add_convert_fusion.refs_0_ = bf16[2048,2560]{1,0:T(8,128)(2,1)} fusion(bf16[2048,2560]{1,0:T(8,128)(2,1)S(1)} %collective-permute-done.55, bf16[2048,2560]{1,0:T(8,128)(2,1)} %get-tuple-element.114), kind=kLoop, calls=%fused_computation.2 | loop fusion | flops 20971520 | bytes 31457280 | tf_op jit(solution)/shard_map/convert_element_type | solution.py:942
  617.5 14.5 %collective-permute-done.56.refs_1_ = bf16[512,2688]{1,0:T(8,128)(2,1)S(1)} collective-permute-done((bf16[512,2688]{1,0:T(8,128)(2,1)S(1)}, bf16[512,2688]{1,0:T(8,128)(2,1)S(1)}, u32[]{:S(2)}, u32[]{:S(2)}) %collective-permute-start.56) | collective-permute-done | bytes 2752544 | tf_op jit(solution)/shard_map/ppermute | solution.py:22
  646.2 18.6 %fusion.3 = f32[2,2560,384]{2,1,0:T(8,128)} fusion(bf16[2,2048,2560]{2,1,0:T(8,128)(2,1)} %get-tuple-element.124, bf16[2,2048,768]{2,1,0:T(8,128)(2,1)} %shard_map.307), kind=kOutput, calls=%fused_computation.17 | convolution fusion | flops 8053063680 | bytes 31981568 | tf_op jit(solution)/shard_map/lrd,lrf->ldf/dot_general | solution.py:193
  664.9 18.6 %fusion.5 = f32[2,2560,384]{2,1,0:T(8,128)} fusion(bf16[2,2048,2560]{2,1,0:T(8,128)(2,1)} %get-tuple-element.124, bf16[2,2048,768]{2,1,0:T(8,128)(2,1)} %shard_map.307), kind=kOutput, calls=%fused_computation.19 | convolution fusion | flops 8053063680 | bytes 31981568 | tf_op jit(solution)/shard_map/lrd,lrf->ldf/dot_general | solution.py:193
  683.4 12.2 %fusion.86 = f32[2,384,2560]{2,1,0:T(8,128)S(1)} fusion(bf16[2,2048,384]{2,1,0:T(8,128)(2,1)S(1)} %copy-done.4, bf16[2,2048,2560]{2,1,0:T(8,128)(2,1)} %get-tuple-element.127), kind=kOutput, calls=%fused_computation.275 | convolution fusion | flops 8053063680 | bytes 31981568 | tf_op jit(solution)/shard_map/lrf,lrd->lfd/dot_general | solution.py:193
  712.5 28.2 %collective-permute-done.64 = bf16[128,2560]{1,0:T(8,128)(2,1)S(1)} collective-permute-done((bf16[128,2560]{1,0:T(8,128)(2,1)S(1)}, bf16[128,2560]{1,0:T(8,128)(2,1)S(1)}, u32[]{:S(2)}, u32[]{:S(2)}) %collective-permute-start.64) | collective-permute-done | bytes 655392 | tf_op jit(solution)/shard_map/ppermute | solution.py:22
  742.4 13.3 %collective-permute-done.65 = bf16[64,2560]{1,0:T(8,128)(2,1)S(1)} collective-permute-done((bf16[64,2560]{1,0:T(8,128)(2,1)S(1)}, bf16[64,2560]{1,0:T(8,128)(2,1)S(1)}, u32[]{:S(2)}, u32[]{:S(2)}) %collective-permute-start.65) | collective-permute-done | bytes 327712 | tf_op jit(solution)/shard_map/ppermute | solution.py:22
  771.4 16.8 %shard_map.310 = (f32[512,640]{1,0:T(8,128)}, bf16[4,512,256]{2,1,0:T(8,128)(2,1)}) custom-call(s32[6]{0:T(128)} %pad_add_fusion.place, bf16[512,640]{1,0:T(8,128)(2,1)} %copy.157.refs_0_, bf16[512,640]{1,0:T(8,128)(2,1)} %convolution_convert_fusion.6.refs_1_, f32[4,128,640]{2,1,0:T(8,128)} %get-tuple-element.128.refs_2_, ...), custom_call_target="tpu_custom_call" | custom-call | flops 6710886400 | bytes 1024 | tf_op jit(solution)/shard_map/pallas_call | solution.py:496
  791.2 10.9 %collective-permute-done.67.refs_1_ = bf16[128,2560]{1,0:T(8,128)(2,1)S(1)} collective-permute-done((bf16[128,2560]{1,0:T(8,128)(2,1)}, bf16[128,2560]{1,0:T(8,128)(2,1)S(1)}, u32[]{:S(2)}, u32[]{:S(2)}) %collective-permute-start.67) | collective-permute-done | bytes 655392 | tf_op jit(solution)/shard_map/ppermute | solution.py:93
  813.6 9.2 collective-permute-done.70
  824.9 10.7 %collective-permute-done.72 = bf16[512,256]{1,0:T(8,128)(2,1)} collective-permute-done((bf16[512,256]{1,0:T(8,128)(2,1)S(1)}, bf16[512,256]{1,0:T(8,128)(2,1)}, u32[]{:S(2)}, u32[]{:S(2)}) %collective-permute-start.72) | collective-permute-done | bytes 262176 | tf_op jit(solution)/shard_map/ppermute | solution.py:22
  858.8 20.6 %collective-permute-done.68 = bf16[128,2560]{1,0:T(8,128)(2,1)} collective-permute-done((bf16[128,2560]{1,0:T(8,128)(2,1)}, bf16[128,2560]{1,0:T(8,128)(2,1)}, u32[]{:S(2)}, u32[]{:S(2)}) %collective-permute-start.68) | collective-permute-done | bytes 655392 | tf_op jit(solution)/shard_map/ppermute | solution.py:93
  940.5 11.4 %collective-permute-done.82 = bf16[128,640]{1,0:T(8,128)(2,1)S(1)} collective-permute-done((bf16[128,640]{1,0:T(8,128)(2,1)S(1)}, bf16[128,640]{1,0:T(8,128)(2,1)S(1)}, u32[]{:S(2)}, u32[]{:S(2)}) %collective-permute-start.82) | collective-permute-done | bytes 163872 | tf_op jit(solution)/shard_map/ppermute | solution.py:22
  (607 shorter events, 355.0 us)
Async XLA Ops:
  7.2 90.4 %all-gather.3.cloned.1.call-start = ((), (), s32[]{:S(2)}) async-start(), calls=%async_computation.4 | async-start | bytes 8847360 | tf_op jit(solution)/shard_map/all_gather | solution.py:806
  11.6 213.5 %all-gather.5.cloned.1.call-start = ((), (), s32[]{:S(2)}) async-start(), calls=%async_computation.5 | async-start | bytes 3276800 | tf_op jit(solution)/shard_map/all_gather | solution.py:850
  134.3 634.2 %reduce-scatter.5.cloned.1.call-start = ((), (), s32[]{:S(2)}) async-start(), calls=%async_computation.6 | async-start | bytes 13107200 | tf_op jit(solution)/shard_map/reduce_scatter | solution.py:943
  160.2 63.0 %collective-permute-start.14 = (bf16[128,2560]{1,0:T(8,128)(2,1)S(1)}, bf16[128,2560]{1,0:T(8,128)(2,1)S(1)}, u32[]{:S(2)}, u32[]{:S(2)}) collective-permute-start(bf16[128,2560]{1,0:T(8,128)(2,1)S(1)} %pad_maximum_fusion.3), channel_id=1, source_target_pairs={{0,4},{4,0},{8,12},{12,8},{1,5},{5,1},{9,13},{13,9},{2,6},{6,2},{1... | collective-permute-start | bytes 1966088 | tf_op jit(solution)/shard_map/ppermute | solution.py:22
  161.5 61.7 %collective-permute-start.16 = (bf16[128,2560]{1,0:T(8,128)(2,1)S(1)}, bf16[128,2560]{1,0:T(8,128)(2,1)}, u32[]{:S(2)}, u32[]{:S(2)}) collective-permute-start(bf16[128,2560]{1,0:T(8,128)(2,1)S(1)} %pad_maximum_fusion.4), channel_id=1, source_target_pairs={{0,8},{4,12},{8,0},{12,4},{1,9},{5,13},{9,1},{13,5},{2,10},{6,14},... | collective-permute-start | bytes 1966088 | tf_op jit(solution)/shard_map/ppermute | solution.py:22
  164.2 34.2 %collective-permute-start.17 = (bf16[512,384]{1,0:T(8,128)(2,1)S(1)}, bf16[512,384]{1,0:T(8,128)(2,1)S(1)}, u32[]{:S(2)}, u32[]{:S(2)}) collective-permute-start(bf16[512,384]{1,0:T(8,128)(2,1)S(1)} %get-tuple-element.186), channel_id=1, source_target_pairs={{0,1},{1,0},{2,3},{3,2},{4,5},{5,4},{6,7},{7,6},{8,9},{9,8},{10,11... | collective-permute-start | bytes 1179656 | tf_op jit(solution)/shard_map/ppermute | solution.py:22
  164.2 36.3 %collective-permute-start.18 = (bf16[512,384]{1,0:T(8,128)(2,1)S(1)}, bf16[512,384]{1,0:T(8,128)(2,1)S(1)}, u32[]{:S(2)}, u32[]{:S(2)}) collective-permute-start(bf16[512,384]{1,0:T(8,128)(2,1)S(1)} %get-tuple-element.185), channel_id=1, source_target_pairs={{0,2},{1,3},{2,0},{3,1},{4,6},{5,7},{6,4},{7,5},{8,10},{9,11},{10,... | collective-permute-start | bytes 1179656 | tf_op jit(solution)/shard_map/ppermute | solution.py:22
  166.6 54.7 %collective-permute-start.19 = (bf16[512,384]{1,0:T(8,128)(2,1)S(1)}, bf16[512,384]{1,0:T(8,128)(2,1)S(1)}, u32[]{:S(2)}, u32[]{:S(2)}) collective-permute-start(bf16[512,384]{1,0:T(8,128)(2,1)S(1)} %get-tuple-element.184), channel_id=1, source_target_pairs={{0,3},{1,2},{2,1},{3,0},{4,7},{5,6},{6,5},{7,4},{8,11},{9,10},{10,... | collective-permute-start | bytes 1179656 | tf_op jit(solution)/shard_map/ppermute | solution.py:22
  229.7 66.0 %collective-permute-start.23 = (bf16[512,2560]{1,0:T(8,128)(2,1)}, bf16[512,2560]{1,0:T(8,128)(2,1)}, u32[]{:S(2)}, u32[]{:S(2)}) collective-permute-start(bf16[512,2560]{1,0:T(8,128)(2,1)} %all-gather.5.cloned.1.call-done.refs_4_), channel_id=1, source_target_pairs={{0,4},{4,0},{8,12},{12,8},{1,5},{5,1},{9,13},{13,9},{2,6},{6,2},{1... | collective-permute-start | bytes 7864328 | tf_op jit(solution)/shard_map/ppermute | solution.py:22
  230.6 65.4 %collective-permute-start.24 = (bf16[512,2560]{1,0:T(8,128)(2,1)}, bf16[512,2560]{1,0:T(8,128)(2,1)S(1)}, u32[]{:S(2)}, u32[]{:S(2)}) collective-permute-start(bf16[512,2560]{1,0:T(8,128)(2,1)} %all-gather.5.cloned.1.call-done.refs_4_), channel_id=1, source_target_pairs={{0,8},{4,12},{8,0},{12,4},{1,9},{5,13},{9,1},{13,5},{2,10},{6,14},... | collective-permute-start | bytes 7864328 | tf_op jit(solution)/shard_map/ppermute | solution.py:22
  231.8 64.4 %collective-permute-start.25 = (bf16[512,2560]{1,0:T(8,128)(2,1)}, bf16[512,2560]{1,0:T(8,128)(2,1)}, u32[]{:S(2)}, u32[]{:S(2)}) collective-permute-start(bf16[512,2560]{1,0:T(8,128)(2,1)} %all-gather.5.cloned.1.call-done.refs_4_), channel_id=1, source_target_pairs={{0,16},{16,0},{1,17},{17,1},{2,18},{18,2},{3,19},{19,3},{4,20},{20... | collective-permute-start | bytes 7864328 | tf_op jit(solution)/shard_map/ppermute | solution.py:22
  237.7 37.1 %collective-permute-start.26 = (bf16[4,512,384]{2,1,0:T(8,128)(2,1)}, bf16[4,512,384]{2,1,0:T(8,128)(2,1)}, u32[]{:S(2)}, u32[]{:S(2)}) collective-permute-start(bf16[4,512,384]{2,1,0:T(8,128)(2,1)} %pad_maximum_fusion.1.refs_0_), channel_id=1, source_target_pairs={{0,16},{16,0},{1,17},{17,1},{2,18},{18,2},{3,19},{19,3},{4,20},{20... | collective-permute-start | bytes 4718600 | tf_op jit(solution)/shard_map/ppermute | solution.py:22
  299.3 61.3 %collective-permute-start.27 = (bf16[512,2688]{1,0:T(8,128)(2,1)}, bf16[512,2688]{1,0:T(8,128)(2,1)S(1)}, u32[]{:S(2)}, u32[]{:S(2)}) collective-permute-start(bf16[512,2688]{1,0:T(8,128)(2,1)} %shard_map.296.refs_0_.refs_2_), channel_id=1, source_target_pairs={{0,8},{4,12},{8,0},{12,4},{1,9},{5,13},{9,1},{13,5},{2,10},{6,14},... | collective-permute-start | bytes 8257544 | tf_op jit(solution)/shard_map/ppermute | solution.py:22
  300.4 60.8 %collective-permute-start.29 = (bf16[512,2688]{1,0:T(8,128)(2,1)}, bf16[512,2688]{1,0:T(8,128)(2,1)}, u32[]{:S(2)}, u32[]{:S(2)}) collective-permute-start(bf16[512,2688]{1,0:T(8,128)(2,1)} %shard_map.296.refs_0_.refs_2_), channel_id=1, source_target_pairs={{0,4},{4,0},{8,12},{12,8},{1,5},{5,1},{9,13},{13,9},{2,6},{6,2},{1... | collective-permute-start | bytes 8257544 | tf_op jit(solution)/shard_map/ppermute | solution.py:22
  366.7 54.0 %collective-permute-start.28 = (bf16[256,2688]{1,0:T(8,128)(2,1)S(1)}, bf16[256,2688]{1,0:T(8,128)(2,1)S(1)}, u32[]{:S(2)}, u32[]{:S(2)}) collective-permute-start(bf16[256,2688]{1,0:T(8,128)(2,1)S(1)} %slice.337), channel_id=1, source_target_pairs={{0,4},{4,0},{8,12},{12,8},{1,5},{5,1},{9,13},{13,9},{2,6},{6,2},{1... | collective-permute-start | bytes 4128776 | tf_op jit(solution)/shard_map/ppermute | solution.py:22
  370.2 50.5 %collective-permute-start.30 = (bf16[256,2688]{1,0:T(8,128)(2,1)}, bf16[256,2688]{1,0:T(8,128)(2,1)S(1)}, u32[]{:S(2)}, u32[]{:S(2)}) collective-permute-start(bf16[256,2688]{1,0:T(8,128)(2,1)} %slice.338), channel_id=1, source_target_pairs={{0,8},{4,12},{8,0},{12,4},{1,9},{5,13},{9,1},{13,5},{2,10},{6,14},... | collective-permute-start | bytes 4128776 | tf_op jit(solution)/shard_map/ppermute | solution.py:22
  428.5 50.8 %collective-permute-start.33 = (bf16[256,2560]{1,0:T(8,128)(2,1)}, bf16[256,2560]{1,0:T(8,128)(2,1)S(1)}, u32[]{:S(2)}, u32[]{:S(2)}) collective-permute-start(bf16[256,2560]{1,0:T(8,128)(2,1)} %slice.339), channel_id=1, source_target_pairs={{0,4},{4,0},{8,12},{12,8},{1,5},{5,1},{9,13},{13,9},{2,6},{6,2},{1... | collective-permute-start | bytes 3932168 | tf_op jit(solution)/shard_map/ppermute | solution.py:22
  430.7 49.8 %collective-permute-start.34 = (bf16[256,2560]{1,0:T(8,128)(2,1)S(1)}, bf16[256,2560]{1,0:T(8,128)(2,1)S(1)}, u32[]{:S(2)}, u32[]{:S(2)}) collective-permute-start(bf16[256,2560]{1,0:T(8,128)(2,1)S(1)} %slice.340), channel_id=1, source_target_pairs={{0,8},{4,12},{8,0},{12,4},{1,9},{5,13},{9,1},{13,5},{2,10},{6,14},... | collective-permute-start | bytes 3932168 | tf_op jit(solution)/shard_map/ppermute | solution.py:22
  482.9 72.7 %collective-permute-start.51 = (bf16[512,2688]{1,0:T(8,128)(2,1)}, bf16[512,2688]{1,0:T(8,128)(2,1)}, u32[]{:S(2)}, u32[]{:S(2)}) collective-permute-start(bf16[512,2688]{1,0:T(8,128)(2,1)} %add_convert_fusion.4.refs_22_), channel_id=1, source_target_pairs={{0,4},{4,0},{8,12},{12,8},{1,5},{5,1},{9,13},{13,9},{2,6},{6,2},{1... | collective-permute-start | bytes 8257544 | tf_op jit(solution)/shard_map/ppermute | solution.py:22
  487.6 68.0 %collective-permute-start.52 = (bf16[512,2688]{1,0:T(8,128)(2,1)S(1)}, bf16[512,2688]{1,0:T(8,128)(2,1)}, u32[]{:S(2)}, u32[]{:S(2)}) collective-permute-start(bf16[512,2688]{1,0:T(8,128)(2,1)S(1)} %add_convert_fusion.3.refs_26_), channel_id=1, source_target_pairs={{0,8},{4,12},{8,0},{12,4},{1,9},{5,13},{9,1},{13,5},{2,10},{6,14},... | collective-permute-start | bytes 8257544 | tf_op jit(solution)/shard_map/ppermute | solution.py:22
  566.8 39.6 %collective-permute-start.55 = (bf16[2048,2560]{1,0:T(8,128)(2,1)}, bf16[2048,2560]{1,0:T(8,128)(2,1)S(1)}, u32[]{:S(2)}, u32[]{:S(2)}) collective-permute-start(bf16[2048,2560]{1,0:T(8,128)(2,1)} %shard_map.305), channel_id=1, source_target_pairs={{0,16},{16,0},{1,17},{17,1},{2,18},{18,2},{3,19},{19,3},{4,20},{20... | collective-permute-start | bytes 31457288 | tf_op jit(solution)/shard_map/ppermute | solution.py:22
  569.5 35.5 %collective-permute-start.59 = (bf16[512,384]{1,0:T(8,128)(2,1)S(1)}, bf16[512,384]{1,0:T(8,128)(2,1)S(1)}, u32[]{:S(2)}, u32[]{:S(2)}) collective-permute-start(bf16[512,384]{1,0:T(8,128)(2,1)S(1)} %get-tuple-element.180), channel_id=1, source_target_pairs={{0,3},{1,2},{2,1},{3,0},{4,7},{5,6},{6,5},{7,4},{8,11},{9,10},{10,... | collective-permute-start | bytes 1179656 | tf_op jit(solution)/shard_map/ppermute | solution.py:22
  571.1 60.9 %collective-permute-start.56 = (bf16[512,2688]{1,0:T(8,128)(2,1)S(1)}, bf16[512,2688]{1,0:T(8,128)(2,1)S(1)}, u32[]{:S(2)}, u32[]{:S(2)}) collective-permute-start(bf16[512,2688]{1,0:T(8,128)(2,1)S(1)} %copy-done.24), channel_id=1, source_target_pairs={{0,12},{4,8},{8,4},{12,0},{1,13},{5,9},{9,5},{13,1},{2,14},{6,10},... | collective-permute-start | bytes 8257544 | tf_op jit(solution)/shard_map/ppermute | solution.py:22
  633.5 257.6 %reduce-scatter.11.cloned.1.call-start = ((), (), s32[]{:S(2)}) async-start(), calls=%async_computation.9 | async-start | bytes 3686400 | tf_op jit(solution)/shard_map/reduce_scatter | solution.py:167
  643.1 60.9 %collective-permute-start.60 = (bf16[128,2688]{1,0:T(8,128)(2,1)}, bf16[128,2688]{1,0:T(8,128)(2,1)}, u32[]{:S(2)}, u32[]{:S(2)}) collective-permute-start(bf16[128,2688]{1,0:T(8,128)(2,1)} %get-tuple-element.162), channel_id=1, source_target_pairs={{0,2},{1,0},{3,1},{2,3},{4,6},{5,4},{7,5},{6,7},{8,10},{9,8},{11,9... | collective-permute-start | bytes 2064392 | tf_op jit(solution)/shard_map/ppermute | solution.py:93
  644.1 59.8 %collective-permute-start.61 = (bf16[128,2688]{1,0:T(8,128)(2,1)}, bf16[128,2688]{1,0:T(8,128)(2,1)}, u32[]{:S(2)}, u32[]{:S(2)}) collective-permute-start(bf16[128,2688]{1,0:T(8,128)(2,1)} %get-tuple-element.164), channel_id=1, source_target_pairs={{0,3},{1,2},{3,0},{2,1},{4,7},{5,6},{7,4},{6,5},{8,11},{9,10},{11,... | collective-permute-start | bytes 2064392 | tf_op jit(solution)/shard_map/ppermute | solution.py:93
  644.4 59.6 %collective-permute-start.62 = (bf16[128,2688]{1,0:T(8,128)(2,1)}, bf16[128,2688]{1,0:T(8,128)(2,1)}, u32[]{:S(2)}, u32[]{:S(2)}) collective-permute-start(bf16[128,2688]{1,0:T(8,128)(2,1)} %get-tuple-element.163), channel_id=1, source_target_pairs={{0,1},{1,3},{3,2},{2,0},{4,5},{5,7},{7,6},{6,4},{8,9},{9,11},{11,1... | collective-permute-start | bytes 2064392 | tf_op jit(solution)/shard_map/ppermute | solution.py:93
  759.6 161.1 %reduce-scatter.7.cloned.1.call-start = ((), (), s32[]{:S(2)}) async-start(), calls=%async_computation.7 | async-start | bytes 3686400 | tf_op jit(solution)/shard_map/reduce_scatter | solution.py:167
  813.5 151.6 %reduce-scatter.9.cloned.1.call-start = ((), (), s32[]{:S(2)}) async-start(), calls=%async_computation.8 | async-start | bytes 1474560 | tf_op jit(solution)/shard_map/reduce_scatter | solution.py:167
  881.6 35.0 %collective-permute-start.69 = (bf16[128,2560]{1,0:T(8,128)(2,1)}, bf16[128,2560]{1,0:T(8,128)(2,1)}, u32[]{:S(2)}, u32[]{:S(2)}) collective-permute-start(bf16[128,2560]{1,0:T(8,128)(2,1)} %add_convert_fusion.8), channel_id=1, source_target_pairs={{0,2},{1,0},{3,1},{2,3},{4,6},{5,4},{7,5},{6,7},{8,10},{9,8},{11,9... | collective-permute-start | bytes 1966088 | tf_op jit(solution)/shard_map/ppermute | solution.py:93
  891.2 60.8 %collective-permute-start.85 = (bf16[320,640]{1,0:T(8,128)(2,1)}, bf16[320,640]{1,0:T(8,128)(2,1)}, u32[]{:S(2)}, u32[]{:S(2)}) collective-permute-start(bf16[320,640]{1,0:T(8,128)(2,1)} %shard_map.317), channel_id=1, source_target_pairs={{0,16},{16,0},{1,17},{17,1},{2,18},{18,2},{3,19},{19,3},{4,20},{20... | collective-permute-start | bytes 1228808 | tf_op jit(solution)/shard_map/ppermute | solution.py:22
  898.9 58.9 %collective-permute-start.93 = (bf16[4,512,384]{2,1,0:T(8,128)(2,1)}, bf16[4,512,384]{2,1,0:T(8,128)(2,1)}, u32[]{:S(2)}, u32[]{:S(2)}) collective-permute-start(bf16[4,512,384]{2,1,0:T(8,128)(2,1)} %shard_map.318.refs_0_), channel_id=1, source_target_pairs={{0,16},{16,0},{1,17},{17,1},{2,18},{18,2},{3,19},{19,3},{4,20},{20... | collective-permute-start | bytes 4718600 | tf_op jit(solution)/shard_map/ppermute | solution.py:22
  (169 other events, 2476.6 us)
Sparse Core Ops, SparseCore 0:
  11.7 85.8 all-gather.2
  134.4 71.5 all-gather.4
  633.6 121.9 reduce-scatter.4
  759.7 57.7 reduce-scatter.10
  819.8 62.2 reduce-scatter.6
  920.8 37.2 reduce-scatter.8

commit v9 on v8

--- a/solution.py
+++ b/solution.py
@@ -802,13 +802,13 @@
     norm_one_parts = row_gather(norm_one)
     norm_one_all = jnp.concatenate(norm_one_parts, axis=0)
 
-    own_weights = own_share(jnp.concatenate([w_key, w_value, w_query, w_output], axis=1))
-    weights = lax.all_gather(own_weights, ("col", "exp"), tiled=True)
-    weight_in = weights[:, : query_width + 2 * key_width]
+    own_in = own_share(jnp.concatenate([w_key, w_value, w_query], axis=1))
+    weight_in = lax.all_gather(own_in, ("col", "exp"), tiled=True)
     raw = dot(norm_one_all, weight_in)
     wait = zero_of(raw)
     here = jnp.stack([e, c]).astype(jnp.int32)
-    weight_out = join_weight(weights, query_width + 2 * key_width, C, E)
+    weight_out = lax.all_gather(own_share(w_output, wait), ("col", "exp"), tiled=True)
+    weight_out = join_weight(weight_out, 0, C, E)
 
     s_width = shared_gate.shape[1] // C
     s_padded = -(-s_width // 128) * 128
@@ -847,7 +847,7 @@
     keys = rotate(raw[:, :key_width].reshape(own_rows, 1, head_width), cosines, sines)
     kv = jnp.concatenate([keys.reshape(own_rows, key_width), raw[:, key_width : 2 * key_width]], axis=1)
     kv_parts = exchange(kv.astype(bf16), "col")
-    g_block = lax.all_gather(after(out_grad, *kv_parts[1:]), "col", axis=1, tiled=True)
+    g_block = lax.all_gather(after(out_grad, *kv_parts[1:], expert_in, shared_cut), "col", axis=1, tiled=True)
     g = lax.dynamic_slice_in_dim(g_block, c * home_rows, home_rows, 0)
     queries = rotate(
         raw[:, 2 * key_width :].reshape(own_rows, group_heads, head_width), cosines, sines

time: 982 us -> 986 us (level)
    all_gather x2 -> x3, waiting for transfers between devices: 26 us -> 0.02 us  [the longest x1 0.02 us: shards(): lax.all_gather(after(out_grad, *kv_parts[1:], expert_in, shared_cut), 'co...]
    ppermute x85, waiting for transfers between devices: 281 us -> 300 us  [swap(): lax.ppermute(x, axis, [(i, i ^ step) for i in range(lax.axis_size(axis))])]
    unnamed x217 -> x191, local copies, waits for them, and re-layouts: 25 us -> 19.8 us
  transfers between devices with their start and end apart: 100 -> 101, of which waited for: 48 -> 49; matrix products, arithmetic and copies ran while one was open for 22% -> 23% of each run, Pallas kernels for 24% -> 24%
where the time goes in v9:
time: 986 us; the launch traced here: 979 us
  waiting for transfers between devices  363 us (37%)
  Pallas kernels  234 us (24%)
  matrix products  107 us (11%)
  starting transfers between devices  98.1 us (10%)
  other arithmetic  76.4 us (8%)
  local copies, waits for them, and re-layouts  69.1 us (7%)
  between operations  31.8 us (3%)
    ppermute x85, waiting for transfers between devices, swap(): lax.ppermute(x, axis, [(i, i ^ step) for i in range(lax.axis_size(axis))])  300 us
    pallas_call x4, Pallas kernels, experts_call(): pl.pallas_call(functools.partial(experts_kernel, counts, len(held) + len(...  171 us
    ppermute x85, starting transfers between devices, swap(): lax.ppermute(x, axis, [(i, i ^ step) for i in range(lax.axis_size(axis))])  89.1 us
    dot_general x4, matrix products, batch_dot(): return jnp.einsum(spec, left, right, preferred_element_type=f32)  55.7 us
    dot_general x9, matrix products, dot(): lax.dot_general(left, right, (((contract[0],), (contract[1],)), ((), ()))...  46.6 us
    ppermute x3, waiting for transfers between devices, ring_gather(): parts.append(lax.ppermute(parts[-1], axis, ring_pairs(n)))  32.2 us
    ppermute x6, waiting for transfers between devices, ring_send(): lax.ppermute(x, axis, [(order[i], order[(i - k) % n]) for i in range(n)])  31.1 us
    pallas_call x2, Pallas kernels, attention_call(): pl.pallas_call(lambda place, *refs: kernel(place, *refs[:len(operands)],...  29.1 us
  transfers between devices with their start and end apart: 101, of which 49 were waited for; matrix products, arithmetic and copies ran while one was open for 23% of the time, Pallas kernels for 24%

profile of v9, /device:TPU:9, one launch (start us, length us, event | category | flops | bytes accessed | tf_op | source)
XLA Modules:
  0.0 978.8 jit_solution(8840828417270919071)
XLA Ops:
  27.6 19.6 %collective-permute-done.2 = bf16[128,640]{1,0:T(8,128)(2,1)S(1)} collective-permute-done((bf16[128,640]{1,0:T(8,128)(2,1)S(1)}, bf16[128,640]{1,0:T(8,128)(2,1)S(1)}, u32[]{:S(2)}, u32[]{:S(2)}) %collective-permute-start.2) | collective-permute-done | bytes 163872 | tf_op jit(solution)/shard_map/ppermute | solution.py:22
  51.0 9.5 collective-permute-done.7
  93.2 9.7 shard_map.289.refs_5_.refs_4_.refs_8_.refs_12_
  107.2 19.5 %collective-permute-done.12.refs_4_.refs_3_.refs_7_ = bf16[512,256]{1,0:T(8,128)(2,1)} collective-permute-done((bf16[512,256]{1,0:T(8,128)(2,1)}, bf16[512,256]{1,0:T(8,128)(2,1)}, u32[]{:S(2)}, u32[]{:S(2)}) %collective-permute-start.12) | collective-permute-done | bytes 262176 | tf_op jit(solution)/shard_map/ppermute | solution.py:22
  128.2 12.5 %shard_map.291 = (bf16[512,640]{1,0:T(8,128)(2,1)}, f32[4,128,640]{2,1,0:T(8,128)}, f32[4,1,640]{2,1,0:T(1,128)}) custom-call(s32[6]{0:T(128)} %pad_add_fusion.place, bf16[512,640]{1,0:T(8,128)(2,1)} %copy.157.refs_0_, bf16[512,256]{1,0:T(8,128)(2,1)} %pad_maximum_fusion.7.refs_1_.refs_4_, bf16[512,256]{1,0:T(8,128)(2,1)} %copy-done.41, ...), custom_call_target="tpu_custom_call" | custom-call | flops 2684354560 | bytes 1024 | tf_op jit(solution)/shard_map/pallas_call | solution.py:496
  165.6 32.3 %collective-permute-done.17 = bf16[512,384]{1,0:T(8,128)(2,1)S(1)} collective-permute-done((bf16[512,384]{1,0:T(8,128)(2,1)S(1)}, bf16[512,384]{1,0:T(8,128)(2,1)S(1)}, u32[]{:S(2)}, u32[]{:S(2)}) %collective-permute-start.17) | collective-permute-done | bytes 393248 | tf_op jit(solution)/shard_map/ppermute | solution.py:22
  203.1 25.4 %collective-permute-done.19 = bf16[512,384]{1,0:T(8,128)(2,1)S(1)} collective-permute-done((bf16[512,384]{1,0:T(8,128)(2,1)S(1)}, bf16[512,384]{1,0:T(8,128)(2,1)S(1)}, u32[]{:S(2)}, u32[]{:S(2)}) %collective-permute-start.19) | collective-permute-done | bytes 393248 | tf_op jit(solution)/shard_map/ppermute | solution.py:22
  245.7 15.6 %collective-permute-done.20 = bf16[128,2688]{1,0:T(8,128)(2,1)} collective-permute-done((bf16[128,2688]{1,0:T(8,128)(2,1)S(1)}, bf16[128,2688]{1,0:T(8,128)(2,1)}, u32[]{:S(2)}, u32[]{:S(2)}) %collective-permute-start.20) | collective-permute-done | bytes 688160 | tf_op jit(solution)/shard_map/ppermute | solution.py:86
  263.6 14.1 %collective-permute-done.21 = bf16[128,2688]{1,0:T(8,128)(2,1)} collective-permute-done((bf16[128,2688]{1,0:T(8,128)(2,1)}, bf16[128,2688]{1,0:T(8,128)(2,1)}, u32[]{:S(2)}, u32[]{:S(2)}) %collective-permute-start.21) | collective-permute-done | bytes 688160 | tf_op jit(solution)/shard_map/ppermute | solution.py:86
  307.2 42.4 %shard_map.297 = (bf16[2,2048,2560]{2,1,0:T(8,128)(2,1)}, bf16[2,2048,2560]{2,1,0:T(8,128)(2,1)}, bf16[2,2048,384]{2,1,0:T(8,128)(2,1)}, bf16[2,2048,768]{2,1,0:...) custom-call(s32[6]{0:T(128)} %get-tuple-element.154.info, ...), custom_call_target="tpu_custom_call" | custom-call | flops 26843545600 | bytes 1024 | tf_op jit(solution)/shard_map/pallas_call | solution.py:734
  349.6 15.2 %collective-permute-done.27.refs_2_.refs_0_ = bf16[512,2688]{1,0:T(8,128)(2,1)} collective-permute-done((bf16[512,2688]{1,0:T(8,128)(2,1)}, bf16[512,2688]{1,0:T(8,128)(2,1)}, u32[]{:S(2)}, u32[]{:S(2)}) %collective-permute-start.27) | collective-permute-done | bytes 2752544 | tf_op jit(solution)/shard_map/ppermute | solution.py:22
  379.4 42.8 %shard_map.299 = (bf16[2,2048,2560]{2,1,0:T(8,128)(2,1)}, bf16[2,2048,2560]{2,1,0:T(8,128)(2,1)}, bf16[2,2048,384]{2,1,0:T(8,128)(2,1)}, bf16[2,2048,768]{2,1,0:...) custom-call(s32[6]{0:T(128)} %get-tuple-element.228.info, ...), custom_call_target="tpu_custom_call", output_to_operand_aliasing={{0}: (13, {}), {1}: (14, {}), {2}: (15, {}), {3}: (16, {}),... | custom-call | flops 26843545600 | bytes 1024 | tf_op jit(solution)/shard_map/pallas_call | solution.py:734
  437.6 42.7 %shard_map.301 = (bf16[2,2048,2560]{2,1,0:T(8,128)(2,1)}, bf16[2,2048,2560]{2,1,0:T(8,128)(2,1)}, bf16[2,2048,384]{2,1,0:T(8,128)(2,1)}, bf16[2,2048,768]{2,1,0:...) custom-call(s32[6]{0:T(128)} %get-tuple-element.229.info, ...), custom_call_target="tpu_custom_call", output_to_operand_aliasing={{0}: (13, {}), {1}: (14, {}), {2}: (15, {}), {3}: (16, {}),... | custom-call | flops 26843545600 | bytes 1024 | tf_op jit(solution)/shard_map/pallas_call | solution.py:734
  493.5 42.9 %shard_map.302 = (bf16[2,2048,2560]{2,1,0:T(8,128)(2,1)}, bf16[2,2048,2560]{2,1,0:T(8,128)(2,1)}, bf16[2,2048,384]{2,1,0:T(8,128)(2,1)}, bf16[2,2048,768]{2,1,0:...) custom-call(s32[6]{0:T(128)} %get-tuple-element.230.info, ...), custom_call_target="tpu_custom_call", output_to_operand_aliasing={{0}: (17, {}), {1}: (18, {}), {2}: (19, {}), {3}: (20, {}),... | custom-call | flops 26843545600 | bytes 1024 | tf_op jit(solution)/shard_map/pallas_call | solution.py:734
  536.5 8.4 convolution_convert_fusion.5.refs_1_
  544.9 7.1 convolution_convert_fusion.2.refs_0_
  574.6 13.2 %collective-permute-done.57 = bf16[512,384]{1,0:T(8,128)(2,1)S(1)} collective-permute-done((bf16[512,384]{1,0:T(8,128)(2,1)S(1)}, bf16[512,384]{1,0:T(8,128)(2,1)S(1)}, u32[]{:S(2)}, u32[]{:S(2)}) %collective-permute-start.57) | collective-permute-done | bytes 393248 | tf_op jit(solution)/shard_map/ppermute | solution.py:22
  587.8 10.4 %collective-permute-done.58 = bf16[512,384]{1,0:T(8,128)(2,1)S(1)} collective-permute-done((bf16[512,384]{1,0:T(8,128)(2,1)S(1)}, bf16[512,384]{1,0:T(8,128)(2,1)S(1)}, u32[]{:S(2)}, u32[]{:S(2)}) %collective-permute-start.58) | collective-permute-done | bytes 393248 | tf_op jit(solution)/shard_map/ppermute | solution.py:22
  598.2 9.5 collective-permute-done.59
  609.0 11.0 %add_convert_fusion.refs_0_ = bf16[2048,2560]{1,0:T(8,128)(2,1)} fusion(bf16[2048,2560]{1,0:T(8,128)(2,1)S(1)} %collective-permute-done.55, bf16[2048,2560]{1,0:T(8,128)(2,1)} %get-tuple-element.114), kind=kLoop, calls=%fused_computation.2 | loop fusion | flops 20971520 | bytes 31457280 | tf_op jit(solution)/shard_map/convert_element_type | solution.py:942
  620.0 14.6 %collective-permute-done.56.refs_1_ = bf16[512,2688]{1,0:T(8,128)(2,1)} collective-permute-done((bf16[512,2688]{1,0:T(8,128)(2,1)S(1)}, bf16[512,2688]{1,0:T(8,128)(2,1)}, u32[]{:S(2)}, u32[]{:S(2)}) %collective-permute-start.56) | collective-permute-done | bytes 2752544 | tf_op jit(solution)/shard_map/ppermute | solution.py:22
  647.6 18.4 %fusion = f32[2,2560,384]{2,1,0:T(8,128)} fusion(bf16[2,2048,2560]{2,1,0:T(8,128)(2,1)} %get-tuple-element.124, bf16[2,2048,768]{2,1,0:T(8,128)(2,1)} %shard_map.307), kind=kOutput, calls=%fused_computation.14 | convolution fusion | flops 8053063680 | bytes 31981568 | tf_op jit(solution)/shard_map/lrd,lrf->ldf/dot_general | solution.py:193
  666.0 18.4 %fusion.2 = f32[2,2560,384]{2,1,0:T(8,128)} fusion(bf16[2,2048,2560]{2,1,0:T(8,128)(2,1)} %get-tuple-element.124, bf16[2,2048,768]{2,1,0:T(8,128)(2,1)} %shard_map.307), kind=kOutput, calls=%fused_computation.16 | convolution fusion | flops 8053063680 | bytes 31981568 | tf_op jit(solution)/shard_map/lrd,lrf->ldf/dot_general | solution.py:193
  684.4 15.3 %fusion.83 = f32[2,384,2560]{2,1,0:T(8,128)S(1)} fusion(bf16[2,2048,384]{2,1,0:T(8,128)(2,1)} %shard_map.308, bf16[2,2048,2560]{2,1,0:T(8,128)(2,1)} %get-tuple-element.127), kind=kOutput, calls=%fused_computation.272 | convolution fusion | flops 8053063680 | bytes 31981568 | tf_op jit(solution)/shard_map/lrf,lrd->lfd/dot_general | solution.py:193
  716.4 28.3 %collective-permute-done.64 = bf16[128,2560]{1,0:T(8,128)(2,1)S(1)} collective-permute-done((bf16[128,2560]{1,0:T(8,128)(2,1)S(1)}, bf16[128,2560]{1,0:T(8,128)(2,1)S(1)}, u32[]{:S(2)}, u32[]{:S(2)}) %collective-permute-start.64) | collective-permute-done | bytes 655392 | tf_op jit(solution)/shard_map/ppermute | solution.py:22
  746.5 12.7 %collective-permute-done.65 = bf16[64,2560]{1,0:T(8,128)(2,1)S(1)} collective-permute-done((bf16[64,2560]{1,0:T(8,128)(2,1)S(1)}, bf16[64,2560]{1,0:T(8,128)(2,1)S(1)}, u32[]{:S(2)}, u32[]{:S(2)}) %collective-permute-start.65) | collective-permute-done | bytes 327712 | tf_op jit(solution)/shard_map/ppermute | solution.py:22
  774.0 16.6 %shard_map.310 = (f32[512,640]{1,0:T(8,128)}, bf16[4,512,256]{2,1,0:T(8,128)(2,1)}) custom-call(s32[6]{0:T(128)} %pad_add_fusion.place, bf16[512,640]{1,0:T(8,128)(2,1)} %copy.157.refs_0_, bf16[512,640]{1,0:T(8,128)(2,1)} %convolution_convert_fusion.6.refs_1_, f32[4,128,640]{2,1,0:T(8,128)} %get-tuple-element.128.refs_2_, ...), custom_call_target="tpu_custom_call" | custom-call | flops 6710886400 | bytes 1024 | tf_op jit(solution)/shard_map/pallas_call | solution.py:496
  794.5 10.4 %collective-permute-done.67.refs_1_ = bf16[128,2560]{1,0:T(8,128)(2,1)S(1)} collective-permute-done((bf16[128,2560]{1,0:T(8,128)(2,1)}, bf16[128,2560]{1,0:T(8,128)(2,1)S(1)}, u32[]{:S(2)}, u32[]{:S(2)}) %collective-permute-start.67) | collective-permute-done | bytes 655392 | tf_op jit(solution)/shard_map/ppermute | solution.py:93
  816.3 9.6 collective-permute-done.70
  828.2 10.6 %collective-permute-done.72 = bf16[512,256]{1,0:T(8,128)(2,1)} collective-permute-done((bf16[512,256]{1,0:T(8,128)(2,1)}, bf16[512,256]{1,0:T(8,128)(2,1)}, u32[]{:S(2)}, u32[]{:S(2)}) %collective-permute-start.72) | collective-permute-done | bytes 262176 | tf_op jit(solution)/shard_map/ppermute | solution.py:22
  862.0 20.6 %collective-permute-done.68 = bf16[128,2560]{1,0:T(8,128)(2,1)} collective-permute-done((bf16[128,2560]{1,0:T(8,128)(2,1)}, bf16[128,2560]{1,0:T(8,128)(2,1)}, u32[]{:S(2)}, u32[]{:S(2)}) %collective-permute-start.68) | collective-permute-done | bytes 655392 | tf_op jit(solution)/shard_map/ppermute | solution.py:93
  944.9 10.8 %collective-permute-done.82 = bf16[128,640]{1,0:T(8,128)(2,1)S(1)} collective-permute-done((bf16[128,640]{1,0:T(8,128)(2,1)S(1)}, bf16[128,640]{1,0:T(8,128)(2,1)S(1)}, u32[]{:S(2)}, u32[]{:S(2)}) %collective-permute-start.82) | collective-permute-done | bytes 163872 | tf_op jit(solution)/shard_map/ppermute | solution.py:22
  (585 shorter events, 356.9 us)
Async XLA Ops:
  7.2 64.4 %all-gather.4.cloned.1.call-start = ((), (), s32[]{:S(2)}) async-start(), calls=%async_computation.4 | async-start | bytes 5160960 | tf_op jit(solution)/shard_map/all_gather | solution.py:806
  11.3 129.4 %all-gather.6.cloned.1.call-start = ((), (), s32[]{:S(2)}) async-start(), calls=%async_computation.5 | async-start | bytes 3686400 | tf_op jit(solution)/shard_map/all_gather | solution.py:810
  80.3 150.8 %all-gather.8.cloned.1.call-start = ((), (), s32[]{:S(2)}) async-start(), calls=%async_computation.6 | async-start | bytes 3276800 | tf_op jit(solution)/shard_map/all_gather | solution.py:850
  89.0 37.8 %collective-permute-start.12 = (bf16[512,256]{1,0:T(8,128)(2,1)}, bf16[512,256]{1,0:T(8,128)(2,1)}, u32[]{:S(2)}, u32[]{:S(2)}) collective-permute-start(bf16[512,256]{1,0:T(8,128)(2,1)} %pad_maximum_fusion.7.refs_1_.refs_4_), channel_id=1, source_target_pairs={{0,3},{1,2},{2,1},{3,0},{4,7},{5,6},{6,5},{7,4},{8,11},{9,10},{10,... | collective-permute-start | bytes 786440 | tf_op jit(solution)/shard_map/ppermute | solution.py:22
  126.8 645.0 %reduce-scatter.5.cloned.1.call-start = ((), (), s32[]{:S(2)}) async-start(), calls=%async_computation.7 | async-start | bytes 13107200 | tf_op jit(solution)/shard_map/reduce_scatter | solution.py:943
  155.2 84.5 %collective-permute-start.14 = (bf16[128,2560]{1,0:T(8,128)(2,1)S(1)}, bf16[128,2560]{1,0:T(8,128)(2,1)}, u32[]{:S(2)}, u32[]{:S(2)}) collective-permute-start(bf16[128,2560]{1,0:T(8,128)(2,1)S(1)} %pad_maximum_fusion.3), channel_id=1, source_target_pairs={{0,4},{4,0},{8,12},{12,8},{1,5},{5,1},{9,13},{13,9},{2,6},{6,2},{1... | collective-permute-start | bytes 1966088 | tf_op jit(solution)/shard_map/ppermute | solution.py:22
  156.6 83.0 %collective-permute-start.16 = (bf16[128,2560]{1,0:T(8,128)(2,1)S(1)}, bf16[128,2560]{1,0:T(8,128)(2,1)S(1)}, u32[]{:S(2)}, u32[]{:S(2)}) collective-permute-start(bf16[128,2560]{1,0:T(8,128)(2,1)S(1)} %pad_maximum_fusion.4), channel_id=1, source_target_pairs={{0,8},{4,12},{8,0},{12,4},{1,9},{5,13},{9,1},{13,5},{2,10},{6,14},... | collective-permute-start | bytes 1966088 | tf_op jit(solution)/shard_map/ppermute | solution.py:22
  159.6 38.3 %collective-permute-start.17 = (bf16[512,384]{1,0:T(8,128)(2,1)S(1)}, bf16[512,384]{1,0:T(8,128)(2,1)S(1)}, u32[]{:S(2)}, u32[]{:S(2)}) collective-permute-start(bf16[512,384]{1,0:T(8,128)(2,1)S(1)} %get-tuple-element.186), channel_id=1, source_target_pairs={{0,1},{1,0},{2,3},{3,2},{4,5},{5,4},{6,7},{7,6},{8,9},{9,8},{10,11... | collective-permute-start | bytes 1179656 | tf_op jit(solution)/shard_map/ppermute | solution.py:22
  164.2 36.3 %collective-permute-start.18 = (bf16[512,384]{1,0:T(8,128)(2,1)S(1)}, bf16[512,384]{1,0:T(8,128)(2,1)S(1)}, u32[]{:S(2)}, u32[]{:S(2)}) collective-permute-start(bf16[512,384]{1,0:T(8,128)(2,1)S(1)} %get-tuple-element.185), channel_id=1, source_target_pairs={{0,2},{1,3},{2,0},{3,1},{4,6},{5,7},{6,4},{7,5},{8,10},{9,11},{10,... | collective-permute-start | bytes 1179656 | tf_op jit(solution)/shard_map/ppermute | solution.py:22
  165.1 63.4 %collective-permute-start.19 = (bf16[512,384]{1,0:T(8,128)(2,1)S(1)}, bf16[512,384]{1,0:T(8,128)(2,1)S(1)}, u32[]{:S(2)}, u32[]{:S(2)}) collective-permute-start(bf16[512,384]{1,0:T(8,128)(2,1)S(1)} %get-tuple-element.184), channel_id=1, source_target_pairs={{0,3},{1,2},{2,1},{3,0},{4,7},{5,6},{6,5},{7,4},{8,11},{9,10},{10,... | collective-permute-start | bytes 1179656 | tf_op jit(solution)/shard_map/ppermute | solution.py:22
  233.6 67.0 %collective-permute-start.23 = (bf16[512,2560]{1,0:T(8,128)(2,1)}, bf16[512,2560]{1,0:T(8,128)(2,1)}, u32[]{:S(2)}, u32[]{:S(2)}) collective-permute-start(bf16[512,2560]{1,0:T(8,128)(2,1)} %all-gather.8.cloned.1.call-done.refs_4_), channel_id=1, source_target_pairs={{0,4},{4,0},{8,12},{12,8},{1,5},{5,1},{9,13},{13,9},{2,6},{6,2},{1... | collective-permute-start | bytes 7864328 | tf_op jit(solution)/shard_map/ppermute | solution.py:22
  234.5 66.1 %collective-permute-start.24 = (bf16[512,2560]{1,0:T(8,128)(2,1)}, bf16[512,2560]{1,0:T(8,128)(2,1)}, u32[]{:S(2)}, u32[]{:S(2)}) collective-permute-start(bf16[512,2560]{1,0:T(8,128)(2,1)} %all-gather.8.cloned.1.call-done.refs_4_), channel_id=1, source_target_pairs={{0,8},{4,12},{8,0},{12,4},{1,9},{5,13},{9,1},{13,5},{2,10},{6,14},... | collective-permute-start | bytes 7864328 | tf_op jit(solution)/shard_map/ppermute | solution.py:22
  235.8 65.3 %collective-permute-start.25 = (bf16[512,2560]{1,0:T(8,128)(2,1)}, bf16[512,2560]{1,0:T(8,128)(2,1)}, u32[]{:S(2)}, u32[]{:S(2)}) collective-permute-start(bf16[512,2560]{1,0:T(8,128)(2,1)} %all-gather.8.cloned.1.call-done.refs_4_), channel_id=1, source_target_pairs={{0,16},{16,0},{1,17},{17,1},{2,18},{18,2},{3,19},{19,3},{4,20},{20... | collective-permute-start | bytes 7864328 | tf_op jit(solution)/shard_map/ppermute | solution.py:22
  245.6 35.6 %collective-permute-start.26 = (bf16[4,512,384]{2,1,0:T(8,128)(2,1)S(1)}, bf16[4,512,384]{2,1,0:T(8,128)(2,1)}, u32[]{:S(2)}, u32[]{:S(2)}) collective-permute-start(bf16[4,512,384]{2,1,0:T(8,128)(2,1)S(1)} %pad_maximum_fusion.1.refs_0_), channel_id=1, source_target_pairs={{0,16},{16,0},{1,17},{17,1},{2,18},{18,2},{3,19},{19,3},{4,20},{20... | collective-permute-start | bytes 4718600 | tf_op jit(solution)/shard_map/ppermute | solution.py:22
  303.5 61.3 %collective-permute-start.27 = (bf16[512,2688]{1,0:T(8,128)(2,1)}, bf16[512,2688]{1,0:T(8,128)(2,1)}, u32[]{:S(2)}, u32[]{:S(2)}) collective-permute-start(bf16[512,2688]{1,0:T(8,128)(2,1)} %shard_map.296.refs_0_.refs_2_), channel_id=1, source_target_pairs={{0,8},{4,12},{8,0},{12,4},{1,9},{5,13},{9,1},{13,5},{2,10},{6,14},... | collective-permute-start | bytes 8257544 | tf_op jit(solution)/shard_map/ppermute | solution.py:22
  304.3 61.1 %collective-permute-start.29 = (bf16[512,2688]{1,0:T(8,128)(2,1)}, bf16[512,2688]{1,0:T(8,128)(2,1)}, u32[]{:S(2)}, u32[]{:S(2)}) collective-permute-start(bf16[512,2688]{1,0:T(8,128)(2,1)} %shard_map.296.refs_0_.refs_2_), channel_id=1, source_target_pairs={{0,4},{4,0},{8,12},{12,8},{1,5},{5,1},{9,13},{13,9},{2,6},{6,2},{1... | collective-permute-start | bytes 8257544 | tf_op jit(solution)/shard_map/ppermute | solution.py:22
  370.2 52.1 %collective-permute-start.28 = (bf16[256,2688]{1,0:T(8,128)(2,1)S(1)}, bf16[256,2688]{1,0:T(8,128)(2,1)S(1)}, u32[]{:S(2)}, u32[]{:S(2)}) collective-permute-start(bf16[256,2688]{1,0:T(8,128)(2,1)S(1)} %slice.333), channel_id=1, source_target_pairs={{0,4},{4,0},{8,12},{12,8},{1,5},{5,1},{9,13},{13,9},{2,6},{6,2},{1... | collective-permute-start | bytes 4128776 | tf_op jit(solution)/shard_map/ppermute | solution.py:22
  372.8 49.5 %collective-permute-start.30 = (bf16[256,2688]{1,0:T(8,128)(2,1)S(1)}, bf16[256,2688]{1,0:T(8,128)(2,1)}, u32[]{:S(2)}, u32[]{:S(2)}) collective-permute-start(bf16[256,2688]{1,0:T(8,128)(2,1)S(1)} %slice.334), channel_id=1, source_target_pairs={{0,8},{4,12},{8,0},{12,4},{1,9},{5,13},{9,1},{13,5},{2,10},{6,14},... | collective-permute-start | bytes 4128776 | tf_op jit(solution)/shard_map/ppermute | solution.py:22
  427.6 53.2 %collective-permute-start.33 = (bf16[256,2560]{1,0:T(8,128)(2,1)}, bf16[256,2560]{1,0:T(8,128)(2,1)S(1)}, u32[]{:S(2)}, u32[]{:S(2)}) collective-permute-start(bf16[256,2560]{1,0:T(8,128)(2,1)} %slice.335), channel_id=1, source_target_pairs={{0,4},{4,0},{8,12},{12,8},{1,5},{5,1},{9,13},{13,9},{2,6},{6,2},{1... | collective-permute-start | bytes 3932168 | tf_op jit(solution)/shard_map/ppermute | solution.py:22
  430.1 51.8 %collective-permute-start.34 = (bf16[256,2560]{1,0:T(8,128)(2,1)S(1)}, bf16[256,2560]{1,0:T(8,128)(2,1)S(1)}, u32[]{:S(2)}, u32[]{:S(2)}) collective-permute-start(bf16[256,2560]{1,0:T(8,128)(2,1)S(1)} %slice.336), channel_id=1, source_target_pairs={{0,8},{4,12},{8,0},{12,4},{1,9},{5,13},{9,1},{13,5},{2,10},{6,14},... | collective-permute-start | bytes 3932168 | tf_op jit(solution)/shard_map/ppermute | solution.py:22
  484.4 72.5 %collective-permute-start.51 = (bf16[512,2688]{1,0:T(8,128)(2,1)}, bf16[512,2688]{1,0:T(8,128)(2,1)}, u32[]{:S(2)}, u32[]{:S(2)}) collective-permute-start(bf16[512,2688]{1,0:T(8,128)(2,1)} %add_convert_fusion.4.refs_22_), channel_id=1, source_target_pairs={{0,4},{4,0},{8,12},{12,8},{1,5},{5,1},{9,13},{13,9},{2,6},{6,2},{1... | collective-permute-start | bytes 8257544 | tf_op jit(solution)/shard_map/ppermute | solution.py:22
  489.1 67.9 %collective-permute-start.52 = (bf16[512,2688]{1,0:T(8,128)(2,1)S(1)}, bf16[512,2688]{1,0:T(8,128)(2,1)}, u32[]{:S(2)}, u32[]{:S(2)}) collective-permute-start(bf16[512,2688]{1,0:T(8,128)(2,1)S(1)} %add_convert_fusion.3.refs_26_), channel_id=1, source_target_pairs={{0,8},{4,12},{8,0},{12,4},{1,9},{5,13},{9,1},{13,5},{2,10},{6,14},... | collective-permute-start | bytes 8257544 | tf_op jit(solution)/shard_map/ppermute | solution.py:22
  568.3 40.7 %collective-permute-start.55 = (bf16[2048,2560]{1,0:T(8,128)(2,1)}, bf16[2048,2560]{1,0:T(8,128)(2,1)S(1)}, u32[]{:S(2)}, u32[]{:S(2)}) collective-permute-start(bf16[2048,2560]{1,0:T(8,128)(2,1)} %shard_map.305), channel_id=1, source_target_pairs={{0,16},{16,0},{1,17},{17,1},{2,18},{18,2},{3,19},{19,3},{4,20},{20... | collective-permute-start | bytes 31457288 | tf_op jit(solution)/shard_map/ppermute | solution.py:22
  573.3 61.3 %collective-permute-start.56 = (bf16[512,2688]{1,0:T(8,128)(2,1)S(1)}, bf16[512,2688]{1,0:T(8,128)(2,1)}, u32[]{:S(2)}, u32[]{:S(2)}) collective-permute-start(bf16[512,2688]{1,0:T(8,128)(2,1)S(1)} %copy-done.15), channel_id=1, source_target_pairs={{0,12},{4,8},{8,4},{12,0},{1,13},{5,9},{9,5},{13,1},{2,14},{6,10},... | collective-permute-start | bytes 8257544 | tf_op jit(solution)/shard_map/ppermute | solution.py:22
  634.6 261.3 %reduce-scatter.11.cloned.1.call-start = ((), (), s32[]{:S(2)}) async-start(), calls=%async_computation.10 | async-start | bytes 3686400 | tf_op jit(solution)/shard_map/reduce_scatter | solution.py:167
  643.1 64.9 %collective-permute-start.60 = (bf16[128,2688]{1,0:T(8,128)(2,1)}, bf16[128,2688]{1,0:T(8,128)(2,1)S(1)}, u32[]{:S(2)}, u32[]{:S(2)}) collective-permute-start(bf16[128,2688]{1,0:T(8,128)(2,1)} %get-tuple-element.162), channel_id=1, source_target_pairs={{0,2},{1,0},{3,1},{2,3},{4,6},{5,4},{7,5},{6,7},{8,10},{9,8},{11,9... | collective-permute-start | bytes 2064392 | tf_op jit(solution)/shard_map/ppermute | solution.py:93
  644.7 63.3 %collective-permute-start.61 = (bf16[128,2688]{1,0:T(8,128)(2,1)}, bf16[128,2688]{1,0:T(8,128)(2,1)}, u32[]{:S(2)}, u32[]{:S(2)}) collective-permute-start(bf16[128,2688]{1,0:T(8,128)(2,1)} %get-tuple-element.164), channel_id=1, source_target_pairs={{0,3},{1,2},{3,0},{2,1},{4,7},{5,6},{7,4},{6,5},{8,11},{9,10},{11,... | collective-permute-start | bytes 2064392 | tf_op jit(solution)/shard_map/ppermute | solution.py:93
  646.3 61.7 %collective-permute-start.62 = (bf16[128,2688]{1,0:T(8,128)(2,1)}, bf16[128,2688]{1,0:T(8,128)(2,1)}, u32[]{:S(2)}, u32[]{:S(2)}) collective-permute-start(bf16[128,2688]{1,0:T(8,128)(2,1)} %get-tuple-element.163), channel_id=1, source_target_pairs={{0,1},{1,3},{3,2},{2,0},{4,5},{5,7},{7,6},{6,4},{8,9},{9,11},{11,1... | collective-permute-start | bytes 2064392 | tf_op jit(solution)/shard_map/ppermute | solution.py:93
  762.9 161.6 %reduce-scatter.7.cloned.1.call-start = ((), (), s32[]{:S(2)}) async-start(), calls=%async_computation.8 | async-start | bytes 3686400 | tf_op jit(solution)/shard_map/reduce_scatter | solution.py:167
  816.2 152.9 %reduce-scatter.9.cloned.1.call-start = ((), (), s32[]{:S(2)}) async-start(), calls=%async_computation.9 | async-start | bytes 1474560 | tf_op jit(solution)/shard_map/reduce_scatter | solution.py:167
  896.0 59.8 %collective-permute-start.85 = (bf16[320,640]{1,0:T(8,128)(2,1)}, bf16[320,640]{1,0:T(8,128)(2,1)}, u32[]{:S(2)}, u32[]{:S(2)}) collective-permute-start(bf16[320,640]{1,0:T(8,128)(2,1)} %shard_map.317), channel_id=1, source_target_pairs={{0,16},{16,0},{1,17},{17,1},{2,18},{18,2},{3,19},{19,3},{4,20},{20... | collective-permute-start | bytes 1228808 | tf_op jit(solution)/shard_map/ppermute | solution.py:22
  902.6 59.3 %collective-permute-start.93 = (bf16[4,512,384]{2,1,0:T(8,128)(2,1)}, bf16[4,512,384]{2,1,0:T(8,128)(2,1)}, u32[]{:S(2)}, u32[]{:S(2)}) collective-permute-start(bf16[4,512,384]{2,1,0:T(8,128)(2,1)} %shard_map.318.refs_0_), channel_id=1, source_target_pairs={{0,16},{16,0},{1,17},{17,1},{2,18},{18,2},{3,19},{19,3},{4,20},{20... | collective-permute-start | bytes 4718600 | tf_op jit(solution)/shard_map/ppermute | solution.py:22
  (157 other events, 2407.6 us)
Sparse Core Ops, SparseCore 0:
  11.5 59.3 all-gather.3
  80.5 58.1 all-gather.5
  140.8 83.1 all-gather.7
  634.8 123.9 reduce-scatter.4
  763.1 58.4 reduce-scatter.10
  823.8 61.6 reduce-scatter.6
  924.7 37.7 reduce-scatter.8
